TPU v7x, 32 devices: a whole 2x2x4 slice. The times are simulated.
32 devices in a mesh: elem: 16 (over z, y, x), band: 2 (over core).
Axes of the slice: x: 2, y: 2, z: 4, core: 2. Of those that a mesh axis runs over, the one named last changes fastest.
Arguments:
- orbitals: bfloat16 [2048, 2, 1536], P('elem', None, 'band'), may hold values from -6 to 6
- elem_count: int32 [16], P('elem'), may hold values from 1 to 4, as said below
- connectivity: int32 [16, 4, 343], P('elem'), may hold values from 0 to 383
- elem_coef: float32 [16, 4], P('elem'), may hold values from 0.5 to 2
- elem_matrix: bfloat16 [343, 343], replicated, may hold values from -1 to 1, as said below
- potential: float32 [2048], P('elem'), may hold values from -1 to 1
- absorber: float32 [2048], P('elem'), may hold values from 0.05 to 1
- rotation: bfloat16 [1536, 2, 512], replicated, may hold values from -0.109375 to 0.109375
Outputs:
- filtered: bfloat16 [2048, 2, 1536], P('elem', None, 'band')
- rotated: bfloat16 [2048, 2, 512], P('elem', None, 'band')
- intersection: float32 [1536, 2, 512], P('band')
Inputs may be any that keep to these rules, and one draw needn't show every extreme that they name: Each block has between 1 and 4 live elements; the first elem_count[b] slots are live. `connectivity`: indices 0 to 127 name the previous block's last owned nodes, 128 to 255 the block's own nodes, the rest the next block's first nodes. `elem_matrix`: symmetric.
All inputs are finite; a program needn't handle non-finite values.
Results may differ from a plain program's by a relative error of at most 0.0055.
Values may be sent and summed in bfloat16 or wider, within the bound.
No kernel may reach another device: no remote copies, remote signals or barrier semaphores. Data moves between devices by JAX's collectives and lax.ppermute only.
A program may use at most 64 MiB of HBM per device.

v0:
```python
import jax
import jax.numpy as jnp
from jax import lax
from jax.sharding import PartitionSpec as P

FACE = 128


FILTER_CENTER = 1.0
FILTER_HALF = 4.0


def with_halo(block, sides, width):
    for axis, dim in sides:
        count = lax.axis_size(axis)
        forward = [(i, i + 1) for i in range(count - 1)]
        backward = [(target, source) for source, target in forward]
        low = lax.ppermute(
            lax.slice_in_dim(block, block.shape[dim] - width, None, axis=dim), axis, forward
        )
        high = lax.ppermute(lax.slice_in_dim(block, 0, width, axis=dim), axis, backward)
        block = jnp.concatenate([low, block, high], axis=dim)
    return block


def assemble(field, elem_count, connectivity, elem_coef, elem_matrix):
    extended = with_halo(field, (("elem", 0),), FACE)
    rows_ext = extended.shape[0]
    flat_field = extended.reshape(rows_ext, -1)
    initial = jnp.zeros((rows_ext, flat_field.shape[1]), jnp.float32)

    def one_element(element, totals):
        node_ids = connectivity[0, element]
        product = jnp.dot(elem_matrix, flat_field[node_ids], preferred_element_type=jnp.float32)
        return totals.at[node_ids].add(product * elem_coef[0, element])

    totals = lax.fori_loop(0, elem_count[0], one_element, initial)
    edges = jnp.concatenate([totals[:FACE], totals[rows_ext - FACE :]], axis=0)
    returned = with_halo(edges, (("elem", 0),), FACE)
    owned = totals[FACE : rows_ext - FACE]
    owned = owned.at[:FACE].add(returned[:FACE])
    owned = owned.at[owned.shape[0] - FACE :].add(returned[returned.shape[0] - FACE :])
    return owned.reshape(field.shape)


def hamiltonian(field, elem_count, connectivity, elem_coef, elem_matrix, potential, absorber):
    summed = assemble(field, elem_count, connectivity, elem_coef, elem_matrix)
    vector = field.astype(jnp.float32)
    pot_col = potential[:, None]
    cap_col = absorber[:, None]
    ham_re = summed[:, 0] + pot_col * vector[:, 0] + cap_col * vector[:, 1]
    ham_im = summed[:, 1] + pot_col * vector[:, 1] - cap_col * vector[:, 0]
    return (ham_re, ham_im, vector)


def complex_block(rot_part):
    rot_re = rot_part[:, 0]
    rot_im = rot_part[:, 1]
    return jnp.concatenate(
        [jnp.concatenate([rot_re, rot_im], axis=1), jnp.concatenate([-rot_im, rot_re], axis=1)],
        axis=0,
    )


def on_device(
    orbitals, elem_count, connectivity, elem_coef, elem_matrix, potential, absorber, rotation
):
    node_rows = orbitals.shape[0]
    band_dev = orbitals.shape[2]
    panel_all = rotation.shape[2]
    ham_re, ham_im, vector = hamiltonian(
        orbitals, elem_count, connectivity, elem_coef, elem_matrix, potential, absorber
    )
    first = jnp.stack(
        [
            (ham_re - FILTER_CENTER * vector[:, 0]) / FILTER_HALF,
            (ham_im - FILTER_CENTER * vector[:, 1]) / FILTER_HALF,
        ],
        axis=1,
    ).astype(jnp.bfloat16)
    ham_re, ham_im, inner = hamiltonian(
        first, elem_count, connectivity, elem_coef, elem_matrix, potential, absorber
    )
    anchor = orbitals.astype(jnp.float32)
    filtered = jnp.stack(
        [
            2.0 * (ham_re - FILTER_CENTER * inner[:, 0]) / FILTER_HALF - anchor[:, 0],
            2.0 * (ham_im - FILTER_CENTER * inner[:, 1]) / FILTER_HALF - anchor[:, 1],
        ],
        axis=1,
    ).astype(jnp.bfloat16)
    flat_bands = filtered.reshape(node_rows, 2 * band_dev)
    cols_dev = panel_all // lax.axis_size("band")
    col_start = lax.axis_index("band") * cols_dev
    rot_mine = lax.dynamic_slice_in_dim(rotation, col_start, cols_dev, 2)
    shard_piece = lax.all_gather(filtered, "band", axis=2, tiled=True)
    piece_width = shard_piece.shape[2]
    piece_flat = shard_piece.reshape(node_rows, 2 * piece_width)
    product = jnp.dot(piece_flat, complex_block(rot_mine), preferred_element_type=jnp.float32)
    panel_part = product.reshape(node_rows, 2, cols_dev)
    rotated = panel_part.astype(jnp.bfloat16)
    inverse_root = 1.0 / jnp.sqrt(jnp.float32(node_rows * lax.axis_size("elem")))
    shard_piece = lax.all_gather(rotated, "band", axis=2, tiled=True)
    piece_width = shard_piece.shape[2]
    piece_flat = shard_piece.reshape(node_rows, 2 * piece_width)
    products = lax.dot_general(
        flat_bands, piece_flat, (((0,), (0,)), ((), ())), preferred_element_type=jnp.float32
    )
    products = products.reshape(2, band_dev, 2, piece_width)
    over_re = products[0, :, 0] - products[1, :, 1]
    over_im = products[0, :, 1] + products[1, :, 0]
    local_intersection = jnp.stack([over_re, over_im], axis=1) * inverse_root
    intersection = lax.psum(local_intersection, "elem")
    return (filtered, rotated, intersection)


def solution(mesh):
    placed = (
        P("elem", None, "band"),
        P("elem"),
        P("elem", None, None),
        P("elem", None),
        P(),
        P("elem"),
        P("elem"),
        P(),
    )
    return jax.shard_map(
        on_device,
        mesh=mesh,
        in_specs=placed,
        out_specs=(P("elem", None, "band"), P("elem", None, "band"), P("band", None, None)),
        check_vma=False,
    )
```

profile of v0, /device:TPU:0, one launch (start us, length us, event | category | flops | bytes accessed | tf_op | source)
XLA Modules:
  0.0 433.2 jit_solution(5810155381438130063)
XLA Ops:
  8.5 5.5 %collective-permute-start = (bf16[128,2,768]{2,1,0:T(2,128)(2,1)}, bf16[128,2,768]{2,1,0:T(2,128)(2,1)S(1)}, u32[]{:S(2)}, u32[]{:S(2)}) collective-permute-start(bf16[128,2,768]{2,1,0:T(2,128)(2,1)} %param.28), channel_id=1, source_target_pairs={{0,2},{2,4},{4,6},{6,8},{8,10},{10,12},{12,14},{14,16},{16,18},{18... | collective-permute-start | bytes 1179656 | tf_op jit(solution)/shard_map/ppermute | solution.py:18
  14.0 8.2 %collective-permute-done.1 = bf16[128,2,768]{2,1,0:T(2,128)(2,1)S(1)} collective-permute-done((bf16[128,2,768]{2,1,0:T(2,128)(2,1)}, bf16[128,2,768]{2,1,0:T(2,128)(2,1)S(1)}, u32[]{:S(2)}, u32[]{:S(2)}) %collective-permute-start.1) | collective-permute-done | bytes 393248 | tf_op jit(solution)/shard_map/ppermute | solution.py:21
  22.2 8.8 %collective-permute-done = bf16[128,2,768]{2,1,0:T(2,128)(2,1)S(1)} collective-permute-done((bf16[128,2,768]{2,1,0:T(2,128)(2,1)}, bf16[128,2,768]{2,1,0:T(2,128)(2,1)S(1)}, u32[]{:S(2)}, u32[]{:S(2)}) %collective-permute-start) | collective-permute-done | bytes 393248 | tf_op jit(solution)/shard_map/ppermute | solution.py:18
  31.0 2.6 pad_maximum_fusion
  34.3 15.1 %while.28 = (s32[]{:T(128)}, f32[384,1536]{1,0:T(8,128)S(1)}, s32[]{:T(128)}, s32[1,4,343]{2,1,0:T(4,128)S(1)}, bf16[384,1536]{1,0:T(8,128)(2,1)S(1)}, /*index=5...) while((s32[]{:T(128)}, f32[384,1536]{1,0:T(8,128)S(1)}, s32[]{:T(128)}, ...), condition=%wide.region_2.0_spmd, body=%wide.region_0.0_spmd.sunk | while | flops 362473472 | bytes 11837073 | solution.py:37
  36.2 2.8 gather_fusion
  39.0 4.0 fusion.38
  43.0 5.8 %scatter_fusion = f32[384,1536]{1,0:T(8,128)S(1)} fusion(f32[384,1536]{1,0:T(8,128)S(1)} %get-tuple-element.310, s32[343]{0:T(512)S(1)} %fusion.37, f32[343,1536]{1,0:T(8,128)} %fusion.38), kind=kCustom, calls=%fused_computation.2.clone.1 | custom fusion | flops 526848 | bytes 6323548 | tf_op jit(solution)/shard_map/while/body/scatter-add | solution.py:35
  49.5 18.8 %collective-permute-start.2 = (f32[128,1536]{1,0:T(8,128)S(1)}, f32[128,1536]{1,0:T(8,128)S(1)}, u32[]{:S(2)}, u32[]{:S(2)}) collective-permute-start(f32[128,1536]{1,0:T(8,128)S(1)} %get-tuple-element.207), channel_id=1, source_target_pairs={{0,2},{2,4},{4,6},{6,8},{8,10},{10,12},{12,14},{14,16},{16,18},{18... | collective-permute-start | bytes 2359304 | tf_op jit(solution)/shard_map/ppermute | solution.py:18
  69.9 32.1 %collective-permute-done.2 = f32[128,1536]{1,0:T(8,128)S(1)} collective-permute-done((f32[128,1536]{1,0:T(8,128)S(1)}, f32[128,1536]{1,0:T(8,128)S(1)}, u32[]{:S(2)}, u32[]{:S(2)}) %collective-permute-start.2) | collective-permute-done | bytes 786464 | tf_op jit(solution)/shard_map/ppermute | solution.py:18
  102.1 28.0 %collective-permute-done.3 = f32[128,1536]{1,0:T(8,128)S(1)} collective-permute-done((f32[128,1536]{1,0:T(8,128)S(1)}, f32[128,1536]{1,0:T(8,128)S(1)}, u32[]{:S(2)}, u32[]{:S(2)}) %collective-permute-start.3) | collective-permute-done | bytes 786464 | tf_op jit(solution)/shard_map/ppermute | solution.py:21
  132.7 2.1 multiply_convert_fusion.1
  138.0 4.8 %collective-permute-start.4 = (bf16[128,2,768]{2,1,0:T(2,128)(2,1)S(1)}, bf16[128,2,768]{2,1,0:T(2,128)(2,1)S(1)}, u32[]{:S(2)}, u32[]{:S(2)}) collective-permute-start(bf16[128,2,768]{2,1,0:T(2,128)(2,1)S(1)} %get-tuple-element.198), channel_id=1, source_target_pairs={{0,2},{2,4},{4,6},{6,8},{8,10},{10,12},{12,14},{14,16},{16,18},{18... | collective-permute-start | bytes 1179656 | tf_op jit(solution)/shard_map/ppermute | solution.py:18
  142.8 5.7 %constant_dynamic-slice_fusion.3 = (bf16[1536,1,256]{2,1,0:T(2,128)(2,1)}, bf16[1536,1,256]{2,1,0:T(2,128)(2,1)S(1)}) fusion(bf16[1536,2,512]{2,1,0:T(2,128)(2,1)} %param.35, s32[]{:T(128)S(6)} %add.133, s32[]{:T(128)S(6)} %select_n.33), kind=kLoop, calls=%fused_computation.51 | loop fusion | bytes 3145736 | tf_op jit(solution)/shard_map/slice | solution.py:58
  150.6 4.2 collective-permute-done.4
  157.0 15.1 %while.29 = (s32[]{:T(128)}, f32[384,1536]{1,0:T(8,128)S(1)}, s32[]{:T(128)}, s32[1,4,343]{2,1,0:T(4,128)S(1)}, bf16[384,1536]{1,0:T(8,128)(2,1)S(1)}, /*index=5...) while((s32[]{:T(128)}, f32[384,1536]{1,0:T(8,128)S(1)}, s32[]{:T(128)}, ...), condition=%wide.region_5.6_spmd, body=%wide.region_3.5_spmd.sunk | while | flops 362473472 | bytes 11837073 | solution.py:37
  158.9 2.8 gather_fusion.1
  161.7 4.0 fusion.42
  165.6 5.8 %scatter_fusion.1 = f32[384,1536]{1,0:T(8,128)S(1)} fusion(f32[384,1536]{1,0:T(8,128)S(1)} %get-tuple-element.340, s32[343]{0:T(512)S(1)} %fusion.41, f32[343,1536]{1,0:T(8,128)} %fusion.42), kind=kCustom, calls=%fused_computation.3.clone.1 | custom fusion | flops 526848 | bytes 6323548 | tf_op jit(solution)/shard_map/while/body/scatter-add | solution.py:35
  173.4 19.8 %collective-permute-start.6 = (f32[128,1536]{1,0:T(8,128)}, f32[128,1536]{1,0:T(8,128)}, u32[]{:S(2)}, u32[]{:S(2)}) collective-permute-start(f32[128,1536]{1,0:T(8,128)} %get-tuple-element.205), channel_id=1, source_target_pairs={{0,2},{2,4},{4,6},{6,8},{8,10},{10,12},{12,14},{14,16},{16,18},{18... | collective-permute-start | bytes 2359304 | tf_op jit(solution)/shard_map/ppermute | solution.py:18
  194.8 11.9 %maximum_bitcast_fusion = bf16[512,3072]{0,1:T(8,128)(2,1)} fusion(bf16[1536,256]{1,0:T(8,128)(2,1)S(1)} %bitcast.79, bf16[1536,256]{1,0:T(8,128)(2,1)S(1)} %get-tuple-element.195, bf16[1536,256]{1,0:T(8,128)(2,1)S(1)} %get-tuple-element.196), kind=kLoop, calls=%fused_computation.16 | loop fusion | flops 12582912 | bytes 5505024 | tf_op jit(solution)/shard_map/dot_general | solution.py:99
  206.8 4.6 %copy.17 = bf16[512,3072]{1,0:T(8,128)(2,1)} copy(bf16[512,3072]{0,1:T(8,128)(2,1)} %maximum_bitcast_fusion) | data formatting | bytes 6291456 | tf_op jit(solution)/shard_map/dot_general | solution.py:99
  211.4 15.0 %collective-permute-done.6 = f32[128,1536]{1,0:T(8,128)} collective-permute-done((f32[128,1536]{1,0:T(8,128)}, f32[128,1536]{1,0:T(8,128)}, u32[]{:S(2)}, u32[]{:S(2)}) %collective-permute-start.6) | collective-permute-done | bytes 786464 | tf_op jit(solution)/shard_map/ppermute | solution.py:18
  226.4 28.7 %collective-permute-done.7 = f32[128,1536]{1,0:T(8,128)} collective-permute-done((f32[128,1536]{1,0:T(8,128)}, f32[128,1536]{1,0:T(8,128)}, u32[]{:S(2)}, u32[]{:S(2)}) %collective-permute-start.7) | collective-permute-done | bytes 786464 | tf_op jit(solution)/shard_map/ppermute | solution.py:21
  255.1 2.4 add_add_fusion
  259.2 3.8 multiply_subtract_fusion.1
  264.5 2.4 all_gather.6
  267.4 3.1 convolution_convert_fusion
  270.5 2.3 all_gather.7
  274.7 2.0 maximum_multiply_fusion
  277.5 142.9 %all-reduce.2.cloned.1.call-done = f32[768,2,512]{2,0,1:T(8,128)} async-done(((f32[768,2,512]{2,0,1:T(8,128)}), f32[768,2,512]{2,0,1:T(8,128)}) %all-reduce.2.cloned.1.call-update) | async-done | bytes 3145744 | tf_op jit(solution)/shard_map/psum | solution.py:113
  420.4 6.0 %copy.21 = f32[768,2,512]{2,1,0:T(2,128)} copy(f32[768,2,512]{2,0,1:T(8,128)} %all-reduce.2.cloned.1.call-done) | data formatting | bytes 6291456
  (56 shorter events, 25.5 us)
Async XLA Ops:
  7.2 413.3 %all-reduce.2.cloned.1.call-start = ((), (), s32[]{:S(2)}) async-start(), calls=%async_computation | async-start | bytes 6291456 | tf_op jit(solution)/shard_map/psum | solution.py:113
  7.2 15.0 %collective-permute-start.1 = (bf16[128,2,768]{2,1,0:T(2,128)(2,1)}, bf16[128,2,768]{2,1,0:T(2,128)(2,1)S(1)}, u32[]{:S(2)}, u32[]{:S(2)}) collective-permute-start(bf16[128,2,768]{2,1,0:T(2,128)(2,1)} %param.28), channel_id=1, source_target_pairs={{2,0},{4,2},{6,4},{8,6},{10,8},{12,10},{14,12},{16,14},{18,16},{20... | collective-permute-start | bytes 1179656 | tf_op jit(solution)/shard_map/ppermute | solution.py:21
  8.5 22.5 %collective-permute-start = (bf16[128,2,768]{2,1,0:T(2,128)(2,1)}, bf16[128,2,768]{2,1,0:T(2,128)(2,1)S(1)}, u32[]{:S(2)}, u32[]{:S(2)}) collective-permute-start(bf16[128,2,768]{2,1,0:T(2,128)(2,1)} %param.28), channel_id=1, source_target_pairs={{0,2},{2,4},{4,6},{6,8},{8,10},{10,12},{12,14},{14,16},{16,18},{18... | collective-permute-start | bytes 1179656 | tf_op jit(solution)/shard_map/ppermute | solution.py:18
  33.6 0.7 copy-start.6
  49.4 20.2 %copy-start.5 = (bf16[128,2,768]{2,1,0:T(2,128)(2,1)S(1)}, bf16[128,2,768]{2,1,0:T(2,128)(2,1)}, u32[]{:S(2)}) copy-start(bf16[128,2,768]{2,1,0:T(2,128)(2,1)} %param.28) | copy-start | bytes 1179652
  49.5 52.5 %collective-permute-start.2 = (f32[128,1536]{1,0:T(8,128)S(1)}, f32[128,1536]{1,0:T(8,128)S(1)}, u32[]{:S(2)}, u32[]{:S(2)}) collective-permute-start(f32[128,1536]{1,0:T(8,128)S(1)} %get-tuple-element.207), channel_id=1, source_target_pairs={{0,2},{2,4},{4,6},{6,8},{8,10},{10,12},{12,14},{14,16},{16,18},{18... | collective-permute-start | bytes 2359304 | tf_op jit(solution)/shard_map/ppermute | solution.py:18
  68.3 61.7 %collective-permute-start.3 = (f32[128,1536]{1,0:T(8,128)S(1)}, f32[128,1536]{1,0:T(8,128)S(1)}, u32[]{:S(2)}, u32[]{:S(2)}) collective-permute-start(f32[128,1536]{1,0:T(8,128)S(1)} %get-tuple-element.208), channel_id=1, source_target_pairs={{2,0},{4,2},{6,4},{8,6},{10,8},{12,10},{14,12},{16,14},{18,16},{20... | collective-permute-start | bytes 2359304 | tf_op jit(solution)/shard_map/ppermute | solution.py:21
  69.9 62.8 %copy-start = (f32[128,2,768]{2,1,0:T(2,128)}, f32[128,2,768]{2,1,0:T(2,128)S(1)}, u32[]{:S(2)}) copy-start(f32[128,2,768]{2,1,0:T(2,128)S(1)} %convert_element_type.18) | copy-start | bytes 2359300
  69.9 62.8 %copy-start.7 = (f32[128]{0:T(128)S(1)}, f32[128]{0:T(128)}, u32[]{:S(2)}) copy-start(f32[128]{0:T(128)} %param.34) | copy-start | bytes 1540
  69.9 62.8 %copy-start.9 = (f32[128]{0:T(128)S(1)}, f32[128]{0:T(128)}, u32[]{:S(2)}) copy-start(f32[128]{0:T(128)} %param.33) | copy-start | bytes 1540
  136.7 13.9 %collective-permute-start.5 = (bf16[128,2,768]{2,1,0:T(2,128)(2,1)S(1)}, bf16[128,2,768]{2,1,0:T(2,128)(2,1)S(1)}, u32[]{:S(2)}, u32[]{:S(2)}) collective-permute-start(bf16[128,2,768]{2,1,0:T(2,128)(2,1)S(1)} %get-tuple-element.198), channel_id=1, source_target_pairs={{2,0},{4,2},{6,4},{8,6},{10,8},{12,10},{14,12},{16,14},{18,16},{20... | collective-permute-start | bytes 1179656 | tf_op jit(solution)/shard_map/ppermute | solution.py:21
  138.0 16.9 %collective-permute-start.4 = (bf16[128,2,768]{2,1,0:T(2,128)(2,1)S(1)}, bf16[128,2,768]{2,1,0:T(2,128)(2,1)S(1)}, u32[]{:S(2)}, u32[]{:S(2)}) collective-permute-start(bf16[128,2,768]{2,1,0:T(2,128)(2,1)S(1)} %get-tuple-element.198), channel_id=1, source_target_pairs={{0,2},{2,4},{4,6},{6,8},{8,10},{10,12},{12,14},{14,16},{16,18},{18... | collective-permute-start | bytes 1179656 | tf_op jit(solution)/shard_map/ppermute | solution.py:18
  172.0 22.7 %copy-start.2 = (bf16[1536,1,256]{2,1,0:T(2,128)(2,1)S(1)}, bf16[1536,1,256]{2,1,0:T(2,128)(2,1)}, u32[]{:S(2)}) copy-start(bf16[1536,1,256]{2,1,0:T(2,128)(2,1)} %get-tuple-element.201) | copy-start | bytes 2359300
  173.4 21.5 %copy-start.4 = (bf16[1536,1,256]{2,0,1:T(8,128)(2,1)S(1)}, bf16[1536,1,256]{2,0,1:T(8,128)(2,1)}, u32[]{:S(2)}) copy-start(bf16[1536,1,256]{2,0,1:T(8,128)(2,1)} %copy.32) | copy-start | bytes 2359300
  173.4 53.1 %collective-permute-start.6 = (f32[128,1536]{1,0:T(8,128)}, f32[128,1536]{1,0:T(8,128)}, u32[]{:S(2)}, u32[]{:S(2)}) collective-permute-start(f32[128,1536]{1,0:T(8,128)} %get-tuple-element.205), channel_id=1, source_target_pairs={{0,2},{2,4},{4,6},{6,8},{8,10},{10,12},{12,14},{14,16},{16,18},{18... | collective-permute-start | bytes 2359304 | tf_op jit(solution)/shard_map/ppermute | solution.py:18
  193.2 62.0 %collective-permute-start.7 = (f32[128,1536]{1,0:T(8,128)}, f32[128,1536]{1,0:T(8,128)}, u32[]{:S(2)}, u32[]{:S(2)}) collective-permute-start(f32[128,1536]{1,0:T(8,128)} %get-tuple-element.206), channel_id=1, source_target_pairs={{2,0},{4,2},{6,4},{8,6},{10,8},{12,10},{14,12},{16,14},{18,16},{20... | collective-permute-start | bytes 2359304 | tf_op jit(solution)/shard_map/ppermute | solution.py:21
  211.4 47.8 %copy-start.1 = (f32[128,2,768]{2,1,0:T(2,128)S(1)}, f32[128,2,768]{2,1,0:T(2,128)}, u32[]{:S(2)}) copy-start(f32[128,2,768]{2,1,0:T(2,128)} %copy-done) | copy-start | bytes 2359300
  211.4 47.8 %copy-start.8 = (f32[128]{0:T(128)S(1)}, f32[128]{0:T(128)}, u32[]{:S(2)}) copy-start(f32[128]{0:T(128)} %param.34) | copy-start | bytes 1540
  211.4 47.8 %copy-start.10 = (f32[128]{0:T(128)S(1)}, f32[128]{0:T(128)}, u32[]{:S(2)}) copy-start(f32[128]{0:T(128)} %param.33) | copy-start | bytes 1540
  263.9 6.5 %copy-start.3 = (bf16[128,2,768]{2,1,0:T(2,128)(2,1)}, bf16[128,2,768]{2,1,0:T(2,128)(2,1)S(1)}, u32[]{:S(2)}) copy-start(bf16[128,2,768]{2,1,0:T(2,128)(2,1)S(1)} %maximum_convert_fusion) | copy-start | bytes 1179652
Sparse Core Ops, SparseCore 0:
  276.9 143.5 all-reduce.1
where the time goes:
time: 432 us; the launch traced here: 433 us
  waiting for transfers between devices  269 us (62%)
  starting transfers between devices  54.3 us (13%)
  other arithmetic  43 us (10%)
  local copies, waits for them, and re-layouts  33.3 us (8%)
  between operations  14.4 us (3%)
  matrix products  12 us (3%)
  blocking collectives  4.62 us (1%)
    psum x1, waiting for transfers between devices, on_device(): intersection = lax.psum(local_intersection, 'elem')  143 us
    ppermute x4, waiting for transfers between devices, with_halo(): lax.ppermute(lax.slice_in_dim(block, 0, width, axis=dim), axis, backward)  66 us
    ppermute x4, waiting for transfers between devices, with_halo(): lax.ppermute(lax.slice_in_dim(block, block.shape[dim] - width, None, axis...  60.2 us
    ppermute x4, starting transfers between devices, with_halo(): lax.ppermute(lax.slice_in_dim(block, block.shape[dim] - width, None, axis...  48.9 us
    dot_general x1, other arithmetic, on_device(): jnp.dot(piece_flat, complex_block(rot_mine), preferred_element_type=jnp.f...  11.9 us
    scatter-add x2, other arithmetic, one_element(): return totals.at[node_ids].add(product * elem_coef[0, element])  11.5 us
  transfers between devices with their start and end apart: 9, of which 9 were waited for; matrix products, arithmetic and copies ran while one was open for 6% of the time, Pallas kernels for 0%

commit v1 on v0

v1 whole, which is shorter than its diff:
```python
import functools

import jax
import jax.numpy as jnp
from jax import lax
from jax.experimental import pallas as pl
from jax.experimental.pallas import tpu as pltpu
from jax.sharding import PartitionSpec as P

FILTER_CENTER = 1.0
FILTER_HALF = 4.0
GROUP = 4
BF16 = jnp.bfloat16
F32 = jnp.float32
SMALL_ROWS = 16
VMEM_LIMIT = 48 * 1024 * 1024


def up(value, step):
    return -(-value // step) * step


def kernel_call(body, out_shape, n_scalars, scratch=(), flops=0, moved=0):
    many = isinstance(out_shape, (list, tuple))
    vmem = pl.BlockSpec(memory_space=pltpu.VMEM)

    def call(scalars, *arrays):
        return pl.pallas_call(
            body,
            out_shape=out_shape,
            in_specs=[pl.BlockSpec(memory_space=pltpu.SMEM)] + [vmem] * len(arrays),
            out_specs=[vmem] * len(out_shape) if many else vmem,
            scratch_shapes=list(scratch),
            compiler_params=pltpu.CompilerParams(vmem_limit_bytes=VMEM_LIMIT),
            cost_estimate=pl.CostEstimate(flops=flops, bytes_accessed=moved, transcendentals=0),
        )(scalars, *arrays)

    return call


def pieces(value):
    top = value.astype(BF16).astype(F32)
    rest = value - top
    middle = rest.astype(BF16).astype(F32)
    return (top, middle, rest - middle)


def small_body(e_cap, elem_nodes, nodes, width, scal, conn, coef, pot, cap, out):
    out[...] = jnp.zeros(out.shape, BF16)
    ids = conn[...]
    high = ids >> 7
    out[0:e_cap, 0:elem_nodes] = (ids - (high << 7)).astype(F32).astype(BF16)
    pad = jnp.full((e_cap, width), 64.0, F32)
    out[4 : 4 + e_cap, :] = pad.astype(BF16)
    out[4 : 4 + e_cap, 0:elem_nodes] = high.astype(F32).astype(BF16)
    lane = lax.broadcasted_iota(jnp.int32, (1, e_cap), 1)
    live = jnp.where(lane < scal[3], coef[...], 0.0)
    for at, part in enumerate(pieces(live)):
        out[8 + at : 9 + at, 0:e_cap] = part.astype(BF16)
    for row, vector in ((11, pot), (12, cap)):
        for at, part in enumerate(pieces(vector[...])):
            out[row : row + 1, at * nodes : (at + 1) * nodes] = part.astype(BF16)


def pack_body(nodes, w, wp, scal, vec, small, small_low, small_high, *outs):
    mine = scal[0]
    for chunk in range(GROUP):
        re = vec[0, :, chunk * w : (chunk + 1) * w]
        im = vec[1, :, chunk * w : (chunk + 1) * w]
        if wp > w:
            fill = jnp.zeros((nodes, wp - w), BF16)
            both = jnp.concatenate([re, fill, im, fill], axis=1)
        else:
            both = jnp.concatenate([re, im], axis=1)
        for k in range(GROUP):

            @pl.when((mine ^ k) == chunk)
            def _():
                outs[k][0:nodes, :] = both

    for k in range(GROUP):
        for at, part in enumerate((small_low, small, small_high)):
            outs[k][nodes + at * SMALL_ROWS : nodes + (at + 1) * SMALL_ROWS, 0 : small.shape[1]] = part[...]


def build_body(nodes, e_cap, rows_out, scal, m0, m1, m2, m3, matrix, k_hi, k_lo, ids, coefs, coefs_s, acc, sem):
    mine = scal[0]
    width = matrix.shape[0]
    blocks = 3 * GROUP
    messages = (m0, m1, m2, m3)
    for k in range(GROUP):
        for dz in range(3):
            at = nodes + dz * SMALL_ROWS
            rows = messages[k][at : at + SMALL_ROWS, 0:width].astype(F32)
            t = dz * GROUP + (mine ^ k)
            ids[t, 0:4, :] = rows[0:4] + 128.0 * rows[4:8]
            coefs[pl.ds(t, 1), :] = (rows[8:9] + rows[9:10] + rows[10:11])[:, 0:128]
    copy = pltpu.make_async_copy(coefs, coefs_s, sem)
    copy.start()
    acc[...] = jnp.zeros(acc.shape, F32)
    copy.wait()
    span = 3 * nodes

    def one(step, carry):
        t = 1 + step // e_cap
        e = step % e_cap
        factor = coefs_s[t, e]

        @pl.when(factor != 0.0)
        def _():
            row = ids[t, pl.ds(e, 1), :]
            place = lax.broadcasted_iota(jnp.int32, (span, width), 0).astype(F32)
            hot = jnp.where(place == row, 1.0, 0.0).astype(BF16)
            half = jnp.dot(hot, matrix[...], preferred_element_type=F32)
            half_hi = half.astype(BF16)
            half_lo = (half - half_hi.astype(F32)).astype(BF16)
            dims = (((1,), (1,)), ((), ()))
            full = lax.dot_general(half_hi, hot, dims, preferred_element_type=F32)
            full = full + lax.dot_general(half_lo, hot, dims, preferred_element_type=F32)
            full = full * factor
            for j in range(3):
                i = t + j - 3

                @pl.when((i >= 0) & (i < rows_out))
                def _():
                    acc[i, :, (2 - j) * nodes : (5 - j) * nodes] += full[j * nodes : (j + 1) * nodes, :]

        return carry

    lax.fori_loop(0, (blocks - 2) * e_cap, one, 0)
    for i in range(rows_out):
        value = acc[i]
        top = value.astype(BF16)
        k_hi[i] = top
        k_lo[i] = (value - top.astype(F32)).astype(BF16)


def filter_body(
    nodes, wp, scal, m0, m1, m2, m3, low, high, k_hi, k_lo, f0, f1, f2, f3, vec, first, cols
):
    mine = scal[0]
    messages = (m0, m1, m2, m3)
    outs = (f0, f1, f2, f3)
    rows_out = 2 * GROUP
    for k in range(GROUP):
        other = mine ^ k
        vec[pl.ds(pl.multiple_of(other * nodes, nodes), nodes), :] = low[k]
        vec[pl.ds(pl.multiple_of((GROUP + other) * nodes, nodes), nodes), :] = messages[k][0:nodes, :]
        vec[pl.ds(pl.multiple_of((2 * GROUP + other) * nodes, nodes), nodes), :] = high[k]
    diag = lax.broadcasted_iota(jnp.int32, (nodes, nodes), 0) == lax.broadcasted_iota(
        jnp.int32, (nodes, nodes), 1
    )
    for k in range(GROUP):
        for dz in range(3):
            at = nodes + dz * SMALL_ROWS
            rows = messages[k][at : at + SMALL_ROWS, :].astype(F32)
            t = dz * GROUP + (mine ^ k)
            for slot, row in ((0, 11), (1, 12)):
                line = rows[row : row + 1, 0:nodes] + rows[row : row + 1, nodes : 2 * nodes]
                line = line + rows[row : row + 1, 2 * nodes : 3 * nodes]
                column = jnp.sum(jnp.where(diag, line, 0.0), axis=1, keepdims=True)
                cols[slot, t] = jnp.broadcast_to(column, (nodes, 128))
    sign = jnp.where(lax.broadcasted_iota(jnp.int32, (1, 2 * wp), 1) < wp, 1.0, -1.0)

    def applied(source, start, i):
        block = source[start * nodes : (start + 5) * nodes, :]
        total = jnp.dot(k_hi[i], block, preferred_element_type=F32)
        total = total + jnp.dot(k_lo[i], block, preferred_element_type=F32)
        own = source[(start + 2) * nodes : (start + 3) * nodes, :].astype(F32)
        turned = pltpu.roll(own, wp, 1)
        pot = cols[0, i + 2][:, 0:1]
        cap = cols[1, i + 2][:, 0:1]
        return (total + pot * own + (cap * sign) * turned, own)

    inside_low = scal[1] > 0
    inside_high = scal[1] < scal[2] - 1
    for i in range(rows_out):
        ham, own = applied(vec, i, i)
        value = (ham - FILTER_CENTER * own) / FILTER_HALF
        if i < 2:
            value = jnp.where(inside_low, value, 0.0)
        if i >= rows_out - 2:
            value = jnp.where(inside_high, value, 0.0)
        first[i * nodes : (i + 1) * nodes, :] = value.astype(BF16)
    for i in range(GROUP):
        ham, own = applied(first, i, i + 2)
        anchor = vec[(GROUP + i) * nodes : (GROUP + i + 1) * nodes, :].astype(F32)
        value = 2.0 * (ham - FILTER_CENTER * own) / FILTER_HALF - anchor
        value = value.astype(BF16)
        for k in range(GROUP):

            @pl.when((mine ^ k) == i)
            def _():
                outs[k][...] = value


def rotate_body(nodes, w, wp, parts, scal, g0, g1, g2, g3, rot, filtered, *out):
    mine = scal[0]
    received = (g0, g1, g2, g3)
    panel = rot.shape[3]
    with_re = jnp.zeros((2 * nodes, panel), F32)
    with_im = jnp.zeros((2 * nodes, panel), F32)
    for k in range(GROUP):
        chunk = mine ^ k
        re = received[k][:, 0:wp]
        im = received[k][:, wp : 2 * wp]
        both = jnp.concatenate([re, im], axis=0)
        with_re = with_re + jnp.dot(both, rot[0, chunk], preferred_element_type=F32)
        with_im = with_im + jnp.dot(both, rot[1, chunk], preferred_element_type=F32)
        for q in range(GROUP):

            @pl.when(chunk == q)
            def _():
                filtered[0, :, q * w : (q + 1) * w] = re[:, 0:w]
                filtered[1, :, q * w : (q + 1) * w] = im[:, 0:w]

    out_re = with_re[0:nodes] - with_im[nodes:]
    out_im = with_im[0:nodes] + with_re[nodes:]
    cols = panel // parts
    for h in range(parts):
        value_re = out_re[:, h * cols : (h + 1) * cols]
        value_im = out_im[:, h * cols : (h + 1) * cols]
        if parts == 2:

            @pl.when(scal[4] == h)
            def _():
                out[0][:, 0:cols] = value_re
                out[0][:, cols : 2 * cols] = value_im

            @pl.when(scal[4] != h)
            def _():
                out[1][:, 0:cols] = value_re
                out[1][:, cols : 2 * cols] = value_im

        else:
            out[0][h, :, 0:cols] = value_re
            out[0][h, :, cols : 2 * cols] = value_im


def overlap_body(nodes, w, wp, parts, cols, scale, split, scal, *refs):
    fields = refs[0:GROUP]
    panels = refs[GROUP : GROUP + GROUP * parts]
    outs = refs[GROUP + GROUP * parts : -3]
    left, right, result = refs[-3:]
    panel = parts * cols
    for k in range(GROUP):
        left[:, k * nodes : (k + 1) * nodes] = jnp.transpose(fields[k][...].astype(F32)).astype(BF16)
        for h in range(parts):
            if parts == 2:

                @pl.when(scal[4] == h)
                def _():
                    right[k * nodes : (k + 1) * nodes, h * 2 * cols : (h + 1) * 2 * cols] = panels[k][...]

                @pl.when(scal[4] != h)
                def _():
                    right[k * nodes : (k + 1) * nodes, h * 2 * cols : (h + 1) * 2 * cols] = panels[
                        GROUP + k
                    ][...]

            else:
                right[k * nodes : (k + 1) * nodes, h * 2 * cols : (h + 1) * 2 * cols] = panels[
                    h * GROUP + k
                ][...]
    product = jnp.dot(left[...], right[...], preferred_element_type=F32)
    top, bottom = product[0:w], product[wp : wp + w]
    for h in range(parts):
        a, b, c = 2 * h * cols, (2 * h + 1) * cols, (2 * h + 2) * cols
        result[:, h * cols : (h + 1) * cols] = (top[:, a:b] - bottom[:, b:c]) * scale
        result[:, panel + h * cols : panel + (h + 1) * cols] = (top[:, b:c] + bottom[:, a:b]) * scale
    if split == 1:
        outs[0][...] = result[...]
    else:
        rows = w // split
        for j in range(split):
            at = pl.multiple_of((scal[1] ^ j) * rows, rows)
            outs[j][...] = result[pl.ds(at, rows), :].astype(BF16)


def sum_body(scal, s0, s1, s2, s3, out):
    total = s0[...].astype(F32) + s1[...].astype(F32)
    total = total + (s2[...].astype(F32) + s3[...].astype(F32))
    out[...] = total.astype(BF16)


def spread_body(w, rows, split, panel, scal, a0, a1, a2, a3, out):
    mine, group = scal[0], scal[1]
    for k, part in enumerate((a0, a1, a2, a3)):
        for j in range(split):
            at = (mine ^ k) * w + ((group ^ j) if split > 1 else 0) * rows
            value = part[j].astype(F32)
            out[pl.ds(at, rows), 0, :] = value[:, 0:panel]
            out[pl.ds(at, rows), 1, :] = value[:, panel : 2 * panel]


def on_device(
    orbitals, elem_count, connectivity, elem_coef, elem_matrix, potential, absorber, rotation
):
    nodes, _, bands = orbitals.shape
    blocks = lax.axis_size("elem")
    parts = lax.axis_size("band")
    e_cap, elem_nodes = connectivity.shape[1:]
    panel = rotation.shape[2]
    groups = blocks // GROUP
    w = bands // GROUP
    wp = up(w, 64)
    lanes = 2 * wp
    span = 3 * nodes
    width = up(max(elem_nodes, span), 128)
    cols = panel // parts
    elem = lax.axis_index("elem")
    band = lax.axis_index("band")
    mine = elem % GROUP
    group = elem // GROUP
    scal = jnp.stack(
        [mine, group, jnp.int32(groups), elem_count[0], band, jnp.int32(0), jnp.int32(0), jnp.int32(0)]
    ).astype(jnp.int32)

    def in_group(k):
        return [(i, i ^ k) for i in range(blocks)]

    def swap(values):
        return [values[0]] + [lax.ppermute(values[k], "elem", in_group(k)) for k in range(1, GROUP)]

    up_perm = [(i, i + GROUP) for i in range(blocks - GROUP)]
    down_perm = [(b, a) for a, b in up_perm]

    def both_ways(value):
        return lax.ppermute(value, "elem", up_perm), lax.ppermute(value, "elem", down_perm)

    small = kernel_call(
        functools.partial(small_body, e_cap, elem_nodes, nodes, width),
        jax.ShapeDtypeStruct((SMALL_ROWS, width), BF16),
        1,
    )(scal, connectivity[0], elem_coef, potential[None], absorber[None])
    small_low, small_high = both_ways(small)
    message = jax.ShapeDtypeStruct((nodes + 3 * SMALL_ROWS, max(lanes, width)), BF16)
    message = jax.ShapeDtypeStruct((nodes + 3 * SMALL_ROWS, lanes if lanes >= width else width), BF16)
    lanes = message.shape[1]
    wp = lanes // 2
    messages = kernel_call(functools.partial(pack_body, nodes, w, wp), [message] * GROUP, 1)(
        scal, jnp.moveaxis(orbitals, 1, 0), small, small_low, small_high
    )
    messages = swap(messages)
    stacked = jnp.stack([m[:nodes] for m in messages])
    low, high = both_ways(stacked)

    matrix = jnp.pad(elem_matrix, ((0, width - elem_nodes), (0, width - elem_nodes)))
    rows_out = 2 * GROUP
    operator = jax.ShapeDtypeStruct((rows_out, nodes, 5 * nodes), BF16)
    k_hi, k_lo = kernel_call(
        functools.partial(build_body, nodes, e_cap, rows_out),
        [operator, operator],
        1,
        scratch=[
            pltpu.VMEM((3 * GROUP, 8, width), F32),
            pltpu.VMEM((up(3 * GROUP, 8), 128), F32),
            pltpu.SMEM((up(3 * GROUP, 8), 128), F32),
            pltpu.VMEM((rows_out, nodes, 5 * nodes), F32),
            pltpu.SemaphoreType.DMA,
        ],
        flops=2 * 20 * 3 * width * width * span,
        moved=4 * rows_out * nodes * 5 * nodes,
    )(scal, *messages, matrix)

    piece = jax.ShapeDtypeStruct((nodes, lanes), BF16)
    fields = kernel_call(
        functools.partial(filter_body, nodes, wp),
        [piece] * GROUP,
        1,
        scratch=[
            pltpu.VMEM((3 * GROUP * nodes, lanes), BF16),
            pltpu.VMEM((rows_out * nodes, lanes), BF16),
            pltpu.VMEM((2, 3 * GROUP, nodes, 128), F32),
        ],
        flops=2 * 2 * 12 * nodes * 5 * nodes * lanes,
        moved=4 * rows_out * nodes * 5 * nodes,
    )(scal, *messages, low, high, k_hi, k_lo)

    received = swap(fields)
    rot = lax.dynamic_slice_in_dim(rotation, band * bands, bands, 0)
    rot = jnp.moveaxis(rot, 1, 0).reshape(2, GROUP, w, panel)
    rot = jnp.pad(rot, ((0, 0), (0, 0), (0, wp - w), (0, 0)))
    half = jax.ShapeDtypeStruct((nodes, 2 * cols), F32)
    partial = jax.ShapeDtypeStruct((parts, nodes, 2 * cols), F32)
    filtered, *sums = kernel_call(
        functools.partial(rotate_body, nodes, w, wp, parts),
        [jax.ShapeDtypeStruct((2, nodes, bands), BF16)] + ([half, half] if parts == 2 else [partial]),
        1,
        flops=2 * nodes * 2 * bands * 2 * panel,
        moved=2 * bands * 2 * panel,
    )(scal, *received, rot)
    filtered = jnp.moveaxis(filtered, 0, 1)
    if parts == 2:
        turn = [(0, 1), (1, 0)]
        rotated = (sums[0] + lax.ppermute(sums[1], "band", turn)).astype(BF16)
        gathered = swap([rotated] * GROUP)
        panels = gathered + [lax.ppermute(x, "band", turn) for x in gathered]
    else:
        rotated = lax.psum_scatter(sums[0], "band", scatter_dimension=0, tiled=True)[0].astype(BF16)
        gathered = lax.all_gather(jnp.stack(swap([rotated] * GROUP)), "band", axis=0)
        panels = [gathered[h, k] for h in range(parts) for k in range(GROUP)]
    scale = 1.0 / (nodes * blocks) ** 0.5
    direct = groups == 4 and w % (groups * 16) == 0
    split = groups if direct else 1
    rows = w // split
    term = jax.ShapeDtypeStruct((rows, 2 * panel), BF16 if direct else F32)
    terms = kernel_call(
        functools.partial(overlap_body, nodes, w, wp, parts, cols, scale, split),
        [term] * split,
        1,
        scratch=[
            pltpu.VMEM((lanes, GROUP * nodes), BF16),
            pltpu.VMEM((GROUP * nodes, 2 * panel), BF16),
            pltpu.VMEM((w, 2 * panel), F32),
        ],
        flops=2 * GROUP * nodes * lanes * 2 * panel,
        moved=4 * GROUP * nodes * panel,
    )(scal, *fields, *panels)
    if direct:

        def across(values):
            return [values[0]] + [
                lax.ppermute(values[j], "elem", [(i, i ^ (GROUP * j)) for i in range(blocks)])
                for j in range(1, split)
            ]

        own = kernel_call(sum_body, term, 1)(scal, *across(terms))
        stack = jnp.stack(across([own] * split))
    else:
        lines = [[GROUP * z + i for z in range(groups)] for i in range(GROUP)]
        stack = lax.psum(terms[0], "elem", axis_index_groups=lines).astype(BF16)[None]
    spread = swap([stack] * GROUP)
    intersection = kernel_call(
        functools.partial(spread_body, w, rows, split, panel),
        jax.ShapeDtypeStruct((bands, 2, panel), F32),
        1,
    )(scal, *spread)
    return (filtered, rotated.reshape(nodes, 2, cols), intersection)


def solution(mesh):
    placed = (
        P("elem", None, "band"),
        P("elem"),
        P("elem", None, None),
        P("elem", None),
        P(),
        P("elem"),
        P("elem"),
        P(),
    )
    return jax.shard_map(
        on_device,
        mesh=mesh,
        in_specs=placed,
        out_specs=(P("elem", None, "band"), P("elem", None, "band"), P("band", None, None)),
        check_vma=False,
    )
```

time: 432 us -> 128 us (0.30)
  waiting for transfers between devices: 269 us -> 47.1 us
  other arithmetic: 43 us -> 0.15 us
  Pallas kernels: 0 us -> 32.1 us
  local copies, waits for them, and re-layouts: 33.3 us -> 9.66 us
  starting transfers between devices: 54.3 us -> 38.4 us
  between operations: 14.4 us -> 1.68 us
  matrix products: 12 us -> 0 us
  blocking collectives: 4.62 us -> 0 us
    psum x1 -> x0, waiting for transfers between devices: 143 us -> none  [on_device(): intersection = lax.psum(local_intersection, 'elem')]
    ppermute x8 -> x27, waiting for transfers between devices: 126 us -> 47.1 us  [the longest x12 27.4 us: swap(): lax.ppermute(values[k], 'elem', in_group(k))]
    pallas_call x0 -> x8, Pallas kernels: none -> 32.1 us  [call(): pl.pallas_call(body, out_shape=out_shape, in_specs=[pl.BlockSpec(memory_s...]
    ppermute x8 -> x27, starting transfers between devices: 54.2 us -> 38.4 us  [the longest x12 14.2 us: swap(): lax.ppermute(values[k], 'elem', in_group(k))]
    dot_general x4 -> x0, matrix products: 12 us -> none  [the longest x2 7.91 us: one_element(): jnp.dot(elem_matrix, flat_field[node_ids], preferred_element_type=jnp.flo...]
    dot_general x1 -> x0, other arithmetic: 11.9 us -> none  [on_device(): jnp.dot(piece_flat, complex_block(rot_mine), preferred_element_type=jnp.f...]
    scatter-add x2 -> x0, other arithmetic: 11.5 us -> none  [one_element(): return totals.at[node_ids].add(product * elem_coef[0, element])]
    slice x3 -> x0, local copies, waits for them, and re-layouts: 7.15 us -> none  [the longest x1 5.74 us: complex_block(): rot_im = rot_part[:, 1]]
  transfers between devices with their start and end apart: 9 -> 27, of which waited for: 9 -> 15; matrix products, arithmetic and copies ran while one was open for 6% -> 5% of each run, Pallas kernels for 0% -> 15%
where the time goes in v1:
time: 128 us; the launch traced here: 129 us
  waiting for transfers between devices  47.1 us (37%)
  starting transfers between devices  38.4 us (30%)
  Pallas kernels  32.1 us (25%)
  local copies, waits for them, and re-layouts  9.66 us (8%)
  between operations  1.68 us (1%)
    pallas_call x8, Pallas kernels, call(): pl.pallas_call(body, out_shape=out_shape, in_specs=[pl.BlockSpec(memory_s...  32.1 us
    ppermute x12, waiting for transfers between devices, swap(): lax.ppermute(values[k], 'elem', in_group(k))  27.4 us
    ppermute x6, waiting for transfers between devices, across(): lax.ppermute(values[j], 'elem', [(i, i ^ GROUP * j) for i in range(blocks)])  15.5 us
    ppermute x12, starting transfers between devices, swap(): lax.ppermute(values[k], 'elem', in_group(k))  14.2 us
    ppermute x6, starting transfers between devices, across(): lax.ppermute(values[j], 'elem', [(i, i ^ GROUP * j) for i in range(blocks)])  12.1 us
    ppermute x2, starting transfers between devices, both_ways(): lax.ppermute(value, 'elem', up_perm)  8.9 us
    unnamed x16, local copies, waits for them, and re-layouts  4.9 us
    ppermute x2, starting transfers between devices, both_ways(): lax.ppermute(value, 'elem', down_perm)  2.57 us
  transfers between devices with their start and end apart: 27, of which 15 were waited for; matrix products, arithmetic and copies ran while one was open for 5% of the time, Pallas kernels for 15%

profile of v1, /device:TPU:0, one launch (start us, length us, event | category | flops | bytes accessed | tf_op | source)
XLA Modules:
  0.0 129.0 jit_solution(13524740545090438176)
XLA Ops:
  4.8 5.5 %collective-permute-start = (bf16[16,384]{1,0:T(8,128)(2,1)S(1)}, bf16[16,384]{1,0:T(8,128)(2,1)}, u32[]{:S(2)}, u32[]{:S(2)}) collective-permute-start(bf16[16,384]{1,0:T(8,128)(2,1)S(1)} %shard_map.103.small), channel_id=1, source_target_pairs={{0,8},{2,10},{4,12},{6,14},{8,16},{10,18},{12,20},{14,22},{16,24},... | collective-permute-start | bytes 36872 | tf_op jit(solution)/shard_map/ppermute | solution.py:329
  10.3 1.3 collective-permute-start.1
  12.7 1.7 %pad.4.matrix = bf16[384,384]{1,0:T(8,128)(2,1)} pad(bf16[343,343]{1,0:T(8,128)(2,1)} %param.12, bf16[]{:T(256)} %constant.43.clone.1), padding=0_41x0_41 | pad | bytes 530212 | tf_op jit(solution)/shard_map/jit(_pad)/pad | solution.py:348
  14.4 1.6 %collective-permute-done.1.small_high = bf16[16,384]{1,0:T(8,128)(2,1)} collective-permute-done((bf16[16,384]{1,0:T(8,128)(2,1)S(1)}, bf16[16,384]{1,0:T(8,128)(2,1)}, u32[]{:S(2)}, u32[]{:S(2)}) %collective-permute-start.1) | collective-permute-done | bytes 12320 | tf_op jit(solution)/shard_map/ppermute | solution.py:329
  17.2 1.6 %collective-permute-start.2 = (bf16[176,384]{1,0:T(8,128)(2,1)S(1)}, bf16[176,384]{1,0:T(8,128)(2,1)S(1)}, u32[]{:S(2)}, u32[]{:S(2)}) collective-permute-start(bf16[176,384]{1,0:T(8,128)(2,1)S(1)} %get-tuple-element.21), channel_id=1, source_target_pairs={{0,2},{2,0},{4,6},{6,4},{8,10},{10,8},{12,14},{14,12},{16,18},{18,... | collective-permute-start | bytes 405512 | tf_op jit(solution)/shard_map/ppermute | solution.py:323
  18.7 1.5 %collective-permute-start.3 = (bf16[176,384]{1,0:T(8,128)(2,1)S(1)}, bf16[176,384]{1,0:T(8,128)(2,1)S(1)}, u32[]{:S(2)}, u32[]{:S(2)}) collective-permute-start(bf16[176,384]{1,0:T(8,128)(2,1)S(1)} %get-tuple-element.22), channel_id=1, source_target_pairs={{0,4},{2,6},{4,0},{6,2},{8,12},{10,14},{12,8},{14,10},{16,20},{18,... | collective-permute-start | bytes 405512 | tf_op jit(solution)/shard_map/ppermute | solution.py:323
  20.7 5.5 %collective-permute-done.4.m3 = bf16[176,384]{1,0:T(8,128)(2,1)S(1)} collective-permute-done((bf16[176,384]{1,0:T(8,128)(2,1)S(1)}, bf16[176,384]{1,0:T(8,128)(2,1)S(1)}, u32[]{:S(2)}, u32[]{:S(2)}) %collective-permute-start.4) | collective-permute-done | bytes 135200 | tf_op jit(solution)/shard_map/ppermute | solution.py:323
  26.3 3.4 %collective-permute-start.5 = (bf16[4,128,384]{2,1,0:T(8,128)(2,1)S(1)}, bf16[4,128,384]{2,1,0:T(8,128)(2,1)S(1)}, u32[]{:S(2)}, u32[]{:S(2)}) collective-permute-start(bf16[4,128,384]{2,1,0:T(8,128)(2,1)S(1)} %pad_maximum_fusion), channel_id=1, source_target_pairs={{0,8},{2,10},{4,12},{6,14},{8,16},{10,18},{12,20},{14,22},{16,24},... | collective-permute-start | bytes 1179656 | tf_op jit(solution)/shard_map/ppermute | solution.py:329
  29.7 1.3 %collective-permute-start.6 = (bf16[4,128,384]{2,1,0:T(8,128)(2,1)S(1)}, bf16[4,128,384]{2,1,0:T(8,128)(2,1)S(1)}, u32[]{:S(2)}, u32[]{:S(2)}) collective-permute-start(bf16[4,128,384]{2,1,0:T(8,128)(2,1)S(1)} %pad_maximum_fusion), channel_id=1, source_target_pairs={{8,0},{10,2},{12,4},{14,6},{16,8},{18,10},{20,12},{22,14},{24,16},... | collective-permute-start | bytes 1179656 | tf_op jit(solution)/shard_map/ppermute | solution.py:329
  31.0 18.7 %shard_map.105 = (bf16[8,128,640]{2,1,0:T(8,128)(2,1)S(1)}, bf16[8,128,640]{2,1,0:T(8,128)(2,1)S(1)}) custom-call(s32[8]{0:T(128)S(1)} %stack.45.scal, bf16[176,384]{1,0:T(8,128)(2,1)S(1)} %get-tuple-element.20.m0, bf16[176,384]{1,0:T(8,128)(2,1)S(1)} %collective-permute-done.2.m1, bf16[176,384]{1,0:T(8,128)(2,1)S(1)} %collective-permute-done.3.m2, ...), custom_call_target="tpu_custom_call" | custom-call | flops 6794772480 | bytes 2621440 | tf_op jit(solution)/shard_map/pallas_call | solution.py:28
  49.8 4.1 %shard_map.106 = (bf16[128,384]{1,0:T(8,128)(2,1)S(1)}, bf16[128,384]{1,0:T(8,128)(2,1)S(1)}, bf16[128,384]{1,0:T(8,128)(2,1)S(1)}, bf16[128,384]{1,0:T(8,128)(2,1)S(1)}) custom-call(s32[8]{0:T(128)S(1)} %stack.45.scal, bf16[176,384]{1,0:T(8,128)(2,1)S(1)} %get-tuple-element.20.m0, bf16[176,384]{1,0:T(8,128)(2,1)S(1)} %collective-permute-done.2.m1, ...), custom_call_target="tpu_custom_call" | custom-call | flops 1509949440 | bytes 2621440 | tf_op jit(solution)/shard_map/pallas_call | solution.py:28
  55.5 2.0 %collective-permute-start.9 = (bf16[128,384]{1,0:T(8,128)(2,1)S(1)}, bf16[128,384]{1,0:T(8,128)(2,1)S(1)}, u32[]{:S(2)}, u32[]{:S(2)}) collective-permute-start(bf16[128,384]{1,0:T(8,128)(2,1)S(1)} %get-tuple-element.29.refs_3_), channel_id=1, source_target_pairs={{0,6},{2,4},{4,2},{6,0},{8,14},{10,12},{12,10},{14,8},{16,22},{18,... | collective-permute-start | bytes 294920 | tf_op jit(solution)/shard_map/ppermute | solution.py:323
  59.3 1.7 %collective-permute-done.9.g3 = bf16[128,384]{1,0:T(8,128)(2,1)S(1)} collective-permute-done((bf16[128,384]{1,0:T(8,128)(2,1)S(1)}, bf16[128,384]{1,0:T(8,128)(2,1)S(1)}, u32[]{:S(2)}, u32[]{:S(2)}) %collective-permute-start.9) | collective-permute-done | bytes 98336 | tf_op jit(solution)/shard_map/ppermute | solution.py:323
  61.0 1.8 %shard_map.107 = (bf16[2,128,768]{2,1,0:T(8,128)(2,1)S(1)}, f32[128,512]{1,0:T(8,128)S(1)}, f32[128,512]{1,0:T(8,128)S(1)}) custom-call(s32[8]{0:T(128)S(1)} %stack.45.scal, bf16[128,384]{1,0:T(8,128)(2,1)S(1)} %get-tuple-element.26.g0.refs_0_, bf16[128,384]{1,0:T(8,128)(2,1)S(1)} %collective-permute-done.7.g1, ...), custom_call_target="tpu_custom_call" | custom-call | flops 402653184 | bytes 1572864 | tf_op jit(solution)/shard_map/pallas_call | solution.py:28
  62.9 1.5 %collective-permute-done.10 = f32[128,512]{1,0:T(8,128)S(1)} collective-permute-done((f32[128,512]{1,0:T(8,128)S(1)}, f32[128,512]{1,0:T(8,128)S(1)}, u32[]{:S(2)}, u32[]{:S(2)}) %collective-permute-start.10) | collective-permute-done | bytes 262176 | tf_op jit(solution)/shard_map/ppermute | solution.py:396
  64.4 1.6 %collective-permute-start.11 = (bf16[128,512]{1,0:T(8,128)(2,1)S(1)}, bf16[128,512]{1,0:T(8,128)(2,1)S(1)}, u32[]{:S(2)}, u32[]{:S(2)}) collective-permute-start(bf16[128,512]{1,0:T(8,128)(2,1)S(1)} %add_convert_fusion.refs_4_), channel_id=1, source_target_pairs={{0,2},{2,0},{4,6},{6,4},{8,10},{10,8},{12,14},{14,12},{16,18},{18,... | collective-permute-start | bytes 393224 | tf_op jit(solution)/shard_map/ppermute | solution.py:323
  68.0 2.3 %collective-permute-done.11.refs_5_ = bf16[128,512]{1,0:T(8,128)(2,1)S(1)} collective-permute-done((bf16[128,512]{1,0:T(8,128)(2,1)S(1)}, bf16[128,512]{1,0:T(8,128)(2,1)S(1)}, u32[]{:S(2)}, u32[]{:S(2)}) %collective-permute-start.11) | collective-permute-done | bytes 131104 | tf_op jit(solution)/shard_map/ppermute | solution.py:323
  70.3 3.8 %collective-permute-done.12.refs_6_ = bf16[128,512]{1,0:T(8,128)(2,1)S(1)} collective-permute-done((bf16[128,512]{1,0:T(8,128)(2,1)S(1)}, bf16[128,512]{1,0:T(8,128)(2,1)S(1)}, u32[]{:S(2)}, u32[]{:S(2)}) %collective-permute-start.12) | collective-permute-done | bytes 131104 | tf_op jit(solution)/shard_map/ppermute | solution.py:323
  75.7 1.7 %shard_map.108 = (bf16[48,1024]{1,0:T(8,128)(2,1)S(1)}, bf16[48,1024]{1,0:T(8,128)(2,1)S(1)}, bf16[48,1024]{1,0:T(8,128)(2,1)S(1)}, bf16[48,1024]{1,0:T(8,128)(2,1)S(1)}) custom-call(s32[8]{0:T(128)S(1)} %stack.45.scal, bf16[128,384]{1,0:T(8,128)(2,1)S(1)} %get-tuple-element.26.g0.refs_0_, bf16[128,384]{1,0:T(8,128)(2,1)S(1)} %get-tuple-element.27.refs_1_, ...), custom_call_target="tpu_custom_call" | custom-call | flops 402653184 | bytes 1048576 | tf_op jit(solution)/shard_map/pallas_call | solution.py:28
  77.4 5.2 %collective-permute-start.18 = (bf16[48,1024]{1,0:T(8,128)(2,1)S(1)}, bf16[48,1024]{1,0:T(8,128)(2,1)S(1)}, u32[]{:S(2)}, u32[]{:S(2)}) collective-permute-start(bf16[48,1024]{1,0:T(8,128)(2,1)S(1)} %get-tuple-element.34), channel_id=1, source_target_pairs={{0,8},{2,10},{4,12},{6,14},{8,0},{10,2},{12,4},{14,6},{16,24},{18,... | collective-permute-start | bytes 294920 | tf_op jit(solution)/shard_map/ppermute | solution.py:424
  82.6 2.4 %collective-permute-start.20 = (bf16[48,1024]{1,0:T(8,128)(2,1)S(1)}, bf16[48,1024]{1,0:T(8,128)(2,1)S(1)}, u32[]{:S(2)}, u32[]{:S(2)}) collective-permute-start(bf16[48,1024]{1,0:T(8,128)(2,1)S(1)} %get-tuple-element.36), channel_id=1, source_target_pairs={{0,24},{2,26},{4,28},{6,30},{8,16},{10,18},{12,20},{14,22},{16,8},... | collective-permute-start | bytes 294920 | tf_op jit(solution)/shard_map/ppermute | solution.py:424
  85.9 7.1 %collective-permute-done.19.s2 = bf16[48,1024]{1,0:T(8,128)(2,1)S(1)} collective-permute-done((bf16[48,1024]{1,0:T(8,128)(2,1)S(1)}, bf16[48,1024]{1,0:T(8,128)(2,1)S(1)}, u32[]{:S(2)}, u32[]{:S(2)}) %collective-permute-start.19) | collective-permute-done | bytes 98336 | tf_op jit(solution)/shard_map/ppermute | solution.py:424
  93.6 1.6 %collective-permute-start.23 = (bf16[48,1024]{1,0:T(8,128)(2,1)S(1)}, bf16[48,1024]{1,0:T(8,128)(2,1)S(1)}, u32[]{:S(2)}, u32[]{:S(2)}) collective-permute-start(bf16[48,1024]{1,0:T(8,128)(2,1)S(1)} %shard_map.109), channel_id=1, source_target_pairs={{0,24},{2,26},{4,28},{6,30},{8,16},{10,18},{12,20},{14,22},{16,8},... | collective-permute-start | bytes 294920 | tf_op jit(solution)/shard_map/ppermute | solution.py:424
  95.2 2.1 %collective-permute-start.22 = (bf16[48,1024]{1,0:T(8,128)(2,1)S(1)}, bf16[48,1024]{1,0:T(8,128)(2,1)S(1)}, u32[]{:S(2)}, u32[]{:S(2)}) collective-permute-start(bf16[48,1024]{1,0:T(8,128)(2,1)S(1)} %shard_map.109), channel_id=1, source_target_pairs={{0,16},{2,18},{4,20},{6,22},{8,24},{10,26},{12,28},{14,30},{16,0},... | collective-permute-start | bytes 294920 | tf_op jit(solution)/shard_map/ppermute | solution.py:424
  98.0 3.0 %collective-permute-done.23 = bf16[48,1024]{1,0:T(8,128)(2,1)S(1)} collective-permute-done((bf16[48,1024]{1,0:T(8,128)(2,1)S(1)}, bf16[48,1024]{1,0:T(8,128)(2,1)S(1)}, u32[]{:S(2)}, u32[]{:S(2)}) %collective-permute-start.23) | collective-permute-done | bytes 98336 | tf_op jit(solution)/shard_map/ppermute | solution.py:424
  101.1 4.5 %collective-permute-done.22 = bf16[48,1024]{1,0:T(8,128)(2,1)S(1)} collective-permute-done((bf16[48,1024]{1,0:T(8,128)(2,1)S(1)}, bf16[48,1024]{1,0:T(8,128)(2,1)S(1)}, u32[]{:S(2)}, u32[]{:S(2)}) %collective-permute-start.22) | collective-permute-done | bytes 98336 | tf_op jit(solution)/shard_map/ppermute | solution.py:424
  107.0 2.2 %collective-permute-start.26 = (bf16[4,48,1024]{2,1,0:T(8,128)(2,1)S(1)}, bf16[4,48,1024]{2,1,0:T(8,128)(2,1)}, u32[]{:S(2)}, u32[]{:S(2)}) collective-permute-start(bf16[4,48,1024]{2,1,0:T(8,128)(2,1)S(1)} %pad_maximum_fusion.1.a0), channel_id=1, source_target_pairs={{0,6},{2,4},{4,2},{6,0},{8,14},{10,12},{12,10},{14,8},{16,22},{18,... | collective-permute-start | bytes 1179656 | tf_op jit(solution)/shard_map/ppermute | solution.py:323
  109.1 1.1 copy.13
  110.3 1.6 %reshape.13 = bf16[128,2,256]{2,1,0:T(2,128)(2,1)} reshape(bf16[128,512]{1,0:T(8,128)(2,1)} %copy-done.1) | data formatting | bytes 262144 | tf_op jit(solution)/shard_map/reshape | solution.py:439
  111.9 5.9 %collective-permute-done.24.a1 = bf16[4,48,1024]{2,1,0:T(8,128)(2,1)} collective-permute-done((bf16[4,48,1024]{2,1,0:T(8,128)(2,1)S(1)}, bf16[4,48,1024]{2,1,0:T(8,128)(2,1)}, u32[]{:S(2)}, u32[]{:S(2)}) %collective-permute-start.24) | collective-permute-done | bytes 393248 | tf_op jit(solution)/shard_map/ppermute | solution.py:323
  117.8 7.7 %collective-permute-done.26.a3 = bf16[4,48,1024]{2,1,0:T(8,128)(2,1)} collective-permute-done((bf16[4,48,1024]{2,1,0:T(8,128)(2,1)S(1)}, bf16[4,48,1024]{2,1,0:T(8,128)(2,1)}, u32[]{:S(2)}, u32[]{:S(2)}) %collective-permute-start.26) | collective-permute-done | bytes 393248 | tf_op jit(solution)/shard_map/ppermute | solution.py:323
  125.5 3.5 %shard_map.110 = f32[768,2,512]{2,1,0:T(2,128)} custom-call(s32[8]{0:T(128)S(1)} %stack.45.scal, bf16[4,48,1024]{2,1,0:T(8,128)(2,1)S(1)} %pad_maximum_fusion.1.a0, bf16[4,48,1024]{2,1,0:T(8,128)(2,1)} %collective-permute-done.24.a1, bf16[4,48,1024]{2,1,0:T(8,128)(2,1)} %collective-permute-done.25.a2, bf16[4,48,1024]{2,1,0:T(8,128)(2,1)} %collective-permute-done.26.a3), custom_call_target="tpu_custom_call" | custom-call | tf_op jit(solution)/shard_map/pallas_call | solution.py:28
  (59 shorter events, 16.8 us)
Async XLA Ops:
  0.6 56.8 %copy-start = (bf16[1536,2,512]{2,1,0:T(2,128)(2,1)S(1)}, bf16[1536,2,512]{2,1,0:T(2,128)(2,1)}, u32[]{:S(2)}) copy-start(bf16[1536,2,512]{2,1,0:T(2,128)(2,1)} %param.15) | copy-start | bytes 9437188
  1.6 0.7 copy-start.3
  2.3 0.7 copy-start.4
  4.8 9.6 %collective-permute-start = (bf16[16,384]{1,0:T(8,128)(2,1)S(1)}, bf16[16,384]{1,0:T(8,128)(2,1)}, u32[]{:S(2)}, u32[]{:S(2)}) collective-permute-start(bf16[16,384]{1,0:T(8,128)(2,1)S(1)} %shard_map.103.small), channel_id=1, source_target_pairs={{0,8},{2,10},{4,12},{6,14},{8,16},{10,18},{12,20},{14,22},{16,24},... | collective-permute-start | bytes 36872 | tf_op jit(solution)/shard_map/ppermute | solution.py:329
  10.3 5.7 %collective-permute-start.1 = (bf16[16,384]{1,0:T(8,128)(2,1)S(1)}, bf16[16,384]{1,0:T(8,128)(2,1)}, u32[]{:S(2)}, u32[]{:S(2)}) collective-permute-start(bf16[16,384]{1,0:T(8,128)(2,1)S(1)} %shard_map.103.small), channel_id=1, source_target_pairs={{8,0},{10,2},{12,4},{14,6},{16,8},{18,10},{20,12},{22,14},{24,16},... | collective-permute-start | bytes 36872 | tf_op jit(solution)/shard_map/ppermute | solution.py:329
  14.4 16.7 %copy-start.2 = (bf16[384,384]{1,0:T(8,128)(2,1)S(1)}, bf16[384,384]{1,0:T(8,128)(2,1)}, u32[]{:S(2)}) copy-start(bf16[384,384]{1,0:T(8,128)(2,1)} %pad.4.matrix) | copy-start | bytes 884740
  17.2 9.1 %collective-permute-start.2 = (bf16[176,384]{1,0:T(8,128)(2,1)S(1)}, bf16[176,384]{1,0:T(8,128)(2,1)S(1)}, u32[]{:S(2)}, u32[]{:S(2)}) collective-permute-start(bf16[176,384]{1,0:T(8,128)(2,1)S(1)} %get-tuple-element.21), channel_id=1, source_target_pairs={{0,2},{2,0},{4,6},{6,4},{8,10},{10,8},{12,14},{14,12},{16,18},{18,... | collective-permute-start | bytes 405512 | tf_op jit(solution)/shard_map/ppermute | solution.py:323
  18.7 7.5 %collective-permute-start.3 = (bf16[176,384]{1,0:T(8,128)(2,1)S(1)}, bf16[176,384]{1,0:T(8,128)(2,1)S(1)}, u32[]{:S(2)}, u32[]{:S(2)}) collective-permute-start(bf16[176,384]{1,0:T(8,128)(2,1)S(1)} %get-tuple-element.22), channel_id=1, source_target_pairs={{0,4},{2,6},{4,0},{6,2},{8,12},{10,14},{12,8},{14,10},{16,20},{18,... | collective-permute-start | bytes 405512 | tf_op jit(solution)/shard_map/ppermute | solution.py:323
  20.2 6.0 %collective-permute-start.4 = (bf16[176,384]{1,0:T(8,128)(2,1)S(1)}, bf16[176,384]{1,0:T(8,128)(2,1)S(1)}, u32[]{:S(2)}, u32[]{:S(2)}) collective-permute-start(bf16[176,384]{1,0:T(8,128)(2,1)S(1)} %get-tuple-element.23), channel_id=1, source_target_pairs={{0,6},{2,4},{4,2},{6,0},{8,14},{10,12},{12,10},{14,8},{16,22},{18,... | collective-permute-start | bytes 405512 | tf_op jit(solution)/shard_map/ppermute | solution.py:323
  26.3 23.4 %collective-permute-start.5 = (bf16[4,128,384]{2,1,0:T(8,128)(2,1)S(1)}, bf16[4,128,384]{2,1,0:T(8,128)(2,1)S(1)}, u32[]{:S(2)}, u32[]{:S(2)}) collective-permute-start(bf16[4,128,384]{2,1,0:T(8,128)(2,1)S(1)} %pad_maximum_fusion), channel_id=1, source_target_pairs={{0,8},{2,10},{4,12},{6,14},{8,16},{10,18},{12,20},{14,22},{16,24},... | collective-permute-start | bytes 1179656 | tf_op jit(solution)/shard_map/ppermute | solution.py:329
  29.7 20.1 %collective-permute-start.6 = (bf16[4,128,384]{2,1,0:T(8,128)(2,1)S(1)}, bf16[4,128,384]{2,1,0:T(8,128)(2,1)S(1)}, u32[]{:S(2)}, u32[]{:S(2)}) collective-permute-start(bf16[4,128,384]{2,1,0:T(8,128)(2,1)S(1)} %pad_maximum_fusion), channel_id=1, source_target_pairs={{8,0},{10,2},{12,4},{14,6},{16,8},{18,10},{20,12},{22,14},{24,16},... | collective-permute-start | bytes 1179656 | tf_op jit(solution)/shard_map/ppermute | solution.py:329
  53.9 4.9 %collective-permute-start.7 = (bf16[128,384]{1,0:T(8,128)(2,1)S(1)}, bf16[128,384]{1,0:T(8,128)(2,1)S(1)}, u32[]{:S(2)}, u32[]{:S(2)}) collective-permute-start(bf16[128,384]{1,0:T(8,128)(2,1)S(1)} %get-tuple-element.27.refs_1_), channel_id=1, source_target_pairs={{0,2},{2,0},{4,6},{6,4},{8,10},{10,8},{12,14},{14,12},{16,18},{18,... | collective-permute-start | bytes 294920 | tf_op jit(solution)/shard_map/ppermute | solution.py:323
  54.7 4.6 %collective-permute-start.8 = (bf16[128,384]{1,0:T(8,128)(2,1)S(1)}, bf16[128,384]{1,0:T(8,128)(2,1)S(1)}, u32[]{:S(2)}, u32[]{:S(2)}) collective-permute-start(bf16[128,384]{1,0:T(8,128)(2,1)S(1)} %get-tuple-element.28.refs_2_), channel_id=1, source_target_pairs={{0,4},{2,6},{4,0},{6,2},{8,12},{10,14},{12,8},{14,10},{16,20},{18,... | collective-permute-start | bytes 294920 | tf_op jit(solution)/shard_map/ppermute | solution.py:323
  55.5 5.5 %collective-permute-start.9 = (bf16[128,384]{1,0:T(8,128)(2,1)S(1)}, bf16[128,384]{1,0:T(8,128)(2,1)S(1)}, u32[]{:S(2)}, u32[]{:S(2)}) collective-permute-start(bf16[128,384]{1,0:T(8,128)(2,1)S(1)} %get-tuple-element.29.refs_3_), channel_id=1, source_target_pairs={{0,6},{2,4},{4,2},{6,0},{8,14},{10,12},{12,10},{14,8},{16,22},{18,... | collective-permute-start | bytes 294920 | tf_op jit(solution)/shard_map/ppermute | solution.py:323
  62.8 1.6 %collective-permute-start.10 = (f32[128,512]{1,0:T(8,128)S(1)}, f32[128,512]{1,0:T(8,128)S(1)}, u32[]{:S(2)}, u32[]{:S(2)}) collective-permute-start(f32[128,512]{1,0:T(8,128)S(1)} %get-tuple-element.32), channel_id=1, source_target_pairs={{0,1},{1,0},{2,3},{3,2},{4,5},{5,4},{6,7},{7,6},{8,9},{9,8},{10,11... | collective-permute-start | bytes 786440 | tf_op jit(solution)/shard_map/ppermute | solution.py:396
  64.4 41.5 %copy-start.1 = (bf16[128,512]{1,0:T(8,128)(2,1)}, bf16[128,512]{1,0:T(8,128)(2,1)S(1)}, u32[]{:S(2)}) copy-start(bf16[128,512]{1,0:T(8,128)(2,1)S(1)} %add_convert_fusion.refs_4_) | copy-start | bytes 393220
  64.4 5.9 %collective-permute-start.11 = (bf16[128,512]{1,0:T(8,128)(2,1)S(1)}, bf16[128,512]{1,0:T(8,128)(2,1)S(1)}, u32[]{:S(2)}, u32[]{:S(2)}) collective-permute-start(bf16[128,512]{1,0:T(8,128)(2,1)S(1)} %add_convert_fusion.refs_4_), channel_id=1, source_target_pairs={{0,2},{2,0},{4,6},{6,4},{8,10},{10,8},{12,14},{14,12},{16,18},{18,... | collective-permute-start | bytes 393224 | tf_op jit(solution)/shard_map/ppermute | solution.py:323
  66.1 8.1 %collective-permute-start.12 = (bf16[128,512]{1,0:T(8,128)(2,1)S(1)}, bf16[128,512]{1,0:T(8,128)(2,1)S(1)}, u32[]{:S(2)}, u32[]{:S(2)}) collective-permute-start(bf16[128,512]{1,0:T(8,128)(2,1)S(1)} %add_convert_fusion.refs_4_), channel_id=1, source_target_pairs={{0,4},{2,6},{4,0},{6,2},{8,12},{10,14},{12,8},{14,10},{16,20},{18,... | collective-permute-start | bytes 393224 | tf_op jit(solution)/shard_map/ppermute | solution.py:323
  67.1 7.1 %collective-permute-start.13 = (bf16[128,512]{1,0:T(8,128)(2,1)S(1)}, bf16[128,512]{1,0:T(8,128)(2,1)S(1)}, u32[]{:S(2)}, u32[]{:S(2)}) collective-permute-start(bf16[128,512]{1,0:T(8,128)(2,1)S(1)} %add_convert_fusion.refs_4_), channel_id=1, source_target_pairs={{0,6},{2,4},{4,2},{6,0},{8,14},{10,12},{12,10},{14,8},{16,22},{18,... | collective-permute-start | bytes 393224 | tf_op jit(solution)/shard_map/ppermute | solution.py:323
  68.0 6.7 %collective-permute-start.14 = (bf16[128,512]{1,0:T(8,128)(2,1)S(1)}, bf16[128,512]{1,0:T(8,128)(2,1)S(1)}, u32[]{:S(2)}, u32[]{:S(2)}) collective-permute-start(bf16[128,512]{1,0:T(8,128)(2,1)S(1)} %add_convert_fusion.refs_4_), channel_id=1, source_target_pairs={{0,1},{1,0},{2,3},{3,2},{4,5},{5,4},{6,7},{7,6},{8,9},{9,8},{10,11... | collective-permute-start | bytes 393224 | tf_op jit(solution)/shard_map/ppermute | solution.py:398
  70.3 4.4 %collective-permute-start.15 = (bf16[128,512]{1,0:T(8,128)(2,1)S(1)}, bf16[128,512]{1,0:T(8,128)(2,1)S(1)}, u32[]{:S(2)}, u32[]{:S(2)}) collective-permute-start(bf16[128,512]{1,0:T(8,128)(2,1)S(1)} %collective-permute-done.11.refs_5_), channel_id=1, source_target_pairs={{0,1},{1,0},{2,3},{3,2},{4,5},{5,4},{6,7},{7,6},{8,9},{9,8},{10,11... | collective-permute-start | bytes 393224 | tf_op jit(solution)/shard_map/ppermute | solution.py:398
  74.1 1.3 %collective-permute-start.16 = (bf16[128,512]{1,0:T(8,128)(2,1)S(1)}, bf16[128,512]{1,0:T(8,128)(2,1)S(1)}, u32[]{:S(2)}, u32[]{:S(2)}) collective-permute-start(bf16[128,512]{1,0:T(8,128)(2,1)S(1)} %collective-permute-done.12.refs_6_), channel_id=1, source_target_pairs={{0,1},{1,0},{2,3},{3,2},{4,5},{5,4},{6,7},{7,6},{8,9},{9,8},{10,11... | collective-permute-start | bytes 393224 | tf_op jit(solution)/shard_map/ppermute | solution.py:398
  74.2 1.5 %collective-permute-start.17 = (bf16[128,512]{1,0:T(8,128)(2,1)S(1)}, bf16[128,512]{1,0:T(8,128)(2,1)S(1)}, u32[]{:S(2)}, u32[]{:S(2)}) collective-permute-start(bf16[128,512]{1,0:T(8,128)(2,1)S(1)} %collective-permute-done.13.refs_7_), channel_id=1, source_target_pairs={{0,1},{1,0},{2,3},{3,2},{4,5},{5,4},{6,7},{7,6},{8,9},{9,8},{10,11... | collective-permute-start | bytes 393224 | tf_op jit(solution)/shard_map/ppermute | solution.py:398
  77.4 8.5 %collective-permute-start.18 = (bf16[48,1024]{1,0:T(8,128)(2,1)S(1)}, bf16[48,1024]{1,0:T(8,128)(2,1)S(1)}, u32[]{:S(2)}, u32[]{:S(2)}) collective-permute-start(bf16[48,1024]{1,0:T(8,128)(2,1)S(1)} %get-tuple-element.34), channel_id=1, source_target_pairs={{0,8},{2,10},{4,12},{6,14},{8,0},{10,2},{12,4},{14,6},{16,24},{18,... | collective-permute-start | bytes 294920 | tf_op jit(solution)/shard_map/ppermute | solution.py:424
  82.6 10.4 %collective-permute-start.19 = (bf16[48,1024]{1,0:T(8,128)(2,1)S(1)}, bf16[48,1024]{1,0:T(8,128)(2,1)S(1)}, u32[]{:S(2)}, u32[]{:S(2)}) collective-permute-start(bf16[48,1024]{1,0:T(8,128)(2,1)S(1)} %get-tuple-element.35), channel_id=1, source_target_pairs={{0,16},{2,18},{4,20},{6,22},{8,24},{10,26},{12,28},{14,30},{16,0},... | collective-permute-start | bytes 294920 | tf_op jit(solution)/shard_map/ppermute | solution.py:424
  82.6 10.4 %collective-permute-start.20 = (bf16[48,1024]{1,0:T(8,128)(2,1)S(1)}, bf16[48,1024]{1,0:T(8,128)(2,1)S(1)}, u32[]{:S(2)}, u32[]{:S(2)}) collective-permute-start(bf16[48,1024]{1,0:T(8,128)(2,1)S(1)} %get-tuple-element.36), channel_id=1, source_target_pairs={{0,24},{2,26},{4,28},{6,30},{8,16},{10,18},{12,20},{14,22},{16,8},... | collective-permute-start | bytes 294920 | tf_op jit(solution)/shard_map/ppermute | solution.py:424
  93.6 7.5 %collective-permute-start.23 = (bf16[48,1024]{1,0:T(8,128)(2,1)S(1)}, bf16[48,1024]{1,0:T(8,128)(2,1)S(1)}, u32[]{:S(2)}, u32[]{:S(2)}) collective-permute-start(bf16[48,1024]{1,0:T(8,128)(2,1)S(1)} %shard_map.109), channel_id=1, source_target_pairs={{0,24},{2,26},{4,28},{6,30},{8,16},{10,18},{12,20},{14,22},{16,8},... | collective-permute-start | bytes 294920 | tf_op jit(solution)/shard_map/ppermute | solution.py:424
  95.2 10.4 %collective-permute-start.22 = (bf16[48,1024]{1,0:T(8,128)(2,1)S(1)}, bf16[48,1024]{1,0:T(8,128)(2,1)S(1)}, u32[]{:S(2)}, u32[]{:S(2)}) collective-permute-start(bf16[48,1024]{1,0:T(8,128)(2,1)S(1)} %shard_map.109), channel_id=1, source_target_pairs={{0,16},{2,18},{4,20},{6,22},{8,24},{10,26},{12,28},{14,30},{16,0},... | collective-permute-start | bytes 294920 | tf_op jit(solution)/shard_map/ppermute | solution.py:424
  97.2 8.3 %collective-permute-start.21 = (bf16[48,1024]{1,0:T(8,128)(2,1)S(1)}, bf16[48,1024]{1,0:T(8,128)(2,1)S(1)}, u32[]{:S(2)}, u32[]{:S(2)}) collective-permute-start(bf16[48,1024]{1,0:T(8,128)(2,1)S(1)} %shard_map.109), channel_id=1, source_target_pairs={{0,8},{2,10},{4,12},{6,14},{8,0},{10,2},{12,4},{14,6},{16,24},{18,... | collective-permute-start | bytes 294920 | tf_op jit(solution)/shard_map/ppermute | solution.py:424
  105.6 12.2 %collective-permute-start.24 = (bf16[4,48,1024]{2,1,0:T(8,128)(2,1)S(1)}, bf16[4,48,1024]{2,1,0:T(8,128)(2,1)}, u32[]{:S(2)}, u32[]{:S(2)}) collective-permute-start(bf16[4,48,1024]{2,1,0:T(8,128)(2,1)S(1)} %pad_maximum_fusion.1.a0), channel_id=1, source_target_pairs={{0,2},{2,0},{4,6},{6,4},{8,10},{10,8},{12,14},{14,12},{16,18},{18,... | collective-permute-start | bytes 1179656 | tf_op jit(solution)/shard_map/ppermute | solution.py:323
  106.0 11.8 %collective-permute-start.25 = (bf16[4,48,1024]{2,1,0:T(8,128)(2,1)S(1)}, bf16[4,48,1024]{2,1,0:T(8,128)(2,1)}, u32[]{:S(2)}, u32[]{:S(2)}) collective-permute-start(bf16[4,48,1024]{2,1,0:T(8,128)(2,1)S(1)} %pad_maximum_fusion.1.a0), channel_id=1, source_target_pairs={{0,4},{2,6},{4,0},{6,2},{8,12},{10,14},{12,8},{14,10},{16,20},{18,... | collective-permute-start | bytes 1179656 | tf_op jit(solution)/shard_map/ppermute | solution.py:323
  107.0 18.5 %collective-permute-start.26 = (bf16[4,48,1024]{2,1,0:T(8,128)(2,1)S(1)}, bf16[4,48,1024]{2,1,0:T(8,128)(2,1)}, u32[]{:S(2)}, u32[]{:S(2)}) collective-permute-start(bf16[4,48,1024]{2,1,0:T(8,128)(2,1)S(1)} %pad_maximum_fusion.1.a0), channel_id=1, source_target_pairs={{0,6},{2,4},{4,2},{6,0},{8,14},{10,12},{12,10},{14,8},{16,22},{18,... | collective-permute-start | bytes 1179656 | tf_op jit(solution)/shard_map/ppermute | solution.py:323
  (2 other events, 1.3 us)

commit v2 on v0

v2 whole, which is shorter than its diff:
```python
import functools

import jax
import jax.numpy as jnp
from jax import lax
from jax.experimental import pallas as pl
from jax.experimental.pallas import tpu as pltpu
from jax.sharding import PartitionSpec as P

FILTER_CENTER = 1.0
FILTER_HALF = 4.0
GROUP = 4
BF16 = jnp.bfloat16
F32 = jnp.float32
SMALL = 16
VMEM_LIMIT = 48 * 1024 * 1024
VMEM = pl.BlockSpec(memory_space=pltpu.VMEM)
SMEM = pl.BlockSpec(memory_space=pltpu.SMEM)
ANY = pl.BlockSpec(memory_space=pl.ANY)


def up(value, step):
    return -(-value // step) * step


def call(body, out_shape, specs, arrays, scratch=(), flops=0, moved=0, out_specs=None, aliases=None):
    if out_specs is None:
        out_specs = [VMEM] * len(out_shape) if isinstance(out_shape, list) else VMEM
    return pl.pallas_call(
        body,
        out_shape=out_shape,
        in_specs=specs,
        out_specs=out_specs,
        scratch_shapes=list(scratch),
        input_output_aliases=aliases or {},
        compiler_params=pltpu.CompilerParams(vmem_limit_bytes=VMEM_LIMIT),
        cost_estimate=pl.CostEstimate(flops=flops, bytes_accessed=moved, transcendentals=0),
    )(*arrays)


def pieces(value):
    top = value.astype(BF16).astype(F32)
    rest = value - top
    middle = rest.astype(BF16).astype(F32)
    return (top, middle, rest - middle)


def paired(re, im, size):
    if size == re.shape[1]:
        return jnp.concatenate([re, im], axis=1)
    fill = jnp.zeros((re.shape[0], size - re.shape[1]), re.dtype)
    return jnp.concatenate([re, fill, im, fill], axis=1)


def pack_body(w, wp, pc, pcp, count, vec, own, other, conn_h, coef_h, pot_h, cap_h, *refs):
    out, conn, coef, pot, cap, small, sems = refs
    copies = [
        pltpu.make_async_copy(src, dst, sems.at[at])
        for at, (src, dst) in enumerate(((conn_h, conn), (coef_h, coef), (pot_h, pot), (cap_h, cap)))
    ]
    for copy in copies:
        copy.start()
    nodes = vec.shape[1]
    cols = pc * GROUP
    total = own[...] + other[...]
    for q in range(GROUP):
        out[q, 0:nodes, 0 : 2 * wp] = paired(
            vec[0, :, q * w : (q + 1) * w], vec[1, :, q * w : (q + 1) * w], wp
        )
        out[q, 0:nodes, 2 * wp :] = paired(
            total[:, q * pc : (q + 1) * pc], total[:, cols + q * pc : cols + (q + 1) * pc], pcp
        ).astype(BF16)
    for copy in copies:
        copy.wait()
    e_cap, elem_nodes = conn.shape
    ids = conn[...]
    high = ids >> 7
    small[...] = jnp.zeros(small.shape, F32)
    small[0:e_cap, 0:elem_nodes] = (ids - (high << 7)).astype(F32)
    small[4 : 4 + e_cap, :] = jnp.full((e_cap, small.shape[1]), 64.0, F32)
    small[4 : 4 + e_cap, 0:elem_nodes] = high.astype(F32)
    lane = lax.broadcasted_iota(jnp.int32, (1, e_cap), 1)
    live = jnp.where(lane < count[0], coef[...], 0.0)
    for at, part in enumerate(pieces(live)):
        small[8 + at : 9 + at, 0:e_cap] = part
    for row, vector in ((11, pot), (12, cap)):
        for at, part in enumerate(pieces(vector[...])):
            small[row : row + 1, at * nodes : (at + 1) * nodes] = part
    for q in range(GROUP):
        out[q, nodes : nodes + SMALL, :] = small[...].astype(BF16)


def rotate_body(parts, scal, vec, rot, *out):
    nodes, bands = vec.shape[1:]
    panel = rot.shape[2]
    mine = pl.ds(pl.multiple_of(scal[3] * bands, bands), bands)
    both = jnp.concatenate([vec[0], vec[1]], axis=0)
    with_re = jnp.dot(both, rot[0, mine, :], preferred_element_type=F32)
    with_im = jnp.dot(both, rot[1, mine, :], preferred_element_type=F32)
    out_re = with_re[0:nodes] - with_im[nodes:]
    out_im = with_im[0:nodes] + with_re[nodes:]
    cols = panel // parts
    for h in range(parts):
        value_re = out_re[:, h * cols : (h + 1) * cols]
        value_im = out_im[:, h * cols : (h + 1) * cols]
        if parts == 2:

            @pl.when(scal[3] == h)
            def _():
                out[0][:, 0:cols] = value_re
                out[0][:, cols : 2 * cols] = value_im

            @pl.when(scal[3] != h)
            def _():
                out[1][:, 0:cols] = value_re
                out[1][:, cols : 2 * cols] = value_im

        else:
            out[0][h, :, 0:cols] = value_re
            out[0][h, :, cols : 2 * cols] = value_im


def column_of(rows, row, nodes):
    line = rows[row : row + 1, 0:nodes] + rows[row : row + 1, nodes : 2 * nodes]
    line = line + rows[row : row + 1, 2 * nodes : 3 * nodes]
    shape = (nodes, nodes)
    diag = lax.broadcasted_iota(jnp.int32, shape, 0) == lax.broadcasted_iota(jnp.int32, shape, 1)
    return jnp.where(diag, line, 0.0), diag


def build_body(nodes, e_cap, scal, own, twin, next_, matrix, k_hi, k_lo, ids, coefs, coefs_s, acc, sem):
    rows_out = k_hi.shape[0]
    width = matrix.shape[0]
    blocks = 3 * GROUP
    odd = scal[1] & 1
    acc[...] = jnp.zeros(acc.shape, F32)
    for source, dz in ((own, 1), (twin, 2 - 2 * odd), (next_, 2 * odd)):
        for p in range(GROUP):
            rows = source[p][:, 0:width].astype(F32)
            t = dz * GROUP + p
            ids[t, 0:4, :] = rows[0:4] + 128.0 * rows[4:8]
            coefs[pl.ds(t, 1), :] = (rows[8:9] + rows[9:10] + rows[10:11])[:, 0:128]
            i = t - 2

            @pl.when((i >= 0) & (i < rows_out))
            def _():
                line, diag = column_of(rows, 11, nodes)
                acc[i, :, 2 * nodes : 3 * nodes] = line - jnp.where(diag, FILTER_CENTER, 0.0)

    copy = pltpu.make_async_copy(coefs, coefs_s, sem)
    copy.start()
    copy.wait()
    span = 3 * nodes

    def one(step, carry):
        t = 1 + step

        def add(count):
            place = lax.broadcasted_iota(jnp.int32, (span, width), 0).astype(F32)
            hots = [jnp.where(place == ids[t, e : e + 1, :], 1.0, 0.0).astype(BF16) for e in range(count)]
            half = jnp.dot(jnp.concatenate(hots, axis=0), matrix[...], preferred_element_type=F32)
            half = [half[e * span : (e + 1) * span] * coefs_s[t, e] for e in range(count)]
            tops = [value.astype(BF16) for value in half]
            lows = [(value - top.astype(F32)).astype(BF16) for value, top in zip(half, tops)]
            full = lax.dot_general(
                jnp.concatenate(tops + lows, axis=1),
                jnp.concatenate(hots + hots, axis=1),
                (((1,), (1,)), ((), ())),
                preferred_element_type=F32,
            )
            for j in range(3):
                i = t + j - 3

                @pl.when((i >= 0) & (i < rows_out))
                def _():
                    acc[i, :, (2 - j) * nodes : (5 - j) * nodes] += full[j * nodes : (j + 1) * nodes, :]

        live = jnp.int32(0)
        for e in range(e_cap):
            live = live + (coefs_s[t, e] != 0.0).astype(jnp.int32)
        steps = [n for n in (1, 2) if n < e_cap] + [e_cap]
        for at, count in enumerate(steps):
            least = steps[at - 1] if at else 0

            @pl.when((live > least) & (live <= count))
            def _():
                add(count)

        return carry

    lax.fori_loop(0, blocks - 2, one, 0)
    for i in range(rows_out):
        value = acc[i] * (1.0 / FILTER_HALF)
        top = value.astype(BF16)
        k_hi[i] = top
        k_lo[i] = (value - top.astype(F32)).astype(BF16)


def filter_body(nodes, wp, pcp, scal, own, twin, next_, k_hi, k_lo, *refs):
    outs = refs[0:GROUP]
    out_left, out_panel, vec, first, cols = refs[GROUP:]
    mine = scal[0]
    lanes = 2 * wp
    rows_out = 2 * GROUP
    odd = scal[1] & 1
    for source, dz in ((own, 1), (twin, 2 - 2 * odd), (next_, 2 * odd)):
        for p in range(GROUP):
            t = dz * GROUP + p
            vec[pl.ds(pl.multiple_of(t * nodes, nodes), nodes), :] = source[p][0:nodes]
            line, _ = column_of(source[p][nodes : nodes + SMALL].astype(F32), 12, nodes)
            column = jnp.sum(line, axis=1, keepdims=True) * (1.0 / FILTER_HALF)
            cols[t] = jnp.broadcast_to(column, (nodes, 128))

    def signs(width):
        return jnp.where(lax.broadcasted_iota(jnp.int32, (1, 2 * width), 1) < width, 1.0, -1.0)

    sign = jnp.concatenate([signs(wp), signs(pcp)], axis=1)

    def applied(source, start, i):
        block = source[start * nodes : (start + 5) * nodes, :]
        total = jnp.dot(k_hi[i], block, preferred_element_type=F32)
        total = total + jnp.dot(k_lo[i], block, preferred_element_type=F32)
        own = source[(start + 2) * nodes : (start + 3) * nodes, :].astype(F32)
        turned = jnp.concatenate(
            [pltpu.roll(own[:, 0:lanes], wp, 1), pltpu.roll(own[:, lanes:], pcp, 1)], axis=1
        )
        return total + (cols[i + 2][:, 0:1] * sign) * turned

    inside_low = scal[1] > 0
    inside_high = scal[1] < scal[2] - 1
    for i in range(rows_out):
        value = applied(vec, i, i)
        if i < 2:
            value = jnp.where(inside_low, value, 0.0)
        if i >= rows_out - 2:
            value = jnp.where(inside_high, value, 0.0)
        first[i * nodes : (i + 1) * nodes, :] = value.astype(BF16)
    for i in range(GROUP):
        anchor = vec[(GROUP + i) * nodes : (GROUP + i + 1) * nodes, :].astype(F32)
        value = (2.0 * applied(first, i, i + 2) - anchor).astype(BF16)
        out_panel[i] = value[:, lanes:]
        out_left[i] = value[:, 0:lanes]
        for k in range(1, GROUP):

            @pl.when((mine ^ k) == i)
            def _():
                outs[k][...] = value[:, 0:lanes]

        @pl.when(mine == i)
        def _():
            outs[0][...] = value[:, 0:lanes]


def collect_body(w, wp, scal, g0, g1, g2, g3, out):
    mine = scal[0]
    for k, part in enumerate((g0, g1, g2, g3)):
        re = part[:, 0:w]
        im = part[:, wp : wp + w]
        for q in range(GROUP):

            @pl.when((mine ^ k) == q)
            def _():
                out[0, :, q * w : (q + 1) * w] = re
                out[1, :, q * w : (q + 1) * w] = im


def overlap_body(w, wp, pc, pcp, parts, scale, split, scal, fields, *refs):
    panels = refs[0 : GROUP * parts]
    outs = refs[GROUP * parts : -4]
    rotated, left, right, result = refs[-4:]
    mine, band = scal[0], scal[3]
    nodes = fields.shape[1]
    tile = 2 * pcp
    chunks = parts * GROUP
    panel = pc * chunks
    for p in range(GROUP):
        left[:, p * nodes : (p + 1) * nodes] = jnp.transpose(fields[p].astype(F32)).astype(BF16)
    for g in range(parts):
        for j in range(GROUP):
            half = (band + g) % parts
            at = pl.multiple_of((half * GROUP + (mine ^ j)) * tile, tile)
            for p in range(GROUP):
                right[p * nodes : (p + 1) * nodes, pl.ds(at, tile)] = panels[g * GROUP + j][p]
    for j in range(GROUP):
        value = panels[j][mine]
        for q in range(GROUP):

            @pl.when((mine ^ j) == q)
            def _():
                rotated[0, :, q * pc : (q + 1) * pc] = value[:, 0:pc]
                rotated[1, :, q * pc : (q + 1) * pc] = value[:, pcp : pcp + pc]

    product = jnp.dot(left[...], right[...], preferred_element_type=F32) * scale
    top, bottom = product[0:w], product[wp : wp + w]
    for s in range(chunks):
        a, b = s * tile, s * tile + pcp
        result[:, s * pc : (s + 1) * pc] = top[:, a : a + pc] - bottom[:, b : b + pc]
        result[:, panel + s * pc : panel + (s + 1) * pc] = top[:, b : b + pc] + bottom[:, a : a + pc]
    if split == 1:
        outs[0][...] = result[...]
    else:
        rows = w // split
        for j in range(split):
            at = pl.multiple_of((scal[1] ^ j) * rows, rows)
            outs[j][...] = result[pl.ds(at, rows), :].astype(BF16)


def sum_body(s0, s1, s2, s3, out):
    total = s0[...].astype(F32) + s1[...].astype(F32)
    total = total + (s2[...].astype(F32) + s3[...].astype(F32))
    out[...] = total.astype(BF16)


def spread_body(w, rows, batch, panel, has_base, scal, *refs):
    parts = refs[0:GROUP]
    out, buffer, sems = refs[GROUP + has_base :]
    mine, group = scal[0], scal[1]
    copies = []
    for k in range(GROUP):
        for at, j in enumerate(batch):
            slot = k * len(batch) + at
            value = parts[k][at].astype(F32)
            buffer[slot, :, 0, :] = value[:, 0:panel]
            buffer[slot, :, 1, :] = value[:, panel : 2 * panel]
            start = (mine ^ k) * w + ((group ^ j) * rows if rows < w else 0)
            copy = pltpu.make_async_copy(buffer.at[slot], out.at[pl.ds(start, rows)], sems.at[slot])
            copy.start()
            copies.append(copy)
    for copy in copies:
        copy.wait()


def on_device(
    orbitals, elem_count, connectivity, elem_coef, elem_matrix, potential, absorber, rotation
):
    nodes, _, bands = orbitals.shape
    blocks = lax.axis_size("elem")
    parts = lax.axis_size("band")
    e_cap, elem_nodes = connectivity.shape[1:]
    panel = rotation.shape[2]
    groups = blocks // GROUP
    w = bands // GROUP
    span = 3 * nodes
    width = up(max(elem_nodes, span), 128)
    wp = max(up(w, 64), width // 2)
    lanes = 2 * wp
    cols = panel // parts
    pc = cols // GROUP
    pcp = up(pc, 64)
    elem = lax.axis_index("elem")
    band = lax.axis_index("band")
    scal = jnp.stack([elem % GROUP, elem // GROUP, jnp.int32(groups), band]).astype(jnp.int32)

    def struct(*shape, dtype=BF16):
        return jax.ShapeDtypeStruct(shape, dtype)

    def in_group(k):
        return [(i, i ^ k) for i in range(blocks)]

    def swap(values):
        return [values[0]] + [lax.ppermute(values[k], "elem", in_group(k)) for k in range(1, GROUP)]

    twins = [(i, i ^ GROUP) for i in range(blocks) if i ^ GROUP < blocks]
    nexts = [(i, i + GROUP) for i in range(blocks - GROUP) if i // GROUP % 2]
    nexts = nexts + [(b, a) for a, b in nexts]

    def neighbours(value):
        return lax.ppermute(value, "elem", twins), lax.ppermute(value, "elem", nexts)

    turn = [(0, 1), (1, 0)]

    vec = jnp.moveaxis(orbitals, 1, 0)
    rot = jnp.moveaxis(rotation, 1, 0)
    half = struct(nodes, 2 * cols, dtype=F32)
    sums = call(
        functools.partial(rotate_body, parts),
        [half, half] if parts == 2 else [struct(parts, nodes, 2 * cols, dtype=F32)],
        [SMEM, VMEM, VMEM],
        (scal, vec, rot),
        flops=2 * nodes * 2 * bands * 2 * panel,
        moved=2 * bands * 2 * panel,
    )
    if parts == 2:
        terms = (sums[0], lax.ppermute(sums[1], "band", turn))
    else:
        whole = lax.psum_scatter(sums[0], "band", scatter_dimension=0, tiled=True)[0]
        terms = (whole, jnp.zeros_like(whole))

    all_lanes = lanes + 2 * pcp
    messages = call(
        functools.partial(pack_body, w, wp, pc, pcp),
        struct(GROUP, nodes + SMALL, all_lanes),
        [SMEM, VMEM, VMEM, VMEM, ANY, ANY, ANY, ANY],
        (elem_count, vec, *terms, connectivity[0], elem_coef, potential[None], absorber[None]),
        scratch=[
            pltpu.VMEM((e_cap, elem_nodes), jnp.int32),
            pltpu.VMEM((1, e_cap), F32),
            pltpu.VMEM((1, nodes), F32),
            pltpu.VMEM((1, nodes), F32),
            pltpu.VMEM((SMALL, all_lanes), F32),
            pltpu.SemaphoreType.DMA((4,)),
        ],
        moved=4 * nodes * bands * 2,
    )
    lines = [[GROUP * z + i for i in range(GROUP)] for z in range(groups)]
    messages = lax.all_to_all(messages, "elem", 0, 0, axis_index_groups=lines, tiled=True)

    small = messages[:, nodes:]
    small_near = neighbours(small)
    near = neighbours(messages)
    matrix = jnp.pad(elem_matrix, ((0, width - elem_nodes), (0, width - elem_nodes)))
    rows_out = 2 * GROUP
    k_hi, k_lo = call(
        functools.partial(build_body, nodes, e_cap),
        [struct(rows_out, nodes, 5 * nodes)] * 2,
        [SMEM] + [VMEM] * 4,
        (scal, small, *small_near, matrix),
        scratch=[
            pltpu.VMEM((3 * GROUP, 8, width), F32),
            pltpu.VMEM((up(3 * GROUP, 8), 128), F32),
            pltpu.SMEM((up(3 * GROUP, 8), 128), F32),
            pltpu.VMEM((rows_out, nodes, 5 * nodes), F32),
            pltpu.SemaphoreType.DMA,
        ],
        flops=2 * 40 * 3 * width * width * span,
        moved=4 * rows_out * nodes * 5 * nodes,
    )
    *fields, left, out_panel = call(
        functools.partial(filter_body, nodes, wp, pcp),
        [struct(nodes, lanes)] * GROUP + [struct(GROUP, nodes, lanes), struct(GROUP, nodes, 2 * pcp)],
        [SMEM] + [VMEM] * 5,
        (scal, messages, *near, k_hi, k_lo),
        scratch=[
            pltpu.VMEM((3 * GROUP * nodes, all_lanes), BF16),
            pltpu.VMEM((rows_out * nodes, all_lanes), BF16),
            pltpu.VMEM((3 * GROUP, nodes, 128), F32),
        ],
        flops=2 * 2 * 12 * nodes * 5 * nodes * all_lanes,
        moved=4 * rows_out * nodes * 5 * nodes,
    )

    gathered = swap([out_panel] * GROUP)
    if parts == 2:
        all_panels = gathered + [lax.ppermute(x, "band", turn) for x in gathered]
    else:
        every = lax.all_gather(jnp.stack(gathered), "band", axis=0)
        every = jnp.roll(every, -band, axis=0)
        all_panels = [every[h, j] for h in range(parts) for j in range(GROUP)]

    direct = groups == 4 and w % (groups * 16) == 0
    split = groups if direct else 1
    rows = w // split
    *terms, rotated = call(
        functools.partial(
            overlap_body, w, wp, pc, pcp, parts, 1.0 / (nodes * blocks) ** 0.5, split
        ),
        [struct(rows, 2 * panel, dtype=BF16 if direct else F32)] * split + [struct(2, nodes, cols)],
        [SMEM] + [VMEM] * (1 + GROUP * parts),
        (scal, left, *all_panels),
        scratch=[
            pltpu.VMEM((lanes, GROUP * nodes), BF16),
            pltpu.VMEM((GROUP * nodes, 2 * pcp * GROUP * parts), BF16),
            pltpu.VMEM((w, 2 * panel), F32),
        ],
        flops=2 * GROUP * nodes * lanes * 2 * panel,
        moved=4 * GROUP * nodes * panel,
    )
    fields, _ = lax.optimization_barrier((list(fields), gathered[GROUP - 1]))
    received = swap(fields)
    filtered = call(
        functools.partial(collect_body, w, wp),
        struct(2, nodes, bands),
        [SMEM] + [VMEM] * GROUP,
        (scal, *received),
    )
    if direct:

        def across(values):
            return [values[0]] + [
                lax.ppermute(values[j], "elem", [(i, i ^ (GROUP * j)) for i in range(blocks)])
                for j in range(1, split)
            ]

        moved = across(terms)
        moved, filtered = lax.optimization_barrier((moved, filtered))
        own = call(sum_body, struct(rows, 2 * panel), [VMEM] * split, moved)
        stack = across([own] * split)
        batches = [[0], list(range(1, split))]
    else:
        lines = [[GROUP * z + i for z in range(groups)] for i in range(GROUP)]
        stack = [lax.psum(terms[0], "elem", axis_index_groups=lines).astype(BF16)]
        batches = [[0]]
    intersection = None
    spread = None
    for batch in batches:
        ready = jnp.stack([stack[j] for j in batch])
        if spread is not None:
            ready, spread = lax.optimization_barrier((ready, spread))
        base = [] if intersection is None else [intersection]
        spread = swap([ready] * GROUP)
        intersection = call(
            functools.partial(spread_body, w, rows, batch, panel, len(base)),
            struct(bands, 2, panel, dtype=F32),
            [SMEM] + [VMEM] * GROUP + [ANY] * len(base),
            (scal, *spread, *base),
            scratch=[
                pltpu.VMEM((GROUP * len(batch), rows, 2, panel), F32),
                pltpu.SemaphoreType.DMA((GROUP * len(batch),)),
            ],
            out_specs=ANY,
            aliases={GROUP + 1: 0} if base else None,
        )
    return (jnp.moveaxis(filtered, 0, 1), jnp.moveaxis(rotated, 0, 1), intersection)


def solution(mesh):
    placed = (
        P("elem", None, "band"),
        P("elem"),
        P("elem", None, None),
        P("elem", None),
        P(),
        P("elem"),
        P("elem"),
        P(),
    )
    return jax.shard_map(
        on_device,
        mesh=mesh,
        in_specs=placed,
        out_specs=(P("elem", None, "band"), P("elem", None, "band"), P("band", None, None)),
        check_vma=False,
    )
```

time: 432 us -> 106 us (0.25)
  waiting for transfers between devices: 269 us -> 24.5 us
  other arithmetic: 43 us -> 0.11 us
  local copies, waits for them, and re-layouts: 33.3 us -> 6.08 us
  Pallas kernels: 0 us -> 22.4 us
  starting transfers between devices: 54.3 us -> 36.2 us
  between operations: 14.4 us -> 1.66 us
  matrix products: 12 us -> 0 us
  blocking collectives: 4.62 us -> 14.6 us
    psum x1 -> x0, waiting for transfers between devices: 143 us -> none  [on_device(): intersection = lax.psum(local_intersection, 'elem')]
    ppermute x8 -> x27, waiting for transfers between devices: 126 us -> 24.5 us  [the longest x12 12.9 us: swap(): lax.ppermute(values[k], 'elem', in_group(k))]
    pallas_call x0 -> x9, Pallas kernels: none -> 22.4 us  [call(): pl.pallas_call(body, out_shape=out_shape, in_specs=specs, out_specs=out_s...]
    ppermute x8 -> x27, starting transfers between devices: 54.2 us -> 36.2 us  [the longest x12 14.5 us: swap(): lax.ppermute(values[k], 'elem', in_group(k))]
    all_to_all x0 -> x1, blocking collectives: none -> 14.6 us  [on_device(): lax.all_to_all(messages, 'elem', 0, 0, axis_index_groups=lines, tiled=True)]
    dot_general x4 -> x0, matrix products: 12 us -> none  [the longest x2 7.91 us: one_element(): jnp.dot(elem_matrix, flat_field[node_ids], preferred_element_type=jnp.flo...]
    dot_general x1 -> x0, other arithmetic: 11.9 us -> none  [on_device(): jnp.dot(piece_flat, complex_block(rot_mine), preferred_element_type=jnp.f...]
    scatter-add x2 -> x0, other arithmetic: 11.5 us -> none  [one_element(): return totals.at[node_ids].add(product * elem_coef[0, element])]
  transfers between devices with their start and end apart: 9 -> 27, of which waited for: 9 -> 11; matrix products, arithmetic and copies ran while one was open for 6% -> 2% of each run, Pallas kernels for 0% -> 14%
where the time goes in v2:
time: 106 us
  starting transfers between devices  36.2 us (34%)
  waiting for transfers between devices  24.5 us (23%)
  Pallas kernels  22.4 us (21%)
  blocking collectives  14.6 us (14%)
  local copies, waits for them, and re-layouts  6.08 us (6%)
  between operations  1.66 us (2%)
    pallas_call x9, Pallas kernels, call(): pl.pallas_call(body, out_shape=out_shape, in_specs=specs, out_specs=out_s...  22.4 us
    all_to_all x1, blocking collectives, on_device(): lax.all_to_all(messages, 'elem', 0, 0, axis_index_groups=lines, tiled=True)  14.6 us
    ppermute x12, starting transfers between devices, swap(): lax.ppermute(values[k], 'elem', in_group(k))  14.5 us
    ppermute x6, starting transfers between devices, across(): lax.ppermute(values[j], 'elem', [(i, i ^ GROUP * j) for i in range(blocks)])  13.2 us
    ppermute x12, waiting for transfers between devices, swap(): lax.ppermute(values[k], 'elem', in_group(k))  12.9 us
    ppermute x6, waiting for transfers between devices, across(): lax.ppermute(values[j], 'elem', [(i, i ^ GROUP * j) for i in range(blocks)])  8.83 us
    ppermute x2, starting transfers between devices, neighbours(): lax.ppermute(value, 'elem', twins)  6.21 us
    unnamed x14, local copies, waits for them, and re-layouts  6.05 us
  transfers between devices with their start and end apart: 27, of which 11 were waited for; matrix products, arithmetic and copies ran while one was open for 2% of the time, Pallas kernels for 14%

profile of v2, /device:TPU:0, one launch (start us, length us, event | category | flops | bytes accessed | tf_op | source)
XLA Modules:
  0.0 105.5 jit_solution(7741416072543541067)
XLA Ops:
  0.6 1.0 copy.19
  1.7 2.4 %copy.18 = bf16[1536,2,512]{2,0,1:T(8,128)(2,1)S(1)} copy(bf16[1536,2,512]{2,1,0:T(2,128)(2,1)} %param.15) | data formatting | bytes 6291456 | tf_op args[7]
  4.2 1.2 %shard_map.103 = (f32[128,512]{1,0:T(8,128)S(1)}, f32[128,512]{1,0:T(8,128)S(1)}) custom-call(s32[4]{0:T(128)S(1)} %pad_add_fusion.scal, bf16[2,128,768]{2,1,0:T(8,128)(2,1)S(1)} %bitcast.19, bf16[2,1536,512]{2,1,0:T(8,128)(2,1)S(1)} %bitcast.18), custom_call_target="tpu_custom_call" | custom-call | flops 402653184 | bytes 1572864 | tf_op jit(solution)/shard_map/pallas_call | solution.py:29
  8.0 14.6 %all_to_all.5.own = bf16[4,144,512]{2,1,0:T(8,128)(2,1)S(1)} all-to-all(bf16[4,144,512]{2,1,0:T(8,128)(2,1)S(1)} %shard_map.104), channel_id=1, replica_groups={{0,2,4,6},{8,10,12,14},{16,18,20,22},{24,26,28,30},{1,3,5,7},{9,11,13,1..., dimensions={0} | all-to-all | bytes 1179648 | tf_op jit(solution)/shard_map/all_to_all | solution.py:406
  23.2 4.5 %collective-permute-start.3 = (bf16[4,16,512]{2,1,0:T(8,128)(2,1)S(1)}, bf16[4,16,512]{2,1,0:T(8,128)(2,1)S(1)}, u32[]{:S(2)}, u32[]{:S(2)}) collective-permute-start(bf16[4,16,512]{2,1,0:T(8,128)(2,1)S(1)} %slice.4.own), channel_id=1, source_target_pairs={{0,8},{2,10},{4,12},{6,14},{8,0},{10,2},{12,4},{14,6},{16,24},{18,... | collective-permute-start | bytes 196616 | tf_op jit(solution)/shard_map/ppermute | solution.py:368
  28.5 1.8 %collective-permute-start.1 = (bf16[4,144,512]{2,1,0:T(8,128)(2,1)S(1)}, bf16[4,144,512]{2,1,0:T(8,128)(2,1)S(1)}, u32[]{:S(2)}, u32[]{:S(2)}) collective-permute-start(bf16[4,144,512]{2,1,0:T(8,128)(2,1)S(1)} %all_to_all.5.own), channel_id=1, source_target_pairs={{0,8},{2,10},{4,12},{6,14},{8,0},{10,2},{12,4},{14,6},{16,24},{18,... | collective-permute-start | bytes 1769480 | tf_op jit(solution)/shard_map/ppermute | solution.py:368
  30.7 10.0 %shard_map.105 = (bf16[8,128,640]{2,1,0:T(8,128)(2,1)S(1)}, bf16[8,128,640]{2,1,0:T(8,128)(2,1)S(1)}) custom-call(s32[4]{0:T(128)S(1)} %pad_add_fusion.scal, bf16[4,16,512]{2,1,0:T(8,128)(2,1)S(1)} %slice.4.own, bf16[4,16,512]{2,1,0:T(8,128)(2,1)S(1)} %collective-permute-done.3.twin, bf16[4,16,512]{2,1,0:T(8,128)(2,1)S(1)} %collective-permute-done.4.next_, ...), custom_call_target="tpu_custom_call" | custom-call | flops 13589544960 | bytes 2621440 | tf_op jit(solution)/shard_map/pallas_call | solution.py:29
  40.7 1.8 %collective-permute-done.1.twin = bf16[4,144,512]{2,1,0:T(8,128)(2,1)S(1)} collective-permute-done((bf16[4,144,512]{2,1,0:T(8,128)(2,1)S(1)}, bf16[4,144,512]{2,1,0:T(8,128)(2,1)S(1)}, u32[]{:S(2)}, u32[]{:S(2)}) %collective-permute-start.1) | collective-permute-done | bytes 589856 | tf_op jit(solution)/shard_map/ppermute | solution.py:368
  42.5 4.1 %shard_map.106 = (bf16[128,384]{1,0:T(8,128)(2,1)S(1)}, bf16[128,384]{1,0:T(8,128)(2,1)S(1)}, bf16[128,384]{1,0:T(8,128)(2,1)S(1)}, bf16[128,384]{1,0:T(8,128)(2...) custom-call(s32[4]{0:T(128)S(1)} %pad_add_fusion.scal, ...), custom_call_target="tpu_custom_call" | custom-call | flops 2013265920 | bytes 2621440 | tf_op jit(solution)/shard_map/pallas_call | solution.py:29
  47.6 1.5 %collective-permute-start.6 = (bf16[4,128,128]{2,1,0:T(8,128)(2,1)S(1)}, bf16[4,128,128]{2,1,0:T(8,128)(2,1)S(1)}, u32[]{:S(2)}, u32[]{:S(2)}) collective-permute-start(bf16[4,128,128]{2,1,0:T(8,128)(2,1)S(1)} %get-tuple-element.33.refs_0_), channel_id=1, source_target_pairs={{0,4},{2,6},{4,0},{6,2},{8,12},{10,14},{12,8},{14,10},{16,20},{18,... | collective-permute-start | bytes 393224 | tf_op jit(solution)/shard_map/ppermute | solution.py:361
  49.0 1.2 %collective-permute-start.5 = (bf16[4,128,128]{2,1,0:T(8,128)(2,1)S(1)}, bf16[4,128,128]{2,1,0:T(8,128)(2,1)S(1)}, u32[]{:S(2)}, u32[]{:S(2)}) collective-permute-start(bf16[4,128,128]{2,1,0:T(8,128)(2,1)S(1)} %get-tuple-element.33.refs_0_), channel_id=1, source_target_pairs={{0,2},{2,0},{4,6},{6,4},{8,10},{10,8},{12,14},{14,12},{16,18},{18,... | collective-permute-start | bytes 393224 | tf_op jit(solution)/shard_map/ppermute | solution.py:361
  50.2 2.5 %collective-permute-done.7.refs_3_ = bf16[4,128,128]{2,1,0:T(8,128)(2,1)S(1)} collective-permute-done((bf16[4,128,128]{2,1,0:T(8,128)(2,1)S(1)}, bf16[4,128,128]{2,1,0:T(8,128)(2,1)S(1)}, u32[]{:S(2)}, u32[]{:S(2)}) %collective-permute-start.7) | collective-permute-done | bytes 131104 | tf_op jit(solution)/shard_map/ppermute | solution.py:361
  52.7 1.2 %collective-permute-done.6.refs_2_ = bf16[4,128,128]{2,1,0:T(8,128)(2,1)S(1)} collective-permute-done((bf16[4,128,128]{2,1,0:T(8,128)(2,1)S(1)}, bf16[4,128,128]{2,1,0:T(8,128)(2,1)S(1)}, u32[]{:S(2)}, u32[]{:S(2)}) %collective-permute-start.6) | collective-permute-done | bytes 131104 | tf_op jit(solution)/shard_map/ppermute | solution.py:361
  56.3 1.6 %collective-permute-start.17 = (bf16[128,384]{1,0:T(8,128)(2,1)S(1)}, bf16[128,384]{1,0:T(8,128)(2,1)S(1)}, u32[]{:S(2)}, u32[]{:S(2)}) collective-permute-start(bf16[128,384]{1,0:T(8,128)(2,1)S(1)} %get-tuple-element.45), channel_id=1, source_target_pairs={{0,6},{2,4},{4,2},{6,0},{8,14},{10,12},{12,10},{14,8},{16,22},{18,... | collective-permute-start | bytes 294920 | tf_op jit(solution)/shard_map/ppermute | solution.py:361
  57.9 2.3 %shard_map.107 = (bf16[48,1024]{1,0:T(8,128)(2,1)S(1)}, bf16[48,1024]{1,0:T(8,128)(2,1)S(1)}, bf16[48,1024]{1,0:T(8,128)(2,1)S(1)}, bf16[48,1024]{1,0:T(8,128)(2,1)S(1)}, bf16[2,128,256]{2,1,0:T(8,128)(2,1)S(1)}) custom-call(s32[4]{0:T(128)S(1)} %pad_add_fusion.scal, bf16[4,128,384]{2,1,0:T(8,128)(2,1)S(1)} %get-tuple-element.32.fields, ...), custom_call_target="tpu_custom_call" | custom-call | flops 402653184 | bytes 1048576 | tf_op jit(solution)/shard_map/pallas_call | solution.py:29
  60.2 6.3 %collective-permute-start.12 = (bf16[48,1024]{1,0:T(8,128)(2,1)S(1)}, bf16[48,1024]{1,0:T(8,128)(2,1)S(1)}, u32[]{:S(2)}, u32[]{:S(2)}) collective-permute-start(bf16[48,1024]{1,0:T(8,128)(2,1)S(1)} %get-tuple-element.35), channel_id=1, source_target_pairs={{0,8},{2,10},{4,12},{6,14},{8,0},{10,2},{12,4},{14,6},{16,24},{18,... | collective-permute-start | bytes 294920 | tf_op jit(solution)/shard_map/ppermute | solution.py:480
  66.5 2.4 %collective-permute-start.14 = (bf16[48,1024]{1,0:T(8,128)(2,1)S(1)}, bf16[48,1024]{1,0:T(8,128)(2,1)S(1)}, u32[]{:S(2)}, u32[]{:S(2)}) collective-permute-start(bf16[48,1024]{1,0:T(8,128)(2,1)S(1)} %get-tuple-element.37), channel_id=1, source_target_pairs={{0,24},{2,26},{4,28},{6,30},{8,16},{10,18},{12,20},{14,22},{16,8},... | collective-permute-start | bytes 294920 | tf_op jit(solution)/shard_map/ppermute | solution.py:480
  69.9 6.1 %collective-permute-done.13.s2 = bf16[48,1024]{1,0:T(8,128)(2,1)S(1)} collective-permute-done((bf16[48,1024]{1,0:T(8,128)(2,1)S(1)}, bf16[48,1024]{1,0:T(8,128)(2,1)S(1)}, u32[]{:S(2)}, u32[]{:S(2)}) %collective-permute-start.13) | collective-permute-done | bytes 98336 | tf_op jit(solution)/shard_map/ppermute | solution.py:480
  76.0 1.6 %collective-permute-start.20 = (bf16[48,1024]{1,0:T(8,128)(2,1)S(1)}, bf16[48,1024]{1,0:T(8,128)(2,1)S(1)}, u32[]{:S(2)}, u32[]{:S(2)}) collective-permute-start(bf16[48,1024]{1,0:T(8,128)(2,1)S(1)} %shard_map.109), channel_id=1, source_target_pairs={{0,24},{2,26},{4,28},{6,30},{8,16},{10,18},{12,20},{14,22},{16,8},... | collective-permute-start | bytes 294920 | tf_op jit(solution)/shard_map/ppermute | solution.py:480
  77.7 1.6 %collective-permute-start.19 = (bf16[48,1024]{1,0:T(8,128)(2,1)S(1)}, bf16[48,1024]{1,0:T(8,128)(2,1)S(1)}, u32[]{:S(2)}, u32[]{:S(2)}) collective-permute-start(bf16[48,1024]{1,0:T(8,128)(2,1)S(1)} %shard_map.109), channel_id=1, source_target_pairs={{0,16},{2,18},{4,20},{6,22},{8,24},{10,26},{12,28},{14,30},{16,0},... | collective-permute-start | bytes 294920 | tf_op jit(solution)/shard_map/ppermute | solution.py:480
  79.3 1.2 %collective-permute-start.18 = (bf16[48,1024]{1,0:T(8,128)(2,1)S(1)}, bf16[48,1024]{1,0:T(8,128)(2,1)S(1)}, u32[]{:S(2)}, u32[]{:S(2)}) collective-permute-start(bf16[48,1024]{1,0:T(8,128)(2,1)S(1)} %shard_map.109), channel_id=1, source_target_pairs={{0,8},{2,10},{4,12},{6,14},{8,0},{10,2},{12,4},{14,6},{16,24},{18,... | collective-permute-start | bytes 294920 | tf_op jit(solution)/shard_map/ppermute | solution.py:480
  80.5 1.5 %collective-permute-start.23 = (bf16[1,48,1024]{2,1,0:T(8,128)(2,1)S(1)}, bf16[1,48,1024]{2,1,0:T(8,128)(2,1)S(1)}, u32[]{:S(2)}, u32[]{:S(2)}) collective-permute-start(bf16[1,48,1024]{2,1,0:T(8,128)(2,1)S(1)} %bitcast.22), channel_id=1, source_target_pairs={{0,6},{2,4},{4,2},{6,0},{8,14},{10,12},{12,10},{14,8},{16,22},{18,... | collective-permute-start | bytes 294920 | tf_op jit(solution)/shard_map/ppermute | solution.py:361
  82.0 1.2 %collective-permute-start.22 = (bf16[1,48,1024]{2,1,0:T(8,128)(2,1)S(1)}, bf16[1,48,1024]{2,1,0:T(8,128)(2,1)S(1)}, u32[]{:S(2)}, u32[]{:S(2)}) collective-permute-start(bf16[1,48,1024]{2,1,0:T(8,128)(2,1)S(1)} %bitcast.23), channel_id=1, source_target_pairs={{0,4},{2,6},{4,0},{6,2},{8,12},{10,14},{12,8},{14,10},{16,20},{18,... | collective-permute-start | bytes 294920 | tf_op jit(solution)/shard_map/ppermute | solution.py:361
  83.2 1.2 %collective-permute-start.21 = (bf16[1,48,1024]{2,1,0:T(8,128)(2,1)S(1)}, bf16[1,48,1024]{2,1,0:T(8,128)(2,1)S(1)}, u32[]{:S(2)}, u32[]{:S(2)}) collective-permute-start(bf16[1,48,1024]{2,1,0:T(8,128)(2,1)S(1)} %bitcast.24), channel_id=1, source_target_pairs={{0,2},{2,0},{4,6},{6,4},{8,10},{10,8},{12,14},{14,12},{16,18},{18,... | collective-permute-start | bytes 294920 | tf_op jit(solution)/shard_map/ppermute | solution.py:361
  84.5 2.7 %collective-permute-done.19 = bf16[48,1024]{1,0:T(8,128)(2,1)S(1)} collective-permute-done((bf16[48,1024]{1,0:T(8,128)(2,1)S(1)}, bf16[48,1024]{1,0:T(8,128)(2,1)S(1)}, u32[]{:S(2)}, u32[]{:S(2)}) %collective-permute-start.19) | collective-permute-done | bytes 98336 | tf_op jit(solution)/shard_map/ppermute | solution.py:480
  87.9 1.7 %collective-permute-start.26 = (bf16[3,48,1024]{2,1,0:T(8,128)(2,1)S(1)}, bf16[3,48,1024]{2,1,0:T(8,128)(2,1)S(1)}, u32[]{:S(2)}, u32[]{:S(2)}) collective-permute-start(bf16[3,48,1024]{2,1,0:T(8,128)(2,1)S(1)} %pad_maximum_fusion.refs_0_), channel_id=1, source_target_pairs={{0,6},{2,4},{4,2},{6,0},{8,14},{10,12},{12,10},{14,8},{16,22},{18,... | collective-permute-start | bytes 884744 | tf_op jit(solution)/shard_map/ppermute | solution.py:361
  89.6 1.0 collective-permute-start.25
  92.1 1.1 %copy.14 = bf16[128,2,768]{2,1,0:T(2,128)(2,1)} copy(bf16[128,2,768]{2,0,1:T(8,128)(2,1)S(1)} %bitcast.21) | data formatting | bytes 786432
  93.3 1.5 %shard_map.110.refs_4_ = f32[768,2,512]{2,1,0:T(2,128)} custom-call(s32[4]{0:T(128)S(1)} %pad_add_fusion.scal, bf16[1,48,1024]{2,1,0:T(8,128)(2,1)S(1)} %bitcast.25, bf16[1,48,1024]{2,1,0:T(8,128)(2,1)S(1)} %collective-permute-done.21.refs_1_, bf16[1,48,1024]{2,1,0:T(8,128)(2,1)S(1)} %collective-permute-done.22.refs_2_, ...), custom_call_target="tpu_custom_call" | custom-call | tf_op jit(solution)/shard_map/pallas_call | solution.py:29
  94.8 4.0 %collective-permute-done.26.refs_3_ = bf16[3,48,1024]{2,1,0:T(8,128)(2,1)S(1)} collective-permute-done((bf16[3,48,1024]{2,1,0:T(8,128)(2,1)S(1)}, bf16[3,48,1024]{2,1,0:T(8,128)(2,1)S(1)}, u32[]{:S(2)}, u32[]{:S(2)}) %collective-permute-start.26) | collective-permute-done | bytes 294944 | tf_op jit(solution)/shard_map/ppermute | solution.py:361
  98.7 4.5 %collective-permute-done.25.refs_2_ = bf16[3,48,1024]{2,1,0:T(8,128)(2,1)S(1)} collective-permute-done((bf16[3,48,1024]{2,1,0:T(8,128)(2,1)S(1)}, bf16[3,48,1024]{2,1,0:T(8,128)(2,1)S(1)}, u32[]{:S(2)}, u32[]{:S(2)}) %collective-permute-start.25) | collective-permute-done | bytes 294944 | tf_op jit(solution)/shard_map/ppermute | solution.py:361
  103.3 2.1 %shard_map.111 = f32[768,2,512]{2,1,0:T(2,128)} custom-call(s32[4]{0:T(128)S(1)} %pad_add_fusion.scal, bf16[3,48,1024]{2,1,0:T(8,128)(2,1)S(1)} %pad_maximum_fusion.refs_0_, bf16[3,48,1024]{2,1,0:T(8,128)(2,1)S(1)} %collective-permute-done.24.refs_1_, bf16[3,48,1024]{2,1,0:T(8,128)(2,1)S(1)} %collective-permute-done.25.refs_2_, ...), custom_call_target="tpu_custom_call", output_to_operand_aliasing={{}: (5, {})} | custom-call | tf_op jit(solution)/shard_map/pallas_call | solution.py:29
  (50 shorter events, 10.4 us)
Async XLA Ops:
  4.1 3.0 %copy-start = (s32[1,4,343]{2,1,0:T(4,128)S(1)}, s32[1,4,343]{2,1,0:T(4,128)}, u32[]{:S(2)}) copy-start(s32[1,4,343]{2,1,0:T(4,128)} %param.10) | copy-start | bytes 16468
  4.1 3.0 %copy-start.1 = (f32[1,4]{1,0:T(1,128)S(1)}, f32[1,4]{1,0:T(1,128)}, u32[]{:S(2)}) copy-start(f32[1,4]{1,0:T(1,128)} %coef_h.1) | copy-start | bytes 52
  4.1 3.0 %copy-start.2 = (f32[128]{0:T(128)S(1)}, f32[128]{0:T(128)}, u32[]{:S(2)}) copy-start(f32[128]{0:T(128)} %param.13) | copy-start | bytes 1540
  4.2 23.5 %copy-start.4 = (bf16[343,343]{1,0:T(8,128)(2,1)S(1)}, bf16[343,343]{1,0:T(8,128)(2,1)}, u32[]{:S(2)}) copy-start(bf16[343,343]{1,0:T(8,128)(2,1)} %param.12) | copy-start | bytes 705898
  5.4 1.7 %collective-permute-start = (f32[128,512]{1,0:T(8,128)S(1)}, f32[128,512]{1,0:T(8,128)S(1)}, u32[]{:S(2)}, u32[]{:S(2)}) collective-permute-start(f32[128,512]{1,0:T(8,128)S(1)} %get-tuple-element.29), channel_id=1, source_target_pairs={{0,1},{1,0},{2,3},{3,2},{4,5},{5,4},{6,7},{7,6},{8,9},{9,8},{10,11... | collective-permute-start | bytes 786440 | tf_op jit(solution)/shard_map/ppermute | solution.py:384
  7.1 0.7 copy-start.3
  22.6 7.6 %collective-permute-start.4 = (bf16[4,16,512]{2,1,0:T(8,128)(2,1)S(1)}, bf16[4,16,512]{2,1,0:T(8,128)(2,1)S(1)}, u32[]{:S(2)}, u32[]{:S(2)}) collective-permute-start(bf16[4,16,512]{2,1,0:T(8,128)(2,1)S(1)} %slice.4.own), channel_id=1, source_target_pairs={{8,16},{10,18},{12,20},{14,22},{16,8},{18,10},{20,12},{22,14},{9,1... | collective-permute-start | bytes 196616 | tf_op jit(solution)/shard_map/ppermute | solution.py:368
  23.2 7.4 %collective-permute-start.3 = (bf16[4,16,512]{2,1,0:T(8,128)(2,1)S(1)}, bf16[4,16,512]{2,1,0:T(8,128)(2,1)S(1)}, u32[]{:S(2)}, u32[]{:S(2)}) collective-permute-start(bf16[4,16,512]{2,1,0:T(8,128)(2,1)S(1)} %slice.4.own), channel_id=1, source_target_pairs={{0,8},{2,10},{4,12},{6,14},{8,0},{10,2},{12,4},{14,6},{16,24},{18,... | collective-permute-start | bytes 196616 | tf_op jit(solution)/shard_map/ppermute | solution.py:368
  27.7 13.0 %collective-permute-start.2 = (bf16[4,144,512]{2,1,0:T(8,128)(2,1)S(1)}, bf16[4,144,512]{2,1,0:T(8,128)(2,1)S(1)}, u32[]{:S(2)}, u32[]{:S(2)}) collective-permute-start(bf16[4,144,512]{2,1,0:T(8,128)(2,1)S(1)} %all_to_all.5.own), channel_id=1, source_target_pairs={{8,16},{10,18},{12,20},{14,22},{16,8},{18,10},{20,12},{22,14},{9,1... | collective-permute-start | bytes 1769480 | tf_op jit(solution)/shard_map/ppermute | solution.py:368
  28.5 14.1 %collective-permute-start.1 = (bf16[4,144,512]{2,1,0:T(8,128)(2,1)S(1)}, bf16[4,144,512]{2,1,0:T(8,128)(2,1)S(1)}, u32[]{:S(2)}, u32[]{:S(2)}) collective-permute-start(bf16[4,144,512]{2,1,0:T(8,128)(2,1)S(1)} %all_to_all.5.own), channel_id=1, source_target_pairs={{0,8},{2,10},{4,12},{6,14},{8,0},{10,2},{12,4},{14,6},{16,24},{18,... | collective-permute-start | bytes 1769480 | tf_op jit(solution)/shard_map/ppermute | solution.py:368
  46.7 6.0 %collective-permute-start.7 = (bf16[4,128,128]{2,1,0:T(8,128)(2,1)S(1)}, bf16[4,128,128]{2,1,0:T(8,128)(2,1)S(1)}, u32[]{:S(2)}, u32[]{:S(2)}) collective-permute-start(bf16[4,128,128]{2,1,0:T(8,128)(2,1)S(1)} %get-tuple-element.33.refs_0_), channel_id=1, source_target_pairs={{0,6},{2,4},{4,2},{6,0},{8,14},{10,12},{12,10},{14,8},{16,22},{18,... | collective-permute-start | bytes 393224 | tf_op jit(solution)/shard_map/ppermute | solution.py:361
  47.6 6.4 %collective-permute-start.6 = (bf16[4,128,128]{2,1,0:T(8,128)(2,1)S(1)}, bf16[4,128,128]{2,1,0:T(8,128)(2,1)S(1)}, u32[]{:S(2)}, u32[]{:S(2)}) collective-permute-start(bf16[4,128,128]{2,1,0:T(8,128)(2,1)S(1)} %get-tuple-element.33.refs_0_), channel_id=1, source_target_pairs={{0,4},{2,6},{4,0},{6,2},{8,12},{10,14},{12,8},{14,10},{16,20},{18,... | collective-permute-start | bytes 393224 | tf_op jit(solution)/shard_map/ppermute | solution.py:361
  49.0 5.0 %collective-permute-start.5 = (bf16[4,128,128]{2,1,0:T(8,128)(2,1)S(1)}, bf16[4,128,128]{2,1,0:T(8,128)(2,1)S(1)}, u32[]{:S(2)}, u32[]{:S(2)}) collective-permute-start(bf16[4,128,128]{2,1,0:T(8,128)(2,1)S(1)} %get-tuple-element.33.refs_0_), channel_id=1, source_target_pairs={{0,2},{2,0},{4,6},{6,4},{8,10},{10,8},{12,14},{14,12},{16,18},{18,... | collective-permute-start | bytes 393224 | tf_op jit(solution)/shard_map/ppermute | solution.py:361
  50.2 5.1 %collective-permute-start.8 = (bf16[4,128,128]{2,1,0:T(8,128)(2,1)S(1)}, bf16[4,128,128]{2,1,0:T(8,128)(2,1)S(1)}, u32[]{:S(2)}, u32[]{:S(2)}) collective-permute-start(bf16[4,128,128]{2,1,0:T(8,128)(2,1)S(1)} %get-tuple-element.33.refs_0_), channel_id=1, source_target_pairs={{0,1},{1,0},{2,3},{3,2},{4,5},{5,4},{6,7},{7,6},{8,9},{9,8},{10,11... | collective-permute-start | bytes 393224 | tf_op jit(solution)/shard_map/ppermute | solution.py:444
  52.7 3.6 %collective-permute-start.11 = (bf16[4,128,128]{2,1,0:T(8,128)(2,1)S(1)}, bf16[4,128,128]{2,1,0:T(8,128)(2,1)S(1)}, u32[]{:S(2)}, u32[]{:S(2)}) collective-permute-start(bf16[4,128,128]{2,1,0:T(8,128)(2,1)S(1)} %collective-permute-done.7.refs_3_), channel_id=1, source_target_pairs={{0,1},{1,0},{2,3},{3,2},{4,5},{5,4},{6,7},{7,6},{8,9},{9,8},{10,11... | collective-permute-start | bytes 393224 | tf_op jit(solution)/shard_map/ppermute | solution.py:444
  53.9 4.0 %collective-permute-start.10 = (bf16[4,128,128]{2,1,0:T(8,128)(2,1)S(1)}, bf16[4,128,128]{2,1,0:T(8,128)(2,1)S(1)}, u32[]{:S(2)}, u32[]{:S(2)}) collective-permute-start(bf16[4,128,128]{2,1,0:T(8,128)(2,1)S(1)} %collective-permute-done.6.refs_2_), channel_id=1, source_target_pairs={{0,1},{1,0},{2,3},{3,2},{4,5},{5,4},{6,7},{7,6},{8,9},{9,8},{10,11... | collective-permute-start | bytes 393224 | tf_op jit(solution)/shard_map/ppermute | solution.py:444
  54.0 4.0 %collective-permute-start.9 = (bf16[4,128,128]{2,1,0:T(8,128)(2,1)S(1)}, bf16[4,128,128]{2,1,0:T(8,128)(2,1)S(1)}, u32[]{:S(2)}, u32[]{:S(2)}) collective-permute-start(bf16[4,128,128]{2,1,0:T(8,128)(2,1)S(1)} %collective-permute-done.5.refs_1_), channel_id=1, source_target_pairs={{0,1},{1,0},{2,3},{3,2},{4,5},{5,4},{6,7},{7,6},{8,9},{9,8},{10,11... | collective-permute-start | bytes 393224 | tf_op jit(solution)/shard_map/ppermute | solution.py:444
  54.4 12.1 %collective-permute-start.15 = (bf16[128,384]{1,0:T(8,128)(2,1)S(1)}, bf16[128,384]{1,0:T(8,128)(2,1)S(1)}, u32[]{:S(2)}, u32[]{:S(2)}) collective-permute-start(bf16[128,384]{1,0:T(8,128)(2,1)S(1)} %get-tuple-element.43), channel_id=1, source_target_pairs={{0,2},{2,0},{4,6},{6,4},{8,10},{10,8},{12,14},{14,12},{16,18},{18,... | collective-permute-start | bytes 294920 | tf_op jit(solution)/shard_map/ppermute | solution.py:361
  55.4 13.6 %collective-permute-start.16 = (bf16[128,384]{1,0:T(8,128)(2,1)S(1)}, bf16[128,384]{1,0:T(8,128)(2,1)S(1)}, u32[]{:S(2)}, u32[]{:S(2)}) collective-permute-start(bf16[128,384]{1,0:T(8,128)(2,1)S(1)} %get-tuple-element.44), channel_id=1, source_target_pairs={{0,4},{2,6},{4,0},{6,2},{8,12},{10,14},{12,8},{14,10},{16,20},{18,... | collective-permute-start | bytes 294920 | tf_op jit(solution)/shard_map/ppermute | solution.py:361
  56.3 12.7 %collective-permute-start.17 = (bf16[128,384]{1,0:T(8,128)(2,1)S(1)}, bf16[128,384]{1,0:T(8,128)(2,1)S(1)}, u32[]{:S(2)}, u32[]{:S(2)}) collective-permute-start(bf16[128,384]{1,0:T(8,128)(2,1)S(1)} %get-tuple-element.45), channel_id=1, source_target_pairs={{0,6},{2,4},{4,2},{6,0},{8,14},{10,12},{12,10},{14,8},{16,22},{18,... | collective-permute-start | bytes 294920 | tf_op jit(solution)/shard_map/ppermute | solution.py:361
  60.2 9.7 %collective-permute-start.12 = (bf16[48,1024]{1,0:T(8,128)(2,1)S(1)}, bf16[48,1024]{1,0:T(8,128)(2,1)S(1)}, u32[]{:S(2)}, u32[]{:S(2)}) collective-permute-start(bf16[48,1024]{1,0:T(8,128)(2,1)S(1)} %get-tuple-element.35), channel_id=1, source_target_pairs={{0,8},{2,10},{4,12},{6,14},{8,0},{10,2},{12,4},{14,6},{16,24},{18,... | collective-permute-start | bytes 294920 | tf_op jit(solution)/shard_map/ppermute | solution.py:480
  66.5 9.5 %collective-permute-start.13 = (bf16[48,1024]{1,0:T(8,128)(2,1)S(1)}, bf16[48,1024]{1,0:T(8,128)(2,1)S(1)}, u32[]{:S(2)}, u32[]{:S(2)}) collective-permute-start(bf16[48,1024]{1,0:T(8,128)(2,1)S(1)} %get-tuple-element.36), channel_id=1, source_target_pairs={{0,16},{2,18},{4,20},{6,22},{8,24},{10,26},{12,28},{14,30},{16,0},... | collective-permute-start | bytes 294920 | tf_op jit(solution)/shard_map/ppermute | solution.py:480
  66.5 9.5 %collective-permute-start.14 = (bf16[48,1024]{1,0:T(8,128)(2,1)S(1)}, bf16[48,1024]{1,0:T(8,128)(2,1)S(1)}, u32[]{:S(2)}, u32[]{:S(2)}) collective-permute-start(bf16[48,1024]{1,0:T(8,128)(2,1)S(1)} %get-tuple-element.37), channel_id=1, source_target_pairs={{0,24},{2,26},{4,28},{6,30},{8,16},{10,18},{12,20},{14,22},{16,8},... | collective-permute-start | bytes 294920 | tf_op jit(solution)/shard_map/ppermute | solution.py:480
  76.0 7.2 %collective-permute-start.20 = (bf16[48,1024]{1,0:T(8,128)(2,1)S(1)}, bf16[48,1024]{1,0:T(8,128)(2,1)S(1)}, u32[]{:S(2)}, u32[]{:S(2)}) collective-permute-start(bf16[48,1024]{1,0:T(8,128)(2,1)S(1)} %shard_map.109), channel_id=1, source_target_pairs={{0,24},{2,26},{4,28},{6,30},{8,16},{10,18},{12,20},{14,22},{16,8},... | collective-permute-start | bytes 294920 | tf_op jit(solution)/shard_map/ppermute | solution.py:480
  77.7 9.5 %collective-permute-start.19 = (bf16[48,1024]{1,0:T(8,128)(2,1)S(1)}, bf16[48,1024]{1,0:T(8,128)(2,1)S(1)}, u32[]{:S(2)}, u32[]{:S(2)}) collective-permute-start(bf16[48,1024]{1,0:T(8,128)(2,1)S(1)} %shard_map.109), channel_id=1, source_target_pairs={{0,16},{2,18},{4,20},{6,22},{8,24},{10,26},{12,28},{14,30},{16,0},... | collective-permute-start | bytes 294920 | tf_op jit(solution)/shard_map/ppermute | solution.py:480
  79.3 7.9 %collective-permute-start.18 = (bf16[48,1024]{1,0:T(8,128)(2,1)S(1)}, bf16[48,1024]{1,0:T(8,128)(2,1)S(1)}, u32[]{:S(2)}, u32[]{:S(2)}) collective-permute-start(bf16[48,1024]{1,0:T(8,128)(2,1)S(1)} %shard_map.109), channel_id=1, source_target_pairs={{0,8},{2,10},{4,12},{6,14},{8,0},{10,2},{12,4},{14,6},{16,24},{18,... | collective-permute-start | bytes 294920 | tf_op jit(solution)/shard_map/ppermute | solution.py:480
  80.5 6.7 %collective-permute-start.23 = (bf16[1,48,1024]{2,1,0:T(8,128)(2,1)S(1)}, bf16[1,48,1024]{2,1,0:T(8,128)(2,1)S(1)}, u32[]{:S(2)}, u32[]{:S(2)}) collective-permute-start(bf16[1,48,1024]{2,1,0:T(8,128)(2,1)S(1)} %bitcast.22), channel_id=1, source_target_pairs={{0,6},{2,4},{4,2},{6,0},{8,14},{10,12},{12,10},{14,8},{16,22},{18,... | collective-permute-start | bytes 294920 | tf_op jit(solution)/shard_map/ppermute | solution.py:361
  82.0 5.2 %collective-permute-start.22 = (bf16[1,48,1024]{2,1,0:T(8,128)(2,1)S(1)}, bf16[1,48,1024]{2,1,0:T(8,128)(2,1)S(1)}, u32[]{:S(2)}, u32[]{:S(2)}) collective-permute-start(bf16[1,48,1024]{2,1,0:T(8,128)(2,1)S(1)} %bitcast.23), channel_id=1, source_target_pairs={{0,4},{2,6},{4,0},{6,2},{8,12},{10,14},{12,8},{14,10},{16,20},{18,... | collective-permute-start | bytes 294920 | tf_op jit(solution)/shard_map/ppermute | solution.py:361
  83.2 4.6 %collective-permute-start.21 = (bf16[1,48,1024]{2,1,0:T(8,128)(2,1)S(1)}, bf16[1,48,1024]{2,1,0:T(8,128)(2,1)S(1)}, u32[]{:S(2)}, u32[]{:S(2)}) collective-permute-start(bf16[1,48,1024]{2,1,0:T(8,128)(2,1)S(1)} %bitcast.24), channel_id=1, source_target_pairs={{0,2},{2,0},{4,6},{6,4},{8,10},{10,8},{12,14},{14,12},{16,18},{18,... | collective-permute-start | bytes 294920 | tf_op jit(solution)/shard_map/ppermute | solution.py:361
  87.9 10.9 %collective-permute-start.26 = (bf16[3,48,1024]{2,1,0:T(8,128)(2,1)S(1)}, bf16[3,48,1024]{2,1,0:T(8,128)(2,1)S(1)}, u32[]{:S(2)}, u32[]{:S(2)}) collective-permute-start(bf16[3,48,1024]{2,1,0:T(8,128)(2,1)S(1)} %pad_maximum_fusion.refs_0_), channel_id=1, source_target_pairs={{0,6},{2,4},{4,2},{6,0},{8,14},{10,12},{12,10},{14,8},{16,22},{18,... | collective-permute-start | bytes 884744 | tf_op jit(solution)/shard_map/ppermute | solution.py:361
  89.6 13.7 %collective-permute-start.25 = (bf16[3,48,1024]{2,1,0:T(8,128)(2,1)S(1)}, bf16[3,48,1024]{2,1,0:T(8,128)(2,1)S(1)}, u32[]{:S(2)}, u32[]{:S(2)}) collective-permute-start(bf16[3,48,1024]{2,1,0:T(8,128)(2,1)S(1)} %pad_maximum_fusion.refs_0_), channel_id=1, source_target_pairs={{0,4},{2,6},{4,0},{6,2},{8,12},{10,14},{12,8},{14,10},{16,20},{18,... | collective-permute-start | bytes 884744 | tf_op jit(solution)/shard_map/ppermute | solution.py:361
  90.6 12.7 %collective-permute-start.24 = (bf16[3,48,1024]{2,1,0:T(8,128)(2,1)S(1)}, bf16[3,48,1024]{2,1,0:T(8,128)(2,1)S(1)}, u32[]{:S(2)}, u32[]{:S(2)}) collective-permute-start(bf16[3,48,1024]{2,1,0:T(8,128)(2,1)S(1)} %pad_maximum_fusion.refs_0_), channel_id=1, source_target_pairs={{0,2},{2,0},{4,6},{6,4},{8,10},{10,8},{12,14},{14,12},{16,18},{18,... | collective-permute-start | bytes 884744 | tf_op jit(solution)/shard_map/ppermute | solution.py:361

commit v3 on v2

v3 whole, which is shorter than its diff:
```python
import functools

import jax
import jax.numpy as jnp
from jax import lax
from jax.experimental import pallas as pl
from jax.experimental.pallas import tpu as pltpu
from jax.sharding import PartitionSpec as P

FILTER_CENTER = 1.0
FILTER_HALF = 4.0
GROUP = 4
BF16 = jnp.bfloat16
F32 = jnp.float32
SMALL = 16
VMEM_LIMIT = 48 * 1024 * 1024
VMEM = pl.BlockSpec(memory_space=pltpu.VMEM)
SMEM = pl.BlockSpec(memory_space=pltpu.SMEM)
ANY = pl.BlockSpec(memory_space=pl.ANY)


def up(value, step):
    return -(-value // step) * step


def call(body, out_shape, specs, arrays, scratch=(), flops=0, moved=0, out_specs=None, aliases=None):
    if out_specs is None:
        out_specs = [VMEM] * len(out_shape) if isinstance(out_shape, list) else VMEM
    return pl.pallas_call(
        body,
        out_shape=out_shape,
        in_specs=specs,
        out_specs=out_specs,
        scratch_shapes=list(scratch),
        input_output_aliases=aliases or {},
        compiler_params=pltpu.CompilerParams(vmem_limit_bytes=VMEM_LIMIT),
        cost_estimate=pl.CostEstimate(flops=flops, bytes_accessed=moved, transcendentals=0),
    )(*arrays)


def pieces(value):
    top = value.astype(BF16).astype(F32)
    rest = value - top
    middle = rest.astype(BF16).astype(F32)
    return (top, middle, rest - middle)


def describe_body(count, conn, values, out, small):
    e_cap, elem_nodes = conn.shape
    nodes = (values.shape[1] - 128) // 2
    small[...] = jnp.zeros(small.shape, F32)
    ids = conn[...]
    high = ids >> 7
    small[0:e_cap, 0:elem_nodes] = (ids - (high << 7)).astype(F32)
    small[4 : 4 + e_cap, :] = jnp.full((e_cap, small.shape[1]), 64.0, F32)
    small[4 : 4 + e_cap, 0:elem_nodes] = high.astype(F32)
    lane = lax.broadcasted_iota(jnp.int32, (1, 128), 1)
    coef = jnp.where(lane < jnp.minimum(count[0], e_cap), values[:, 0:128], 0.0)
    for at, part in enumerate(pieces(coef)):
        small[8 + at : 9 + at, 0:128] = part
    for row in (0, 1):
        for at, part in enumerate(pieces(values[:, 128 + row * nodes : 128 + (row + 1) * nodes])):
            small[11 + row : 12 + row, at * nodes : (at + 1) * nodes] = part
    out[...] = small[...].astype(BF16)


def order_body(scal, a0, a1, a2, a3, out, small):
    nodes = out.shape[1]
    for k, part in enumerate((a0, a1, a2, a3)):
        out[scal[0] ^ k] = part[0:nodes]
        small[scal[0] ^ k] = part[nodes:, 0 : small.shape[2]]


def paired(re, im, size):
    if size == re.shape[1]:
        return jnp.concatenate([re, im], axis=1)
    fill = jnp.zeros((re.shape[0], size - re.shape[1]), re.dtype)
    return jnp.concatenate([re, fill, im, fill], axis=1)


def pack_body(w, wp, pc, pcp, scal, vec, own, other, small, twin, next_, *outs):
    cols = pc * GROUP
    nodes = vec.shape[1]
    total = own[...] + other[...]
    for q in range(GROUP):
        bands = paired(vec[0, :, q * w : (q + 1) * w], vec[1, :, q * w : (q + 1) * w], wp)
        panel = paired(
            total[:, q * pc : (q + 1) * pc], total[:, cols + q * pc : cols + (q + 1) * pc], pcp
        ).astype(BF16)
        for k in range(GROUP):

            @pl.when((scal[0] ^ k) == q)
            def _():
                outs[k][0:nodes, 0 : 2 * wp] = bands
                outs[k][0:nodes, 2 * wp :] = panel

    for k in range(GROUP):
        for at, part in enumerate((small, twin, next_)):
            row = nodes + at * SMALL
            outs[k][row : row + SMALL, 0 : small.shape[1]] = part[...]


def rotate_body(parts, scal, vec, rot, *out):
    nodes, bands = vec.shape[1:]
    panel = rot.shape[2]
    mine = pl.ds(pl.multiple_of(scal[3] * bands, bands), bands)
    both = jnp.concatenate([vec[0], vec[1]], axis=0)
    with_re = jnp.dot(both, rot[0, mine, :], preferred_element_type=F32)
    with_im = jnp.dot(both, rot[1, mine, :], preferred_element_type=F32)
    out_re = with_re[0:nodes] - with_im[nodes:]
    out_im = with_im[0:nodes] + with_re[nodes:]
    cols = panel // parts
    for h in range(parts):
        value_re = out_re[:, h * cols : (h + 1) * cols]
        value_im = out_im[:, h * cols : (h + 1) * cols]
        if parts == 2:

            @pl.when(scal[3] == h)
            def _():
                out[0][:, 0:cols] = value_re
                out[0][:, cols : 2 * cols] = value_im

            @pl.when(scal[3] != h)
            def _():
                out[1][:, 0:cols] = value_re
                out[1][:, cols : 2 * cols] = value_im

        else:
            out[0][h, :, 0:cols] = value_re
            out[0][h, :, cols : 2 * cols] = value_im


def spread_line(rows, row, nodes):
    line = rows[row : row + 1, 0:nodes] + rows[row : row + 1, nodes : 2 * nodes]
    line = line + rows[row : row + 1, 2 * nodes : 3 * nodes]
    shape = (nodes, nodes)
    diag = lax.broadcasted_iota(jnp.int32, shape, 0) == lax.broadcasted_iota(jnp.int32, shape, 1)
    return jnp.where(diag, line, 0.0), diag


def add_block(t, first, thirds, nodes, e_cap, ids, coefs_s, matrix, acc, base):
    width = matrix.shape[0]
    span = 3 * nodes
    rows = thirds * nodes

    def add(count):
        place = lax.broadcasted_iota(jnp.int32, (span, width), 0).astype(F32)
        marks = [ids[t, e : e + 1, :] for e in range(count)]
        hots = [jnp.where(place == mark, 1.0, 0.0).astype(BF16) for mark in marks]
        if thirds == 3:
            used = hots
        else:
            shift = (first * nodes).astype(F32)
            used = [jnp.where(place[:rows] == mark - shift, 1.0, 0.0).astype(BF16) for mark in marks]
        half = jnp.dot(jnp.concatenate(used, axis=0), matrix[...], preferred_element_type=F32)
        half = [half[e * rows : (e + 1) * rows] * coefs_s[t, e] for e in range(count)]
        tops = [value.astype(BF16) for value in half]
        lows = [(value - part.astype(F32)).astype(BF16) for value, part in zip(half, tops)]
        full = lax.dot_general(
            jnp.concatenate(tops + lows, axis=1),
            jnp.concatenate(hots + hots, axis=1),
            (((1,), (1,)), ((), ())),
            preferred_element_type=F32,
        )
        for j in range(thirds):
            third = first + j
            i = t + third - 3 - base
            at = pl.multiple_of((2 - third) * nodes, nodes)
            acc[i, :, pl.ds(at, span)] += full[j * nodes : (j + 1) * nodes]

    live = jnp.int32(0)
    for e in range(e_cap):
        live = live + (coefs_s[t, e] != 0.0).astype(jnp.int32)
    steps = [n for n in (1, 2) if n < e_cap] + [e_cap]
    for at, count in enumerate(steps):
        least = steps[at - 1] if at else 0

        @pl.when((live > least) & (live <= count))
        def _():
            add(count)


def build_body(nodes, e_cap, scal, side_s, small, matrix, *refs):
    outs = refs[0:GROUP]
    ids, coefs, coefs_s, acc, sem = refs[GROUP:]
    side = side_s[0]
    odd = scal[1] & 1
    base = side * GROUP
    coefs[...] = jnp.zeros(coefs.shape, F32)
    acc[...] = jnp.zeros(acc.shape, F32)
    sources = ((0, 1), (1, 2 - 2 * odd), (2, 2 * odd))
    for source, dz in sources:
        for p in range(GROUP):
            rows = small[p, source * SMALL : (source + 1) * SMALL].astype(F32)
            t = dz * GROUP + p
            ids[t, 0:4, :] = rows[0:4] + 128.0 * rows[4:8]
            coefs[pl.ds(t, 1), :] = (rows[8:9] + rows[9:10] + rows[10:11])[:, 0:128]
    copy = pltpu.make_async_copy(coefs, coefs_s, sem)
    copy.start()
    for source, dz in sources:
        for p in range(GROUP):
            i = dz * GROUP + p - 2 - base

            @pl.when((i >= 0) & (i < GROUP))
            def _():
                rows = small[p, source * SMALL : (source + 1) * SMALL].astype(F32)
                line, diag = spread_line(rows, 11, nodes)
                acc[i, :, 2 * nodes : 3 * nodes] = line - jnp.where(diag, FILTER_CENTER, 0.0)

    copy.wait()
    args = (nodes, e_cap, ids, coefs_s, matrix, acc, base)
    low = side == 0

    def whole(step, carry):
        add_block(GROUP - 1 + side * GROUP + step, 0, 3, *args)
        return carry

    def two(step, carry):
        outer = step == 0
        t = jnp.where(low, jnp.where(outer, 2, 5), jnp.where(outer, 9, 6))
        add_block(t, jnp.where(low == outer, 1, 0), 2, *args)
        return carry

    def one(step, carry):
        outer = step == 0
        t = jnp.where(low, jnp.where(outer, 1, 6), jnp.where(outer, 10, 5))
        add_block(t, jnp.where(low == outer, 2, 0), 1, *args)
        return carry

    lax.fori_loop(0, 2, whole, 0)
    lax.fori_loop(0, 2, two, 0)
    lax.fori_loop(0, 2, one, 0)
    for i in range(GROUP):
        value = acc[i] * (1.0 / FILTER_HALF)
        top = value.astype(BF16)
        outs[i][0] = top
        outs[i][1] = (value - top.astype(F32)).astype(BF16)


def join_body(scal, own, twin, next_, small, vec, cols):
    nodes = own.shape[1]
    rows_out = cols.shape[0]
    odd = scal[1] & 1
    for source, (array, dz) in enumerate(((own, 1), (twin, 2 - 2 * odd), (next_, 2 * odd))):
        for p in range(GROUP):
            t = dz * GROUP + p
            vec[pl.ds(pl.multiple_of(t * nodes, nodes), nodes), :] = array[p]
            i = t - 2

            @pl.when((i >= 0) & (i < rows_out))
            def _():
                rows = small[p, source * SMALL : (source + 1) * SMALL].astype(F32)
                line, _ = spread_line(rows, 12, nodes)
                column = jnp.sum(line, axis=1, keepdims=True) * (1.0 / FILTER_HALF)
                cols[i] = jnp.broadcast_to(column, cols.shape[1:])


def filter_body(at, half, scal, side_s, vec, cols, *refs):
    k_one, k_two, refs = refs[:GROUP], refs[GROUP : 2 * GROUP], refs[2 * GROUP :]
    first, keep = refs[-2:]
    outs = refs[:-2]
    rows_out = 2 * GROUP
    nodes = cols.shape[1]
    sign = jnp.where(lax.broadcasted_iota(jnp.int32, (1, 2 * half), 1) < half, 1.0, -1.0)

    def rows_at(block, count):
        return pl.ds(pl.multiple_of(block * nodes, nodes), count * nodes)

    def applied(source, lanes, start, i, rows):
        block = source[rows_at(start, 5), lanes]
        total = jnp.dot(rows[0], block, preferred_element_type=F32)
        total = total + jnp.dot(rows[1], block, preferred_element_type=F32)
        mid = source[rows_at(start + 2, 1), lanes].astype(F32)
        return total + (cols[i][:, 0:1] * sign) * pltpu.roll(mid, half, 1)

    inside_low = scal[1] > 0
    inside_high = scal[1] < scal[2] - 1
    sides = ((k_one, side_s[0]), (k_two, 1 - side_s[0]))
    for parts, side in sides:
        for local in range(GROUP):
            i = side * GROUP + local
            value = applied(vec, slice(at, at + 2 * half), i, i, parts[local])
            kept = ((i >= 2) | inside_low) & ((i < rows_out - 2) | inside_high)
            first[rows_at(i, 1), :] = jnp.where(kept, value, 0.0).astype(BF16)
    for low in (True, False):
        for step in range(GROUP // 2):
            local = GROUP // 2 + step if low else step
            i = step if low else GROUP // 2 + step
            anchor = vec[rows_at(GROUP + i, 1), at : at + 2 * half].astype(F32)
            for parts, side in sides:

                @pl.when((side == 0) == low)
                def _():
                    keep[...] = applied(first, slice(None), i, i + 2, parts[local])

            value = 2.0 * keep[...] - anchor
            if len(outs) == 1:
                outs[0][i] = value.astype(BF16)
                continue
            outs[GROUP][:, rows_at(i, 1)] = jnp.transpose(value).astype(BF16)
            value = value.astype(BF16)
            for k in range(GROUP):

                @pl.when((scal[0] ^ k) == i)
                def _():
                    outs[k][...] = value


def collect_body(w, wp, scal, g0, g1, g2, g3, out):
    mine = scal[0]
    for k, part in enumerate((g0, g1, g2, g3)):
        re = part[:, 0:w]
        im = part[:, wp : wp + w]
        for q in range(GROUP):

            @pl.when((mine ^ k) == q)
            def _():
                out[0, :, q * w : (q + 1) * w] = re
                out[1, :, q * w : (q + 1) * w] = im


def overlap_body(w, wp, pc, pcp, parts, scale, split, scal, left, *refs):
    panels = refs[0 : GROUP * parts]
    outs = refs[GROUP * parts : -3]
    rotated, right, result = refs[-3:]
    mine, band = scal[0], scal[3]
    nodes = panels[0].shape[1]
    tile = 2 * pcp
    chunks = parts * GROUP
    panel = pc * chunks
    for g in range(parts):
        for j in range(GROUP):
            half = (band + g) % parts
            at = pl.multiple_of((half * GROUP + (mine ^ j)) * tile, tile)
            for p in range(GROUP):
                right[p * nodes : (p + 1) * nodes, pl.ds(at, tile)] = panels[g * GROUP + j][p]
    for j in range(GROUP):
        value = panels[j][mine]
        for q in range(GROUP):

            @pl.when((mine ^ j) == q)
            def _():
                rotated[0, :, q * pc : (q + 1) * pc] = value[:, 0:pc]
                rotated[1, :, q * pc : (q + 1) * pc] = value[:, pcp : pcp + pc]

    product = jnp.dot(left[...], right[...], preferred_element_type=F32) * scale
    top, bottom = product[0:w], product[wp : wp + w]
    for s in range(chunks):
        a, b = s * tile, s * tile + pcp
        result[:, s * pc : (s + 1) * pc] = top[:, a : a + pc] - bottom[:, b : b + pc]
        result[:, panel + s * pc : panel + (s + 1) * pc] = top[:, b : b + pc] + bottom[:, a : a + pc]
    if split == 1:
        outs[0][...] = result[...]
    else:
        rows = w // split
        for j in range(split):
            at = pl.multiple_of((scal[1] ^ j) * rows, rows)
            outs[j][...] = result[pl.ds(at, rows), :].astype(BF16)


def sum_body(s0, s1, s2, s3, out):
    total = s0[...].astype(F32) + s1[...].astype(F32)
    total = total + (s2[...].astype(F32) + s3[...].astype(F32))
    out[...] = total.astype(BF16)


def spread_body(w, rows, batch, panel, has_base, scal, *refs):
    parts = refs[0:GROUP]
    out, buffer, sems = refs[GROUP + has_base :]
    mine, group = scal[0], scal[1]
    copies = []
    for k in range(GROUP):
        for at, j in enumerate(batch):
            slot = k * len(batch) + at
            value = parts[k][at].astype(F32)
            buffer[slot, :, 0, :] = value[:, 0:panel]
            buffer[slot, :, 1, :] = value[:, panel : 2 * panel]
            start = (mine ^ k) * w + ((group ^ j) * rows if rows < w else 0)
            copy = pltpu.make_async_copy(buffer.at[slot], out.at[pl.ds(start, rows)], sems.at[slot])
            copy.start()
            copies.append(copy)
    for copy in copies:
        copy.wait()


def on_device(
    orbitals, elem_count, connectivity, elem_coef, elem_matrix, potential, absorber, rotation
):
    nodes, _, bands = orbitals.shape
    blocks = lax.axis_size("elem")
    parts = lax.axis_size("band")
    e_cap, elem_nodes = connectivity.shape[1:]
    panel = rotation.shape[2]
    groups = blocks // GROUP
    w = bands // GROUP
    span = 3 * nodes
    width = up(max(elem_nodes, span), 128)
    wp = max(up(w, 64), width // 2)
    lanes = 2 * wp
    cols = panel // parts
    pc = cols // GROUP
    pcp = up(pc, 64)
    elem = lax.axis_index("elem")
    band = lax.axis_index("band")
    scal = jnp.stack([elem % GROUP, elem // GROUP, jnp.int32(groups), band]).astype(jnp.int32)

    def struct(*shape, dtype=BF16):
        return jax.ShapeDtypeStruct(shape, dtype)

    def in_group(k):
        return [(i, i ^ k) for i in range(blocks)]

    def swap(values):
        return [values[0]] + [lax.ppermute(values[k], "elem", in_group(k)) for k in range(1, GROUP)]

    twins = [(i, i ^ GROUP) for i in range(blocks) if i ^ GROUP < blocks]
    nexts = [(i, i + GROUP) for i in range(blocks - GROUP) if i // GROUP % 2]
    nexts = nexts + [(b, a) for a, b in nexts]

    def neighbours(value):
        return lax.ppermute(value, "elem", twins), lax.ppermute(value, "elem", nexts)

    turn = [(0, 1), (1, 0)]

    values = jnp.concatenate([jnp.pad(elem_coef[0], (0, 128 - e_cap)), potential, absorber])[None]
    small = call(
        describe_body,
        struct(SMALL, width),
        [SMEM, VMEM, VMEM],
        (elem_count, connectivity[0], values),
        scratch=[pltpu.VMEM((SMALL, width), F32)],
    )
    small_near = neighbours(small)
    orbitals, rotation, small = lax.optimization_barrier((orbitals, rotation, small))

    vec = jnp.moveaxis(orbitals, 1, 0)
    rot = jnp.moveaxis(rotation, 1, 0)
    half = struct(nodes, 2 * cols, dtype=F32)
    sums = call(
        functools.partial(rotate_body, parts),
        [half, half] if parts == 2 else [struct(parts, nodes, 2 * cols, dtype=F32)],
        [SMEM, VMEM, VMEM],
        (scal, vec, rot),
        flops=2 * nodes * 2 * bands * 2 * panel,
        moved=2 * bands * 2 * panel,
    )
    if parts == 2:
        terms = (sums[0], lax.ppermute(sums[1], "band", turn))
    else:
        whole = lax.psum_scatter(sums[0], "band", scatter_dimension=0, tiled=True)[0]
        terms = (whole, jnp.zeros_like(whole))

    all_lanes = lanes + 2 * pcp
    messages = call(
        functools.partial(pack_body, w, wp, pc, pcp),
        [struct(nodes + 3 * SMALL, all_lanes)] * GROUP,
        [SMEM] + [VMEM] * 6,
        (scal, vec, *terms, small, *small_near),
        moved=4 * nodes * bands * 2,
    )
    messages, small = call(
        order_body,
        [struct(GROUP, nodes, all_lanes), struct(GROUP, 3 * SMALL, width)],
        [SMEM] + [VMEM] * GROUP,
        (scal, *swap(messages)),
    )
    near = neighbours(messages)

    matrix = jnp.pad(elem_matrix, ((0, width - elem_nodes), (0, width - elem_nodes)))
    table = (up(3 * GROUP, 8), 128)

    def operator(side):
        return call(
            functools.partial(build_body, nodes, e_cap),
            [struct(2, nodes, 5 * nodes)] * GROUP,
            [SMEM, SMEM, VMEM, VMEM],
            (scal, side, small, matrix),
            scratch=[
                pltpu.VMEM((3 * GROUP, 8, width), F32),
                pltpu.VMEM(table, F32),
                pltpu.SMEM(table, F32),
                pltpu.VMEM((GROUP, nodes, 5 * nodes), F32),
                pltpu.SemaphoreType.DMA,
            ],
            flops=4 * 2 * 6 * width * width * span,
            moved=8 * GROUP * nodes * 5 * nodes,
        )

    if parts == 2:
        side = band[None].astype(jnp.int32)
        halves = [operator(side)]
        halves.append([lax.ppermute(part, "band", turn) for part in halves[0]])
    else:
        side = jnp.zeros((1,), jnp.int32)
        halves = [operator(side), operator(side + 1)]

    vec, absorb = call(
        join_body,
        [struct(3 * GROUP * nodes, all_lanes), struct(2 * GROUP, nodes, 128, dtype=F32)],
        [SMEM] + [VMEM] * 4,
        (scal, messages, *near, small),
    )

    def filtered_lanes(at, size, out_shape):
        return call(
            functools.partial(filter_body, at, size // 2),
            out_shape,
            [SMEM, SMEM] + [VMEM] * (2 + 2 * GROUP),
            (scal, side, vec, absorb, *halves[0], *halves[1]),
            scratch=[pltpu.VMEM((2 * GROUP * nodes, size), BF16), pltpu.VMEM((nodes, size), F32)],
            flops=2 * 2 * 12 * nodes * 5 * nodes * size,
            moved=8 * GROUP * nodes * 5 * nodes,
        )

    out_panel = filtered_lanes(lanes, 2 * pcp, struct(GROUP, nodes, 2 * pcp))
    *fields, left = filtered_lanes(
        0, lanes, [struct(nodes, lanes)] * GROUP + [struct(lanes, GROUP * nodes)]
    )

    gathered = swap([out_panel] * GROUP)
    gathered, left, fields = lax.optimization_barrier((gathered, left, list(fields)))
    if parts == 2:
        all_panels = gathered + [lax.ppermute(x, "band", turn) for x in gathered]
    else:
        every = lax.all_gather(jnp.stack(gathered), "band", axis=0)
        every = jnp.roll(every, -band, axis=0)
        all_panels = [every[h, j] for h in range(parts) for j in range(GROUP)]

    direct = groups == 4 and w % (groups * 16) == 0
    split = groups if direct else 1
    rows = w // split
    *terms, rotated = call(
        functools.partial(
            overlap_body, w, wp, pc, pcp, parts, 1.0 / (nodes * blocks) ** 0.5, split
        ),
        [struct(rows, 2 * panel, dtype=BF16 if direct else F32)] * split + [struct(2, nodes, cols)],
        [SMEM] + [VMEM] * (1 + GROUP * parts),
        (scal, left, *all_panels),
        scratch=[
            pltpu.VMEM((GROUP * nodes, 2 * pcp * GROUP * parts), BF16),
            pltpu.VMEM((w, 2 * panel), F32),
        ],
        flops=2 * GROUP * nodes * lanes * 2 * panel,
        moved=4 * GROUP * nodes * panel,
    )
    if direct:

        def across(values):
            return [values[0]] + [
                lax.ppermute(values[j], "elem", [(i, i ^ (GROUP * j)) for i in range(blocks)])
                for j in range(1, split)
            ]

        moved = across(terms)
        moved[1], fields = lax.optimization_barrier((moved[1], fields))
        own = call(sum_body, struct(rows, 2 * panel), [VMEM] * split, moved)
        stack = across([own] * split)
        batches = [[0], list(range(1, split))]
    else:
        lines = [[GROUP * z + i for z in range(groups)] for i in range(GROUP)]
        stack = [lax.psum(terms[0], "elem", axis_index_groups=lines).astype(BF16)]
        batches = [[0]]
    received = swap(fields)
    filtered = call(
        functools.partial(collect_body, w, wp),
        struct(2, nodes, bands),
        [SMEM] + [VMEM] * GROUP,
        (scal, *received),
    )
    intersection = None
    earliest = None
    for batch in batches:
        ready = jnp.stack([stack[j] for j in batch])
        if earliest is not None:
            ready, filtered, _ = lax.optimization_barrier((ready, filtered, earliest))
        base = [] if intersection is None else [intersection]
        spread = swap([ready] * GROUP)
        if earliest is None:
            earliest = spread
        intersection = call(
            functools.partial(spread_body, w, rows, batch, panel, len(base)),
            struct(bands, 2, panel, dtype=F32),
            [SMEM] + [VMEM] * GROUP + [ANY] * len(base),
            (scal, *spread, *base),
            scratch=[
                pltpu.VMEM((GROUP * len(batch), rows, 2, panel), F32),
                pltpu.SemaphoreType.DMA((GROUP * len(batch),)),
            ],
            out_specs=ANY,
            aliases={GROUP + 1: 0} if base else None,
        )
    return (jnp.moveaxis(filtered, 0, 1), jnp.moveaxis(rotated, 0, 1), intersection)


def solution(mesh):
    placed = (
        P("elem", None, "band"),
        P("elem"),
        P("elem", None, None),
        P("elem", None),
        P(),
        P("elem"),
        P("elem"),
        P(),
    )
    return jax.shard_map(
        on_device,
        mesh=mesh,
        in_specs=placed,
        out_specs=(P("elem", None, "band"), P("elem", None, "band"), P("band", None, None)),
        check_vma=False,
    )
```

time: 106 us -> 102 us (0.962)
  blocking collectives: 14.6 us -> 0 us
  waiting for transfers between devices: 24.5 us -> 31 us
  starting transfers between devices: 36.2 us -> 40.5 us
    all_to_all x1 -> x0, blocking collectives: 14.6 us -> none  [on_device(): lax.all_to_all(messages, 'elem', 0, 0, axis_index_groups=lines, tiled=True)]
    ppermute x2, waiting for transfers between devices: 2.23 us -> 6.21 us  [neighbours(): lax.ppermute(value, 'elem', twins)]
    ppermute x12 -> x15, waiting for transfers between devices: 12.9 us -> 16.5 us  [swap(): lax.ppermute(values[k], 'elem', in_group(k))]
    ppermute x6, starting transfers between devices: 13.2 us -> 9.63 us  [across(): lax.ppermute(values[j], 'elem', [(i, i ^ GROUP * j) for i in range(blocks)])]
    optimization_barrier x0 -> x2, local copies, waits for them, and re-layouts: none -> 3.43 us  [on_device(): lax.optimization_barrier((orbitals, rotation, small))]
    unnamed x14 -> x6, local copies, waits for them, and re-layouts: 6.05 us -> 2.63 us
    ppermute x12 -> x15, starting transfers between devices: 14.5 us -> 17.6 us  [swap(): lax.ppermute(values[k], 'elem', in_group(k))]
    ppermute x2, starting transfers between devices: 6.21 us -> 9.16 us  [neighbours(): lax.ppermute(value, 'elem', twins)]
  transfers between devices with their start and end apart: 27 -> 34, of which waited for: 11 -> 14; matrix products, arithmetic and copies ran while one was open for 2% -> 2% of each run, Pallas kernels for 14% -> 12%
where the time goes in v3:
time: 102 us
  starting transfers between devices  40.5 us (40%)
  waiting for transfers between devices  31 us (30%)
  Pallas kernels  21.7 us (21%)
  local copies, waits for them, and re-layouts  6.1 us (6%)
  between operations  1.74 us (2%)
    pallas_call x13, Pallas kernels, call(): pl.pallas_call(body, out_shape=out_shape, in_specs=specs, out_specs=out_s...  21.7 us
    ppermute x15, starting transfers between devices, swap(): lax.ppermute(values[k], 'elem', in_group(k))  17.6 us
    ppermute x15, waiting for transfers between devices, swap(): lax.ppermute(values[k], 'elem', in_group(k))  16.5 us
    ppermute x6, starting transfers between devices, across(): lax.ppermute(values[j], 'elem', [(i, i ^ GROUP * j) for i in range(blocks)])  9.63 us
    ppermute x2, starting transfers between devices, neighbours(): lax.ppermute(value, 'elem', twins)  9.16 us
    ppermute x6, waiting for transfers between devices, across(): lax.ppermute(values[j], 'elem', [(i, i ^ GROUP * j) for i in range(blocks)])  7.31 us
    ppermute x2, waiting for transfers between devices, neighbours(): lax.ppermute(value, 'elem', twins)  6.21 us
    optimization_barrier x2, local copies, waits for them, and re-layouts, on_device(): lax.optimization_barrier((orbitals, rotation, small))  3.43 us
  transfers between devices with their start and end apart: 34, of which 14 were waited for; matrix products, arithmetic and copies ran while one was open for 2% of the time, Pallas kernels for 12%

profile of v3, /device:TPU:0, one launch (start us, length us, event | category | flops | bytes accessed | tf_op | source)
XLA Modules:
  0.0 101.8 jit_solution(4184633275703286651)
XLA Ops:
  3.8 2.4 %copy.18 = bf16[1536,2,512]{2,0,1:T(8,128)(2,1)S(1)} copy(bf16[1536,2,512]{2,1,0:T(2,128)(2,1)} %param.15) | data formatting | bytes 6291456 | tf_op jit(solution)/shard_map/optimization_barrier | solution.py:434
  6.3 1.2 %shard_map.104 = (f32[128,512]{1,0:T(8,128)S(1)}, f32[128,512]{1,0:T(8,128)S(1)}) custom-call(s32[4]{0:T(128)S(1)} %pad_add_fusion.scal, bf16[2,128,768]{2,1,0:T(8,128)(2,1)S(1)} %bitcast.18, bf16[2,1536,512]{2,1,0:T(8,128)(2,1)S(1)} %bitcast.17), custom_call_target="tpu_custom_call" | custom-call | flops 402653184 | bytes 1572864 | tf_op jit(solution)/shard_map/pallas_call | solution.py:29
  8.6 5.5 %collective-permute-start.1 = (bf16[16,384]{1,0:T(8,128)(2,1)S(1)}, bf16[16,384]{1,0:T(8,128)(2,1)S(1)}, u32[]{:S(2)}, u32[]{:S(2)}) collective-permute-start(bf16[16,384]{1,0:T(8,128)(2,1)S(1)} %shard_map.103.small), channel_id=1, source_target_pairs={{0,8},{2,10},{4,12},{6,14},{8,0},{10,2},{12,4},{14,6},{16,24},{18,... | collective-permute-start | bytes 36872 | tf_op jit(solution)/shard_map/ppermute | solution.py:421
  14.1 1.7 %collective-permute-done.1.twin = bf16[16,384]{1,0:T(8,128)(2,1)S(1)} collective-permute-done((bf16[16,384]{1,0:T(8,128)(2,1)S(1)}, bf16[16,384]{1,0:T(8,128)(2,1)S(1)}, u32[]{:S(2)}, u32[]{:S(2)}) %collective-permute-start.1) | collective-permute-done | bytes 12320 | tf_op jit(solution)/shard_map/ppermute | solution.py:421
  16.8 1.6 %collective-permute-start.3 = (bf16[176,512]{1,0:T(8,128)(2,1)S(1)}, bf16[176,512]{1,0:T(8,128)(2,1)S(1)}, u32[]{:S(2)}, u32[]{:S(2)}) collective-permute-start(bf16[176,512]{1,0:T(8,128)(2,1)S(1)} %get-tuple-element.52), channel_id=1, source_target_pairs={{0,2},{2,0},{4,6},{6,4},{8,10},{10,8},{12,14},{14,12},{16,18},{18,... | collective-permute-start | bytes 540680 | tf_op jit(solution)/shard_map/ppermute | solution.py:414
  18.4 1.5 %collective-permute-start.4 = (bf16[176,512]{1,0:T(8,128)(2,1)S(1)}, bf16[176,512]{1,0:T(8,128)(2,1)S(1)}, u32[]{:S(2)}, u32[]{:S(2)}) collective-permute-start(bf16[176,512]{1,0:T(8,128)(2,1)S(1)} %get-tuple-element.53), channel_id=1, source_target_pairs={{0,4},{2,6},{4,0},{6,2},{8,12},{10,14},{12,8},{14,10},{16,20},{18,... | collective-permute-start | bytes 540680 | tf_op jit(solution)/shard_map/ppermute | solution.py:414
  20.4 3.8 %collective-permute-done.3.a1 = bf16[176,512]{1,0:T(8,128)(2,1)S(1)} collective-permute-done((bf16[176,512]{1,0:T(8,128)(2,1)S(1)}, bf16[176,512]{1,0:T(8,128)(2,1)S(1)}, u32[]{:S(2)}, u32[]{:S(2)}) %collective-permute-start.3) | collective-permute-done | bytes 180256 | tf_op jit(solution)/shard_map/ppermute | solution.py:414
  24.2 3.6 %collective-permute-done.4.a2 = bf16[176,512]{1,0:T(8,128)(2,1)S(1)} collective-permute-done((bf16[176,512]{1,0:T(8,128)(2,1)S(1)}, bf16[176,512]{1,0:T(8,128)(2,1)S(1)}, u32[]{:S(2)}, u32[]{:S(2)}) %collective-permute-start.4) | collective-permute-done | bytes 180256 | tf_op jit(solution)/shard_map/ppermute | solution.py:414
  29.1 3.7 %collective-permute-start.6 = (bf16[4,128,512]{2,1,0:T(8,128)(2,1)S(1)}, bf16[4,128,512]{2,1,0:T(8,128)(2,1)S(1)}, u32[]{:S(2)}, u32[]{:S(2)}) collective-permute-start(bf16[4,128,512]{2,1,0:T(8,128)(2,1)S(1)} %get-tuple-element.55.own), channel_id=1, source_target_pairs={{0,8},{2,10},{4,12},{6,14},{8,0},{10,2},{12,4},{14,6},{16,24},{18,... | collective-permute-start | bytes 1572872 | tf_op jit(solution)/shard_map/ppermute | solution.py:421
  32.8 4.3 %shard_map.108 = (bf16[2,128,640]{2,1,0:T(8,128)(2,1)S(1)}, bf16[2,128,640]{2,1,0:T(8,128)(2,1)S(1)}, bf16[2,128,640]{2,1,0:T(8,128)(2,1)S(1)}, bf16[2,128,640]{2,1,0:T(8,128)(2,1)S(1)}) custom-call(s32[4]{0:T(128)S(1)} %pad_add_fusion.scal, s32[1]{0:T(128)} %bitcast.2.side_s, bf16[4,48,384]{2,1,0:T(8,128)(2,1)S(1)} %get-tuple-element.56.small, ...), custom_call_target="tpu_custom_call" | custom-call | flops 2717908992 | bytes 2621440 | tf_op jit(solution)/shard_map/pallas_call | solution.py:29
  38.2 4.5 %collective-permute-done.6.twin = bf16[4,128,512]{2,1,0:T(8,128)(2,1)S(1)} collective-permute-done((bf16[4,128,512]{2,1,0:T(8,128)(2,1)S(1)}, bf16[4,128,512]{2,1,0:T(8,128)(2,1)S(1)}, u32[]{:S(2)}, u32[]{:S(2)}) %collective-permute-start.6) | collective-permute-done | bytes 524320 | tf_op jit(solution)/shard_map/ppermute | solution.py:421
  42.7 1.3 %shard_map.107 = (bf16[1536,512]{1,0:T(8,128)(2,1)S(1)}, f32[8,128,128]{2,1,0:T(8,128)S(1)}) custom-call(s32[4]{0:T(128)S(1)} %pad_add_fusion.scal, bf16[4,128,512]{2,1,0:T(8,128)(2,1)S(1)} %get-tuple-element.55.own, bf16[4,128,512]{2,1,0:T(8,128)(2,1)S(1)} %collective-permute-done.6.twin, bf16[4,128,512]{2,1,0:T(8,128)(2,1)S(1)} %collective-permute-done.7.next_, ...), custom_call_target="tpu_custom_call" | custom-call | tf_op jit(solution)/shard_map/pallas_call | solution.py:29
  44.0 2.5 %shard_map.109.refs_0_ = bf16[4,128,128]{2,1,0:T(8,128)(2,1)S(1)} custom-call(s32[4]{0:T(128)S(1)} %pad_add_fusion.scal, s32[1]{0:T(128)} %bitcast.2.side_s, bf16[1536,512]{1,0:T(8,128)(2,1)S(1)} %get-tuple-element.57.vec, f32[8,128,128]{2,1,0:T(8,128)S(1)} %get-tuple-element.58.cols, bf16[2,128,640]{2,1,0:T(8,128)(2,1)S(1)} %get-tuple-element.59.refs_0_, ...), custom_call_target="tpu_custom_call" | custom-call | flops 503316480 | bytes 2621440 | tf_op jit(solution)/shard_map/pallas_call | solution.py:29
  47.3 1.5 %collective-permute-start.13 = (bf16[4,128,128]{2,1,0:T(8,128)(2,1)S(1)}, bf16[4,128,128]{2,1,0:T(8,128)(2,1)S(1)}, u32[]{:S(2)}, u32[]{:S(2)}) collective-permute-start(bf16[4,128,128]{2,1,0:T(8,128)(2,1)S(1)} %shard_map.109.refs_0_), channel_id=1, source_target_pairs={{0,4},{2,6},{4,0},{6,2},{8,12},{10,14},{12,8},{14,10},{16,20},{18,... | collective-permute-start | bytes 393224 | tf_op jit(solution)/shard_map/ppermute | solution.py:414
  48.8 1.3 %collective-permute-start.12 = (bf16[4,128,128]{2,1,0:T(8,128)(2,1)S(1)}, bf16[4,128,128]{2,1,0:T(8,128)(2,1)S(1)}, u32[]{:S(2)}, u32[]{:S(2)}) collective-permute-start(bf16[4,128,128]{2,1,0:T(8,128)(2,1)S(1)} %shard_map.109.refs_0_), channel_id=1, source_target_pairs={{0,2},{2,0},{4,6},{6,4},{8,10},{10,8},{12,14},{14,12},{16,18},{18,... | collective-permute-start | bytes 393224 | tf_op jit(solution)/shard_map/ppermute | solution.py:414
  50.0 4.3 %shard_map.110 = (bf16[128,384]{1,0:T(8,128)(2,1)S(1)}, bf16[128,384]{1,0:T(8,128)(2,1)S(1)}, bf16[128,384]{1,0:T(8,128)(2,1)S(1)}, bf16[128,384]{1,0:T(8,128)(2,1)S(1)}, bf16[384,512]{1,0:T(8,128)(2,1)S(1)}) custom-call(s32[4]{0:T(128)S(1)} %pad_add_fusion.scal, s32[1]{0:T(128)} %bitcast.2.side_s, bf16[1536,512]{1,0:T(8,128)(2,1)S(1)} %get-tuple-element.57.vec, ...), custom_call_target="tpu_custom_call" | custom-call | flops 1509949440 | bytes 2621440 | tf_op jit(solution)/shard_map/pallas_call | solution.py:29
  56.5 2.0 %shard_map.111 = (bf16[48,1024]{1,0:T(8,128)(2,1)S(1)}, bf16[48,1024]{1,0:T(8,128)(2,1)S(1)}, bf16[48,1024]{1,0:T(8,128)(2,1)S(1)}, bf16[48,1024]{1,0:T(8,128)(2,1)S(1)}, bf16[2,128,256]{2,1,0:T(8,128)(2,1)S(1)}) custom-call(s32[4]{0:T(128)S(1)} %pad_add_fusion.scal, bf16[384,512]{1,0:T(8,128)(2,1)S(1)} %get-tuple-element.68.left, ...), custom_call_target="tpu_custom_call" | custom-call | flops 402653184 | bytes 1048576 | tf_op jit(solution)/shard_map/pallas_call | solution.py:29
  58.5 2.7 %collective-permute-start.19 = (bf16[48,1024]{1,0:T(8,128)(2,1)S(1)}, bf16[48,1024]{1,0:T(8,128)(2,1)S(1)}, u32[]{:S(2)}, u32[]{:S(2)}) collective-permute-start(bf16[48,1024]{1,0:T(8,128)(2,1)S(1)} %get-tuple-element.74), channel_id=1, source_target_pairs={{0,8},{2,10},{4,12},{6,14},{8,0},{10,2},{12,4},{14,6},{16,24},{18,... | collective-permute-start | bytes 294920 | tf_op jit(solution)/shard_map/ppermute | solution.py:550
  62.3 1.4 %collective-permute-start.21 = (bf16[48,1024]{1,0:T(8,128)(2,1)S(1)}, bf16[48,1024]{1,0:T(8,128)(2,1)S(1)}, u32[]{:S(2)}, u32[]{:S(2)}) collective-permute-start(bf16[48,1024]{1,0:T(8,128)(2,1)S(1)} %get-tuple-element.81), channel_id=1, source_target_pairs={{0,24},{2,26},{4,28},{6,30},{8,16},{10,18},{12,20},{14,22},{16,8},... | collective-permute-start | bytes 294920 | tf_op jit(solution)/shard_map/ppermute | solution.py:550
  64.6 1.3 %collective-permute-start.25 = (bf16[128,384]{1,0:T(8,128)(2,1)S(1)}, bf16[128,384]{1,0:T(8,128)(2,1)S(1)}, u32[]{:S(2)}, u32[]{:S(2)}) collective-permute-start(bf16[128,384]{1,0:T(8,128)(2,1)S(1)} %get-tuple-element.83), channel_id=1, source_target_pairs={{0,2},{2,0},{4,6},{6,4},{8,10},{10,8},{12,14},{14,12},{16,18},{18,... | collective-permute-start | bytes 294920 | tf_op jit(solution)/shard_map/ppermute | solution.py:414
  66.4 1.6 %collective-permute-start.27 = (bf16[128,384]{1,0:T(8,128)(2,1)S(1)}, bf16[128,384]{1,0:T(8,128)(2,1)S(1)}, u32[]{:S(2)}, u32[]{:S(2)}) collective-permute-start(bf16[128,384]{1,0:T(8,128)(2,1)S(1)} %get-tuple-element.85), channel_id=1, source_target_pairs={{0,6},{2,4},{4,2},{6,0},{8,14},{10,12},{12,10},{14,8},{16,22},{18,... | collective-permute-start | bytes 294920 | tf_op jit(solution)/shard_map/ppermute | solution.py:414
  68.1 3.7 %collective-permute-done.20.s2 = bf16[48,1024]{1,0:T(8,128)(2,1)S(1)} collective-permute-done((bf16[48,1024]{1,0:T(8,128)(2,1)S(1)}, bf16[48,1024]{1,0:T(8,128)(2,1)S(1)}, u32[]{:S(2)}, u32[]{:S(2)}) %collective-permute-start.20) | collective-permute-done | bytes 98336 | tf_op jit(solution)/shard_map/ppermute | solution.py:550
  71.9 1.9 %collective-permute-start.24 = (bf16[48,1024]{1,0:T(8,128)(2,1)S(1)}, bf16[48,1024]{1,0:T(8,128)(2,1)S(1)}, u32[]{:S(2)}, u32[]{:S(2)}) collective-permute-start(bf16[48,1024]{1,0:T(8,128)(2,1)S(1)} %shard_map.112), channel_id=1, source_target_pairs={{0,24},{2,26},{4,28},{6,30},{8,16},{10,18},{12,20},{14,22},{16,8},... | collective-permute-start | bytes 294920 | tf_op jit(solution)/shard_map/ppermute | solution.py:550
  73.8 1.6 %collective-permute-start.23 = (bf16[48,1024]{1,0:T(8,128)(2,1)S(1)}, bf16[48,1024]{1,0:T(8,128)(2,1)S(1)}, u32[]{:S(2)}, u32[]{:S(2)}) collective-permute-start(bf16[48,1024]{1,0:T(8,128)(2,1)S(1)} %shard_map.112), channel_id=1, source_target_pairs={{0,16},{2,18},{4,20},{6,22},{8,24},{10,26},{12,28},{14,30},{16,0},... | collective-permute-start | bytes 294920 | tf_op jit(solution)/shard_map/ppermute | solution.py:550
  76.3 1.2 %collective-permute-start.30 = (bf16[1,48,1024]{2,1,0:T(8,128)(2,1)S(1)}, bf16[1,48,1024]{2,1,0:T(8,128)(2,1)S(1)}, u32[]{:S(2)}, u32[]{:S(2)}) collective-permute-start(bf16[1,48,1024]{2,1,0:T(8,128)(2,1)S(1)} %bitcast.21), channel_id=1, source_target_pairs={{0,6},{2,4},{4,2},{6,0},{8,14},{10,12},{12,10},{14,8},{16,22},{18,... | collective-permute-start | bytes 294920 | tf_op jit(solution)/shard_map/ppermute | solution.py:414
  77.5 1.4 %collective-permute-start.29 = (bf16[1,48,1024]{2,1,0:T(8,128)(2,1)S(1)}, bf16[1,48,1024]{2,1,0:T(8,128)(2,1)S(1)}, u32[]{:S(2)}, u32[]{:S(2)}) collective-permute-start(bf16[1,48,1024]{2,1,0:T(8,128)(2,1)S(1)} %bitcast.22), channel_id=1, source_target_pairs={{0,4},{2,6},{4,0},{6,2},{8,12},{10,14},{12,8},{14,10},{16,20},{18,... | collective-permute-start | bytes 294920 | tf_op jit(solution)/shard_map/ppermute | solution.py:414
  80.8 2.7 %collective-permute-done.23 = bf16[48,1024]{1,0:T(8,128)(2,1)S(1)} collective-permute-done((bf16[48,1024]{1,0:T(8,128)(2,1)S(1)}, bf16[48,1024]{1,0:T(8,128)(2,1)S(1)}, u32[]{:S(2)}, u32[]{:S(2)}) %collective-permute-start.23) | collective-permute-done | bytes 98336 | tf_op jit(solution)/shard_map/ppermute | solution.py:550
  84.6 1.3 %collective-permute-start.33 = (bf16[3,48,1024]{2,1,0:T(8,128)(2,1)S(1)}, bf16[3,48,1024]{2,1,0:T(8,128)(2,1)S(1)}, u32[]{:S(2)}, u32[]{:S(2)}) collective-permute-start(bf16[3,48,1024]{2,1,0:T(8,128)(2,1)S(1)} %pad_maximum_fusion.refs_0_), channel_id=1, source_target_pairs={{0,6},{2,4},{4,2},{6,0},{8,14},{10,12},{12,10},{14,8},{16,22},{18,... | collective-permute-start | bytes 884744 | tf_op jit(solution)/shard_map/ppermute | solution.py:414
  90.0 1.5 %shard_map.114.refs_4_ = f32[768,2,512]{2,1,0:T(2,128)} custom-call(s32[4]{0:T(128)S(1)} %pad_add_fusion.scal, bf16[1,48,1024]{2,1,0:T(8,128)(2,1)S(1)} %bitcast.24, bf16[1,48,1024]{2,1,0:T(8,128)(2,1)S(1)} %collective-permute-done.28.refs_1_, bf16[1,48,1024]{2,1,0:T(8,128)(2,1)S(1)} %collective-permute-done.29.refs_2_, ...), custom_call_target="tpu_custom_call" | custom-call | tf_op jit(solution)/shard_map/pallas_call | solution.py:29
  91.5 3.9 %collective-permute-done.33.refs_3_ = bf16[3,48,1024]{2,1,0:T(8,128)(2,1)S(1)} collective-permute-done((bf16[3,48,1024]{2,1,0:T(8,128)(2,1)S(1)}, bf16[3,48,1024]{2,1,0:T(8,128)(2,1)S(1)}, u32[]{:S(2)}, u32[]{:S(2)}) %collective-permute-start.33) | collective-permute-done | bytes 294944 | tf_op jit(solution)/shard_map/ppermute | solution.py:414
  95.4 4.2 %collective-permute-done.32.refs_2_ = bf16[3,48,1024]{2,1,0:T(8,128)(2,1)S(1)} collective-permute-done((bf16[3,48,1024]{2,1,0:T(8,128)(2,1)S(1)}, bf16[3,48,1024]{2,1,0:T(8,128)(2,1)S(1)}, u32[]{:S(2)}, u32[]{:S(2)}) %collective-permute-start.32) | collective-permute-done | bytes 294944 | tf_op jit(solution)/shard_map/ppermute | solution.py:414
  99.6 2.1 %shard_map.115 = f32[768,2,512]{2,1,0:T(2,128)} custom-call(s32[4]{0:T(128)S(1)} %pad_add_fusion.scal, bf16[3,48,1024]{2,1,0:T(8,128)(2,1)S(1)} %pad_maximum_fusion.refs_0_, bf16[3,48,1024]{2,1,0:T(8,128)(2,1)S(1)} %collective-permute-done.31.refs_1_, bf16[3,48,1024]{2,1,0:T(8,128)(2,1)S(1)} %collective-permute-done.32.refs_2_, ...), custom_call_target="tpu_custom_call", output_to_operand_aliasing={{}: (5, {})} | custom-call | tf_op jit(solution)/shard_map/pallas_call | solution.py:29
  (62 shorter events, 20.9 us)
Async XLA Ops:
  7.4 8.3 %collective-permute-start = (f32[128,512]{1,0:T(8,128)S(1)}, f32[128,512]{1,0:T(8,128)S(1)}, u32[]{:S(2)}, u32[]{:S(2)}) collective-permute-start(f32[128,512]{1,0:T(8,128)S(1)} %get-tuple-element.49), channel_id=1, source_target_pairs={{0,1},{1,0},{2,3},{3,2},{4,5},{5,4},{6,7},{7,6},{8,9},{9,8},{10,11... | collective-permute-start | bytes 786440 | tf_op jit(solution)/shard_map/ppermute | solution.py:448
  7.9 6.1 %collective-permute-start.2 = (bf16[16,384]{1,0:T(8,128)(2,1)S(1)}, bf16[16,384]{1,0:T(8,128)(2,1)S(1)}, u32[]{:S(2)}, u32[]{:S(2)}) collective-permute-start(bf16[16,384]{1,0:T(8,128)(2,1)S(1)} %shard_map.103.small), channel_id=1, source_target_pairs={{8,16},{10,18},{12,20},{14,22},{16,8},{18,10},{20,12},{22,14},{9,1... | collective-permute-start | bytes 36872 | tf_op jit(solution)/shard_map/ppermute | solution.py:421
  8.6 7.2 %collective-permute-start.1 = (bf16[16,384]{1,0:T(8,128)(2,1)S(1)}, bf16[16,384]{1,0:T(8,128)(2,1)S(1)}, u32[]{:S(2)}, u32[]{:S(2)}) collective-permute-start(bf16[16,384]{1,0:T(8,128)(2,1)S(1)} %shard_map.103.small), channel_id=1, source_target_pairs={{0,8},{2,10},{4,12},{6,14},{8,0},{10,2},{12,4},{14,6},{16,24},{18,... | collective-permute-start | bytes 36872 | tf_op jit(solution)/shard_map/ppermute | solution.py:421
  16.8 7.3 %collective-permute-start.3 = (bf16[176,512]{1,0:T(8,128)(2,1)S(1)}, bf16[176,512]{1,0:T(8,128)(2,1)S(1)}, u32[]{:S(2)}, u32[]{:S(2)}) collective-permute-start(bf16[176,512]{1,0:T(8,128)(2,1)S(1)} %get-tuple-element.52), channel_id=1, source_target_pairs={{0,2},{2,0},{4,6},{6,4},{8,10},{10,8},{12,14},{14,12},{16,18},{18,... | collective-permute-start | bytes 540680 | tf_op jit(solution)/shard_map/ppermute | solution.py:414
  18.4 9.4 %collective-permute-start.4 = (bf16[176,512]{1,0:T(8,128)(2,1)S(1)}, bf16[176,512]{1,0:T(8,128)(2,1)S(1)}, u32[]{:S(2)}, u32[]{:S(2)}) collective-permute-start(bf16[176,512]{1,0:T(8,128)(2,1)S(1)} %get-tuple-element.53), channel_id=1, source_target_pairs={{0,4},{2,6},{4,0},{6,2},{8,12},{10,14},{12,8},{14,10},{16,20},{18,... | collective-permute-start | bytes 540680 | tf_op jit(solution)/shard_map/ppermute | solution.py:414
  19.9 7.9 %collective-permute-start.5 = (bf16[176,512]{1,0:T(8,128)(2,1)S(1)}, bf16[176,512]{1,0:T(8,128)(2,1)S(1)}, u32[]{:S(2)}, u32[]{:S(2)}) collective-permute-start(bf16[176,512]{1,0:T(8,128)(2,1)S(1)} %get-tuple-element.54), channel_id=1, source_target_pairs={{0,6},{2,4},{4,2},{6,0},{8,14},{10,12},{12,10},{14,8},{16,22},{18,... | collective-permute-start | bytes 540680 | tf_op jit(solution)/shard_map/ppermute | solution.py:414
  28.4 9.4 %collective-permute-start.7 = (bf16[4,128,512]{2,1,0:T(8,128)(2,1)S(1)}, bf16[4,128,512]{2,1,0:T(8,128)(2,1)S(1)}, u32[]{:S(2)}, u32[]{:S(2)}) collective-permute-start(bf16[4,128,512]{2,1,0:T(8,128)(2,1)S(1)} %get-tuple-element.55.own), channel_id=1, source_target_pairs={{8,16},{10,18},{12,20},{14,22},{16,8},{18,10},{20,12},{22,14},{9,1... | collective-permute-start | bytes 1572872 | tf_op jit(solution)/shard_map/ppermute | solution.py:421
  29.1 13.6 %collective-permute-start.6 = (bf16[4,128,512]{2,1,0:T(8,128)(2,1)S(1)}, bf16[4,128,512]{2,1,0:T(8,128)(2,1)S(1)}, u32[]{:S(2)}, u32[]{:S(2)}) collective-permute-start(bf16[4,128,512]{2,1,0:T(8,128)(2,1)S(1)} %get-tuple-element.55.own), channel_id=1, source_target_pairs={{0,8},{2,10},{4,12},{6,14},{8,0},{10,2},{12,4},{14,6},{16,24},{18,... | collective-permute-start | bytes 1572872 | tf_op jit(solution)/shard_map/ppermute | solution.py:421
  37.1 6.9 %collective-permute-start.8 = (bf16[2,128,640]{2,1,0:T(8,128)(2,1)S(1)}, bf16[2,128,640]{2,1,0:T(8,128)(2,1)S(1)}, u32[]{:S(2)}, u32[]{:S(2)}) collective-permute-start(bf16[2,128,640]{2,1,0:T(8,128)(2,1)S(1)} %get-tuple-element.59.refs_0_), channel_id=1, source_target_pairs={{0,1},{1,0},{2,3},{3,2},{4,5},{5,4},{6,7},{7,6},{8,9},{9,8},{10,11... | collective-permute-start | bytes 983048 | tf_op jit(solution)/shard_map/ppermute | solution.py:492
  37.1 6.9 %collective-permute-start.9 = (bf16[2,128,640]{2,1,0:T(8,128)(2,1)S(1)}, bf16[2,128,640]{2,1,0:T(8,128)(2,1)S(1)}, u32[]{:S(2)}, u32[]{:S(2)}) collective-permute-start(bf16[2,128,640]{2,1,0:T(8,128)(2,1)S(1)} %get-tuple-element.60.refs_1_), channel_id=1, source_target_pairs={{0,1},{1,0},{2,3},{3,2},{4,5},{5,4},{6,7},{7,6},{8,9},{9,8},{10,11... | collective-permute-start | bytes 983048 | tf_op jit(solution)/shard_map/ppermute | solution.py:492
  37.6 6.4 %collective-permute-start.10 = (bf16[2,128,640]{2,1,0:T(8,128)(2,1)S(1)}, bf16[2,128,640]{2,1,0:T(8,128)(2,1)S(1)}, u32[]{:S(2)}, u32[]{:S(2)}) collective-permute-start(bf16[2,128,640]{2,1,0:T(8,128)(2,1)S(1)} %get-tuple-element.61.refs_2_), channel_id=1, source_target_pairs={{0,1},{1,0},{2,3},{3,2},{4,5},{5,4},{6,7},{7,6},{8,9},{9,8},{10,11... | collective-permute-start | bytes 983048 | tf_op jit(solution)/shard_map/ppermute | solution.py:492
  37.7 6.3 %collective-permute-start.11 = (bf16[2,128,640]{2,1,0:T(8,128)(2,1)S(1)}, bf16[2,128,640]{2,1,0:T(8,128)(2,1)S(1)}, u32[]{:S(2)}, u32[]{:S(2)}) collective-permute-start(bf16[2,128,640]{2,1,0:T(8,128)(2,1)S(1)} %get-tuple-element.62.refs_3_), channel_id=1, source_target_pairs={{0,1},{1,0},{2,3},{3,2},{4,5},{5,4},{6,7},{7,6},{8,9},{9,8},{10,11... | collective-permute-start | bytes 983048 | tf_op jit(solution)/shard_map/ppermute | solution.py:492
  46.5 7.9 %collective-permute-start.14 = (bf16[4,128,128]{2,1,0:T(8,128)(2,1)S(1)}, bf16[4,128,128]{2,1,0:T(8,128)(2,1)S(1)}, u32[]{:S(2)}, u32[]{:S(2)}) collective-permute-start(bf16[4,128,128]{2,1,0:T(8,128)(2,1)S(1)} %shard_map.109.refs_0_), channel_id=1, source_target_pairs={{0,6},{2,4},{4,2},{6,0},{8,14},{10,12},{12,10},{14,8},{16,22},{18,... | collective-permute-start | bytes 393224 | tf_op jit(solution)/shard_map/ppermute | solution.py:414
  47.3 7.1 %collective-permute-start.13 = (bf16[4,128,128]{2,1,0:T(8,128)(2,1)S(1)}, bf16[4,128,128]{2,1,0:T(8,128)(2,1)S(1)}, u32[]{:S(2)}, u32[]{:S(2)}) collective-permute-start(bf16[4,128,128]{2,1,0:T(8,128)(2,1)S(1)} %shard_map.109.refs_0_), channel_id=1, source_target_pairs={{0,4},{2,6},{4,0},{6,2},{8,12},{10,14},{12,8},{14,10},{16,20},{18,... | collective-permute-start | bytes 393224 | tf_op jit(solution)/shard_map/ppermute | solution.py:414
  48.8 5.6 %collective-permute-start.12 = (bf16[4,128,128]{2,1,0:T(8,128)(2,1)S(1)}, bf16[4,128,128]{2,1,0:T(8,128)(2,1)S(1)}, u32[]{:S(2)}, u32[]{:S(2)}) collective-permute-start(bf16[4,128,128]{2,1,0:T(8,128)(2,1)S(1)} %shard_map.109.refs_0_), channel_id=1, source_target_pairs={{0,2},{2,0},{4,6},{6,4},{8,10},{10,8},{12,14},{14,12},{16,18},{18,... | collective-permute-start | bytes 393224 | tf_op jit(solution)/shard_map/ppermute | solution.py:414
  54.5 1.5 %collective-permute-start.16 = (bf16[4,128,128]{2,1,0:T(8,128)(2,1)S(1)}, bf16[4,128,128]{2,1,0:T(8,128)(2,1)S(1)}, u32[]{:S(2)}, u32[]{:S(2)}) collective-permute-start(bf16[4,128,128]{2,1,0:T(8,128)(2,1)S(1)} %collective-permute-done.12.refs_1_), channel_id=1, source_target_pairs={{0,1},{1,0},{2,3},{3,2},{4,5},{5,4},{6,7},{7,6},{8,9},{9,8},{10,11... | collective-permute-start | bytes 393224 | tf_op jit(solution)/shard_map/ppermute | solution.py:523
  55.1 1.5 %collective-permute-start.18 = (bf16[4,128,128]{2,1,0:T(8,128)(2,1)S(1)}, bf16[4,128,128]{2,1,0:T(8,128)(2,1)S(1)}, u32[]{:S(2)}, u32[]{:S(2)}) collective-permute-start(bf16[4,128,128]{2,1,0:T(8,128)(2,1)S(1)} %collective-permute-done.14.refs_3_), channel_id=1, source_target_pairs={{0,1},{1,0},{2,3},{3,2},{4,5},{5,4},{6,7},{7,6},{8,9},{9,8},{10,11... | collective-permute-start | bytes 393224 | tf_op jit(solution)/shard_map/ppermute | solution.py:523
  58.5 6.0 %collective-permute-start.19 = (bf16[48,1024]{1,0:T(8,128)(2,1)S(1)}, bf16[48,1024]{1,0:T(8,128)(2,1)S(1)}, u32[]{:S(2)}, u32[]{:S(2)}) collective-permute-start(bf16[48,1024]{1,0:T(8,128)(2,1)S(1)} %get-tuple-element.74), channel_id=1, source_target_pairs={{0,8},{2,10},{4,12},{6,14},{8,0},{10,2},{12,4},{14,6},{16,24},{18,... | collective-permute-start | bytes 294920 | tf_op jit(solution)/shard_map/ppermute | solution.py:550
  61.3 10.5 %collective-permute-start.20 = (bf16[48,1024]{1,0:T(8,128)(2,1)S(1)}, bf16[48,1024]{1,0:T(8,128)(2,1)S(1)}, u32[]{:S(2)}, u32[]{:S(2)}) collective-permute-start(bf16[48,1024]{1,0:T(8,128)(2,1)S(1)} %get-tuple-element.80), channel_id=1, source_target_pairs={{0,16},{2,18},{4,20},{6,22},{8,24},{10,26},{12,28},{14,30},{16,0},... | collective-permute-start | bytes 294920 | tf_op jit(solution)/shard_map/ppermute | solution.py:550
  62.3 9.5 %collective-permute-start.21 = (bf16[48,1024]{1,0:T(8,128)(2,1)S(1)}, bf16[48,1024]{1,0:T(8,128)(2,1)S(1)}, u32[]{:S(2)}, u32[]{:S(2)}) collective-permute-start(bf16[48,1024]{1,0:T(8,128)(2,1)S(1)} %get-tuple-element.81), channel_id=1, source_target_pairs={{0,24},{2,26},{4,28},{6,30},{8,16},{10,18},{12,20},{14,22},{16,8},... | collective-permute-start | bytes 294920 | tf_op jit(solution)/shard_map/ppermute | solution.py:550
  64.6 10.8 %collective-permute-start.25 = (bf16[128,384]{1,0:T(8,128)(2,1)S(1)}, bf16[128,384]{1,0:T(8,128)(2,1)S(1)}, u32[]{:S(2)}, u32[]{:S(2)}) collective-permute-start(bf16[128,384]{1,0:T(8,128)(2,1)S(1)} %get-tuple-element.83), channel_id=1, source_target_pairs={{0,2},{2,0},{4,6},{6,4},{8,10},{10,8},{12,14},{14,12},{16,18},{18,... | collective-permute-start | bytes 294920 | tf_op jit(solution)/shard_map/ppermute | solution.py:414
  65.8 10.5 %collective-permute-start.26 = (bf16[128,384]{1,0:T(8,128)(2,1)S(1)}, bf16[128,384]{1,0:T(8,128)(2,1)S(1)}, u32[]{:S(2)}, u32[]{:S(2)}) collective-permute-start(bf16[128,384]{1,0:T(8,128)(2,1)S(1)} %get-tuple-element.84), channel_id=1, source_target_pairs={{0,4},{2,6},{4,0},{6,2},{8,12},{10,14},{12,8},{14,10},{16,20},{18,... | collective-permute-start | bytes 294920 | tf_op jit(solution)/shard_map/ppermute | solution.py:414
  66.4 11.1 %collective-permute-start.27 = (bf16[128,384]{1,0:T(8,128)(2,1)S(1)}, bf16[128,384]{1,0:T(8,128)(2,1)S(1)}, u32[]{:S(2)}, u32[]{:S(2)}) collective-permute-start(bf16[128,384]{1,0:T(8,128)(2,1)S(1)} %get-tuple-element.85), channel_id=1, source_target_pairs={{0,6},{2,4},{4,2},{6,0},{8,14},{10,12},{12,10},{14,8},{16,22},{18,... | collective-permute-start | bytes 294920 | tf_op jit(solution)/shard_map/ppermute | solution.py:414
  71.9 8.0 %collective-permute-start.24 = (bf16[48,1024]{1,0:T(8,128)(2,1)S(1)}, bf16[48,1024]{1,0:T(8,128)(2,1)S(1)}, u32[]{:S(2)}, u32[]{:S(2)}) collective-permute-start(bf16[48,1024]{1,0:T(8,128)(2,1)S(1)} %shard_map.112), channel_id=1, source_target_pairs={{0,24},{2,26},{4,28},{6,30},{8,16},{10,18},{12,20},{14,22},{16,8},... | collective-permute-start | bytes 294920 | tf_op jit(solution)/shard_map/ppermute | solution.py:550
  73.8 9.8 %collective-permute-start.23 = (bf16[48,1024]{1,0:T(8,128)(2,1)S(1)}, bf16[48,1024]{1,0:T(8,128)(2,1)S(1)}, u32[]{:S(2)}, u32[]{:S(2)}) collective-permute-start(bf16[48,1024]{1,0:T(8,128)(2,1)S(1)} %shard_map.112), channel_id=1, source_target_pairs={{0,16},{2,18},{4,20},{6,22},{8,24},{10,26},{12,28},{14,30},{16,0},... | collective-permute-start | bytes 294920 | tf_op jit(solution)/shard_map/ppermute | solution.py:550
  75.4 8.2 %collective-permute-start.22 = (bf16[48,1024]{1,0:T(8,128)(2,1)S(1)}, bf16[48,1024]{1,0:T(8,128)(2,1)S(1)}, u32[]{:S(2)}, u32[]{:S(2)}) collective-permute-start(bf16[48,1024]{1,0:T(8,128)(2,1)S(1)} %shard_map.112), channel_id=1, source_target_pairs={{0,8},{2,10},{4,12},{6,14},{8,0},{10,2},{12,4},{14,6},{16,24},{18,... | collective-permute-start | bytes 294920 | tf_op jit(solution)/shard_map/ppermute | solution.py:550
  76.3 7.3 %collective-permute-start.30 = (bf16[1,48,1024]{2,1,0:T(8,128)(2,1)S(1)}, bf16[1,48,1024]{2,1,0:T(8,128)(2,1)S(1)}, u32[]{:S(2)}, u32[]{:S(2)}) collective-permute-start(bf16[1,48,1024]{2,1,0:T(8,128)(2,1)S(1)} %bitcast.21), channel_id=1, source_target_pairs={{0,6},{2,4},{4,2},{6,0},{8,14},{10,12},{12,10},{14,8},{16,22},{18,... | collective-permute-start | bytes 294920 | tf_op jit(solution)/shard_map/ppermute | solution.py:414
  77.5 6.1 %collective-permute-start.29 = (bf16[1,48,1024]{2,1,0:T(8,128)(2,1)S(1)}, bf16[1,48,1024]{2,1,0:T(8,128)(2,1)S(1)}, u32[]{:S(2)}, u32[]{:S(2)}) collective-permute-start(bf16[1,48,1024]{2,1,0:T(8,128)(2,1)S(1)} %bitcast.22), channel_id=1, source_target_pairs={{0,4},{2,6},{4,0},{6,2},{8,12},{10,14},{12,8},{14,10},{16,20},{18,... | collective-permute-start | bytes 294920 | tf_op jit(solution)/shard_map/ppermute | solution.py:414
  79.9 4.7 %collective-permute-start.28 = (bf16[1,48,1024]{2,1,0:T(8,128)(2,1)S(1)}, bf16[1,48,1024]{2,1,0:T(8,128)(2,1)S(1)}, u32[]{:S(2)}, u32[]{:S(2)}) collective-permute-start(bf16[1,48,1024]{2,1,0:T(8,128)(2,1)S(1)} %bitcast.23), channel_id=1, source_target_pairs={{0,2},{2,0},{4,6},{6,4},{8,10},{10,8},{12,14},{14,12},{16,18},{18,... | collective-permute-start | bytes 294920 | tf_op jit(solution)/shard_map/ppermute | solution.py:414
  84.6 10.9 %collective-permute-start.33 = (bf16[3,48,1024]{2,1,0:T(8,128)(2,1)S(1)}, bf16[3,48,1024]{2,1,0:T(8,128)(2,1)S(1)}, u32[]{:S(2)}, u32[]{:S(2)}) collective-permute-start(bf16[3,48,1024]{2,1,0:T(8,128)(2,1)S(1)} %pad_maximum_fusion.refs_0_), channel_id=1, source_target_pairs={{0,6},{2,4},{4,2},{6,0},{8,14},{10,12},{12,10},{14,8},{16,22},{18,... | collective-permute-start | bytes 884744 | tf_op jit(solution)/shard_map/ppermute | solution.py:414
  85.9 13.7 %collective-permute-start.32 = (bf16[3,48,1024]{2,1,0:T(8,128)(2,1)S(1)}, bf16[3,48,1024]{2,1,0:T(8,128)(2,1)S(1)}, u32[]{:S(2)}, u32[]{:S(2)}) collective-permute-start(bf16[3,48,1024]{2,1,0:T(8,128)(2,1)S(1)} %pad_maximum_fusion.refs_0_), channel_id=1, source_target_pairs={{0,4},{2,6},{4,0},{6,2},{8,12},{10,14},{12,8},{14,10},{16,20},{18,... | collective-permute-start | bytes 884744 | tf_op jit(solution)/shard_map/ppermute | solution.py:414
  86.9 12.7 %collective-permute-start.31 = (bf16[3,48,1024]{2,1,0:T(8,128)(2,1)S(1)}, bf16[3,48,1024]{2,1,0:T(8,128)(2,1)S(1)}, u32[]{:S(2)}, u32[]{:S(2)}) collective-permute-start(bf16[3,48,1024]{2,1,0:T(8,128)(2,1)S(1)} %pad_maximum_fusion.refs_0_), channel_id=1, source_target_pairs={{0,2},{2,0},{4,6},{6,4},{8,10},{10,8},{12,14},{14,12},{16,18},{18,... | collective-permute-start | bytes 884744 | tf_op jit(solution)/shard_map/ppermute | solution.py:414
  (4 other events, 26.3 us)

commit v4 on v3

--- a/solution.py
+++ b/solution.py
@@ -14,6 +14,7 @@
 F32 = jnp.float32
 SMALL = 16
 VMEM_LIMIT = 48 * 1024 * 1024
+WEIGHT = 4 * 10**9
 VMEM = pl.BlockSpec(memory_space=pltpu.VMEM)
 SMEM = pl.BlockSpec(memory_space=pltpu.SMEM)
 ANY = pl.BlockSpec(memory_space=pl.ANY)
@@ -237,15 +238,12 @@
         outs[i][1] = (value - top.astype(F32)).astype(BF16)
 
 
-def join_body(scal, own, twin, next_, small, vec, cols):
-    nodes = own.shape[1]
-    rows_out = cols.shape[0]
+def columns_body(scal, small, cols):
+    rows_out, nodes = cols.shape[0:2]
     odd = scal[1] & 1
-    for source, (array, dz) in enumerate(((own, 1), (twin, 2 - 2 * odd), (next_, 2 * odd))):
+    for source, dz in ((0, 1), (1, 2 - 2 * odd), (2, 2 * odd)):
         for p in range(GROUP):
-            t = dz * GROUP + p
-            vec[pl.ds(pl.multiple_of(t * nodes, nodes), nodes), :] = array[p]
-            i = t - 2
+            i = dz * GROUP + p - 2
 
             @pl.when((i >= 0) & (i < rows_out))
             def _():
@@ -253,6 +251,15 @@
                 line, _ = spread_line(rows, 12, nodes)
                 column = jnp.sum(line, axis=1, keepdims=True) * (1.0 / FILTER_HALF)
                 cols[i] = jnp.broadcast_to(column, cols.shape[1:])
+
+
+def join_body(scal, own, twin, next_, vec):
+    nodes = own.shape[1]
+    odd = scal[1] & 1
+    for array, dz in ((own, 1), (twin, 2 - 2 * odd), (next_, 2 * odd)):
+        for p in range(GROUP):
+            t = dz * GROUP + p
+            vec[pl.ds(pl.multiple_of(t * nodes, nodes), nodes), :] = array[p]
 
 
 def filter_body(at, half, scal, side_s, vec, cols, *refs):
@@ -364,21 +371,22 @@
     out[...] = total.astype(BF16)
 
 
-def spread_body(w, rows, batch, panel, has_base, scal, *refs):
-    parts = refs[0:GROUP]
-    out, buffer, sems = refs[GROUP + has_base :]
+def copy_body(given, out):
+    out[...] = given[...]
+
+
+def spread_body(w, rows, plan, count, panel, scal, *refs):
+    out, buffer, sems = refs[-3:]
     mine, group = scal[0], scal[1]
     copies = []
-    for k in range(GROUP):
-        for at, j in enumerate(batch):
-            slot = k * len(batch) + at
-            value = parts[k][at].astype(F32)
-            buffer[slot, :, 0, :] = value[:, 0:panel]
-            buffer[slot, :, 1, :] = value[:, panel : 2 * panel]
-            start = (mine ^ k) * w + ((group ^ j) * rows if rows < w else 0)
-            copy = pltpu.make_async_copy(buffer.at[slot], out.at[pl.ds(start, rows)], sems.at[slot])
-            copy.start()
-            copies.append(copy)
+    for slot, (array, at, k, j) in enumerate(plan):
+        value = refs[array][at].astype(F32)
+        buffer[slot, :, 0, :] = value[:, 0:panel]
+        buffer[slot, :, 1, :] = value[:, panel : 2 * panel]
+        start = (mine ^ k) * w + ((group ^ j) * rows if rows < w else 0)
+        copy = pltpu.make_async_copy(buffer.at[slot], out.at[pl.ds(start, rows)], sems.at[slot])
+        copy.start()
+        copies.append(copy)
     for copy in copies:
         copy.wait()
 
@@ -431,7 +439,8 @@
         scratch=[pltpu.VMEM((SMALL, width), F32)],
     )
     small_near = neighbours(small)
-    orbitals, rotation, small = lax.optimization_barrier((orbitals, rotation, small))
+    orbitals, small = lax.optimization_barrier((orbitals, small))
+    rotation, small_near = lax.optimization_barrier((rotation, small_near))
 
     vec = jnp.moveaxis(orbitals, 1, 0)
     rot = jnp.moveaxis(rotation, 1, 0)
@@ -494,11 +503,14 @@
         side = jnp.zeros((1,), jnp.int32)
         halves = [operator(side), operator(side + 1)]
 
-    vec, absorb = call(
+    absorb = call(
+        columns_body, struct(2 * GROUP, nodes, 128, dtype=F32), [SMEM, VMEM], (scal, small)
+    )
+    vec = call(
         join_body,
-        [struct(3 * GROUP * nodes, all_lanes), struct(2 * GROUP, nodes, 128, dtype=F32)],
-        [SMEM] + [VMEM] * 4,
-        (scal, messages, *near, small),
+        struct(3 * GROUP * nodes, all_lanes),
+        [SMEM] + [VMEM] * 3,
+        (scal, messages, *near),
     )
 
     def filtered_lanes(at, size, out_shape):
@@ -545,50 +557,54 @@
     )
     if direct:
 
-        def across(values):
-            return [values[0]] + [
+        def across(values, least=1):
+            return values[:least] + [
                 lax.ppermute(values[j], "elem", [(i, i ^ (GROUP * j)) for i in range(blocks)])
-                for j in range(1, split)
+                for j in range(least, split)
             ]
 
         moved = across(terms)
         moved[1], fields = lax.optimization_barrier((moved[1], fields))
+        received = swap(fields)
+        moved[2:], received = lax.optimization_barrier((moved[2:], received))
         own = call(sum_body, struct(rows, 2 * panel), [VMEM] * split, moved)
-        stack = across([own] * split)
-        batches = [[0], list(range(1, split))]
+        stack = [own, None] + across([own] * split, 2)[2:]
     else:
+        received = swap(fields)
         lines = [[GROUP * z + i for z in range(groups)] for i in range(GROUP)]
         stack = [lax.psum(terms[0], "elem", axis_index_groups=lines).astype(BF16)]
-        batches = [[0]]
-    received = swap(fields)
+    def write(arrays, plan, base=None):
+        more = [] if base is None else [base]
+        return call(
+            functools.partial(spread_body, w, rows, plan, len(arrays), panel),
+            struct(bands, 2, panel, dtype=F32),
+            [SMEM] + [VMEM] * len(arrays) + [ANY] * len(more),
+            (scal, *arrays, *more),
+            scratch=[pltpu.VMEM((len(plan), rows, 2, panel), F32), pltpu.SemaphoreType.DMA((len(plan),))],
+            out_specs=ANY,
+            aliases=None if base is None else {1 + len(arrays): 0},
+        )
+
+    everywhere = range(GROUP)
+    mine = stack[0][None]
+    if direct:
+        mine = call(copy_body, struct(1, rows, 2 * panel), [VMEM], (mine,), flops=WEIGHT, moved=WEIGHT // 256)
+    near_pieces = swap([mine] * GROUP)
+    intersection = write(near_pieces, [(k, 0, k, 0) for k in everywhere])
+    if direct:
+        far = jnp.stack(stack[2:])
+        twin_pieces, far = lax.optimization_barrier((jnp.concatenate(near_pieces), far))
+        far_pieces = swap([far] * GROUP)
+        twin_pieces = lax.ppermute(twin_pieces, "elem", twins)
+        intersection = write([twin_pieces], [(0, k, k, 1) for k in everywhere], intersection)
+        plan = [(k, j - 2, k, j) for k in everywhere for j in range(2, split)]
+        intersection = write(far_pieces, plan, intersection)
     filtered = call(
         functools.partial(collect_body, w, wp),
         struct(2, nodes, bands),
         [SMEM] + [VMEM] * GROUP,
         (scal, *received),
     )
-    intersection = None
-    earliest = None
-    for batch in batches:
-        ready = jnp.stack([stack[j] for j in batch])
-        if earliest is not None:
-            ready, filtered, _ = lax.optimization_barrier((ready, filtered, earliest))
-        base = [] if intersection is None else [intersection]
-        spread = swap([ready] * GROUP)
-        if earliest is None:
-            earliest = spread
-        intersection = call(
-            functools.partial(spread_body, w, rows, batch, panel, len(base)),
-            struct(bands, 2, panel, dtype=F32),
-            [SMEM] + [VMEM] * GROUP + [ANY] * len(base),
-            (scal, *spread, *base),
-            scratch=[
-                pltpu.VMEM((GROUP * len(batch), rows, 2, panel), F32),
-                pltpu.SemaphoreType.DMA((GROUP * len(batch),)),
-            ],
-            out_specs=ANY,
-            aliases={GROUP + 1: 0} if base else None,
-        )
     return (jnp.moveaxis(filtered, 0, 1), jnp.moveaxis(rotated, 0, 1), intersection)
 
 

time: 102 us -> 99.4 us (0.975)
  waiting for transfers between devices: 31 us -> 24.4 us
  Pallas kernels: 21.7 us -> 23.9 us
  starting transfers between devices: 40.5 us -> 42.5 us
    ppermute x2, waiting for transfers between devices: 6.21 us -> 1.43 us  [neighbours(): lax.ppermute(value, 'elem', twins)]
    ppermute x4, starting transfers between devices: 1.08 us -> 4.31 us  [on_device(): halves.append([lax.ppermute(part, 'band', turn) for part in halves[0]])]
    ppermute x15, waiting for transfers between devices: 16.5 us -> 13.8 us  [swap(): lax.ppermute(values[k], 'elem', in_group(k))]
    pallas_call x13 -> x16, Pallas kernels: 21.7 us -> 23.9 us  [call(): pl.pallas_call(body, out_shape=out_shape, in_specs=specs, out_specs=out_s...]
    ppermute x6 -> x5, waiting for transfers between devices: 7.31 us -> 5.71 us  [across(): lax.ppermute(values[j], 'elem', [(i, i ^ GROUP * j) for i in range(blocks)])]
    ppermute x1, waiting for transfers between devices: 0.01 us -> 1.52 us  [on_device(): terms = (sums[0], lax.ppermute(sums[1], 'band', turn))]
    ppermute x2, starting transfers between devices: 9.16 us -> 7.75 us  [neighbours(): lax.ppermute(value, 'elem', twins)]
    ppermute x6 -> x5, starting transfers between devices: 9.63 us -> 10.3 us  [across(): lax.ppermute(values[j], 'elem', [(i, i ^ GROUP * j) for i in range(blocks)])]
  transfers between devices with their start and end apart: 34 -> 34, of which waited for: 14 -> 16; matrix products, arithmetic and copies ran while one was open for 2% -> 3% of each run, Pallas kernels for 12% -> 15%
where the time goes in v4:
time: 99.4 us; the launch traced here: 99.5 us
  starting transfers between devices  42.5 us (43%)
  waiting for transfers between devices  24.4 us (25%)
  Pallas kernels  23.9 us (24%)
  local copies, waits for them, and re-layouts  6.1 us (6%)
  between operations  1.75 us (2%)
    pallas_call x16, Pallas kernels, call(): pl.pallas_call(body, out_shape=out_shape, in_specs=specs, out_specs=out_s...  23.9 us
    ppermute x15, starting transfers between devices, swap(): lax.ppermute(values[k], 'elem', in_group(k))  17.7 us
    ppermute x15, waiting for transfers between devices, swap(): lax.ppermute(values[k], 'elem', in_group(k))  13.8 us
    ppermute x5, starting transfers between devices, across(): lax.ppermute(values[j], 'elem', [(i, i ^ GROUP * j) for i in range(blocks)])  10.3 us
    ppermute x2, starting transfers between devices, neighbours(): lax.ppermute(value, 'elem', twins)  7.75 us
    ppermute x5, waiting for transfers between devices, across(): lax.ppermute(values[j], 'elem', [(i, i ^ GROUP * j) for i in range(blocks)])  5.71 us
    ppermute x4, starting transfers between devices, on_device(): halves.append([lax.ppermute(part, 'band', turn) for part in halves[0]])  4.31 us
    unnamed x6, local copies, waits for them, and re-layouts  2.63 us
  transfers between devices with their start and end apart: 34, of which 16 were waited for; matrix products, arithmetic and copies ran while one was open for 3% of the time, Pallas kernels for 15%

profile of v4, /device:TPU:0, one launch (start us, length us, event | category | flops | bytes accessed | tf_op | source)
XLA Modules:
  0.0 99.5 jit_solution(5365490185706255997)
XLA Ops:
  2.7 3.1 %collective-permute-start = (bf16[16,384]{1,0:T(8,128)(2,1)S(1)}, bf16[16,384]{1,0:T(8,128)(2,1)S(1)}, u32[]{:S(2)}, u32[]{:S(2)}) collective-permute-start(bf16[16,384]{1,0:T(8,128)(2,1)S(1)} %shard_map.103.small), channel_id=1, source_target_pairs={{0,8},{2,10},{4,12},{6,14},{8,0},{10,2},{12,4},{14,6},{16,24},{18,... | collective-permute-start | bytes 36872 | tf_op jit(solution)/shard_map/ppermute | solution.py:429
  7.6 2.4 %copy.19 = bf16[1536,2,512]{2,0,1:T(8,128)(2,1)S(1)} copy(bf16[1536,2,512]{2,1,0:T(2,128)(2,1)} %param.15) | data formatting | bytes 6291456 | tf_op jit(solution)/shard_map/optimization_barrier | solution.py:443
  11.3 1.5 %collective-permute-done.2.other = f32[128,512]{1,0:T(8,128)S(1)} collective-permute-done((f32[128,512]{1,0:T(8,128)S(1)}, f32[128,512]{1,0:T(8,128)S(1)}, u32[]{:S(2)}, u32[]{:S(2)}) %collective-permute-start.2) | collective-permute-done | bytes 262176 | tf_op jit(solution)/shard_map/ppermute | solution.py:457
  13.8 1.9 %collective-permute-start.3 = (bf16[176,512]{1,0:T(8,128)(2,1)S(1)}, bf16[176,512]{1,0:T(8,128)(2,1)S(1)}, u32[]{:S(2)}, u32[]{:S(2)}) collective-permute-start(bf16[176,512]{1,0:T(8,128)(2,1)S(1)} %get-tuple-element.60), channel_id=1, source_target_pairs={{0,2},{2,0},{4,6},{6,4},{8,10},{10,8},{12,14},{14,12},{16,18},{18,... | collective-permute-start | bytes 540680 | tf_op jit(solution)/shard_map/ppermute | solution.py:422
  15.7 1.5 %collective-permute-start.4 = (bf16[176,512]{1,0:T(8,128)(2,1)S(1)}, bf16[176,512]{1,0:T(8,128)(2,1)S(1)}, u32[]{:S(2)}, u32[]{:S(2)}) collective-permute-start(bf16[176,512]{1,0:T(8,128)(2,1)S(1)} %get-tuple-element.61), channel_id=1, source_target_pairs={{0,4},{2,6},{4,0},{6,2},{8,12},{10,14},{12,8},{14,10},{16,20},{18,... | collective-permute-start | bytes 540680 | tf_op jit(solution)/shard_map/ppermute | solution.py:422
  17.4 3.9 %collective-permute-done.3.a1 = bf16[176,512]{1,0:T(8,128)(2,1)S(1)} collective-permute-done((bf16[176,512]{1,0:T(8,128)(2,1)S(1)}, bf16[176,512]{1,0:T(8,128)(2,1)S(1)}, u32[]{:S(2)}, u32[]{:S(2)}) %collective-permute-start.3) | collective-permute-done | bytes 180256 | tf_op jit(solution)/shard_map/ppermute | solution.py:422
  21.3 4.6 %collective-permute-done.4.a2 = bf16[176,512]{1,0:T(8,128)(2,1)S(1)} collective-permute-done((bf16[176,512]{1,0:T(8,128)(2,1)S(1)}, bf16[176,512]{1,0:T(8,128)(2,1)S(1)}, u32[]{:S(2)}, u32[]{:S(2)}) %collective-permute-start.4) | collective-permute-done | bytes 180256 | tf_op jit(solution)/shard_map/ppermute | solution.py:422
  26.5 4.7 %collective-permute-start.6 = (bf16[4,128,512]{2,1,0:T(8,128)(2,1)S(1)}, bf16[4,128,512]{2,1,0:T(8,128)(2,1)S(1)}, u32[]{:S(2)}, u32[]{:S(2)}) collective-permute-start(bf16[4,128,512]{2,1,0:T(8,128)(2,1)S(1)} %get-tuple-element.63.own), channel_id=1, source_target_pairs={{0,8},{2,10},{4,12},{6,14},{8,0},{10,2},{12,4},{14,6},{16,24},{18,... | collective-permute-start | bytes 1572872 | tf_op jit(solution)/shard_map/ppermute | solution.py:429
  31.9 4.7 %shard_map.109 = (bf16[2,128,640]{2,1,0:T(8,128)(2,1)S(1)}, bf16[2,128,640]{2,1,0:T(8,128)(2,1)S(1)}, bf16[2,128,640]{2,1,0:T(8,128)(2,1)S(1)}, bf16[2,128,640]{2,1,0:T(8,128)(2,1)S(1)}) custom-call(s32[4]{0:T(128)S(1)} %pad_add_fusion.scal, s32[1]{0:T(128)} %bitcast.2.side_s, bf16[4,48,384]{2,1,0:T(8,128)(2,1)S(1)} %get-tuple-element.64.small, ...), custom_call_target="tpu_custom_call" | custom-call | flops 2717908992 | bytes 2621440 | tf_op jit(solution)/shard_map/pallas_call | solution.py:30
  36.6 3.8 %collective-permute-start.10 = (bf16[2,128,640]{2,1,0:T(8,128)(2,1)S(1)}, bf16[2,128,640]{2,1,0:T(8,128)(2,1)S(1)}, u32[]{:S(2)}, u32[]{:S(2)}) collective-permute-start(bf16[2,128,640]{2,1,0:T(8,128)(2,1)S(1)} %get-tuple-element.67.refs_2_), channel_id=1, source_target_pairs={{0,1},{1,0},{2,3},{3,2},{4,5},{5,4},{6,7},{7,6},{8,9},{9,8},{10,11... | collective-permute-start | bytes 983048 | tf_op jit(solution)/shard_map/ppermute | solution.py:501
  40.9 1.4 %collective-permute-done.6.twin = bf16[4,128,512]{2,1,0:T(8,128)(2,1)S(1)} collective-permute-done((bf16[4,128,512]{2,1,0:T(8,128)(2,1)S(1)}, bf16[4,128,512]{2,1,0:T(8,128)(2,1)S(1)}, u32[]{:S(2)}, u32[]{:S(2)}) %collective-permute-start.6) | collective-permute-done | bytes 524320 | tf_op jit(solution)/shard_map/ppermute | solution.py:429
  42.3 1.2 %shard_map.108.cols = f32[8,128,128]{2,1,0:T(8,128)S(1)} custom-call(s32[4]{0:T(128)S(1)} %pad_add_fusion.scal, bf16[4,48,384]{2,1,0:T(8,128)(2,1)S(1)} %get-tuple-element.64.small), custom_call_target="tpu_custom_call" | custom-call | tf_op jit(solution)/shard_map/pallas_call | solution.py:30
  44.3 2.4 %shard_map.110.refs_0_ = bf16[4,128,128]{2,1,0:T(8,128)(2,1)S(1)} custom-call(s32[4]{0:T(128)S(1)} %pad_add_fusion.scal, s32[1]{0:T(128)} %bitcast.2.side_s, bf16[1536,512]{1,0:T(8,128)(2,1)S(1)} %shard_map.107.vec, f32[8,128,128]{2,1,0:T(8,128)S(1)} %shard_map.108.cols, bf16[2,128,640]{2,1,0:T(8,128)(2,1)S(1)} %get-tuple-element.65.refs_0_, ...), custom_call_target="tpu_custom_call" | custom-call | flops 503316480 | bytes 2621440 | tf_op jit(solution)/shard_map/pallas_call | solution.py:30
  46.7 1.5 %collective-permute-start.12 = (bf16[4,128,128]{2,1,0:T(8,128)(2,1)S(1)}, bf16[4,128,128]{2,1,0:T(8,128)(2,1)S(1)}, u32[]{:S(2)}, u32[]{:S(2)}) collective-permute-start(bf16[4,128,128]{2,1,0:T(8,128)(2,1)S(1)} %shard_map.110.refs_0_), channel_id=1, source_target_pairs={{0,2},{2,0},{4,6},{6,4},{8,10},{10,8},{12,14},{14,12},{16,18},{18,... | collective-permute-start | bytes 393224 | tf_op jit(solution)/shard_map/ppermute | solution.py:422
  48.8 1.5 %collective-permute-start.14 = (bf16[4,128,128]{2,1,0:T(8,128)(2,1)S(1)}, bf16[4,128,128]{2,1,0:T(8,128)(2,1)S(1)}, u32[]{:S(2)}, u32[]{:S(2)}) collective-permute-start(bf16[4,128,128]{2,1,0:T(8,128)(2,1)S(1)} %shard_map.110.refs_0_), channel_id=1, source_target_pairs={{0,6},{2,4},{4,2},{6,0},{8,14},{10,12},{12,10},{14,8},{16,22},{18,... | collective-permute-start | bytes 393224 | tf_op jit(solution)/shard_map/ppermute | solution.py:422
  50.3 4.3 %shard_map.111 = (bf16[128,384]{1,0:T(8,128)(2,1)S(1)}, bf16[128,384]{1,0:T(8,128)(2,1)S(1)}, bf16[128,384]{1,0:T(8,128)(2,1)S(1)}, bf16[128,384]{1,0:T(8,128)(2,1)S(1)}, bf16[384,512]{1,0:T(8,128)(2,1)S(1)}) custom-call(s32[4]{0:T(128)S(1)} %pad_add_fusion.scal, s32[1]{0:T(128)} %bitcast.2.side_s, bf16[1536,512]{1,0:T(8,128)(2,1)S(1)} %shard_map.107.vec, ...), custom_call_target="tpu_custom_call" | custom-call | flops 1509949440 | bytes 2621440 | tf_op jit(solution)/shard_map/pallas_call | solution.py:30
  54.6 2.1 %collective-permute-done.13.refs_2_ = bf16[4,128,128]{2,1,0:T(8,128)(2,1)S(1)} collective-permute-done((bf16[4,128,128]{2,1,0:T(8,128)(2,1)S(1)}, bf16[4,128,128]{2,1,0:T(8,128)(2,1)S(1)}, u32[]{:S(2)}, u32[]{:S(2)}) %collective-permute-start.13) | collective-permute-done | bytes 131104 | tf_op jit(solution)/shard_map/ppermute | solution.py:422
  58.7 2.0 %shard_map.112 = (bf16[48,1024]{1,0:T(8,128)(2,1)S(1)}, bf16[48,1024]{1,0:T(8,128)(2,1)S(1)}, bf16[48,1024]{1,0:T(8,128)(2,1)S(1)}, bf16[48,1024]{1,0:T(8,128)(2,1)S(1)}, bf16[2,128,256]{2,1,0:T(8,128)(2,1)S(1)}) custom-call(s32[4]{0:T(128)S(1)} %pad_add_fusion.scal, bf16[384,512]{1,0:T(8,128)(2,1)S(1)} %get-tuple-element.74.left, ...), custom_call_target="tpu_custom_call" | custom-call | flops 402653184 | bytes 1048576 | tf_op jit(solution)/shard_map/pallas_call | solution.py:30
  60.7 3.1 %collective-permute-start.21 = (bf16[48,1024]{1,0:T(8,128)(2,1)S(1)}, bf16[48,1024]{1,0:T(8,128)(2,1)S(1)}, u32[]{:S(2)}, u32[]{:S(2)}) collective-permute-start(bf16[48,1024]{1,0:T(8,128)(2,1)S(1)} %get-tuple-element.81), channel_id=1, source_target_pairs={{0,8},{2,10},{4,12},{6,14},{8,0},{10,2},{12,4},{14,6},{16,24},{18,... | collective-permute-start | bytes 294920 | tf_op jit(solution)/shard_map/ppermute | solution.py:562
  64.3 1.9 %collective-permute-start.20 = (bf16[48,1024]{1,0:T(8,128)(2,1)S(1)}, bf16[48,1024]{1,0:T(8,128)(2,1)S(1)}, u32[]{:S(2)}, u32[]{:S(2)}) collective-permute-start(bf16[48,1024]{1,0:T(8,128)(2,1)S(1)} %get-tuple-element.80), channel_id=1, source_target_pairs={{0,24},{2,26},{4,28},{6,30},{8,16},{10,18},{12,20},{14,22},{16,8},... | collective-permute-start | bytes 294920 | tf_op jit(solution)/shard_map/ppermute | solution.py:562
  67.9 1.5 %collective-permute-start.23 = (bf16[128,384]{1,0:T(8,128)(2,1)S(1)}, bf16[128,384]{1,0:T(8,128)(2,1)S(1)}, u32[]{:S(2)}, u32[]{:S(2)}) collective-permute-start(bf16[128,384]{1,0:T(8,128)(2,1)S(1)} %get-tuple-element.88), channel_id=1, source_target_pairs={{0,4},{2,6},{4,0},{6,2},{8,12},{10,14},{12,8},{14,10},{16,20},{18,... | collective-permute-start | bytes 294920 | tf_op jit(solution)/shard_map/ppermute | solution.py:422
  70.6 3.8 %collective-permute-done.19.s2 = bf16[48,1024]{1,0:T(8,128)(2,1)S(1)} collective-permute-done((bf16[48,1024]{1,0:T(8,128)(2,1)S(1)}, bf16[48,1024]{1,0:T(8,128)(2,1)S(1)}, u32[]{:S(2)}, u32[]{:S(2)}) %collective-permute-start.19) | collective-permute-done | bytes 98336 | tf_op jit(solution)/shard_map/ppermute | solution.py:562
  75.0 2.3 %collective-permute-start.28 = (bf16[48,1024]{1,0:T(8,128)(2,1)S(1)}, bf16[48,1024]{1,0:T(8,128)(2,1)S(1)}, u32[]{:S(2)}, u32[]{:S(2)}) collective-permute-start(bf16[48,1024]{1,0:T(8,128)(2,1)S(1)} %shard_map.114), channel_id=1, source_target_pairs={{0,16},{2,18},{4,20},{6,22},{8,24},{10,26},{12,28},{14,30},{16,0},... | collective-permute-start | bytes 294920 | tf_op jit(solution)/shard_map/ppermute | solution.py:562
  77.3 2.5 %collective-permute-start.29 = (bf16[48,1024]{1,0:T(8,128)(2,1)S(1)}, bf16[48,1024]{1,0:T(8,128)(2,1)S(1)}, u32[]{:S(2)}, u32[]{:S(2)}) collective-permute-start(bf16[48,1024]{1,0:T(8,128)(2,1)S(1)} %shard_map.114), channel_id=1, source_target_pairs={{0,24},{2,26},{4,28},{6,30},{8,16},{10,18},{12,20},{14,22},{16,8},... | collective-permute-start | bytes 294920 | tf_op jit(solution)/shard_map/ppermute | solution.py:562
  80.4 1.2 %collective-permute-start.26 = (bf16[1,48,1024]{2,1,0:T(8,128)(2,1)S(1)}, bf16[1,48,1024]{2,1,0:T(8,128)(2,1)S(1)}, u32[]{:S(2)}, u32[]{:S(2)}) collective-permute-start(bf16[1,48,1024]{2,1,0:T(8,128)(2,1)S(1)} %shard_map.115.refs_0_), channel_id=1, source_target_pairs={{0,4},{2,6},{4,0},{6,2},{8,12},{10,14},{12,8},{14,10},{16,20},{18,... | collective-permute-start | bytes 294920 | tf_op jit(solution)/shard_map/ppermute | solution.py:422
  81.5 1.8 %collective-permute-start.27 = (bf16[1,48,1024]{2,1,0:T(8,128)(2,1)S(1)}, bf16[1,48,1024]{2,1,0:T(8,128)(2,1)S(1)}, u32[]{:S(2)}, u32[]{:S(2)}) collective-permute-start(bf16[1,48,1024]{2,1,0:T(8,128)(2,1)S(1)} %shard_map.115.refs_0_), channel_id=1, source_target_pairs={{0,6},{2,4},{4,2},{6,0},{8,14},{10,12},{12,10},{14,8},{16,22},{18,... | collective-permute-start | bytes 294920 | tf_op jit(solution)/shard_map/ppermute | solution.py:422
  85.6 1.5 %collective-permute-done.27.refs_3_ = bf16[1,48,1024]{2,1,0:T(8,128)(2,1)S(1)} collective-permute-done((bf16[1,48,1024]{2,1,0:T(8,128)(2,1)S(1)}, bf16[1,48,1024]{2,1,0:T(8,128)(2,1)S(1)}, u32[]{:S(2)}, u32[]{:S(2)}) %collective-permute-start.27) | collective-permute-done | bytes 98336 | tf_op jit(solution)/shard_map/ppermute | solution.py:422
  88.1 1.5 %collective-permute-start.31 = (bf16[2,48,1024]{2,1,0:T(8,128)(2,1)S(1)}, bf16[2,48,1024]{2,1,0:T(8,128)(2,1)S(1)}, u32[]{:S(2)}, u32[]{:S(2)}) collective-permute-start(bf16[2,48,1024]{2,1,0:T(8,128)(2,1)S(1)} %pad_maximum_fusion.1.refs_0_), channel_id=1, source_target_pairs={{0,4},{2,6},{4,0},{6,2},{8,12},{10,14},{12,8},{14,10},{16,20},{18,... | collective-permute-start | bytes 589832 | tf_op jit(solution)/shard_map/ppermute | solution.py:422
  89.6 1.2 %collective-permute-start.32 = (bf16[2,48,1024]{2,1,0:T(8,128)(2,1)S(1)}, bf16[2,48,1024]{2,1,0:T(8,128)(2,1)S(1)}, u32[]{:S(2)}, u32[]{:S(2)}) collective-permute-start(bf16[2,48,1024]{2,1,0:T(8,128)(2,1)S(1)} %pad_maximum_fusion.1.refs_0_), channel_id=1, source_target_pairs={{0,6},{2,4},{4,2},{6,0},{8,14},{10,12},{12,10},{14,8},{16,22},{18,... | collective-permute-start | bytes 589832 | tf_op jit(solution)/shard_map/ppermute | solution.py:422
  93.7 1.5 %shard_map.116.refs_1_ = f32[768,2,512]{2,1,0:T(2,128)} custom-call(s32[4]{0:T(128)S(1)} %pad_add_fusion.scal, bf16[1,48,1024]{2,1,0:T(8,128)(2,1)S(1)} %shard_map.115.refs_0_, bf16[1,48,1024]{2,1,0:T(8,128)(2,1)S(1)} %collective-permute-done.25.refs_1_, bf16[1,48,1024]{2,1,0:T(8,128)(2,1)S(1)} %collective-permute-done.26.refs_2_, ...), custom_call_target="tpu_custom_call" | custom-call | tf_op jit(solution)/shard_map/pallas_call | solution.py:30
  96.1 1.5 %shard_map.117.refs_4_ = f32[768,2,512]{2,1,0:T(2,128)} custom-call(s32[4]{0:T(128)S(1)} %pad_add_fusion.scal, bf16[4,48,1024]{2,1,0:T(8,128)(2,1)S(1)} %collective-permute-done.33.refs_0_, f32[768,2,512]{2,1,0:T(2,128)} %shard_map.116.refs_1_), custom_call_target="tpu_custom_call", output_to_operand_aliasing={{}: (2, {})} | custom-call | tf_op jit(solution)/shard_map/pallas_call | solution.py:30
  97.6 1.8 %shard_map.118 = f32[768,2,512]{2,1,0:T(2,128)} custom-call(s32[4]{0:T(128)S(1)} %pad_add_fusion.scal, bf16[2,48,1024]{2,1,0:T(8,128)(2,1)S(1)} %pad_maximum_fusion.1.refs_0_, bf16[2,48,1024]{2,1,0:T(8,128)(2,1)S(1)} %collective-permute-done.30.refs_1_, bf16[2,48,1024]{2,1,0:T(8,128)(2,1)S(1)} %collective-permute-done.31.refs_2_, ...), custom_call_target="tpu_custom_call", output_to_operand_aliasing={{}: (5, {})} | custom-call | tf_op jit(solution)/shard_map/pallas_call | solution.py:30
  (66 shorter events, 22.2 us)
Async XLA Ops:
  2.7 4.9 %collective-permute-start = (bf16[16,384]{1,0:T(8,128)(2,1)S(1)}, bf16[16,384]{1,0:T(8,128)(2,1)S(1)}, u32[]{:S(2)}, u32[]{:S(2)}) collective-permute-start(bf16[16,384]{1,0:T(8,128)(2,1)S(1)} %shard_map.103.small), channel_id=1, source_target_pairs={{0,8},{2,10},{4,12},{6,14},{8,0},{10,2},{12,4},{14,6},{16,24},{18,... | collective-permute-start | bytes 36872 | tf_op jit(solution)/shard_map/ppermute | solution.py:429
  5.8 1.8 %collective-permute-start.1 = (bf16[16,384]{1,0:T(8,128)(2,1)S(1)}, bf16[16,384]{1,0:T(8,128)(2,1)S(1)}, u32[]{:S(2)}, u32[]{:S(2)}) collective-permute-start(bf16[16,384]{1,0:T(8,128)(2,1)S(1)} %shard_map.103.small), channel_id=1, source_target_pairs={{8,16},{10,18},{12,20},{14,22},{16,8},{18,10},{20,12},{22,14},{9,1... | collective-permute-start | bytes 36872 | tf_op jit(solution)/shard_map/ppermute | solution.py:429
  11.2 1.6 %collective-permute-start.2 = (f32[128,512]{1,0:T(8,128)S(1)}, f32[128,512]{1,0:T(8,128)S(1)}, u32[]{:S(2)}, u32[]{:S(2)}) collective-permute-start(f32[128,512]{1,0:T(8,128)S(1)} %get-tuple-element.55), channel_id=1, source_target_pairs={{0,1},{1,0},{2,3},{3,2},{4,5},{5,4},{6,7},{7,6},{8,9},{9,8},{10,11... | collective-permute-start | bytes 786440 | tf_op jit(solution)/shard_map/ppermute | solution.py:457
  13.8 7.5 %collective-permute-start.3 = (bf16[176,512]{1,0:T(8,128)(2,1)S(1)}, bf16[176,512]{1,0:T(8,128)(2,1)S(1)}, u32[]{:S(2)}, u32[]{:S(2)}) collective-permute-start(bf16[176,512]{1,0:T(8,128)(2,1)S(1)} %get-tuple-element.60), channel_id=1, source_target_pairs={{0,2},{2,0},{4,6},{6,4},{8,10},{10,8},{12,14},{14,12},{16,18},{18,... | collective-permute-start | bytes 540680 | tf_op jit(solution)/shard_map/ppermute | solution.py:422
  15.7 10.2 %collective-permute-start.4 = (bf16[176,512]{1,0:T(8,128)(2,1)S(1)}, bf16[176,512]{1,0:T(8,128)(2,1)S(1)}, u32[]{:S(2)}, u32[]{:S(2)}) collective-permute-start(bf16[176,512]{1,0:T(8,128)(2,1)S(1)} %get-tuple-element.61), channel_id=1, source_target_pairs={{0,4},{2,6},{4,0},{6,2},{8,12},{10,14},{12,8},{14,10},{16,20},{18,... | collective-permute-start | bytes 540680 | tf_op jit(solution)/shard_map/ppermute | solution.py:422
  17.2 8.7 %collective-permute-start.5 = (bf16[176,512]{1,0:T(8,128)(2,1)S(1)}, bf16[176,512]{1,0:T(8,128)(2,1)S(1)}, u32[]{:S(2)}, u32[]{:S(2)}) collective-permute-start(bf16[176,512]{1,0:T(8,128)(2,1)S(1)} %get-tuple-element.62), channel_id=1, source_target_pairs={{0,6},{2,4},{4,2},{6,0},{8,14},{10,12},{12,10},{14,8},{16,22},{18,... | collective-permute-start | bytes 540680 | tf_op jit(solution)/shard_map/ppermute | solution.py:422
  26.5 15.8 %collective-permute-start.6 = (bf16[4,128,512]{2,1,0:T(8,128)(2,1)S(1)}, bf16[4,128,512]{2,1,0:T(8,128)(2,1)S(1)}, u32[]{:S(2)}, u32[]{:S(2)}) collective-permute-start(bf16[4,128,512]{2,1,0:T(8,128)(2,1)S(1)} %get-tuple-element.63.own), channel_id=1, source_target_pairs={{0,8},{2,10},{4,12},{6,14},{8,0},{10,2},{12,4},{14,6},{16,24},{18,... | collective-permute-start | bytes 1572872 | tf_op jit(solution)/shard_map/ppermute | solution.py:429
  31.2 12.4 %collective-permute-start.7 = (bf16[4,128,512]{2,1,0:T(8,128)(2,1)S(1)}, bf16[4,128,512]{2,1,0:T(8,128)(2,1)S(1)}, u32[]{:S(2)}, u32[]{:S(2)}) collective-permute-start(bf16[4,128,512]{2,1,0:T(8,128)(2,1)S(1)} %get-tuple-element.63.own), channel_id=1, source_target_pairs={{8,16},{10,18},{12,20},{14,22},{16,8},{18,10},{20,12},{22,14},{9,1... | collective-permute-start | bytes 1572872 | tf_op jit(solution)/shard_map/ppermute | solution.py:429
  36.6 7.7 %collective-permute-start.10 = (bf16[2,128,640]{2,1,0:T(8,128)(2,1)S(1)}, bf16[2,128,640]{2,1,0:T(8,128)(2,1)S(1)}, u32[]{:S(2)}, u32[]{:S(2)}) collective-permute-start(bf16[2,128,640]{2,1,0:T(8,128)(2,1)S(1)} %get-tuple-element.67.refs_2_), channel_id=1, source_target_pairs={{0,1},{1,0},{2,3},{3,2},{4,5},{5,4},{6,7},{7,6},{8,9},{9,8},{10,11... | collective-permute-start | bytes 983048 | tf_op jit(solution)/shard_map/ppermute | solution.py:501
  40.4 3.9 %collective-permute-start.11 = (bf16[2,128,640]{2,1,0:T(8,128)(2,1)S(1)}, bf16[2,128,640]{2,1,0:T(8,128)(2,1)S(1)}, u32[]{:S(2)}, u32[]{:S(2)}) collective-permute-start(bf16[2,128,640]{2,1,0:T(8,128)(2,1)S(1)} %get-tuple-element.68.refs_3_), channel_id=1, source_target_pairs={{0,1},{1,0},{2,3},{3,2},{4,5},{5,4},{6,7},{7,6},{8,9},{9,8},{10,11... | collective-permute-start | bytes 983048 | tf_op jit(solution)/shard_map/ppermute | solution.py:501
  40.5 3.8 %collective-permute-start.8 = (bf16[2,128,640]{2,1,0:T(8,128)(2,1)S(1)}, bf16[2,128,640]{2,1,0:T(8,128)(2,1)S(1)}, u32[]{:S(2)}, u32[]{:S(2)}) collective-permute-start(bf16[2,128,640]{2,1,0:T(8,128)(2,1)S(1)} %get-tuple-element.65.refs_0_), channel_id=1, source_target_pairs={{0,1},{1,0},{2,3},{3,2},{4,5},{5,4},{6,7},{7,6},{8,9},{9,8},{10,11... | collective-permute-start | bytes 983048 | tf_op jit(solution)/shard_map/ppermute | solution.py:501
  42.3 2.0 %collective-permute-start.9 = (bf16[2,128,640]{2,1,0:T(8,128)(2,1)S(1)}, bf16[2,128,640]{2,1,0:T(8,128)(2,1)S(1)}, u32[]{:S(2)}, u32[]{:S(2)}) collective-permute-start(bf16[2,128,640]{2,1,0:T(8,128)(2,1)S(1)} %get-tuple-element.66.refs_1_), channel_id=1, source_target_pairs={{0,1},{1,0},{2,3},{3,2},{4,5},{5,4},{6,7},{7,6},{8,9},{9,8},{10,11... | collective-permute-start | bytes 983048 | tf_op jit(solution)/shard_map/ppermute | solution.py:501
  46.7 7.9 %collective-permute-start.12 = (bf16[4,128,128]{2,1,0:T(8,128)(2,1)S(1)}, bf16[4,128,128]{2,1,0:T(8,128)(2,1)S(1)}, u32[]{:S(2)}, u32[]{:S(2)}) collective-permute-start(bf16[4,128,128]{2,1,0:T(8,128)(2,1)S(1)} %shard_map.110.refs_0_), channel_id=1, source_target_pairs={{0,2},{2,0},{4,6},{6,4},{8,10},{10,8},{12,14},{14,12},{16,18},{18,... | collective-permute-start | bytes 393224 | tf_op jit(solution)/shard_map/ppermute | solution.py:422
  48.2 8.4 %collective-permute-start.13 = (bf16[4,128,128]{2,1,0:T(8,128)(2,1)S(1)}, bf16[4,128,128]{2,1,0:T(8,128)(2,1)S(1)}, u32[]{:S(2)}, u32[]{:S(2)}) collective-permute-start(bf16[4,128,128]{2,1,0:T(8,128)(2,1)S(1)} %shard_map.110.refs_0_), channel_id=1, source_target_pairs={{0,4},{2,6},{4,0},{6,2},{8,12},{10,14},{12,8},{14,10},{16,20},{18,... | collective-permute-start | bytes 393224 | tf_op jit(solution)/shard_map/ppermute | solution.py:422
  48.8 7.9 %collective-permute-start.14 = (bf16[4,128,128]{2,1,0:T(8,128)(2,1)S(1)}, bf16[4,128,128]{2,1,0:T(8,128)(2,1)S(1)}, u32[]{:S(2)}, u32[]{:S(2)}) collective-permute-start(bf16[4,128,128]{2,1,0:T(8,128)(2,1)S(1)} %shard_map.110.refs_0_), channel_id=1, source_target_pairs={{0,6},{2,4},{4,2},{6,0},{8,14},{10,12},{12,10},{14,8},{16,22},{18,... | collective-permute-start | bytes 393224 | tf_op jit(solution)/shard_map/ppermute | solution.py:422
  56.7 1.5 %collective-permute-start.16 = (bf16[4,128,128]{2,1,0:T(8,128)(2,1)S(1)}, bf16[4,128,128]{2,1,0:T(8,128)(2,1)S(1)}, u32[]{:S(2)}, u32[]{:S(2)}) collective-permute-start(bf16[4,128,128]{2,1,0:T(8,128)(2,1)S(1)} %collective-permute-done.12.refs_1_), channel_id=1, source_target_pairs={{0,1},{1,0},{2,3},{3,2},{4,5},{5,4},{6,7},{7,6},{8,9},{9,8},{10,11... | collective-permute-start | bytes 393224 | tf_op jit(solution)/shard_map/ppermute | solution.py:535
  57.2 1.5 %collective-permute-start.18 = (bf16[4,128,128]{2,1,0:T(8,128)(2,1)S(1)}, bf16[4,128,128]{2,1,0:T(8,128)(2,1)S(1)}, u32[]{:S(2)}, u32[]{:S(2)}) collective-permute-start(bf16[4,128,128]{2,1,0:T(8,128)(2,1)S(1)} %collective-permute-done.14.refs_3_), channel_id=1, source_target_pairs={{0,1},{1,0},{2,3},{3,2},{4,5},{5,4},{6,7},{7,6},{8,9},{9,8},{10,11... | collective-permute-start | bytes 393224 | tf_op jit(solution)/shard_map/ppermute | solution.py:535
  60.7 6.3 %collective-permute-start.21 = (bf16[48,1024]{1,0:T(8,128)(2,1)S(1)}, bf16[48,1024]{1,0:T(8,128)(2,1)S(1)}, u32[]{:S(2)}, u32[]{:S(2)}) collective-permute-start(bf16[48,1024]{1,0:T(8,128)(2,1)S(1)} %get-tuple-element.81), channel_id=1, source_target_pairs={{0,8},{2,10},{4,12},{6,14},{8,0},{10,2},{12,4},{14,6},{16,24},{18,... | collective-permute-start | bytes 294920 | tf_op jit(solution)/shard_map/ppermute | solution.py:562
  63.8 10.6 %collective-permute-start.19 = (bf16[48,1024]{1,0:T(8,128)(2,1)S(1)}, bf16[48,1024]{1,0:T(8,128)(2,1)S(1)}, u32[]{:S(2)}, u32[]{:S(2)}) collective-permute-start(bf16[48,1024]{1,0:T(8,128)(2,1)S(1)} %get-tuple-element.79), channel_id=1, source_target_pairs={{0,16},{2,18},{4,20},{6,22},{8,24},{10,26},{12,28},{14,30},{16,0},... | collective-permute-start | bytes 294920 | tf_op jit(solution)/shard_map/ppermute | solution.py:562
  64.3 10.1 %collective-permute-start.20 = (bf16[48,1024]{1,0:T(8,128)(2,1)S(1)}, bf16[48,1024]{1,0:T(8,128)(2,1)S(1)}, u32[]{:S(2)}, u32[]{:S(2)}) collective-permute-start(bf16[48,1024]{1,0:T(8,128)(2,1)S(1)} %get-tuple-element.80), channel_id=1, source_target_pairs={{0,24},{2,26},{4,28},{6,30},{8,16},{10,18},{12,20},{14,22},{16,8},... | collective-permute-start | bytes 294920 | tf_op jit(solution)/shard_map/ppermute | solution.py:562
  67.1 7.3 %collective-permute-start.22 = (bf16[128,384]{1,0:T(8,128)(2,1)S(1)}, bf16[128,384]{1,0:T(8,128)(2,1)S(1)}, u32[]{:S(2)}, u32[]{:S(2)}) collective-permute-start(bf16[128,384]{1,0:T(8,128)(2,1)S(1)} %get-tuple-element.87), channel_id=1, source_target_pairs={{0,2},{2,0},{4,6},{6,4},{8,10},{10,8},{12,14},{14,12},{16,18},{18,... | collective-permute-start | bytes 294920 | tf_op jit(solution)/shard_map/ppermute | solution.py:422
  67.9 6.5 %collective-permute-start.23 = (bf16[128,384]{1,0:T(8,128)(2,1)S(1)}, bf16[128,384]{1,0:T(8,128)(2,1)S(1)}, u32[]{:S(2)}, u32[]{:S(2)}) collective-permute-start(bf16[128,384]{1,0:T(8,128)(2,1)S(1)} %get-tuple-element.88), channel_id=1, source_target_pairs={{0,4},{2,6},{4,0},{6,2},{8,12},{10,14},{12,8},{14,10},{16,20},{18,... | collective-permute-start | bytes 294920 | tf_op jit(solution)/shard_map/ppermute | solution.py:422
  69.4 5.5 %collective-permute-start.24 = (bf16[128,384]{1,0:T(8,128)(2,1)S(1)}, bf16[128,384]{1,0:T(8,128)(2,1)S(1)}, u32[]{:S(2)}, u32[]{:S(2)}) collective-permute-start(bf16[128,384]{1,0:T(8,128)(2,1)S(1)} %get-tuple-element.89), channel_id=1, source_target_pairs={{0,6},{2,4},{4,2},{6,0},{8,14},{10,12},{12,10},{14,8},{16,22},{18,... | collective-permute-start | bytes 294920 | tf_op jit(solution)/shard_map/ppermute | solution.py:422
  75.0 9.4 %collective-permute-start.28 = (bf16[48,1024]{1,0:T(8,128)(2,1)S(1)}, bf16[48,1024]{1,0:T(8,128)(2,1)S(1)}, u32[]{:S(2)}, u32[]{:S(2)}) collective-permute-start(bf16[48,1024]{1,0:T(8,128)(2,1)S(1)} %shard_map.114), channel_id=1, source_target_pairs={{0,16},{2,18},{4,20},{6,22},{8,24},{10,26},{12,28},{14,30},{16,0},... | collective-permute-start | bytes 294920 | tf_op jit(solution)/shard_map/ppermute | solution.py:562
  77.3 7.1 %collective-permute-start.29 = (bf16[48,1024]{1,0:T(8,128)(2,1)S(1)}, bf16[48,1024]{1,0:T(8,128)(2,1)S(1)}, u32[]{:S(2)}, u32[]{:S(2)}) collective-permute-start(bf16[48,1024]{1,0:T(8,128)(2,1)S(1)} %shard_map.114), channel_id=1, source_target_pairs={{0,24},{2,26},{4,28},{6,30},{8,16},{10,18},{12,20},{14,22},{16,8},... | collective-permute-start | bytes 294920 | tf_op jit(solution)/shard_map/ppermute | solution.py:562
  79.8 4.7 %collective-permute-start.25 = (bf16[1,48,1024]{2,1,0:T(8,128)(2,1)S(1)}, bf16[1,48,1024]{2,1,0:T(8,128)(2,1)S(1)}, u32[]{:S(2)}, u32[]{:S(2)}) collective-permute-start(bf16[1,48,1024]{2,1,0:T(8,128)(2,1)S(1)} %shard_map.115.refs_0_), channel_id=1, source_target_pairs={{0,2},{2,0},{4,6},{6,4},{8,10},{10,8},{12,14},{14,12},{16,18},{18,... | collective-permute-start | bytes 294920 | tf_op jit(solution)/shard_map/ppermute | solution.py:422
  80.4 5.2 %collective-permute-start.26 = (bf16[1,48,1024]{2,1,0:T(8,128)(2,1)S(1)}, bf16[1,48,1024]{2,1,0:T(8,128)(2,1)S(1)}, u32[]{:S(2)}, u32[]{:S(2)}) collective-permute-start(bf16[1,48,1024]{2,1,0:T(8,128)(2,1)S(1)} %shard_map.115.refs_0_), channel_id=1, source_target_pairs={{0,4},{2,6},{4,0},{6,2},{8,12},{10,14},{12,8},{14,10},{16,20},{18,... | collective-permute-start | bytes 294920 | tf_op jit(solution)/shard_map/ppermute | solution.py:422
  81.5 5.6 %collective-permute-start.27 = (bf16[1,48,1024]{2,1,0:T(8,128)(2,1)S(1)}, bf16[1,48,1024]{2,1,0:T(8,128)(2,1)S(1)}, u32[]{:S(2)}, u32[]{:S(2)}) collective-permute-start(bf16[1,48,1024]{2,1,0:T(8,128)(2,1)S(1)} %shard_map.115.refs_0_), channel_id=1, source_target_pairs={{0,6},{2,4},{4,2},{6,0},{8,14},{10,12},{12,10},{14,8},{16,22},{18,... | collective-permute-start | bytes 294920 | tf_op jit(solution)/shard_map/ppermute | solution.py:422
  87.2 8.9 %collective-permute-start.33 = (bf16[4,48,1024]{2,1,0:T(8,128)(2,1)S(1)}, bf16[4,48,1024]{2,1,0:T(8,128)(2,1)S(1)}, u32[]{:S(2)}, u32[]{:S(2)}) collective-permute-start(bf16[4,48,1024]{2,1,0:T(8,128)(2,1)S(1)} %pad_maximum_fusion), channel_id=1, source_target_pairs={{0,8},{2,10},{4,12},{6,14},{8,0},{10,2},{12,4},{14,6},{16,24},{18,... | collective-permute-start | bytes 1179656 | tf_op jit(solution)/shard_map/ppermute | solution.py:598
  87.2 10.3 %collective-permute-start.30 = (bf16[2,48,1024]{2,1,0:T(8,128)(2,1)S(1)}, bf16[2,48,1024]{2,1,0:T(8,128)(2,1)S(1)}, u32[]{:S(2)}, u32[]{:S(2)}) collective-permute-start(bf16[2,48,1024]{2,1,0:T(8,128)(2,1)S(1)} %pad_maximum_fusion.1.refs_0_), channel_id=1, source_target_pairs={{0,2},{2,0},{4,6},{6,4},{8,10},{10,8},{12,14},{14,12},{16,18},{18,... | collective-permute-start | bytes 589832 | tf_op jit(solution)/shard_map/ppermute | solution.py:422
  88.1 9.5 %collective-permute-start.31 = (bf16[2,48,1024]{2,1,0:T(8,128)(2,1)S(1)}, bf16[2,48,1024]{2,1,0:T(8,128)(2,1)S(1)}, u32[]{:S(2)}, u32[]{:S(2)}) collective-permute-start(bf16[2,48,1024]{2,1,0:T(8,128)(2,1)S(1)} %pad_maximum_fusion.1.refs_0_), channel_id=1, source_target_pairs={{0,4},{2,6},{4,0},{6,2},{8,12},{10,14},{12,8},{14,10},{16,20},{18,... | collective-permute-start | bytes 589832 | tf_op jit(solution)/shard_map/ppermute | solution.py:422
  89.6 8.0 %collective-permute-start.32 = (bf16[2,48,1024]{2,1,0:T(8,128)(2,1)S(1)}, bf16[2,48,1024]{2,1,0:T(8,128)(2,1)S(1)}, u32[]{:S(2)}, u32[]{:S(2)}) collective-permute-start(bf16[2,48,1024]{2,1,0:T(8,128)(2,1)S(1)} %pad_maximum_fusion.1.refs_0_), channel_id=1, source_target_pairs={{0,6},{2,4},{4,2},{6,0},{8,14},{10,12},{12,10},{14,8},{16,22},{18,... | collective-permute-start | bytes 589832 | tf_op jit(solution)/shard_map/ppermute | solution.py:422
  (4 other events, 24.5 us)

commit v5 on v4

--- a/solution.py
+++ b/solution.py
@@ -65,11 +65,18 @@
     out[...] = small[...].astype(BF16)
 
 
-def order_body(scal, a0, a1, a2, a3, out, small):
-    nodes = out.shape[1]
+def order_body(scal, a0, a1, a2, a3, out):
     for k, part in enumerate((a0, a1, a2, a3)):
-        out[scal[0] ^ k] = part[0:nodes]
-        small[scal[0] ^ k] = part[nodes:, 0 : small.shape[2]]
+        out[scal[0] ^ k] = part[...]
+
+
+def combine_body(scal, bands, a0, a1, a2, a3, out, small):
+    nodes, lanes = bands.shape[1:]
+    tile = out.shape[2] - lanes
+    out[:, :, 0:lanes] = bands[...]
+    for k, part in enumerate((a0, a1, a2, a3)):
+        out[scal[0] ^ k, :, lanes:] = part[0:nodes, 0:tile]
+        small[scal[0] ^ k] = part[nodes:]
 
 
 def paired(re, im, size):
@@ -79,12 +86,21 @@
     return jnp.concatenate([re, fill, im, fill], axis=1)
 
 
-def pack_body(w, wp, pc, pcp, scal, vec, own, other, small, twin, next_, *outs):
-    cols = pc * GROUP
-    nodes = vec.shape[1]
-    total = own[...] + other[...]
+def pack_bands_body(w, wp, scal, vec, *outs):
     for q in range(GROUP):
         bands = paired(vec[0, :, q * w : (q + 1) * w], vec[1, :, q * w : (q + 1) * w], wp)
+        for k in range(GROUP):
+
+            @pl.when((scal[0] ^ k) == q)
+            def _():
+                outs[k][...] = bands
+
+
+def pack_panel_body(pc, pcp, scal, own, other, small, twin, next_, *outs):
+    cols = pc * GROUP
+    total = own[...] + other[...]
+    nodes = total.shape[0]
+    for q in range(GROUP):
         panel = paired(
             total[:, q * pc : (q + 1) * pc], total[:, cols + q * pc : cols + (q + 1) * pc], pcp
         ).astype(BF16)
@@ -92,13 +108,15 @@
 
             @pl.when((scal[0] ^ k) == q)
             def _():
-                outs[k][0:nodes, 0 : 2 * wp] = bands
-                outs[k][0:nodes, 2 * wp :] = panel
-
+                outs[k][0:nodes, :] = panel
+
+    tile = 2 * pcp
     for k in range(GROUP):
-        for at, part in enumerate((small, twin, next_)):
-            row = nodes + at * SMALL
-            outs[k][row : row + SMALL, 0 : small.shape[1]] = part[...]
+        row = nodes
+        for part in (small, twin, next_):
+            for at in range(0, part.shape[1], tile):
+                outs[k][row : row + SMALL, :] = part[:, at : at + tile]
+                row += SMALL
 
 
 def rotate_body(parts, scal, vec, rot, *out):
@@ -129,6 +147,14 @@
         else:
             out[0][h, :, 0:cols] = value_re
             out[0][h, :, cols : 2 * cols] = value_im
+
+
+def described(small, p, source, width):
+    tile = small.shape[2]
+    count = small.shape[1] // (3 * SMALL)
+    start = source * count
+    parts = [small[p, (start + at) * SMALL : (start + at + 1) * SMALL] for at in range(count)]
+    return jnp.concatenate(parts, axis=1)[:, 0:width].astype(F32)
 
 
 def spread_line(rows, row, nodes):
@@ -172,7 +198,7 @@
     live = jnp.int32(0)
     for e in range(e_cap):
         live = live + (coefs_s[t, e] != 0.0).astype(jnp.int32)
-    steps = [n for n in (1, 2) if n < e_cap] + [e_cap]
+    steps = [n for n in (1, 2, 3) if n < e_cap] + [e_cap]
     for at, count in enumerate(steps):
         least = steps[at - 1] if at else 0
 
@@ -192,7 +218,7 @@
     sources = ((0, 1), (1, 2 - 2 * odd), (2, 2 * odd))
     for source, dz in sources:
         for p in range(GROUP):
-            rows = small[p, source * SMALL : (source + 1) * SMALL].astype(F32)
+            rows = described(small, p, source, matrix.shape[0])
             t = dz * GROUP + p
             ids[t, 0:4, :] = rows[0:4] + 128.0 * rows[4:8]
             coefs[pl.ds(t, 1), :] = (rows[8:9] + rows[9:10] + rows[10:11])[:, 0:128]
@@ -204,7 +230,7 @@
 
             @pl.when((i >= 0) & (i < GROUP))
             def _():
-                rows = small[p, source * SMALL : (source + 1) * SMALL].astype(F32)
+                rows = described(small, p, source, matrix.shape[0])
                 line, diag = spread_line(rows, 11, nodes)
                 acc[i, :, 2 * nodes : 3 * nodes] = line - jnp.where(diag, FILTER_CENTER, 0.0)
 
@@ -247,7 +273,7 @@
 
             @pl.when((i >= 0) & (i < rows_out))
             def _():
-                rows = small[p, source * SMALL : (source + 1) * SMALL].astype(F32)
+                rows = described(small, p, source, 3 * nodes)
                 line, _ = spread_line(rows, 12, nodes)
                 column = jnp.sum(line, axis=1, keepdims=True) * (1.0 / FILTER_HALF)
                 cols[i] = jnp.broadcast_to(column, cols.shape[1:])
@@ -440,9 +466,19 @@
     )
     small_near = neighbours(small)
     orbitals, small = lax.optimization_barrier((orbitals, small))
-    rotation, small_near = lax.optimization_barrier((rotation, small_near))
-
     vec = jnp.moveaxis(orbitals, 1, 0)
+    messages = call(
+        functools.partial(pack_bands_body, w, wp),
+        [struct(nodes, lanes)] * GROUP,
+        [SMEM, VMEM],
+        (scal, vec),
+        moved=4 * nodes * bands * 2,
+    )
+    messages, rotation, small_near = lax.optimization_barrier((messages, rotation, small_near))
+    messages = call(
+        order_body, struct(GROUP, nodes, lanes), [SMEM] + [VMEM] * GROUP, (scal, *swap(messages))
+    )
+
     rot = jnp.moveaxis(rotation, 1, 0)
     half = struct(nodes, 2 * cols, dtype=F32)
     sums = call(
@@ -450,8 +486,8 @@
         [half, half] if parts == 2 else [struct(parts, nodes, 2 * cols, dtype=F32)],
         [SMEM, VMEM, VMEM],
         (scal, vec, rot),
-        flops=2 * nodes * 2 * bands * 2 * panel,
-        moved=2 * bands * 2 * panel,
+        flops=WEIGHT,
+        moved=WEIGHT // 256,
     )
     if parts == 2:
         terms = (sums[0], lax.ppermute(sums[1], "band", turn))
@@ -460,18 +496,19 @@
         terms = (whole, jnp.zeros_like(whole))
 
     all_lanes = lanes + 2 * pcp
-    messages = call(
-        functools.partial(pack_body, w, wp, pc, pcp),
-        [struct(nodes + 3 * SMALL, all_lanes)] * GROUP,
-        [SMEM] + [VMEM] * 6,
-        (scal, vec, *terms, small, *small_near),
-        moved=4 * nodes * bands * 2,
+    tall = 3 * SMALL * (up(width, 2 * pcp) // (2 * pcp))
+    panels = call(
+        functools.partial(pack_panel_body, pc, pcp),
+        [struct(nodes + tall, 2 * pcp)] * GROUP,
+        [SMEM] + [VMEM] * 5,
+        (scal, *terms, small, *small_near),
+        moved=8 * nodes * cols,
     )
     messages, small = call(
-        order_body,
-        [struct(GROUP, nodes, all_lanes), struct(GROUP, 3 * SMALL, width)],
-        [SMEM] + [VMEM] * GROUP,
-        (scal, *swap(messages)),
+        combine_body,
+        [struct(GROUP, nodes, all_lanes), struct(GROUP, tall, 2 * pcp)],
+        [SMEM] + [VMEM] * (1 + GROUP),
+        (scal, messages, *swap(panels)),
     )
     near = neighbours(messages)
 
@@ -557,10 +594,10 @@
     )
     if direct:
 
-        def across(values, least=1):
-            return values[:least] + [
+        def across(values):
+            return [values[0]] + [
                 lax.ppermute(values[j], "elem", [(i, i ^ (GROUP * j)) for i in range(blocks)])
-                for j in range(least, split)
+                for j in range(1, split)
             ]
 
         moved = across(terms)
@@ -568,7 +605,8 @@
         received = swap(fields)
         moved[2:], received = lax.optimization_barrier((moved[2:], received))
         own = call(sum_body, struct(rows, 2 * panel), [VMEM] * split, moved)
-        stack = [own, None] + across([own] * split, 2)[2:]
+        stack = [own, None, lax.ppermute(own, "elem", [(i, i ^ (2 * GROUP)) for i in range(blocks)])]
+        stack.append(lax.ppermute(stack[2], "elem", twins))
     else:
         received = swap(fields)
         lines = [[GROUP * z + i for z in range(groups)] for i in range(GROUP)]
@@ -596,9 +634,10 @@
         twin_pieces, far = lax.optimization_barrier((jnp.concatenate(near_pieces), far))
         far_pieces = swap([far] * GROUP)
         twin_pieces = lax.ppermute(twin_pieces, "elem", twins)
-        intersection = write([twin_pieces], [(0, k, k, 1) for k in everywhere], intersection)
-        plan = [(k, j - 2, k, j) for k in everywhere for j in range(2, split)]
-        intersection = write(far_pieces, plan, intersection)
+        plan = [(0, k, k, 1) for k in everywhere] + [(1, j - 2, 0, j) for j in range(2, split)]
+        intersection = write([twin_pieces, far], plan, intersection)
+        plan = [(k - 1, j - 2, k, j) for k in range(1, GROUP) for j in range(2, split)]
+        intersection = write(far_pieces[1:], plan, intersection)
     filtered = call(
         functools.partial(collect_body, w, wp),
         struct(2, nodes, bands),

time: 99.4 us -> 97.2 us (0.978)
  waiting for transfers between devices: 24.4 us -> 17.9 us
  starting transfers between devices: 42.5 us -> 45.2 us
  Pallas kernels: 23.9 us -> 25.1 us
    ppermute x15 -> x18, waiting for transfers between devices: 13.8 us -> 7.46 us  [swap(): lax.ppermute(values[k], 'elem', in_group(k))]
    ppermute x5 -> x3, starting transfers between devices: 10.3 us -> 5.57 us  [across(): lax.ppermute(values[j], 'elem', [(i, i ^ GROUP * j) for i in range(blocks)])]
    ppermute x15 -> x18, starting transfers between devices: 17.7 us -> 21.3 us  [swap(): lax.ppermute(values[k], 'elem', in_group(k))]
    ppermute x0 -> x2, starting transfers between devices: none -> 3.56 us  [the longest x1 3.04 us: on_device(): lax.ppermute(own, 'elem', [(i, i ^ 2 * GROUP) for i in range(blocks)])]
    ppermute x4, starting transfers between devices: 4.31 us -> 1.12 us  [on_device(): halves.append([lax.ppermute(part, 'band', turn) for part in halves[0]])]
    ppermute x2, starting transfers between devices: 7.75 us -> 10.3 us  [neighbours(): lax.ppermute(value, 'elem', twins)]
    ppermute x0 -> x2, waiting for transfers between devices: none -> 1.64 us  [the longest x1 1.05 us: on_device(): stack.append(lax.ppermute(stack[2], 'elem', twins))]
    ppermute x2, waiting for transfers between devices: 1.43 us -> 2.96 us  [neighbours(): lax.ppermute(value, 'elem', twins)]
  transfers between devices with their start and end apart: 34 -> 37, of which waited for: 16 -> 16; matrix products, arithmetic and copies ran while one was open for 3% -> 3% of each run, Pallas kernels for 15% -> 18%
where the time goes in v5:
time: 97.2 us; the launch traced here: 96.9 us
  starting transfers between devices  45.2 us (47%)
  Pallas kernels  25.1 us (26%)
  waiting for transfers between devices  17.9 us (18%)
  local copies, waits for them, and re-layouts  6.1 us (6%)
  between operations  1.82 us (2%)
    pallas_call x18, Pallas kernels, call(): pl.pallas_call(body, out_shape=out_shape, in_specs=specs, out_specs=out_s...  25.1 us
    ppermute x18, starting transfers between devices, swap(): lax.ppermute(values[k], 'elem', in_group(k))  21.3 us
    ppermute x2, starting transfers between devices, neighbours(): lax.ppermute(value, 'elem', twins)  10.3 us
    ppermute x18, waiting for transfers between devices, swap(): lax.ppermute(values[k], 'elem', in_group(k))  7.46 us
    ppermute x3, starting transfers between devices, across(): lax.ppermute(values[j], 'elem', [(i, i ^ GROUP * j) for i in range(blocks)])  5.57 us
    ppermute x3, waiting for transfers between devices, across(): lax.ppermute(values[j], 'elem', [(i, i ^ GROUP * j) for i in range(blocks)])  4.79 us
    ppermute x1, starting transfers between devices, on_device(): lax.ppermute(own, 'elem', [(i, i ^ 2 * GROUP) for i in range(blocks)])  3.04 us
    ppermute x2, waiting for transfers between devices, neighbours(): lax.ppermute(value, 'elem', twins)  2.96 us
  transfers between devices with their start and end apart: 37, of which 16 were waited for; matrix products, arithmetic and copies ran while one was open for 3% of the time, Pallas kernels for 18%

profile of v5, /device:TPU:0, one launch (start us, length us, event | category | flops | bytes accessed | tf_op | source)
XLA Modules:
  0.0 96.9 jit_solution(2957330927467416980)
XLA Ops:
  2.7 3.1 %collective-permute-start = (bf16[16,384]{1,0:T(8,128)(2,1)S(1)}, bf16[16,384]{1,0:T(8,128)(2,1)S(1)}, u32[]{:S(2)}, u32[]{:S(2)}) collective-permute-start(bf16[16,384]{1,0:T(8,128)(2,1)S(1)} %shard_map.103.small), channel_id=1, source_target_pairs={{0,8},{2,10},{4,12},{6,14},{8,0},{10,2},{12,4},{14,6},{16,24},{18,... | collective-permute-start | bytes 36872 | tf_op jit(solution)/shard_map/ppermute | solution.py:455
  8.6 2.4 %copy.19 = bf16[1536,2,512]{2,0,1:T(8,128)(2,1)S(1)} copy(bf16[1536,2,512]{2,1,0:T(2,128)(2,1)} %param.15) | data formatting | bytes 6291456 | tf_op jit(solution)/shard_map/optimization_barrier | solution.py:477
  11.0 1.2 %shard_map.106 = (f32[128,512]{1,0:T(8,128)S(1)}, f32[128,512]{1,0:T(8,128)S(1)}) custom-call(s32[4]{0:T(128)S(1)} %pad_add_fusion.scal, bf16[2,128,768]{2,1,0:T(8,128)(2,1)S(1)} %bitcast.18, bf16[2,1536,512]{2,1,0:T(8,128)(2,1)S(1)} %bitcast.16), custom_call_target="tpu_custom_call" | custom-call | flops 4000000000 | bytes 15625000 | tf_op jit(solution)/shard_map/pallas_call | solution.py:30
  12.2 1.6 %collective-permute-start.2 = (bf16[128,384]{1,0:T(8,128)(2,1)S(1)}, bf16[128,384]{1,0:T(8,128)(2,1)S(1)}, u32[]{:S(2)}, u32[]{:S(2)}) collective-permute-start(bf16[128,384]{1,0:T(8,128)(2,1)S(1)} %get-tuple-element.66), channel_id=1, source_target_pairs={{0,2},{2,0},{4,6},{6,4},{8,10},{10,8},{12,14},{14,12},{16,18},{18,... | collective-permute-start | bytes 294920 | tf_op jit(solution)/shard_map/ppermute | solution.py:448
  13.8 1.5 %collective-permute-start.3 = (bf16[128,384]{1,0:T(8,128)(2,1)S(1)}, bf16[128,384]{1,0:T(8,128)(2,1)S(1)}, u32[]{:S(2)}, u32[]{:S(2)}) collective-permute-start(bf16[128,384]{1,0:T(8,128)(2,1)S(1)} %get-tuple-element.67), channel_id=1, source_target_pairs={{0,4},{2,6},{4,0},{6,2},{8,12},{10,14},{12,8},{14,10},{16,20},{18,... | collective-permute-start | bytes 294920 | tf_op jit(solution)/shard_map/ppermute | solution.py:448
  16.7 1.6 %collective-permute-start.6 = (bf16[272,128]{1,0:T(8,128)(2,1)S(1)}, bf16[272,128]{1,0:T(8,128)(2,1)S(1)}, u32[]{:S(2)}, u32[]{:S(2)}) collective-permute-start(bf16[272,128]{1,0:T(8,128)(2,1)S(1)} %get-tuple-element.76), channel_id=1, source_target_pairs={{0,2},{2,0},{4,6},{6,4},{8,10},{10,8},{12,14},{14,12},{16,18},{18,... | collective-permute-start | bytes 208904 | tf_op jit(solution)/shard_map/ppermute | solution.py:448
  18.3 1.5 %collective-permute-start.7 = (bf16[272,128]{1,0:T(8,128)(2,1)S(1)}, bf16[272,128]{1,0:T(8,128)(2,1)S(1)}, u32[]{:S(2)}, u32[]{:S(2)}) collective-permute-start(bf16[272,128]{1,0:T(8,128)(2,1)S(1)} %get-tuple-element.77), channel_id=1, source_target_pairs={{0,4},{2,6},{4,0},{6,2},{8,12},{10,14},{12,8},{14,10},{16,20},{18,... | collective-permute-start | bytes 208904 | tf_op jit(solution)/shard_map/ppermute | solution.py:448
  20.3 1.3 %collective-permute-done.4.a3 = bf16[128,384]{1,0:T(8,128)(2,1)S(1)} collective-permute-done((bf16[128,384]{1,0:T(8,128)(2,1)S(1)}, bf16[128,384]{1,0:T(8,128)(2,1)S(1)}, u32[]{:S(2)}, u32[]{:S(2)}) %collective-permute-start.4) | collective-permute-done | bytes 98336 | tf_op jit(solution)/shard_map/ppermute | solution.py:448
  23.3 1.7 %collective-permute-done.8.a3 = bf16[272,128]{1,0:T(8,128)(2,1)S(1)} collective-permute-done((bf16[272,128]{1,0:T(8,128)(2,1)S(1)}, bf16[272,128]{1,0:T(8,128)(2,1)S(1)}, u32[]{:S(2)}, u32[]{:S(2)}) %collective-permute-start.8) | collective-permute-done | bytes 69664 | tf_op jit(solution)/shard_map/ppermute | solution.py:448
  26.4 7.2 %collective-permute-start.9 = (bf16[4,128,512]{2,1,0:T(8,128)(2,1)S(1)}, bf16[4,128,512]{2,1,0:T(8,128)(2,1)S(1)}, u32[]{:S(2)}, u32[]{:S(2)}) collective-permute-start(bf16[4,128,512]{2,1,0:T(8,128)(2,1)S(1)} %get-tuple-element.79.own), channel_id=1, source_target_pairs={{0,8},{2,10},{4,12},{6,14},{8,0},{10,2},{12,4},{14,6},{16,24},{18,... | collective-permute-start | bytes 1572872 | tf_op jit(solution)/shard_map/ppermute | solution.py:455
  33.6 4.7 %shard_map.111 = (bf16[2,128,640]{2,1,0:T(8,128)(2,1)S(1)}, bf16[2,128,640]{2,1,0:T(8,128)(2,1)S(1)}, bf16[2,128,640]{2,1,0:T(8,128)(2,1)S(1)}, bf16[2,128,640]{2,1,0:T(8,128)(2,1)S(1)}) custom-call(s32[4]{0:T(128)S(1)} %pad_add_fusion.scal, s32[1]{0:T(128)} %bitcast.2.side_s, bf16[4,144,128]{2,1,0:T(8,128)(2,1)S(1)} %get-tuple-element.80.small, ...), custom_call_target="tpu_custom_call" | custom-call | flops 2717908992 | bytes 2621440 | tf_op jit(solution)/shard_map/pallas_call | solution.py:30
  39.4 1.1 %shard_map.110.cols = f32[8,128,128]{2,1,0:T(8,128)S(1)} custom-call(s32[4]{0:T(128)S(1)} %pad_add_fusion.scal, bf16[4,144,128]{2,1,0:T(8,128)(2,1)S(1)} %get-tuple-element.80.small), custom_call_target="tpu_custom_call" | custom-call | tf_op jit(solution)/shard_map/pallas_call | solution.py:30
  40.5 3.0 %collective-permute-done.9.twin = bf16[4,128,512]{2,1,0:T(8,128)(2,1)S(1)} collective-permute-done((bf16[4,128,512]{2,1,0:T(8,128)(2,1)S(1)}, bf16[4,128,512]{2,1,0:T(8,128)(2,1)S(1)}, u32[]{:S(2)}, u32[]{:S(2)}) %collective-permute-start.9) | collective-permute-done | bytes 524320 | tf_op jit(solution)/shard_map/ppermute | solution.py:455
  44.1 2.4 %shard_map.112.refs_0_ = bf16[4,128,128]{2,1,0:T(8,128)(2,1)S(1)} custom-call(s32[4]{0:T(128)S(1)} %pad_add_fusion.scal, s32[1]{0:T(128)} %bitcast.2.side_s, bf16[1536,512]{1,0:T(8,128)(2,1)S(1)} %shard_map.109.vec, f32[8,128,128]{2,1,0:T(8,128)S(1)} %shard_map.110.cols, bf16[2,128,640]{2,1,0:T(8,128)(2,1)S(1)} %get-tuple-element.81.refs_0_, ...), custom_call_target="tpu_custom_call" | custom-call | flops 503316480 | bytes 2621440 | tf_op jit(solution)/shard_map/pallas_call | solution.py:30
  46.6 1.2 %collective-permute-start.15 = (bf16[4,128,128]{2,1,0:T(8,128)(2,1)S(1)}, bf16[4,128,128]{2,1,0:T(8,128)(2,1)S(1)}, u32[]{:S(2)}, u32[]{:S(2)}) collective-permute-start(bf16[4,128,128]{2,1,0:T(8,128)(2,1)S(1)} %shard_map.112.refs_0_), channel_id=1, source_target_pairs={{0,2},{2,0},{4,6},{6,4},{8,10},{10,8},{12,14},{14,12},{16,18},{18,... | collective-permute-start | bytes 393224 | tf_op jit(solution)/shard_map/ppermute | solution.py:448
  48.3 1.8 %collective-permute-start.17 = (bf16[4,128,128]{2,1,0:T(8,128)(2,1)S(1)}, bf16[4,128,128]{2,1,0:T(8,128)(2,1)S(1)}, u32[]{:S(2)}, u32[]{:S(2)}) collective-permute-start(bf16[4,128,128]{2,1,0:T(8,128)(2,1)S(1)} %shard_map.112.refs_0_), channel_id=1, source_target_pairs={{0,6},{2,4},{4,2},{6,0},{8,14},{10,12},{12,10},{14,8},{16,22},{18,... | collective-permute-start | bytes 393224 | tf_op jit(solution)/shard_map/ppermute | solution.py:448
  50.1 4.3 %shard_map.113 = (bf16[128,384]{1,0:T(8,128)(2,1)S(1)}, bf16[128,384]{1,0:T(8,128)(2,1)S(1)}, bf16[128,384]{1,0:T(8,128)(2,1)S(1)}, bf16[128,384]{1,0:T(8,128)(2,1)S(1)}, bf16[384,512]{1,0:T(8,128)(2,1)S(1)}) custom-call(s32[4]{0:T(128)S(1)} %pad_add_fusion.scal, s32[1]{0:T(128)} %bitcast.2.side_s, bf16[1536,512]{1,0:T(8,128)(2,1)S(1)} %shard_map.109.vec, ...), custom_call_target="tpu_custom_call" | custom-call | flops 1509949440 | bytes 2621440 | tf_op jit(solution)/shard_map/pallas_call | solution.py:30
  56.6 2.0 %shard_map.114 = (bf16[48,1024]{1,0:T(8,128)(2,1)S(1)}, bf16[48,1024]{1,0:T(8,128)(2,1)S(1)}, bf16[48,1024]{1,0:T(8,128)(2,1)S(1)}, bf16[48,1024]{1,0:T(8,128)(2,1)S(1)}, bf16[2,128,256]{2,1,0:T(8,128)(2,1)S(1)}) custom-call(s32[4]{0:T(128)S(1)} %pad_add_fusion.scal, bf16[384,512]{1,0:T(8,128)(2,1)S(1)} %get-tuple-element.90.left, ...), custom_call_target="tpu_custom_call" | custom-call | flops 402653184 | bytes 1048576 | tf_op jit(solution)/shard_map/pallas_call | solution.py:30
  58.6 3.1 %collective-permute-start.24 = (bf16[48,1024]{1,0:T(8,128)(2,1)S(1)}, bf16[48,1024]{1,0:T(8,128)(2,1)S(1)}, u32[]{:S(2)}, u32[]{:S(2)}) collective-permute-start(bf16[48,1024]{1,0:T(8,128)(2,1)S(1)} %get-tuple-element.97), channel_id=1, source_target_pairs={{0,8},{2,10},{4,12},{6,14},{8,0},{10,2},{12,4},{14,6},{16,24},{18,... | collective-permute-start | bytes 294920 | tf_op jit(solution)/shard_map/ppermute | solution.py:599
  62.8 1.4 %collective-permute-start.23 = (bf16[48,1024]{1,0:T(8,128)(2,1)S(1)}, bf16[48,1024]{1,0:T(8,128)(2,1)S(1)}, u32[]{:S(2)}, u32[]{:S(2)}) collective-permute-start(bf16[48,1024]{1,0:T(8,128)(2,1)S(1)} %get-tuple-element.96), channel_id=1, source_target_pairs={{0,24},{2,26},{4,28},{6,30},{8,16},{10,18},{12,20},{14,22},{16,8},... | collective-permute-start | bytes 294920 | tf_op jit(solution)/shard_map/ppermute | solution.py:599
  66.9 1.6 %collective-permute-start.27 = (bf16[128,384]{1,0:T(8,128)(2,1)S(1)}, bf16[128,384]{1,0:T(8,128)(2,1)S(1)}, u32[]{:S(2)}, u32[]{:S(2)}) collective-permute-start(bf16[128,384]{1,0:T(8,128)(2,1)S(1)} %get-tuple-element.105), channel_id=1, source_target_pairs={{0,6},{2,4},{4,2},{6,0},{8,14},{10,12},{12,10},{14,8},{16,22},{18,... | collective-permute-start | bytes 294920 | tf_op jit(solution)/shard_map/ppermute | solution.py:448
  68.5 3.9 %collective-permute-done.22.s2 = bf16[48,1024]{1,0:T(8,128)(2,1)S(1)} collective-permute-done((bf16[48,1024]{1,0:T(8,128)(2,1)S(1)}, bf16[48,1024]{1,0:T(8,128)(2,1)S(1)}, u32[]{:S(2)}, u32[]{:S(2)}) %collective-permute-start.22) | collective-permute-done | bytes 98336 | tf_op jit(solution)/shard_map/ppermute | solution.py:599
  72.8 3.0 %collective-permute-start.31 = (bf16[48,1024]{1,0:T(8,128)(2,1)S(1)}, bf16[48,1024]{1,0:T(8,128)(2,1)S(1)}, u32[]{:S(2)}, u32[]{:S(2)}) collective-permute-start(bf16[48,1024]{1,0:T(8,128)(2,1)S(1)} %shard_map.116), channel_id=1, source_target_pairs={{0,16},{2,18},{4,20},{6,22},{8,24},{10,26},{12,28},{14,30},{16,0},... | collective-permute-start | bytes 294920 | tf_op jit(solution)/shard_map/ppermute | solution.py:608
  76.7 1.4 %collective-permute-start.29 = (bf16[1,48,1024]{2,1,0:T(8,128)(2,1)S(1)}, bf16[1,48,1024]{2,1,0:T(8,128)(2,1)S(1)}, u32[]{:S(2)}, u32[]{:S(2)}) collective-permute-start(bf16[1,48,1024]{2,1,0:T(8,128)(2,1)S(1)} %shard_map.117.refs_0_), channel_id=1, source_target_pairs={{0,4},{2,6},{4,0},{6,2},{8,12},{10,14},{12,8},{14,10},{16,20},{18,... | collective-permute-start | bytes 294920 | tf_op jit(solution)/shard_map/ppermute | solution.py:448
  78.1 1.3 %collective-permute-start.30 = (bf16[1,48,1024]{2,1,0:T(8,128)(2,1)S(1)}, bf16[1,48,1024]{2,1,0:T(8,128)(2,1)S(1)}, u32[]{:S(2)}, u32[]{:S(2)}) collective-permute-start(bf16[1,48,1024]{2,1,0:T(8,128)(2,1)S(1)} %shard_map.117.refs_0_), channel_id=1, source_target_pairs={{0,6},{2,4},{4,2},{6,0},{8,14},{10,12},{12,10},{14,8},{16,22},{18,... | collective-permute-start | bytes 294920 | tf_op jit(solution)/shard_map/ppermute | solution.py:448
  81.7 1.9 %collective-permute-done.30.refs_3_ = bf16[1,48,1024]{2,1,0:T(8,128)(2,1)S(1)} collective-permute-done((bf16[1,48,1024]{2,1,0:T(8,128)(2,1)S(1)}, bf16[1,48,1024]{2,1,0:T(8,128)(2,1)S(1)}, u32[]{:S(2)}, u32[]{:S(2)}) %collective-permute-start.30) | collective-permute-done | bytes 98336 | tf_op jit(solution)/shard_map/ppermute | solution.py:448
  86.3 1.7 %collective-permute-start.34 = (bf16[2,48,1024]{2,1,0:T(8,128)(2,1)S(1)}, bf16[2,48,1024]{2,1,0:T(8,128)(2,1)S(1)}, u32[]{:S(2)}, u32[]{:S(2)}) collective-permute-start(bf16[2,48,1024]{2,1,0:T(8,128)(2,1)S(1)} %pad_maximum_fusion.1.refs_1_), channel_id=1, source_target_pairs={{0,4},{2,6},{4,0},{6,2},{8,12},{10,14},{12,8},{14,10},{16,20},{18,... | collective-permute-start | bytes 589832 | tf_op jit(solution)/shard_map/ppermute | solution.py:448
  87.9 1.1 %collective-permute-start.35 = (bf16[2,48,1024]{2,1,0:T(8,128)(2,1)S(1)}, bf16[2,48,1024]{2,1,0:T(8,128)(2,1)S(1)}, u32[]{:S(2)}, u32[]{:S(2)}) collective-permute-start(bf16[2,48,1024]{2,1,0:T(8,128)(2,1)S(1)} %pad_maximum_fusion.1.refs_1_), channel_id=1, source_target_pairs={{0,6},{2,4},{4,2},{6,0},{8,14},{10,12},{12,10},{14,8},{16,22},{18,... | collective-permute-start | bytes 589832 | tf_op jit(solution)/shard_map/ppermute | solution.py:448
  90.8 1.2 %copy.15 = bf16[128,2,768]{2,1,0:T(2,128)(2,1)} copy(bf16[128,2,768]{2,0,1:T(8,128)(2,1)S(1)} %bitcast.19) | data formatting | bytes 786432
  91.9 1.5 %shard_map.118.refs_2_ = f32[768,2,512]{2,1,0:T(2,128)} custom-call(s32[4]{0:T(128)S(1)} %pad_add_fusion.scal, bf16[1,48,1024]{2,1,0:T(8,128)(2,1)S(1)} %shard_map.117.refs_0_, bf16[1,48,1024]{2,1,0:T(8,128)(2,1)S(1)} %collective-permute-done.28.refs_1_, bf16[1,48,1024]{2,1,0:T(8,128)(2,1)S(1)} %collective-permute-done.29.refs_2_, ...), custom_call_target="tpu_custom_call" | custom-call | tf_op jit(solution)/shard_map/pallas_call | solution.py:30
  93.4 1.6 %shard_map.119.refs_3_ = f32[768,2,512]{2,1,0:T(2,128)} custom-call(s32[4]{0:T(128)S(1)} %pad_add_fusion.scal, bf16[4,48,1024]{2,1,0:T(8,128)(2,1)S(1)} %collective-permute-done.36.refs_0_, bf16[2,48,1024]{2,1,0:T(8,128)(2,1)S(1)} %pad_maximum_fusion.1.refs_1_, f32[768,2,512]{2,1,0:T(2,128)} %shard_map.118.refs_2_), custom_call_target="tpu_custom_call", output_to_operand_aliasing={{}: (3, {})} | custom-call | tf_op jit(solution)/shard_map/pallas_call | solution.py:30
  95.1 1.6 %shard_map.120 = f32[768,2,512]{2,1,0:T(2,128)} custom-call(s32[4]{0:T(128)S(1)} %pad_add_fusion.scal, bf16[2,48,1024]{2,1,0:T(8,128)(2,1)S(1)} %collective-permute-done.33.refs_0_, bf16[2,48,1024]{2,1,0:T(8,128)(2,1)S(1)} %collective-permute-done.34.refs_1_, ...), custom_call_target="tpu_custom_call", output_to_operand_aliasing={{}: (4, {})} | custom-call | tf_op jit(solution)/shard_map/pallas_call | solution.py:30
  (74 shorter events, 25.3 us)
Async XLA Ops:
  2.7 5.8 %collective-permute-start = (bf16[16,384]{1,0:T(8,128)(2,1)S(1)}, bf16[16,384]{1,0:T(8,128)(2,1)S(1)}, u32[]{:S(2)}, u32[]{:S(2)}) collective-permute-start(bf16[16,384]{1,0:T(8,128)(2,1)S(1)} %shard_map.103.small), channel_id=1, source_target_pairs={{0,8},{2,10},{4,12},{6,14},{8,0},{10,2},{12,4},{14,6},{16,24},{18,... | collective-permute-start | bytes 36872 | tf_op jit(solution)/shard_map/ppermute | solution.py:455
  12.1 3.6 %collective-permute-start.5 = (f32[128,512]{1,0:T(8,128)S(1)}, f32[128,512]{1,0:T(8,128)S(1)}, u32[]{:S(2)}, u32[]{:S(2)}) collective-permute-start(f32[128,512]{1,0:T(8,128)S(1)} %get-tuple-element.71), channel_id=1, source_target_pairs={{0,1},{1,0},{2,3},{3,2},{4,5},{5,4},{6,7},{7,6},{8,9},{9,8},{10,11... | collective-permute-start | bytes 786440 | tf_op jit(solution)/shard_map/ppermute | solution.py:493
  12.2 7.6 %collective-permute-start.2 = (bf16[128,384]{1,0:T(8,128)(2,1)S(1)}, bf16[128,384]{1,0:T(8,128)(2,1)S(1)}, u32[]{:S(2)}, u32[]{:S(2)}) collective-permute-start(bf16[128,384]{1,0:T(8,128)(2,1)S(1)} %get-tuple-element.66), channel_id=1, source_target_pairs={{0,2},{2,0},{4,6},{6,4},{8,10},{10,8},{12,14},{14,12},{16,18},{18,... | collective-permute-start | bytes 294920 | tf_op jit(solution)/shard_map/ppermute | solution.py:448
  13.8 6.6 %collective-permute-start.3 = (bf16[128,384]{1,0:T(8,128)(2,1)S(1)}, bf16[128,384]{1,0:T(8,128)(2,1)S(1)}, u32[]{:S(2)}, u32[]{:S(2)}) collective-permute-start(bf16[128,384]{1,0:T(8,128)(2,1)S(1)} %get-tuple-element.67), channel_id=1, source_target_pairs={{0,4},{2,6},{4,0},{6,2},{8,12},{10,14},{12,8},{14,10},{16,20},{18,... | collective-permute-start | bytes 294920 | tf_op jit(solution)/shard_map/ppermute | solution.py:448
  15.3 6.4 %collective-permute-start.4 = (bf16[128,384]{1,0:T(8,128)(2,1)S(1)}, bf16[128,384]{1,0:T(8,128)(2,1)S(1)}, u32[]{:S(2)}, u32[]{:S(2)}) collective-permute-start(bf16[128,384]{1,0:T(8,128)(2,1)S(1)} %get-tuple-element.68), channel_id=1, source_target_pairs={{0,6},{2,4},{4,2},{6,0},{8,14},{10,12},{12,10},{14,8},{16,22},{18,... | collective-permute-start | bytes 294920 | tf_op jit(solution)/shard_map/ppermute | solution.py:448
  16.7 5.6 %collective-permute-start.6 = (bf16[272,128]{1,0:T(8,128)(2,1)S(1)}, bf16[272,128]{1,0:T(8,128)(2,1)S(1)}, u32[]{:S(2)}, u32[]{:S(2)}) collective-permute-start(bf16[272,128]{1,0:T(8,128)(2,1)S(1)} %get-tuple-element.76), channel_id=1, source_target_pairs={{0,2},{2,0},{4,6},{6,4},{8,10},{10,8},{12,14},{14,12},{16,18},{18,... | collective-permute-start | bytes 208904 | tf_op jit(solution)/shard_map/ppermute | solution.py:448
  18.3 5.1 %collective-permute-start.7 = (bf16[272,128]{1,0:T(8,128)(2,1)S(1)}, bf16[272,128]{1,0:T(8,128)(2,1)S(1)}, u32[]{:S(2)}, u32[]{:S(2)}) collective-permute-start(bf16[272,128]{1,0:T(8,128)(2,1)S(1)} %get-tuple-element.77), channel_id=1, source_target_pairs={{0,4},{2,6},{4,0},{6,2},{8,12},{10,14},{12,8},{14,10},{16,20},{18,... | collective-permute-start | bytes 208904 | tf_op jit(solution)/shard_map/ppermute | solution.py:448
  19.8 5.2 %collective-permute-start.8 = (bf16[272,128]{1,0:T(8,128)(2,1)S(1)}, bf16[272,128]{1,0:T(8,128)(2,1)S(1)}, u32[]{:S(2)}, u32[]{:S(2)}) collective-permute-start(bf16[272,128]{1,0:T(8,128)(2,1)S(1)} %get-tuple-element.78), channel_id=1, source_target_pairs={{0,6},{2,4},{4,2},{6,0},{8,14},{10,12},{12,10},{14,8},{16,22},{18,... | collective-permute-start | bytes 208904 | tf_op jit(solution)/shard_map/ppermute | solution.py:448
  25.6 13.7 %collective-permute-start.10 = (bf16[4,128,512]{2,1,0:T(8,128)(2,1)S(1)}, bf16[4,128,512]{2,1,0:T(8,128)(2,1)S(1)}, u32[]{:S(2)}, u32[]{:S(2)}) collective-permute-start(bf16[4,128,512]{2,1,0:T(8,128)(2,1)S(1)} %get-tuple-element.79.own), channel_id=1, source_target_pairs={{8,16},{10,18},{12,20},{14,22},{16,8},{18,10},{20,12},{22,14},{9,1... | collective-permute-start | bytes 1572872 | tf_op jit(solution)/shard_map/ppermute | solution.py:455
  26.4 17.0 %collective-permute-start.9 = (bf16[4,128,512]{2,1,0:T(8,128)(2,1)S(1)}, bf16[4,128,512]{2,1,0:T(8,128)(2,1)S(1)}, u32[]{:S(2)}, u32[]{:S(2)}) collective-permute-start(bf16[4,128,512]{2,1,0:T(8,128)(2,1)S(1)} %get-tuple-element.79.own), channel_id=1, source_target_pairs={{0,8},{2,10},{4,12},{6,14},{8,0},{10,2},{12,4},{14,6},{16,24},{18,... | collective-permute-start | bytes 1572872 | tf_op jit(solution)/shard_map/ppermute | solution.py:455
  38.3 5.8 %collective-permute-start.11 = (bf16[2,128,640]{2,1,0:T(8,128)(2,1)S(1)}, bf16[2,128,640]{2,1,0:T(8,128)(2,1)S(1)}, u32[]{:S(2)}, u32[]{:S(2)}) collective-permute-start(bf16[2,128,640]{2,1,0:T(8,128)(2,1)S(1)} %get-tuple-element.81.refs_0_), channel_id=1, source_target_pairs={{0,1},{1,0},{2,3},{3,2},{4,5},{5,4},{6,7},{7,6},{8,9},{9,8},{10,11... | collective-permute-start | bytes 983048 | tf_op jit(solution)/shard_map/ppermute | solution.py:538
  38.8 5.3 %collective-permute-start.12 = (bf16[2,128,640]{2,1,0:T(8,128)(2,1)S(1)}, bf16[2,128,640]{2,1,0:T(8,128)(2,1)S(1)}, u32[]{:S(2)}, u32[]{:S(2)}) collective-permute-start(bf16[2,128,640]{2,1,0:T(8,128)(2,1)S(1)} %get-tuple-element.82.refs_1_), channel_id=1, source_target_pairs={{0,1},{1,0},{2,3},{3,2},{4,5},{5,4},{6,7},{7,6},{8,9},{9,8},{10,11... | collective-permute-start | bytes 983048 | tf_op jit(solution)/shard_map/ppermute | solution.py:538
  38.9 5.2 %collective-permute-start.13 = (bf16[2,128,640]{2,1,0:T(8,128)(2,1)S(1)}, bf16[2,128,640]{2,1,0:T(8,128)(2,1)S(1)}, u32[]{:S(2)}, u32[]{:S(2)}) collective-permute-start(bf16[2,128,640]{2,1,0:T(8,128)(2,1)S(1)} %get-tuple-element.83.refs_2_), channel_id=1, source_target_pairs={{0,1},{1,0},{2,3},{3,2},{4,5},{5,4},{6,7},{7,6},{8,9},{9,8},{10,11... | collective-permute-start | bytes 983048 | tf_op jit(solution)/shard_map/ppermute | solution.py:538
  39.3 4.8 %collective-permute-start.14 = (bf16[2,128,640]{2,1,0:T(8,128)(2,1)S(1)}, bf16[2,128,640]{2,1,0:T(8,128)(2,1)S(1)}, u32[]{:S(2)}, u32[]{:S(2)}) collective-permute-start(bf16[2,128,640]{2,1,0:T(8,128)(2,1)S(1)} %get-tuple-element.84.refs_3_), channel_id=1, source_target_pairs={{0,1},{1,0},{2,3},{3,2},{4,5},{5,4},{6,7},{7,6},{8,9},{9,8},{10,11... | collective-permute-start | bytes 983048 | tf_op jit(solution)/shard_map/ppermute | solution.py:538
  46.6 7.9 %collective-permute-start.15 = (bf16[4,128,128]{2,1,0:T(8,128)(2,1)S(1)}, bf16[4,128,128]{2,1,0:T(8,128)(2,1)S(1)}, u32[]{:S(2)}, u32[]{:S(2)}) collective-permute-start(bf16[4,128,128]{2,1,0:T(8,128)(2,1)S(1)} %shard_map.112.refs_0_), channel_id=1, source_target_pairs={{0,2},{2,0},{4,6},{6,4},{8,10},{10,8},{12,14},{14,12},{16,18},{18,... | collective-permute-start | bytes 393224 | tf_op jit(solution)/shard_map/ppermute | solution.py:448
  47.7 6.7 %collective-permute-start.16 = (bf16[4,128,128]{2,1,0:T(8,128)(2,1)S(1)}, bf16[4,128,128]{2,1,0:T(8,128)(2,1)S(1)}, u32[]{:S(2)}, u32[]{:S(2)}) collective-permute-start(bf16[4,128,128]{2,1,0:T(8,128)(2,1)S(1)} %shard_map.112.refs_0_), channel_id=1, source_target_pairs={{0,4},{2,6},{4,0},{6,2},{8,12},{10,14},{12,8},{14,10},{16,20},{18,... | collective-permute-start | bytes 393224 | tf_op jit(solution)/shard_map/ppermute | solution.py:448
  48.3 6.2 %collective-permute-start.17 = (bf16[4,128,128]{2,1,0:T(8,128)(2,1)S(1)}, bf16[4,128,128]{2,1,0:T(8,128)(2,1)S(1)}, u32[]{:S(2)}, u32[]{:S(2)}) collective-permute-start(bf16[4,128,128]{2,1,0:T(8,128)(2,1)S(1)} %shard_map.112.refs_0_), channel_id=1, source_target_pairs={{0,6},{2,4},{4,2},{6,0},{8,14},{10,12},{12,10},{14,8},{16,22},{18,... | collective-permute-start | bytes 393224 | tf_op jit(solution)/shard_map/ppermute | solution.py:448
  58.6 6.4 %collective-permute-start.24 = (bf16[48,1024]{1,0:T(8,128)(2,1)S(1)}, bf16[48,1024]{1,0:T(8,128)(2,1)S(1)}, u32[]{:S(2)}, u32[]{:S(2)}) collective-permute-start(bf16[48,1024]{1,0:T(8,128)(2,1)S(1)} %get-tuple-element.97), channel_id=1, source_target_pairs={{0,8},{2,10},{4,12},{6,14},{8,0},{10,2},{12,4},{14,6},{16,24},{18,... | collective-permute-start | bytes 294920 | tf_op jit(solution)/shard_map/ppermute | solution.py:599
  61.7 10.7 %collective-permute-start.22 = (bf16[48,1024]{1,0:T(8,128)(2,1)S(1)}, bf16[48,1024]{1,0:T(8,128)(2,1)S(1)}, u32[]{:S(2)}, u32[]{:S(2)}) collective-permute-start(bf16[48,1024]{1,0:T(8,128)(2,1)S(1)} %get-tuple-element.95), channel_id=1, source_target_pairs={{0,16},{2,18},{4,20},{6,22},{8,24},{10,26},{12,28},{14,30},{16,0},... | collective-permute-start | bytes 294920 | tf_op jit(solution)/shard_map/ppermute | solution.py:599
  62.8 9.7 %collective-permute-start.23 = (bf16[48,1024]{1,0:T(8,128)(2,1)S(1)}, bf16[48,1024]{1,0:T(8,128)(2,1)S(1)}, u32[]{:S(2)}, u32[]{:S(2)}) collective-permute-start(bf16[48,1024]{1,0:T(8,128)(2,1)S(1)} %get-tuple-element.96), channel_id=1, source_target_pairs={{0,24},{2,26},{4,28},{6,30},{8,16},{10,18},{12,20},{14,22},{16,8},... | collective-permute-start | bytes 294920 | tf_op jit(solution)/shard_map/ppermute | solution.py:599
  65.0 7.4 %collective-permute-start.25 = (bf16[128,384]{1,0:T(8,128)(2,1)S(1)}, bf16[128,384]{1,0:T(8,128)(2,1)S(1)}, u32[]{:S(2)}, u32[]{:S(2)}) collective-permute-start(bf16[128,384]{1,0:T(8,128)(2,1)S(1)} %get-tuple-element.103), channel_id=1, source_target_pairs={{0,2},{2,0},{4,6},{6,4},{8,10},{10,8},{12,14},{14,12},{16,18},{18,... | collective-permute-start | bytes 294920 | tf_op jit(solution)/shard_map/ppermute | solution.py:448
  66.0 6.7 %collective-permute-start.26 = (bf16[128,384]{1,0:T(8,128)(2,1)S(1)}, bf16[128,384]{1,0:T(8,128)(2,1)S(1)}, u32[]{:S(2)}, u32[]{:S(2)}) collective-permute-start(bf16[128,384]{1,0:T(8,128)(2,1)S(1)} %get-tuple-element.104), channel_id=1, source_target_pairs={{0,4},{2,6},{4,0},{6,2},{8,12},{10,14},{12,8},{14,10},{16,20},{18,... | collective-permute-start | bytes 294920 | tf_op jit(solution)/shard_map/ppermute | solution.py:448
  66.9 5.8 %collective-permute-start.27 = (bf16[128,384]{1,0:T(8,128)(2,1)S(1)}, bf16[128,384]{1,0:T(8,128)(2,1)S(1)}, u32[]{:S(2)}, u32[]{:S(2)}) collective-permute-start(bf16[128,384]{1,0:T(8,128)(2,1)S(1)} %get-tuple-element.105), channel_id=1, source_target_pairs={{0,6},{2,4},{4,2},{6,0},{8,14},{10,12},{12,10},{14,8},{16,22},{18,... | collective-permute-start | bytes 294920 | tf_op jit(solution)/shard_map/ppermute | solution.py:448
  72.8 7.2 %collective-permute-start.31 = (bf16[48,1024]{1,0:T(8,128)(2,1)S(1)}, bf16[48,1024]{1,0:T(8,128)(2,1)S(1)}, u32[]{:S(2)}, u32[]{:S(2)}) collective-permute-start(bf16[48,1024]{1,0:T(8,128)(2,1)S(1)} %shard_map.116), channel_id=1, source_target_pairs={{0,16},{2,18},{4,20},{6,22},{8,24},{10,26},{12,28},{14,30},{16,0},... | collective-permute-start | bytes 294920 | tf_op jit(solution)/shard_map/ppermute | solution.py:608
  75.8 5.4 %collective-permute-start.28 = (bf16[1,48,1024]{2,1,0:T(8,128)(2,1)S(1)}, bf16[1,48,1024]{2,1,0:T(8,128)(2,1)S(1)}, u32[]{:S(2)}, u32[]{:S(2)}) collective-permute-start(bf16[1,48,1024]{2,1,0:T(8,128)(2,1)S(1)} %shard_map.117.refs_0_), channel_id=1, source_target_pairs={{0,2},{2,0},{4,6},{6,4},{8,10},{10,8},{12,14},{14,12},{16,18},{18,... | collective-permute-start | bytes 294920 | tf_op jit(solution)/shard_map/ppermute | solution.py:448
  76.7 5.0 %collective-permute-start.29 = (bf16[1,48,1024]{2,1,0:T(8,128)(2,1)S(1)}, bf16[1,48,1024]{2,1,0:T(8,128)(2,1)S(1)}, u32[]{:S(2)}, u32[]{:S(2)}) collective-permute-start(bf16[1,48,1024]{2,1,0:T(8,128)(2,1)S(1)} %shard_map.117.refs_0_), channel_id=1, source_target_pairs={{0,4},{2,6},{4,0},{6,2},{8,12},{10,14},{12,8},{14,10},{16,20},{18,... | collective-permute-start | bytes 294920 | tf_op jit(solution)/shard_map/ppermute | solution.py:448
  78.1 5.5 %collective-permute-start.30 = (bf16[1,48,1024]{2,1,0:T(8,128)(2,1)S(1)}, bf16[1,48,1024]{2,1,0:T(8,128)(2,1)S(1)}, u32[]{:S(2)}, u32[]{:S(2)}) collective-permute-start(bf16[1,48,1024]{2,1,0:T(8,128)(2,1)S(1)} %shard_map.117.refs_0_), channel_id=1, source_target_pairs={{0,6},{2,4},{4,2},{6,0},{8,14},{10,12},{12,10},{14,8},{16,22},{18,... | collective-permute-start | bytes 294920 | tf_op jit(solution)/shard_map/ppermute | solution.py:448
  79.9 4.7 %collective-permute-start.32 = (bf16[48,1024]{1,0:T(8,128)(2,1)S(1)}, bf16[48,1024]{1,0:T(8,128)(2,1)S(1)}, u32[]{:S(2)}, u32[]{:S(2)}) collective-permute-start(bf16[48,1024]{1,0:T(8,128)(2,1)S(1)} %collective-permute-done.31), channel_id=1, source_target_pairs={{0,8},{2,10},{4,12},{6,14},{8,0},{10,2},{12,4},{14,6},{16,24},{18,... | collective-permute-start | bytes 294920 | tf_op jit(solution)/shard_map/ppermute | solution.py:609
  84.7 8.7 %collective-permute-start.36 = (bf16[4,48,1024]{2,1,0:T(8,128)(2,1)S(1)}, bf16[4,48,1024]{2,1,0:T(8,128)(2,1)S(1)}, u32[]{:S(2)}, u32[]{:S(2)}) collective-permute-start(bf16[4,48,1024]{2,1,0:T(8,128)(2,1)S(1)} %pad_maximum_fusion), channel_id=1, source_target_pairs={{0,8},{2,10},{4,12},{6,14},{8,0},{10,2},{12,4},{14,6},{16,24},{18,... | collective-permute-start | bytes 1179656 | tf_op jit(solution)/shard_map/ppermute | solution.py:636
  85.6 9.5 %collective-permute-start.33 = (bf16[2,48,1024]{2,1,0:T(8,128)(2,1)S(1)}, bf16[2,48,1024]{2,1,0:T(8,128)(2,1)S(1)}, u32[]{:S(2)}, u32[]{:S(2)}) collective-permute-start(bf16[2,48,1024]{2,1,0:T(8,128)(2,1)S(1)} %pad_maximum_fusion.1.refs_1_), channel_id=1, source_target_pairs={{0,2},{2,0},{4,6},{6,4},{8,10},{10,8},{12,14},{14,12},{16,18},{18,... | collective-permute-start | bytes 589832 | tf_op jit(solution)/shard_map/ppermute | solution.py:448
  86.3 8.8 %collective-permute-start.34 = (bf16[2,48,1024]{2,1,0:T(8,128)(2,1)S(1)}, bf16[2,48,1024]{2,1,0:T(8,128)(2,1)S(1)}, u32[]{:S(2)}, u32[]{:S(2)}) collective-permute-start(bf16[2,48,1024]{2,1,0:T(8,128)(2,1)S(1)} %pad_maximum_fusion.1.refs_1_), channel_id=1, source_target_pairs={{0,4},{2,6},{4,0},{6,2},{8,12},{10,14},{12,8},{14,10},{16,20},{18,... | collective-permute-start | bytes 589832 | tf_op jit(solution)/shard_map/ppermute | solution.py:448
  87.9 7.2 %collective-permute-start.35 = (bf16[2,48,1024]{2,1,0:T(8,128)(2,1)S(1)}, bf16[2,48,1024]{2,1,0:T(8,128)(2,1)S(1)}, u32[]{:S(2)}, u32[]{:S(2)}) collective-permute-start(bf16[2,48,1024]{2,1,0:T(8,128)(2,1)S(1)} %pad_maximum_fusion.1.refs_1_), channel_id=1, source_target_pairs={{0,6},{2,4},{4,2},{6,0},{8,14},{10,12},{12,10},{14,8},{16,22},{18,... | collective-permute-start | bytes 589832 | tf_op jit(solution)/shard_map/ppermute | solution.py:448
  (7 other events, 24.6 us)

commit v6 on v5

--- a/solution.py
+++ b/solution.py
@@ -260,16 +260,19 @@
     for i in range(GROUP):
         value = acc[i] * (1.0 / FILTER_HALF)
         top = value.astype(BF16)
-        outs[i][0] = top
-        outs[i][1] = (value - top.astype(F32)).astype(BF16)
-
-
-def columns_body(scal, small, cols):
-    rows_out, nodes = cols.shape[0:2]
+        outs[i][:, 0 : 5 * nodes] = top
+        outs[i][:, 5 * nodes :] = (value - top.astype(F32)).astype(BF16)
+
+
+def join_body(scal, own, twin, next_, small, vec, cols):
+    nodes = own.shape[1]
+    rows_out = cols.shape[0]
     odd = scal[1] & 1
-    for source, dz in ((0, 1), (1, 2 - 2 * odd), (2, 2 * odd)):
+    for source, (array, dz) in enumerate(((own, 1), (twin, 2 - 2 * odd), (next_, 2 * odd))):
         for p in range(GROUP):
-            i = dz * GROUP + p - 2
+            t = dz * GROUP + p
+            vec[pl.ds(pl.multiple_of(t * nodes, nodes), nodes), :] = array[p]
+            i = t - 2
 
             @pl.when((i >= 0) & (i < rows_out))
             def _():
@@ -277,15 +280,6 @@
                 line, _ = spread_line(rows, 12, nodes)
                 column = jnp.sum(line, axis=1, keepdims=True) * (1.0 / FILTER_HALF)
                 cols[i] = jnp.broadcast_to(column, cols.shape[1:])
-
-
-def join_body(scal, own, twin, next_, vec):
-    nodes = own.shape[1]
-    odd = scal[1] & 1
-    for array, dz in ((own, 1), (twin, 2 - 2 * odd), (next_, 2 * odd)):
-        for p in range(GROUP):
-            t = dz * GROUP + p
-            vec[pl.ds(pl.multiple_of(t * nodes, nodes), nodes), :] = array[p]
 
 
 def filter_body(at, half, scal, side_s, vec, cols, *refs):
@@ -301,8 +295,8 @@
 
     def applied(source, lanes, start, i, rows):
         block = source[rows_at(start, 5), lanes]
-        total = jnp.dot(rows[0], block, preferred_element_type=F32)
-        total = total + jnp.dot(rows[1], block, preferred_element_type=F32)
+        twice = jnp.concatenate([block, block], axis=0)
+        total = jnp.dot(rows[...], twice, preferred_element_type=F32)
         mid = source[rows_at(start + 2, 1), lanes].astype(F32)
         return total + (cols[i][:, 0:1] * sign) * pltpu.roll(mid, half, 1)
 
@@ -518,7 +512,7 @@
     def operator(side):
         return call(
             functools.partial(build_body, nodes, e_cap),
-            [struct(2, nodes, 5 * nodes)] * GROUP,
+            [struct(nodes, 10 * nodes)] * GROUP,
             [SMEM, SMEM, VMEM, VMEM],
             (scal, side, small, matrix),
             scratch=[
@@ -540,14 +534,11 @@
         side = jnp.zeros((1,), jnp.int32)
         halves = [operator(side), operator(side + 1)]
 
-    absorb = call(
-        columns_body, struct(2 * GROUP, nodes, 128, dtype=F32), [SMEM, VMEM], (scal, small)
-    )
-    vec = call(
+    vec, absorb = call(
         join_body,
-        struct(3 * GROUP * nodes, all_lanes),
-        [SMEM] + [VMEM] * 3,
-        (scal, messages, *near),
+        [struct(3 * GROUP * nodes, all_lanes), struct(2 * GROUP, nodes, 128, dtype=F32)],
+        [SMEM] + [VMEM] * 4,
+        (scal, messages, *near, small),
     )
 
     def filtered_lanes(at, size, out_shape):
@@ -611,6 +602,14 @@
         received = swap(fields)
         lines = [[GROUP * z + i for z in range(groups)] for i in range(GROUP)]
         stack = [lax.psum(terms[0], "elem", axis_index_groups=lines).astype(BF16)]
+    filtered = call(
+        functools.partial(collect_body, w, wp),
+        struct(2, nodes, bands),
+        [SMEM] + [VMEM] * GROUP,
+        (scal, *received),
+    )
+    filtered, rotated = jnp.moveaxis(filtered, 0, 1), jnp.moveaxis(rotated, 0, 1)
+
     def write(arrays, plan, base=None):
         more = [] if base is None else [base]
         return call(
@@ -631,20 +630,16 @@
     intersection = write(near_pieces, [(k, 0, k, 0) for k in everywhere])
     if direct:
         far = jnp.stack(stack[2:])
-        twin_pieces, far = lax.optimization_barrier((jnp.concatenate(near_pieces), far))
+        twin_pieces, far, filtered, rotated = lax.optimization_barrier(
+            (jnp.concatenate(near_pieces), far, filtered, rotated)
+        )
         far_pieces = swap([far] * GROUP)
         twin_pieces = lax.ppermute(twin_pieces, "elem", twins)
         plan = [(0, k, k, 1) for k in everywhere] + [(1, j - 2, 0, j) for j in range(2, split)]
         intersection = write([twin_pieces, far], plan, intersection)
         plan = [(k - 1, j - 2, k, j) for k in range(1, GROUP) for j in range(2, split)]
         intersection = write(far_pieces[1:], plan, intersection)
-    filtered = call(
-        functools.partial(collect_body, w, wp),
-        struct(2, nodes, bands),
-        [SMEM] + [VMEM] * GROUP,
-        (scal, *received),
-    )
-    return (jnp.moveaxis(filtered, 0, 1), jnp.moveaxis(rotated, 0, 1), intersection)
+    return (filtered, rotated, intersection)
 
 
 def solution(mesh):

time: 97.2 us -> 96.7 us (level)
  waiting for transfers between devices: 17.9 us -> 19.8 us
  Pallas kernels: 25.1 us -> 23.8 us
  starting transfers between devices: 45.2 us -> 44.1 us
    ppermute x2, waiting for transfers between devices: 2.96 us -> 4.47 us  [neighbours(): lax.ppermute(value, 'elem', twins)]
    pallas_call x18 -> x17, Pallas kernels: 25.1 us -> 23.8 us  [call(): pl.pallas_call(body, out_shape=out_shape, in_specs=specs, out_specs=out_s...]
  transfers between devices with their start and end apart: 37 -> 37, of which waited for: 16 -> 16; matrix products, arithmetic and copies ran while one was open for 3% -> 3% of each run, Pallas kernels for 18% -> 16%
where the time goes in v6:
time: 96.7 us; the launch traced here: 96.4 us
  starting transfers between devices  44.1 us (46%)
  Pallas kernels  23.8 us (25%)
  waiting for transfers between devices  19.8 us (20%)
  local copies, waits for them, and re-layouts  6.1 us (6%)
  between operations  1.81 us (2%)
    pallas_call x17, Pallas kernels, call(): pl.pallas_call(body, out_shape=out_shape, in_specs=specs, out_specs=out_s...  23.8 us
    ppermute x18, starting transfers between devices, swap(): lax.ppermute(values[k], 'elem', in_group(k))  21.3 us
    ppermute x2, starting transfers between devices, neighbours(): lax.ppermute(value, 'elem', twins)  10.3 us
    ppermute x18, waiting for transfers between devices, swap(): lax.ppermute(values[k], 'elem', in_group(k))  7.19 us
    ppermute x3, starting transfers between devices, across(): lax.ppermute(values[j], 'elem', [(i, i ^ GROUP * j) for i in range(blocks)])  5.02 us
    ppermute x3, waiting for transfers between devices, across(): lax.ppermute(values[j], 'elem', [(i, i ^ GROUP * j) for i in range(blocks)])  4.84 us
    ppermute x2, waiting for transfers between devices, neighbours(): lax.ppermute(value, 'elem', twins)  4.47 us
    ppermute x1, starting transfers between devices, on_device(): lax.ppermute(own, 'elem', [(i, i ^ 2 * GROUP) for i in range(blocks)])  2.71 us
  transfers between devices with their start and end apart: 37, of which 16 were waited for; matrix products, arithmetic and copies ran while one was open for 3% of the time, Pallas kernels for 16%

profile of v6, /device:TPU:0, one launch (start us, length us, event | category | flops | bytes accessed | tf_op | source)
XLA Modules:
  0.0 96.4 jit_solution(8625741779694032343)
XLA Ops:
  2.7 3.1 %collective-permute-start = (bf16[16,384]{1,0:T(8,128)(2,1)S(1)}, bf16[16,384]{1,0:T(8,128)(2,1)S(1)}, u32[]{:S(2)}, u32[]{:S(2)}) collective-permute-start(bf16[16,384]{1,0:T(8,128)(2,1)S(1)} %shard_map.103.small), channel_id=1, source_target_pairs={{0,8},{2,10},{4,12},{6,14},{8,0},{10,2},{12,4},{14,6},{16,24},{18,... | collective-permute-start | bytes 36872 | tf_op jit(solution)/shard_map/ppermute | solution.py:449
  8.6 2.4 %copy.19 = bf16[1536,2,512]{2,0,1:T(8,128)(2,1)S(1)} copy(bf16[1536,2,512]{2,1,0:T(2,128)(2,1)} %param.15) | data formatting | bytes 6291456 | tf_op jit(solution)/shard_map/optimization_barrier | solution.py:471
  11.0 1.2 %shard_map.106 = (f32[128,512]{1,0:T(8,128)S(1)}, f32[128,512]{1,0:T(8,128)S(1)}) custom-call(s32[4]{0:T(128)S(1)} %pad_add_fusion.scal, bf16[2,128,768]{2,1,0:T(8,128)(2,1)S(1)} %bitcast.18, bf16[2,1536,512]{2,1,0:T(8,128)(2,1)S(1)} %bitcast.16), custom_call_target="tpu_custom_call" | custom-call | flops 4000000000 | bytes 15625000 | tf_op jit(solution)/shard_map/pallas_call | solution.py:30
  12.2 1.6 %collective-permute-start.2 = (bf16[128,384]{1,0:T(8,128)(2,1)S(1)}, bf16[128,384]{1,0:T(8,128)(2,1)S(1)}, u32[]{:S(2)}, u32[]{:S(2)}) collective-permute-start(bf16[128,384]{1,0:T(8,128)(2,1)S(1)} %get-tuple-element.70), channel_id=1, source_target_pairs={{0,2},{2,0},{4,6},{6,4},{8,10},{10,8},{12,14},{14,12},{16,18},{18,... | collective-permute-start | bytes 294920 | tf_op jit(solution)/shard_map/ppermute | solution.py:442
  13.8 1.5 %collective-permute-start.3 = (bf16[128,384]{1,0:T(8,128)(2,1)S(1)}, bf16[128,384]{1,0:T(8,128)(2,1)S(1)}, u32[]{:S(2)}, u32[]{:S(2)}) collective-permute-start(bf16[128,384]{1,0:T(8,128)(2,1)S(1)} %get-tuple-element.71), channel_id=1, source_target_pairs={{0,4},{2,6},{4,0},{6,2},{8,12},{10,14},{12,8},{14,10},{16,20},{18,... | collective-permute-start | bytes 294920 | tf_op jit(solution)/shard_map/ppermute | solution.py:442
  16.7 1.6 %collective-permute-start.6 = (bf16[272,128]{1,0:T(8,128)(2,1)S(1)}, bf16[272,128]{1,0:T(8,128)(2,1)S(1)}, u32[]{:S(2)}, u32[]{:S(2)}) collective-permute-start(bf16[272,128]{1,0:T(8,128)(2,1)S(1)} %get-tuple-element.80), channel_id=1, source_target_pairs={{0,2},{2,0},{4,6},{6,4},{8,10},{10,8},{12,14},{14,12},{16,18},{18,... | collective-permute-start | bytes 208904 | tf_op jit(solution)/shard_map/ppermute | solution.py:442
  18.3 1.5 %collective-permute-start.7 = (bf16[272,128]{1,0:T(8,128)(2,1)S(1)}, bf16[272,128]{1,0:T(8,128)(2,1)S(1)}, u32[]{:S(2)}, u32[]{:S(2)}) collective-permute-start(bf16[272,128]{1,0:T(8,128)(2,1)S(1)} %get-tuple-element.81), channel_id=1, source_target_pairs={{0,4},{2,6},{4,0},{6,2},{8,12},{10,14},{12,8},{14,10},{16,20},{18,... | collective-permute-start | bytes 208904 | tf_op jit(solution)/shard_map/ppermute | solution.py:442
  20.3 1.3 %collective-permute-done.4.a3 = bf16[128,384]{1,0:T(8,128)(2,1)S(1)} collective-permute-done((bf16[128,384]{1,0:T(8,128)(2,1)S(1)}, bf16[128,384]{1,0:T(8,128)(2,1)S(1)}, u32[]{:S(2)}, u32[]{:S(2)}) %collective-permute-start.4) | collective-permute-done | bytes 98336 | tf_op jit(solution)/shard_map/ppermute | solution.py:442
  23.3 1.7 %collective-permute-done.8.a3 = bf16[272,128]{1,0:T(8,128)(2,1)S(1)} collective-permute-done((bf16[272,128]{1,0:T(8,128)(2,1)S(1)}, bf16[272,128]{1,0:T(8,128)(2,1)S(1)}, u32[]{:S(2)}, u32[]{:S(2)}) %collective-permute-start.8) | collective-permute-done | bytes 69664 | tf_op jit(solution)/shard_map/ppermute | solution.py:442
  26.4 7.2 %collective-permute-start.9 = (bf16[4,128,512]{2,1,0:T(8,128)(2,1)S(1)}, bf16[4,128,512]{2,1,0:T(8,128)(2,1)S(1)}, u32[]{:S(2)}, u32[]{:S(2)}) collective-permute-start(bf16[4,128,512]{2,1,0:T(8,128)(2,1)S(1)} %get-tuple-element.83.own), channel_id=1, source_target_pairs={{0,8},{2,10},{4,12},{6,14},{8,0},{10,2},{12,4},{14,6},{16,24},{18,... | collective-permute-start | bytes 1572872 | tf_op jit(solution)/shard_map/ppermute | solution.py:449
  33.6 4.2 %shard_map.110 = (bf16[128,1280]{1,0:T(8,128)(2,1)S(1)}, bf16[128,1280]{1,0:T(8,128)(2,1)S(1)}, bf16[128,1280]{1,0:T(8,128)(2,1)S(1)}, bf16[128,1280]{1,0:T(8,128)(2,1)S(1)}) custom-call(s32[4]{0:T(128)S(1)} %pad_add_fusion.scal, s32[1]{0:T(128)} %bitcast.2.side_s, bf16[4,144,128]{2,1,0:T(8,128)(2,1)S(1)} %get-tuple-element.84.small, ...), custom_call_target="tpu_custom_call" | custom-call | flops 2717908992 | bytes 2621440 | tf_op jit(solution)/shard_map/pallas_call | solution.py:30
  38.9 4.5 %collective-permute-done.9.twin = bf16[4,128,512]{2,1,0:T(8,128)(2,1)S(1)} collective-permute-done((bf16[4,128,512]{2,1,0:T(8,128)(2,1)S(1)}, bf16[4,128,512]{2,1,0:T(8,128)(2,1)S(1)}, u32[]{:S(2)}, u32[]{:S(2)}) %collective-permute-start.9) | collective-permute-done | bytes 524320 | tf_op jit(solution)/shard_map/ppermute | solution.py:449
  44.6 2.4 %shard_map.111.refs_0_ = bf16[4,128,128]{2,1,0:T(8,128)(2,1)S(1)} custom-call(s32[4]{0:T(128)S(1)} %pad_add_fusion.scal, s32[1]{0:T(128)} %bitcast.2.side_s, bf16[1536,512]{1,0:T(8,128)(2,1)S(1)} %get-tuple-element.85.vec, f32[8,128,128]{2,1,0:T(8,128)S(1)} %get-tuple-element.86.cols, bf16[128,1280]{1,0:T(8,128)(2,1)S(1)} %get-tuple-element.87.refs_0_, ...), custom_call_target="tpu_custom_call" | custom-call | flops 503316480 | bytes 2621440 | tf_op jit(solution)/shard_map/pallas_call | solution.py:30
  47.0 1.2 %collective-permute-start.15 = (bf16[4,128,128]{2,1,0:T(8,128)(2,1)S(1)}, bf16[4,128,128]{2,1,0:T(8,128)(2,1)S(1)}, u32[]{:S(2)}, u32[]{:S(2)}) collective-permute-start(bf16[4,128,128]{2,1,0:T(8,128)(2,1)S(1)} %shard_map.111.refs_0_), channel_id=1, source_target_pairs={{0,2},{2,0},{4,6},{6,4},{8,10},{10,8},{12,14},{14,12},{16,18},{18,... | collective-permute-start | bytes 393224 | tf_op jit(solution)/shard_map/ppermute | solution.py:442
  48.8 1.8 %collective-permute-start.17 = (bf16[4,128,128]{2,1,0:T(8,128)(2,1)S(1)}, bf16[4,128,128]{2,1,0:T(8,128)(2,1)S(1)}, u32[]{:S(2)}, u32[]{:S(2)}) collective-permute-start(bf16[4,128,128]{2,1,0:T(8,128)(2,1)S(1)} %shard_map.111.refs_0_), channel_id=1, source_target_pairs={{0,6},{2,4},{4,2},{6,0},{8,14},{10,12},{12,10},{14,8},{16,22},{18,... | collective-permute-start | bytes 393224 | tf_op jit(solution)/shard_map/ppermute | solution.py:442
  50.5 4.1 %shard_map.112 = (bf16[128,384]{1,0:T(8,128)(2,1)S(1)}, bf16[128,384]{1,0:T(8,128)(2,1)S(1)}, bf16[128,384]{1,0:T(8,128)(2,1)S(1)}, bf16[128,384]{1,0:T(8,128)(2,1)S(1)}, bf16[384,512]{1,0:T(8,128)(2,1)S(1)}) custom-call(s32[4]{0:T(128)S(1)} %pad_add_fusion.scal, s32[1]{0:T(128)} %bitcast.2.side_s, bf16[1536,512]{1,0:T(8,128)(2,1)S(1)} %get-tuple-element.85.vec, ...), custom_call_target="tpu_custom_call" | custom-call | flops 1509949440 | bytes 2621440 | tf_op jit(solution)/shard_map/pallas_call | solution.py:30
  56.8 2.0 %shard_map.113 = (bf16[48,1024]{1,0:T(8,128)(2,1)S(1)}, bf16[48,1024]{1,0:T(8,128)(2,1)S(1)}, bf16[48,1024]{1,0:T(8,128)(2,1)S(1)}, bf16[48,1024]{1,0:T(8,128)(2,1)S(1)}, bf16[2,128,256]{2,1,0:T(8,128)(2,1)S(1)}) custom-call(s32[4]{0:T(128)S(1)} %pad_add_fusion.scal, bf16[384,512]{1,0:T(8,128)(2,1)S(1)} %get-tuple-element.96.left, ...), custom_call_target="tpu_custom_call" | custom-call | flops 402653184 | bytes 1048576 | tf_op jit(solution)/shard_map/pallas_call | solution.py:30
  58.8 2.6 %collective-permute-start.22 = (bf16[48,1024]{1,0:T(8,128)(2,1)S(1)}, bf16[48,1024]{1,0:T(8,128)(2,1)S(1)}, u32[]{:S(2)}, u32[]{:S(2)}) collective-permute-start(bf16[48,1024]{1,0:T(8,128)(2,1)S(1)} %get-tuple-element.102), channel_id=1, source_target_pairs={{0,8},{2,10},{4,12},{6,14},{8,0},{10,2},{12,4},{14,6},{16,24},{18,... | collective-permute-start | bytes 294920 | tf_op jit(solution)/shard_map/ppermute | solution.py:590
  62.2 1.6 %collective-permute-start.24 = (bf16[48,1024]{1,0:T(8,128)(2,1)S(1)}, bf16[48,1024]{1,0:T(8,128)(2,1)S(1)}, u32[]{:S(2)}, u32[]{:S(2)}) collective-permute-start(bf16[48,1024]{1,0:T(8,128)(2,1)S(1)} %get-tuple-element.109), channel_id=1, source_target_pairs={{0,24},{2,26},{4,28},{6,30},{8,16},{10,18},{12,20},{14,22},{16,8},... | collective-permute-start | bytes 294920 | tf_op jit(solution)/shard_map/ppermute | solution.py:590
  64.6 1.1 %collective-permute-start.25 = (bf16[128,384]{1,0:T(8,128)(2,1)S(1)}, bf16[128,384]{1,0:T(8,128)(2,1)S(1)}, u32[]{:S(2)}, u32[]{:S(2)}) collective-permute-start(bf16[128,384]{1,0:T(8,128)(2,1)S(1)} %get-tuple-element.111), channel_id=1, source_target_pairs={{0,2},{2,0},{4,6},{6,4},{8,10},{10,8},{12,14},{14,12},{16,18},{18,... | collective-permute-start | bytes 294920 | tf_op jit(solution)/shard_map/ppermute | solution.py:442
  66.8 1.3 %collective-permute-start.27 = (bf16[128,384]{1,0:T(8,128)(2,1)S(1)}, bf16[128,384]{1,0:T(8,128)(2,1)S(1)}, u32[]{:S(2)}, u32[]{:S(2)}) collective-permute-start(bf16[128,384]{1,0:T(8,128)(2,1)S(1)} %get-tuple-element.113), channel_id=1, source_target_pairs={{0,6},{2,4},{4,2},{6,0},{8,14},{10,12},{12,10},{14,8},{16,22},{18,... | collective-permute-start | bytes 294920 | tf_op jit(solution)/shard_map/ppermute | solution.py:442
  68.1 4.0 %collective-permute-done.23.s2 = bf16[48,1024]{1,0:T(8,128)(2,1)S(1)} collective-permute-done((bf16[48,1024]{1,0:T(8,128)(2,1)S(1)}, bf16[48,1024]{1,0:T(8,128)(2,1)S(1)}, u32[]{:S(2)}, u32[]{:S(2)}) %collective-permute-start.23) | collective-permute-done | bytes 98336 | tf_op jit(solution)/shard_map/ppermute | solution.py:590
  72.5 2.7 %collective-permute-start.31 = (bf16[48,1024]{1,0:T(8,128)(2,1)S(1)}, bf16[48,1024]{1,0:T(8,128)(2,1)S(1)}, u32[]{:S(2)}, u32[]{:S(2)}) collective-permute-start(bf16[48,1024]{1,0:T(8,128)(2,1)S(1)} %shard_map.114), channel_id=1, source_target_pairs={{0,16},{2,18},{4,20},{6,22},{8,24},{10,26},{12,28},{14,30},{16,0},... | collective-permute-start | bytes 294920 | tf_op jit(solution)/shard_map/ppermute | solution.py:599
  76.1 1.4 %collective-permute-start.29 = (bf16[1,48,1024]{2,1,0:T(8,128)(2,1)S(1)}, bf16[1,48,1024]{2,1,0:T(8,128)(2,1)S(1)}, u32[]{:S(2)}, u32[]{:S(2)}) collective-permute-start(bf16[1,48,1024]{2,1,0:T(8,128)(2,1)S(1)} %shard_map.115.refs_0_), channel_id=1, source_target_pairs={{0,4},{2,6},{4,0},{6,2},{8,12},{10,14},{12,8},{14,10},{16,20},{18,... | collective-permute-start | bytes 294920 | tf_op jit(solution)/shard_map/ppermute | solution.py:442
  77.5 1.3 %collective-permute-start.30 = (bf16[1,48,1024]{2,1,0:T(8,128)(2,1)S(1)}, bf16[1,48,1024]{2,1,0:T(8,128)(2,1)S(1)}, u32[]{:S(2)}, u32[]{:S(2)}) collective-permute-start(bf16[1,48,1024]{2,1,0:T(8,128)(2,1)S(1)} %shard_map.115.refs_0_), channel_id=1, source_target_pairs={{0,6},{2,4},{4,2},{6,0},{8,14},{10,12},{12,10},{14,8},{16,22},{18,... | collective-permute-start | bytes 294920 | tf_op jit(solution)/shard_map/ppermute | solution.py:442
  80.9 2.1 %collective-permute-done.30.refs_3_ = bf16[1,48,1024]{2,1,0:T(8,128)(2,1)S(1)} collective-permute-done((bf16[1,48,1024]{2,1,0:T(8,128)(2,1)S(1)}, bf16[1,48,1024]{2,1,0:T(8,128)(2,1)S(1)}, u32[]{:S(2)}, u32[]{:S(2)}) %collective-permute-start.30) | collective-permute-done | bytes 98336 | tf_op jit(solution)/shard_map/ppermute | solution.py:442
  83.1 2.0 %collective-permute-done.32 = bf16[48,1024]{1,0:T(8,128)(2,1)S(1)} collective-permute-done((bf16[48,1024]{1,0:T(8,128)(2,1)S(1)}, bf16[48,1024]{1,0:T(8,128)(2,1)S(1)}, u32[]{:S(2)}, u32[]{:S(2)}) %collective-permute-start.32) | collective-permute-done | bytes 98336 | tf_op jit(solution)/shard_map/ppermute | solution.py:600
  87.6 1.6 %collective-permute-start.35 = (bf16[2,48,1024]{2,1,0:T(8,128)(2,1)S(1)}, bf16[2,48,1024]{2,1,0:T(8,128)(2,1)S(1)}, u32[]{:S(2)}, u32[]{:S(2)}) collective-permute-start(bf16[2,48,1024]{2,1,0:T(8,128)(2,1)S(1)} %pad_maximum_fusion.1.refs_1_), channel_id=1, source_target_pairs={{0,6},{2,4},{4,2},{6,0},{8,14},{10,12},{12,10},{14,8},{16,22},{18,... | collective-permute-start | bytes 589832 | tf_op jit(solution)/shard_map/ppermute | solution.py:442
  89.2 1.5 %shard_map.117.refs_2_ = f32[768,2,512]{2,1,0:T(2,128)} custom-call(s32[4]{0:T(128)S(1)} %pad_add_fusion.scal, bf16[1,48,1024]{2,1,0:T(8,128)(2,1)S(1)} %shard_map.115.refs_0_, bf16[1,48,1024]{2,1,0:T(8,128)(2,1)S(1)} %collective-permute-done.28.refs_1_, bf16[1,48,1024]{2,1,0:T(8,128)(2,1)S(1)} %collective-permute-done.29.refs_2_, ...), custom_call_target="tpu_custom_call" | custom-call | tf_op jit(solution)/shard_map/pallas_call | solution.py:30
  90.7 1.2 %copy.15 = bf16[128,2,768]{2,1,0:T(2,128)(2,1)} copy(bf16[128,2,768]{2,0,1:T(8,128)(2,1)S(1)} %bitcast.19) | data formatting | bytes 786432
  92.9 1.6 %shard_map.118.refs_3_ = f32[768,2,512]{2,1,0:T(2,128)} custom-call(s32[4]{0:T(128)S(1)} %pad_add_fusion.scal, bf16[4,48,1024]{2,1,0:T(8,128)(2,1)S(1)} %collective-permute-done.36.refs_0_, bf16[2,48,1024]{2,1,0:T(8,128)(2,1)S(1)} %pad_maximum_fusion.1.refs_1_, f32[768,2,512]{2,1,0:T(2,128)} %shard_map.117.refs_2_), custom_call_target="tpu_custom_call", output_to_operand_aliasing={{}: (3, {})} | custom-call | tf_op jit(solution)/shard_map/pallas_call | solution.py:30
  94.6 1.6 %shard_map.119 = f32[768,2,512]{2,1,0:T(2,128)} custom-call(s32[4]{0:T(128)S(1)} %pad_add_fusion.scal, bf16[2,48,1024]{2,1,0:T(8,128)(2,1)S(1)} %collective-permute-done.33.refs_0_, bf16[2,48,1024]{2,1,0:T(8,128)(2,1)S(1)} %collective-permute-done.34.refs_1_, ...), custom_call_target="tpu_custom_call", output_to_operand_aliasing={{}: (4, {})} | custom-call | tf_op jit(solution)/shard_map/pallas_call | solution.py:30
  (73 shorter events, 23.8 us)
Async XLA Ops:
  2.7 5.8 %collective-permute-start = (bf16[16,384]{1,0:T(8,128)(2,1)S(1)}, bf16[16,384]{1,0:T(8,128)(2,1)S(1)}, u32[]{:S(2)}, u32[]{:S(2)}) collective-permute-start(bf16[16,384]{1,0:T(8,128)(2,1)S(1)} %shard_map.103.small), channel_id=1, source_target_pairs={{0,8},{2,10},{4,12},{6,14},{8,0},{10,2},{12,4},{14,6},{16,24},{18,... | collective-permute-start | bytes 36872 | tf_op jit(solution)/shard_map/ppermute | solution.py:449
  12.1 3.6 %collective-permute-start.5 = (f32[128,512]{1,0:T(8,128)S(1)}, f32[128,512]{1,0:T(8,128)S(1)}, u32[]{:S(2)}, u32[]{:S(2)}) collective-permute-start(f32[128,512]{1,0:T(8,128)S(1)} %get-tuple-element.75), channel_id=1, source_target_pairs={{0,1},{1,0},{2,3},{3,2},{4,5},{5,4},{6,7},{7,6},{8,9},{9,8},{10,11... | collective-permute-start | bytes 786440 | tf_op jit(solution)/shard_map/ppermute | solution.py:487
  12.2 7.6 %collective-permute-start.2 = (bf16[128,384]{1,0:T(8,128)(2,1)S(1)}, bf16[128,384]{1,0:T(8,128)(2,1)S(1)}, u32[]{:S(2)}, u32[]{:S(2)}) collective-permute-start(bf16[128,384]{1,0:T(8,128)(2,1)S(1)} %get-tuple-element.70), channel_id=1, source_target_pairs={{0,2},{2,0},{4,6},{6,4},{8,10},{10,8},{12,14},{14,12},{16,18},{18,... | collective-permute-start | bytes 294920 | tf_op jit(solution)/shard_map/ppermute | solution.py:442
  13.8 6.6 %collective-permute-start.3 = (bf16[128,384]{1,0:T(8,128)(2,1)S(1)}, bf16[128,384]{1,0:T(8,128)(2,1)S(1)}, u32[]{:S(2)}, u32[]{:S(2)}) collective-permute-start(bf16[128,384]{1,0:T(8,128)(2,1)S(1)} %get-tuple-element.71), channel_id=1, source_target_pairs={{0,4},{2,6},{4,0},{6,2},{8,12},{10,14},{12,8},{14,10},{16,20},{18,... | collective-permute-start | bytes 294920 | tf_op jit(solution)/shard_map/ppermute | solution.py:442
  15.3 6.4 %collective-permute-start.4 = (bf16[128,384]{1,0:T(8,128)(2,1)S(1)}, bf16[128,384]{1,0:T(8,128)(2,1)S(1)}, u32[]{:S(2)}, u32[]{:S(2)}) collective-permute-start(bf16[128,384]{1,0:T(8,128)(2,1)S(1)} %get-tuple-element.72), channel_id=1, source_target_pairs={{0,6},{2,4},{4,2},{6,0},{8,14},{10,12},{12,10},{14,8},{16,22},{18,... | collective-permute-start | bytes 294920 | tf_op jit(solution)/shard_map/ppermute | solution.py:442
  16.7 5.6 %collective-permute-start.6 = (bf16[272,128]{1,0:T(8,128)(2,1)S(1)}, bf16[272,128]{1,0:T(8,128)(2,1)S(1)}, u32[]{:S(2)}, u32[]{:S(2)}) collective-permute-start(bf16[272,128]{1,0:T(8,128)(2,1)S(1)} %get-tuple-element.80), channel_id=1, source_target_pairs={{0,2},{2,0},{4,6},{6,4},{8,10},{10,8},{12,14},{14,12},{16,18},{18,... | collective-permute-start | bytes 208904 | tf_op jit(solution)/shard_map/ppermute | solution.py:442
  18.3 5.1 %collective-permute-start.7 = (bf16[272,128]{1,0:T(8,128)(2,1)S(1)}, bf16[272,128]{1,0:T(8,128)(2,1)S(1)}, u32[]{:S(2)}, u32[]{:S(2)}) collective-permute-start(bf16[272,128]{1,0:T(8,128)(2,1)S(1)} %get-tuple-element.81), channel_id=1, source_target_pairs={{0,4},{2,6},{4,0},{6,2},{8,12},{10,14},{12,8},{14,10},{16,20},{18,... | collective-permute-start | bytes 208904 | tf_op jit(solution)/shard_map/ppermute | solution.py:442
  19.8 5.2 %collective-permute-start.8 = (bf16[272,128]{1,0:T(8,128)(2,1)S(1)}, bf16[272,128]{1,0:T(8,128)(2,1)S(1)}, u32[]{:S(2)}, u32[]{:S(2)}) collective-permute-start(bf16[272,128]{1,0:T(8,128)(2,1)S(1)} %get-tuple-element.82), channel_id=1, source_target_pairs={{0,6},{2,4},{4,2},{6,0},{8,14},{10,12},{12,10},{14,8},{16,22},{18,... | collective-permute-start | bytes 208904 | tf_op jit(solution)/shard_map/ppermute | solution.py:442
  25.6 13.0 %collective-permute-start.10 = (bf16[4,128,512]{2,1,0:T(8,128)(2,1)S(1)}, bf16[4,128,512]{2,1,0:T(8,128)(2,1)S(1)}, u32[]{:S(2)}, u32[]{:S(2)}) collective-permute-start(bf16[4,128,512]{2,1,0:T(8,128)(2,1)S(1)} %get-tuple-element.83.own), channel_id=1, source_target_pairs={{8,16},{10,18},{12,20},{14,22},{16,8},{18,10},{20,12},{22,14},{9,1... | collective-permute-start | bytes 1572872 | tf_op jit(solution)/shard_map/ppermute | solution.py:449
  26.4 17.0 %collective-permute-start.9 = (bf16[4,128,512]{2,1,0:T(8,128)(2,1)S(1)}, bf16[4,128,512]{2,1,0:T(8,128)(2,1)S(1)}, u32[]{:S(2)}, u32[]{:S(2)}) collective-permute-start(bf16[4,128,512]{2,1,0:T(8,128)(2,1)S(1)} %get-tuple-element.83.own), channel_id=1, source_target_pairs={{0,8},{2,10},{4,12},{6,14},{8,0},{10,2},{12,4},{14,6},{16,24},{18,... | collective-permute-start | bytes 1572872 | tf_op jit(solution)/shard_map/ppermute | solution.py:449
  37.9 6.7 %collective-permute-start.11 = (bf16[128,1280]{1,0:T(8,128)(2,1)S(1)}, bf16[128,1280]{1,0:T(8,128)(2,1)S(1)}, u32[]{:S(2)}, u32[]{:S(2)}) collective-permute-start(bf16[128,1280]{1,0:T(8,128)(2,1)S(1)} %get-tuple-element.87.refs_0_), channel_id=1, source_target_pairs={{0,1},{1,0},{2,3},{3,2},{4,5},{5,4},{6,7},{7,6},{8,9},{9,8},{10,11... | collective-permute-start | bytes 983048 | tf_op jit(solution)/shard_map/ppermute | solution.py:532
  38.1 6.5 %collective-permute-start.12 = (bf16[128,1280]{1,0:T(8,128)(2,1)S(1)}, bf16[128,1280]{1,0:T(8,128)(2,1)S(1)}, u32[]{:S(2)}, u32[]{:S(2)}) collective-permute-start(bf16[128,1280]{1,0:T(8,128)(2,1)S(1)} %get-tuple-element.88.refs_1_), channel_id=1, source_target_pairs={{0,1},{1,0},{2,3},{3,2},{4,5},{5,4},{6,7},{7,6},{8,9},{9,8},{10,11... | collective-permute-start | bytes 983048 | tf_op jit(solution)/shard_map/ppermute | solution.py:532
  38.4 6.1 %collective-permute-start.13 = (bf16[128,1280]{1,0:T(8,128)(2,1)S(1)}, bf16[128,1280]{1,0:T(8,128)(2,1)S(1)}, u32[]{:S(2)}, u32[]{:S(2)}) collective-permute-start(bf16[128,1280]{1,0:T(8,128)(2,1)S(1)} %get-tuple-element.89.refs_2_), channel_id=1, source_target_pairs={{0,1},{1,0},{2,3},{3,2},{4,5},{5,4},{6,7},{7,6},{8,9},{9,8},{10,11... | collective-permute-start | bytes 983048 | tf_op jit(solution)/shard_map/ppermute | solution.py:532
  38.6 6.0 %collective-permute-start.14 = (bf16[128,1280]{1,0:T(8,128)(2,1)S(1)}, bf16[128,1280]{1,0:T(8,128)(2,1)S(1)}, u32[]{:S(2)}, u32[]{:S(2)}) collective-permute-start(bf16[128,1280]{1,0:T(8,128)(2,1)S(1)} %get-tuple-element.90.refs_3_), channel_id=1, source_target_pairs={{0,1},{1,0},{2,3},{3,2},{4,5},{5,4},{6,7},{7,6},{8,9},{9,8},{10,11... | collective-permute-start | bytes 983048 | tf_op jit(solution)/shard_map/ppermute | solution.py:532
  47.0 7.6 %collective-permute-start.15 = (bf16[4,128,128]{2,1,0:T(8,128)(2,1)S(1)}, bf16[4,128,128]{2,1,0:T(8,128)(2,1)S(1)}, u32[]{:S(2)}, u32[]{:S(2)}) collective-permute-start(bf16[4,128,128]{2,1,0:T(8,128)(2,1)S(1)} %shard_map.111.refs_0_), channel_id=1, source_target_pairs={{0,2},{2,0},{4,6},{6,4},{8,10},{10,8},{12,14},{14,12},{16,18},{18,... | collective-permute-start | bytes 393224 | tf_op jit(solution)/shard_map/ppermute | solution.py:442
  48.1 6.5 %collective-permute-start.16 = (bf16[4,128,128]{2,1,0:T(8,128)(2,1)S(1)}, bf16[4,128,128]{2,1,0:T(8,128)(2,1)S(1)}, u32[]{:S(2)}, u32[]{:S(2)}) collective-permute-start(bf16[4,128,128]{2,1,0:T(8,128)(2,1)S(1)} %shard_map.111.refs_0_), channel_id=1, source_target_pairs={{0,4},{2,6},{4,0},{6,2},{8,12},{10,14},{12,8},{14,10},{16,20},{18,... | collective-permute-start | bytes 393224 | tf_op jit(solution)/shard_map/ppermute | solution.py:442
  48.8 5.9 %collective-permute-start.17 = (bf16[4,128,128]{2,1,0:T(8,128)(2,1)S(1)}, bf16[4,128,128]{2,1,0:T(8,128)(2,1)S(1)}, u32[]{:S(2)}, u32[]{:S(2)}) collective-permute-start(bf16[4,128,128]{2,1,0:T(8,128)(2,1)S(1)} %shard_map.111.refs_0_), channel_id=1, source_target_pairs={{0,6},{2,4},{4,2},{6,0},{8,14},{10,12},{12,10},{14,8},{16,22},{18,... | collective-permute-start | bytes 393224 | tf_op jit(solution)/shard_map/ppermute | solution.py:442
  58.8 5.9 %collective-permute-start.22 = (bf16[48,1024]{1,0:T(8,128)(2,1)S(1)}, bf16[48,1024]{1,0:T(8,128)(2,1)S(1)}, u32[]{:S(2)}, u32[]{:S(2)}) collective-permute-start(bf16[48,1024]{1,0:T(8,128)(2,1)S(1)} %get-tuple-element.102), channel_id=1, source_target_pairs={{0,8},{2,10},{4,12},{6,14},{8,0},{10,2},{12,4},{14,6},{16,24},{18,... | collective-permute-start | bytes 294920 | tf_op jit(solution)/shard_map/ppermute | solution.py:590
  61.3 10.8 %collective-permute-start.23 = (bf16[48,1024]{1,0:T(8,128)(2,1)S(1)}, bf16[48,1024]{1,0:T(8,128)(2,1)S(1)}, u32[]{:S(2)}, u32[]{:S(2)}) collective-permute-start(bf16[48,1024]{1,0:T(8,128)(2,1)S(1)} %get-tuple-element.108), channel_id=1, source_target_pairs={{0,16},{2,18},{4,20},{6,22},{8,24},{10,26},{12,28},{14,30},{16,0},... | collective-permute-start | bytes 294920 | tf_op jit(solution)/shard_map/ppermute | solution.py:590
  62.2 9.9 %collective-permute-start.24 = (bf16[48,1024]{1,0:T(8,128)(2,1)S(1)}, bf16[48,1024]{1,0:T(8,128)(2,1)S(1)}, u32[]{:S(2)}, u32[]{:S(2)}) collective-permute-start(bf16[48,1024]{1,0:T(8,128)(2,1)S(1)} %get-tuple-element.109), channel_id=1, source_target_pairs={{0,24},{2,26},{4,28},{6,30},{8,16},{10,18},{12,20},{14,22},{16,8},... | collective-permute-start | bytes 294920 | tf_op jit(solution)/shard_map/ppermute | solution.py:590
  64.6 7.5 %collective-permute-start.25 = (bf16[128,384]{1,0:T(8,128)(2,1)S(1)}, bf16[128,384]{1,0:T(8,128)(2,1)S(1)}, u32[]{:S(2)}, u32[]{:S(2)}) collective-permute-start(bf16[128,384]{1,0:T(8,128)(2,1)S(1)} %get-tuple-element.111), channel_id=1, source_target_pairs={{0,2},{2,0},{4,6},{6,4},{8,10},{10,8},{12,14},{14,12},{16,18},{18,... | collective-permute-start | bytes 294920 | tf_op jit(solution)/shard_map/ppermute | solution.py:442
  65.7 6.7 %collective-permute-start.26 = (bf16[128,384]{1,0:T(8,128)(2,1)S(1)}, bf16[128,384]{1,0:T(8,128)(2,1)S(1)}, u32[]{:S(2)}, u32[]{:S(2)}) collective-permute-start(bf16[128,384]{1,0:T(8,128)(2,1)S(1)} %get-tuple-element.112), channel_id=1, source_target_pairs={{0,4},{2,6},{4,0},{6,2},{8,12},{10,14},{12,8},{14,10},{16,20},{18,... | collective-permute-start | bytes 294920 | tf_op jit(solution)/shard_map/ppermute | solution.py:442
  66.8 5.7 %collective-permute-start.27 = (bf16[128,384]{1,0:T(8,128)(2,1)S(1)}, bf16[128,384]{1,0:T(8,128)(2,1)S(1)}, u32[]{:S(2)}, u32[]{:S(2)}) collective-permute-start(bf16[128,384]{1,0:T(8,128)(2,1)S(1)} %get-tuple-element.113), channel_id=1, source_target_pairs={{0,6},{2,4},{4,2},{6,0},{8,14},{10,12},{12,10},{14,8},{16,22},{18,... | collective-permute-start | bytes 294920 | tf_op jit(solution)/shard_map/ppermute | solution.py:442
  72.5 7.2 %collective-permute-start.31 = (bf16[48,1024]{1,0:T(8,128)(2,1)S(1)}, bf16[48,1024]{1,0:T(8,128)(2,1)S(1)}, u32[]{:S(2)}, u32[]{:S(2)}) collective-permute-start(bf16[48,1024]{1,0:T(8,128)(2,1)S(1)} %shard_map.114), channel_id=1, source_target_pairs={{0,16},{2,18},{4,20},{6,22},{8,24},{10,26},{12,28},{14,30},{16,0},... | collective-permute-start | bytes 294920 | tf_op jit(solution)/shard_map/ppermute | solution.py:599
  75.2 5.3 %collective-permute-start.28 = (bf16[1,48,1024]{2,1,0:T(8,128)(2,1)S(1)}, bf16[1,48,1024]{2,1,0:T(8,128)(2,1)S(1)}, u32[]{:S(2)}, u32[]{:S(2)}) collective-permute-start(bf16[1,48,1024]{2,1,0:T(8,128)(2,1)S(1)} %shard_map.115.refs_0_), channel_id=1, source_target_pairs={{0,2},{2,0},{4,6},{6,4},{8,10},{10,8},{12,14},{14,12},{16,18},{18,... | collective-permute-start | bytes 294920 | tf_op jit(solution)/shard_map/ppermute | solution.py:442
  76.1 4.8 %collective-permute-start.29 = (bf16[1,48,1024]{2,1,0:T(8,128)(2,1)S(1)}, bf16[1,48,1024]{2,1,0:T(8,128)(2,1)S(1)}, u32[]{:S(2)}, u32[]{:S(2)}) collective-permute-start(bf16[1,48,1024]{2,1,0:T(8,128)(2,1)S(1)} %shard_map.115.refs_0_), channel_id=1, source_target_pairs={{0,4},{2,6},{4,0},{6,2},{8,12},{10,14},{12,8},{14,10},{16,20},{18,... | collective-permute-start | bytes 294920 | tf_op jit(solution)/shard_map/ppermute | solution.py:442
  77.5 5.5 %collective-permute-start.30 = (bf16[1,48,1024]{2,1,0:T(8,128)(2,1)S(1)}, bf16[1,48,1024]{2,1,0:T(8,128)(2,1)S(1)}, u32[]{:S(2)}, u32[]{:S(2)}) collective-permute-start(bf16[1,48,1024]{2,1,0:T(8,128)(2,1)S(1)} %shard_map.115.refs_0_), channel_id=1, source_target_pairs={{0,6},{2,4},{4,2},{6,0},{8,14},{10,12},{12,10},{14,8},{16,22},{18,... | collective-permute-start | bytes 294920 | tf_op jit(solution)/shard_map/ppermute | solution.py:442
  79.7 5.3 %collective-permute-start.32 = (bf16[48,1024]{1,0:T(8,128)(2,1)S(1)}, bf16[48,1024]{1,0:T(8,128)(2,1)S(1)}, u32[]{:S(2)}, u32[]{:S(2)}) collective-permute-start(bf16[48,1024]{1,0:T(8,128)(2,1)S(1)} %collective-permute-done.31), channel_id=1, source_target_pairs={{0,8},{2,10},{4,12},{6,14},{8,0},{10,2},{12,4},{14,6},{16,24},{18,... | collective-permute-start | bytes 294920 | tf_op jit(solution)/shard_map/ppermute | solution.py:600
  85.1 7.8 %collective-permute-start.36 = (bf16[4,48,1024]{2,1,0:T(8,128)(2,1)S(1)}, bf16[4,48,1024]{2,1,0:T(8,128)(2,1)S(1)}, u32[]{:S(2)}, u32[]{:S(2)}) collective-permute-start(bf16[4,48,1024]{2,1,0:T(8,128)(2,1)S(1)} %pad_maximum_fusion), channel_id=1, source_target_pairs={{0,8},{2,10},{4,12},{6,14},{8,0},{10,2},{12,4},{14,6},{16,24},{18,... | collective-permute-start | bytes 1179656 | tf_op jit(solution)/shard_map/ppermute | solution.py:637
  85.8 8.8 %collective-permute-start.33 = (bf16[2,48,1024]{2,1,0:T(8,128)(2,1)S(1)}, bf16[2,48,1024]{2,1,0:T(8,128)(2,1)S(1)}, u32[]{:S(2)}, u32[]{:S(2)}) collective-permute-start(bf16[2,48,1024]{2,1,0:T(8,128)(2,1)S(1)} %pad_maximum_fusion.1.refs_1_), channel_id=1, source_target_pairs={{0,2},{2,0},{4,6},{6,4},{8,10},{10,8},{12,14},{14,12},{16,18},{18,... | collective-permute-start | bytes 589832 | tf_op jit(solution)/shard_map/ppermute | solution.py:442
  86.7 7.8 %collective-permute-start.34 = (bf16[2,48,1024]{2,1,0:T(8,128)(2,1)S(1)}, bf16[2,48,1024]{2,1,0:T(8,128)(2,1)S(1)}, u32[]{:S(2)}, u32[]{:S(2)}) collective-permute-start(bf16[2,48,1024]{2,1,0:T(8,128)(2,1)S(1)} %pad_maximum_fusion.1.refs_1_), channel_id=1, source_target_pairs={{0,4},{2,6},{4,0},{6,2},{8,12},{10,14},{12,8},{14,10},{16,20},{18,... | collective-permute-start | bytes 589832 | tf_op jit(solution)/shard_map/ppermute | solution.py:442
  87.6 6.9 %collective-permute-start.35 = (bf16[2,48,1024]{2,1,0:T(8,128)(2,1)S(1)}, bf16[2,48,1024]{2,1,0:T(8,128)(2,1)S(1)}, u32[]{:S(2)}, u32[]{:S(2)}) collective-permute-start(bf16[2,48,1024]{2,1,0:T(8,128)(2,1)S(1)} %pad_maximum_fusion.1.refs_1_), channel_id=1, source_target_pairs={{0,6},{2,4},{4,2},{6,0},{8,14},{10,12},{12,10},{14,8},{16,22},{18,... | collective-permute-start | bytes 589832 | tf_op jit(solution)/shard_map/ppermute | solution.py:442
  (7 other events, 24.6 us)

commit v7 on v6

--- a/solution.py
+++ b/solution.py
@@ -630,9 +630,8 @@
     intersection = write(near_pieces, [(k, 0, k, 0) for k in everywhere])
     if direct:
         far = jnp.stack(stack[2:])
-        twin_pieces, far, filtered, rotated = lax.optimization_barrier(
-            (jnp.concatenate(near_pieces), far, filtered, rotated)
-        )
+        twin_pieces = jnp.concatenate(near_pieces)
+        _, far, filtered, rotated = lax.optimization_barrier((twin_pieces, far, filtered, rotated))
         far_pieces = swap([far] * GROUP)
         twin_pieces = lax.ppermute(twin_pieces, "elem", twins)
         plan = [(0, k, k, 1) for k in everywhere] + [(1, j - 2, 0, j) for j in range(2, split)]

time: 96.7 us -> 95.7 us (0.990)
  waiting for transfers between devices: 19.8 us -> 17.8 us
    ppermute x1, waiting for transfers between devices: 1.99 us -> 0.2 us  [on_device(): stack.append(lax.ppermute(stack[2], 'elem', twins))]
  transfers between devices with their start and end apart: 37 -> 37, of which waited for: 16 -> 17; matrix products, arithmetic and copies ran while one was open for 3% -> 3% of each run, Pallas kernels for 16% -> 17%
where the time goes in v7:
time: 95.7 us; the launch traced here: 95.4 us
  starting transfers between devices  44.5 us (46%)
  Pallas kernels  24.3 us (25%)
  waiting for transfers between devices  17.8 us (19%)
  local copies, waits for them, and re-layouts  6.1 us (6%)
  between operations  1.8 us (2%)
    pallas_call x17, Pallas kernels, call(): pl.pallas_call(body, out_shape=out_shape, in_specs=specs, out_specs=out_s...  24.3 us
    ppermute x18, starting transfers between devices, swap(): lax.ppermute(values[k], 'elem', in_group(k))  21.3 us
    ppermute x2, starting transfers between devices, neighbours(): lax.ppermute(value, 'elem', twins)  10.3 us
    ppermute x18, waiting for transfers between devices, swap(): lax.ppermute(values[k], 'elem', in_group(k))  7.31 us
    ppermute x3, starting transfers between devices, across(): lax.ppermute(values[j], 'elem', [(i, i ^ GROUP * j) for i in range(blocks)])  5.02 us
    ppermute x3, waiting for transfers between devices, across(): lax.ppermute(values[j], 'elem', [(i, i ^ GROUP * j) for i in range(blocks)])  4.84 us
    ppermute x2, waiting for transfers between devices, neighbours(): lax.ppermute(value, 'elem', twins)  3.91 us
    ppermute x1, starting transfers between devices, on_device(): lax.ppermute(own, 'elem', [(i, i ^ 2 * GROUP) for i in range(blocks)])  2.71 us
  transfers between devices with their start and end apart: 37, of which 17 were waited for; matrix products, arithmetic and copies ran while one was open for 3% of the time, Pallas kernels for 17%

profile of v7, /device:TPU:0, one launch (start us, length us, event | category | flops | bytes accessed | tf_op | source)
XLA Modules:
  0.0 95.4 jit_solution(7814035914074336385)
XLA Ops:
  2.7 3.1 %collective-permute-start = (bf16[16,384]{1,0:T(8,128)(2,1)S(1)}, bf16[16,384]{1,0:T(8,128)(2,1)S(1)}, u32[]{:S(2)}, u32[]{:S(2)}) collective-permute-start(bf16[16,384]{1,0:T(8,128)(2,1)S(1)} %shard_map.103.small), channel_id=1, source_target_pairs={{0,8},{2,10},{4,12},{6,14},{8,0},{10,2},{12,4},{14,6},{16,24},{18,... | collective-permute-start | bytes 36872 | tf_op jit(solution)/shard_map/ppermute | solution.py:449
  8.6 2.4 %copy.19 = bf16[1536,2,512]{2,0,1:T(8,128)(2,1)S(1)} copy(bf16[1536,2,512]{2,1,0:T(2,128)(2,1)} %param.15) | data formatting | bytes 6291456 | tf_op jit(solution)/shard_map/optimization_barrier | solution.py:471
  11.0 1.2 %shard_map.106 = (f32[128,512]{1,0:T(8,128)S(1)}, f32[128,512]{1,0:T(8,128)S(1)}) custom-call(s32[4]{0:T(128)S(1)} %pad_add_fusion.scal, bf16[2,128,768]{2,1,0:T(8,128)(2,1)S(1)} %bitcast.18, bf16[2,1536,512]{2,1,0:T(8,128)(2,1)S(1)} %bitcast.16), custom_call_target="tpu_custom_call" | custom-call | flops 4000000000 | bytes 15625000 | tf_op jit(solution)/shard_map/pallas_call | solution.py:30
  12.2 1.6 %collective-permute-start.2 = (bf16[128,384]{1,0:T(8,128)(2,1)S(1)}, bf16[128,384]{1,0:T(8,128)(2,1)S(1)}, u32[]{:S(2)}, u32[]{:S(2)}) collective-permute-start(bf16[128,384]{1,0:T(8,128)(2,1)S(1)} %get-tuple-element.69), channel_id=1, source_target_pairs={{0,2},{2,0},{4,6},{6,4},{8,10},{10,8},{12,14},{14,12},{16,18},{18,... | collective-permute-start | bytes 294920 | tf_op jit(solution)/shard_map/ppermute | solution.py:442
  13.8 1.5 %collective-permute-start.3 = (bf16[128,384]{1,0:T(8,128)(2,1)S(1)}, bf16[128,384]{1,0:T(8,128)(2,1)S(1)}, u32[]{:S(2)}, u32[]{:S(2)}) collective-permute-start(bf16[128,384]{1,0:T(8,128)(2,1)S(1)} %get-tuple-element.70), channel_id=1, source_target_pairs={{0,4},{2,6},{4,0},{6,2},{8,12},{10,14},{12,8},{14,10},{16,20},{18,... | collective-permute-start | bytes 294920 | tf_op jit(solution)/shard_map/ppermute | solution.py:442
  16.7 1.6 %collective-permute-start.6 = (bf16[272,128]{1,0:T(8,128)(2,1)S(1)}, bf16[272,128]{1,0:T(8,128)(2,1)S(1)}, u32[]{:S(2)}, u32[]{:S(2)}) collective-permute-start(bf16[272,128]{1,0:T(8,128)(2,1)S(1)} %get-tuple-element.79), channel_id=1, source_target_pairs={{0,2},{2,0},{4,6},{6,4},{8,10},{10,8},{12,14},{14,12},{16,18},{18,... | collective-permute-start | bytes 208904 | tf_op jit(solution)/shard_map/ppermute | solution.py:442
  18.3 1.5 %collective-permute-start.7 = (bf16[272,128]{1,0:T(8,128)(2,1)S(1)}, bf16[272,128]{1,0:T(8,128)(2,1)S(1)}, u32[]{:S(2)}, u32[]{:S(2)}) collective-permute-start(bf16[272,128]{1,0:T(8,128)(2,1)S(1)} %get-tuple-element.80), channel_id=1, source_target_pairs={{0,4},{2,6},{4,0},{6,2},{8,12},{10,14},{12,8},{14,10},{16,20},{18,... | collective-permute-start | bytes 208904 | tf_op jit(solution)/shard_map/ppermute | solution.py:442
  20.3 1.3 %collective-permute-done.4.a3 = bf16[128,384]{1,0:T(8,128)(2,1)S(1)} collective-permute-done((bf16[128,384]{1,0:T(8,128)(2,1)S(1)}, bf16[128,384]{1,0:T(8,128)(2,1)S(1)}, u32[]{:S(2)}, u32[]{:S(2)}) %collective-permute-start.4) | collective-permute-done | bytes 98336 | tf_op jit(solution)/shard_map/ppermute | solution.py:442
  23.3 1.7 %collective-permute-done.8.a3 = bf16[272,128]{1,0:T(8,128)(2,1)S(1)} collective-permute-done((bf16[272,128]{1,0:T(8,128)(2,1)S(1)}, bf16[272,128]{1,0:T(8,128)(2,1)S(1)}, u32[]{:S(2)}, u32[]{:S(2)}) %collective-permute-start.8) | collective-permute-done | bytes 69664 | tf_op jit(solution)/shard_map/ppermute | solution.py:442
  26.4 7.2 %collective-permute-start.9 = (bf16[4,128,512]{2,1,0:T(8,128)(2,1)S(1)}, bf16[4,128,512]{2,1,0:T(8,128)(2,1)S(1)}, u32[]{:S(2)}, u32[]{:S(2)}) collective-permute-start(bf16[4,128,512]{2,1,0:T(8,128)(2,1)S(1)} %get-tuple-element.82.own), channel_id=1, source_target_pairs={{0,8},{2,10},{4,12},{6,14},{8,0},{10,2},{12,4},{14,6},{16,24},{18,... | collective-permute-start | bytes 1572872 | tf_op jit(solution)/shard_map/ppermute | solution.py:449
  33.6 4.8 %shard_map.110 = (bf16[128,1280]{1,0:T(8,128)(2,1)S(1)}, bf16[128,1280]{1,0:T(8,128)(2,1)S(1)}, bf16[128,1280]{1,0:T(8,128)(2,1)S(1)}, bf16[128,1280]{1,0:T(8,128)(2,1)S(1)}) custom-call(s32[4]{0:T(128)S(1)} %pad_add_fusion.scal, s32[1]{0:T(128)} %bitcast.2.side_s, bf16[4,144,128]{2,1,0:T(8,128)(2,1)S(1)} %get-tuple-element.83.small, ...), custom_call_target="tpu_custom_call" | custom-call | flops 2717908992 | bytes 2621440 | tf_op jit(solution)/shard_map/pallas_call | solution.py:30
  39.5 3.9 %collective-permute-done.9.twin = bf16[4,128,512]{2,1,0:T(8,128)(2,1)S(1)} collective-permute-done((bf16[4,128,512]{2,1,0:T(8,128)(2,1)S(1)}, bf16[4,128,512]{2,1,0:T(8,128)(2,1)S(1)}, u32[]{:S(2)}, u32[]{:S(2)}) %collective-permute-start.9) | collective-permute-done | bytes 524320 | tf_op jit(solution)/shard_map/ppermute | solution.py:449
  44.6 2.4 %shard_map.111.refs_0_ = bf16[4,128,128]{2,1,0:T(8,128)(2,1)S(1)} custom-call(s32[4]{0:T(128)S(1)} %pad_add_fusion.scal, s32[1]{0:T(128)} %bitcast.2.side_s, bf16[1536,512]{1,0:T(8,128)(2,1)S(1)} %get-tuple-element.84.vec, f32[8,128,128]{2,1,0:T(8,128)S(1)} %get-tuple-element.85.cols, bf16[128,1280]{1,0:T(8,128)(2,1)S(1)} %get-tuple-element.86.refs_0_, ...), custom_call_target="tpu_custom_call" | custom-call | flops 503316480 | bytes 2621440 | tf_op jit(solution)/shard_map/pallas_call | solution.py:30
  47.0 1.2 %collective-permute-start.15 = (bf16[4,128,128]{2,1,0:T(8,128)(2,1)S(1)}, bf16[4,128,128]{2,1,0:T(8,128)(2,1)S(1)}, u32[]{:S(2)}, u32[]{:S(2)}) collective-permute-start(bf16[4,128,128]{2,1,0:T(8,128)(2,1)S(1)} %shard_map.111.refs_0_), channel_id=1, source_target_pairs={{0,2},{2,0},{4,6},{6,4},{8,10},{10,8},{12,14},{14,12},{16,18},{18,... | collective-permute-start | bytes 393224 | tf_op jit(solution)/shard_map/ppermute | solution.py:442
  48.8 1.8 %collective-permute-start.17 = (bf16[4,128,128]{2,1,0:T(8,128)(2,1)S(1)}, bf16[4,128,128]{2,1,0:T(8,128)(2,1)S(1)}, u32[]{:S(2)}, u32[]{:S(2)}) collective-permute-start(bf16[4,128,128]{2,1,0:T(8,128)(2,1)S(1)} %shard_map.111.refs_0_), channel_id=1, source_target_pairs={{0,6},{2,4},{4,2},{6,0},{8,14},{10,12},{12,10},{14,8},{16,22},{18,... | collective-permute-start | bytes 393224 | tf_op jit(solution)/shard_map/ppermute | solution.py:442
  50.5 4.1 %shard_map.112 = (bf16[128,384]{1,0:T(8,128)(2,1)S(1)}, bf16[128,384]{1,0:T(8,128)(2,1)S(1)}, bf16[128,384]{1,0:T(8,128)(2,1)S(1)}, bf16[128,384]{1,0:T(8,128)(2,1)S(1)}, bf16[384,512]{1,0:T(8,128)(2,1)S(1)}) custom-call(s32[4]{0:T(128)S(1)} %pad_add_fusion.scal, s32[1]{0:T(128)} %bitcast.2.side_s, bf16[1536,512]{1,0:T(8,128)(2,1)S(1)} %get-tuple-element.84.vec, ...), custom_call_target="tpu_custom_call" | custom-call | flops 1509949440 | bytes 2621440 | tf_op jit(solution)/shard_map/pallas_call | solution.py:30
  56.8 2.0 %shard_map.113 = (bf16[48,1024]{1,0:T(8,128)(2,1)S(1)}, bf16[48,1024]{1,0:T(8,128)(2,1)S(1)}, bf16[48,1024]{1,0:T(8,128)(2,1)S(1)}, bf16[48,1024]{1,0:T(8,128)(2,1)S(1)}, bf16[2,128,256]{2,1,0:T(8,128)(2,1)S(1)}) custom-call(s32[4]{0:T(128)S(1)} %pad_add_fusion.scal, bf16[384,512]{1,0:T(8,128)(2,1)S(1)} %get-tuple-element.95.left, ...), custom_call_target="tpu_custom_call" | custom-call | flops 402653184 | bytes 1048576 | tf_op jit(solution)/shard_map/pallas_call | solution.py:30
  58.8 2.6 %collective-permute-start.22 = (bf16[48,1024]{1,0:T(8,128)(2,1)S(1)}, bf16[48,1024]{1,0:T(8,128)(2,1)S(1)}, u32[]{:S(2)}, u32[]{:S(2)}) collective-permute-start(bf16[48,1024]{1,0:T(8,128)(2,1)S(1)} %get-tuple-element.101), channel_id=1, source_target_pairs={{0,8},{2,10},{4,12},{6,14},{8,0},{10,2},{12,4},{14,6},{16,24},{18,... | collective-permute-start | bytes 294920 | tf_op jit(solution)/shard_map/ppermute | solution.py:590
  62.2 1.6 %collective-permute-start.24 = (bf16[48,1024]{1,0:T(8,128)(2,1)S(1)}, bf16[48,1024]{1,0:T(8,128)(2,1)S(1)}, u32[]{:S(2)}, u32[]{:S(2)}) collective-permute-start(bf16[48,1024]{1,0:T(8,128)(2,1)S(1)} %get-tuple-element.108), channel_id=1, source_target_pairs={{0,24},{2,26},{4,28},{6,30},{8,16},{10,18},{12,20},{14,22},{16,8},... | collective-permute-start | bytes 294920 | tf_op jit(solution)/shard_map/ppermute | solution.py:590
  64.6 1.1 %collective-permute-start.25 = (bf16[128,384]{1,0:T(8,128)(2,1)S(1)}, bf16[128,384]{1,0:T(8,128)(2,1)S(1)}, u32[]{:S(2)}, u32[]{:S(2)}) collective-permute-start(bf16[128,384]{1,0:T(8,128)(2,1)S(1)} %get-tuple-element.110), channel_id=1, source_target_pairs={{0,2},{2,0},{4,6},{6,4},{8,10},{10,8},{12,14},{14,12},{16,18},{18,... | collective-permute-start | bytes 294920 | tf_op jit(solution)/shard_map/ppermute | solution.py:442
  66.8 1.3 %collective-permute-start.27 = (bf16[128,384]{1,0:T(8,128)(2,1)S(1)}, bf16[128,384]{1,0:T(8,128)(2,1)S(1)}, u32[]{:S(2)}, u32[]{:S(2)}) collective-permute-start(bf16[128,384]{1,0:T(8,128)(2,1)S(1)} %get-tuple-element.112), channel_id=1, source_target_pairs={{0,6},{2,4},{4,2},{6,0},{8,14},{10,12},{12,10},{14,8},{16,22},{18,... | collective-permute-start | bytes 294920 | tf_op jit(solution)/shard_map/ppermute | solution.py:442
  68.1 4.0 %collective-permute-done.23.s2 = bf16[48,1024]{1,0:T(8,128)(2,1)S(1)} collective-permute-done((bf16[48,1024]{1,0:T(8,128)(2,1)S(1)}, bf16[48,1024]{1,0:T(8,128)(2,1)S(1)}, u32[]{:S(2)}, u32[]{:S(2)}) %collective-permute-start.23) | collective-permute-done | bytes 98336 | tf_op jit(solution)/shard_map/ppermute | solution.py:590
  72.5 2.7 %collective-permute-start.31 = (bf16[48,1024]{1,0:T(8,128)(2,1)S(1)}, bf16[48,1024]{1,0:T(8,128)(2,1)S(1)}, u32[]{:S(2)}, u32[]{:S(2)}) collective-permute-start(bf16[48,1024]{1,0:T(8,128)(2,1)S(1)} %shard_map.114), channel_id=1, source_target_pairs={{0,16},{2,18},{4,20},{6,22},{8,24},{10,26},{12,28},{14,30},{16,0},... | collective-permute-start | bytes 294920 | tf_op jit(solution)/shard_map/ppermute | solution.py:599
  76.1 1.4 %collective-permute-start.29 = (bf16[1,48,1024]{2,1,0:T(8,128)(2,1)S(1)}, bf16[1,48,1024]{2,1,0:T(8,128)(2,1)S(1)}, u32[]{:S(2)}, u32[]{:S(2)}) collective-permute-start(bf16[1,48,1024]{2,1,0:T(8,128)(2,1)S(1)} %shard_map.115.refs_0_), channel_id=1, source_target_pairs={{0,4},{2,6},{4,0},{6,2},{8,12},{10,14},{12,8},{14,10},{16,20},{18,... | collective-permute-start | bytes 294920 | tf_op jit(solution)/shard_map/ppermute | solution.py:442
  77.5 1.3 %collective-permute-start.30 = (bf16[1,48,1024]{2,1,0:T(8,128)(2,1)S(1)}, bf16[1,48,1024]{2,1,0:T(8,128)(2,1)S(1)}, u32[]{:S(2)}, u32[]{:S(2)}) collective-permute-start(bf16[1,48,1024]{2,1,0:T(8,128)(2,1)S(1)} %shard_map.115.refs_0_), channel_id=1, source_target_pairs={{0,6},{2,4},{4,2},{6,0},{8,14},{10,12},{12,10},{14,8},{16,22},{18,... | collective-permute-start | bytes 294920 | tf_op jit(solution)/shard_map/ppermute | solution.py:442
  78.8 1.5 %collective-permute-start.32 = (bf16[48,1024]{1,0:T(8,128)(2,1)S(1)}, bf16[48,1024]{1,0:T(8,128)(2,1)S(1)}, u32[]{:S(2)}, u32[]{:S(2)}) collective-permute-start(bf16[48,1024]{1,0:T(8,128)(2,1)S(1)} %collective-permute-done.31), channel_id=1, source_target_pairs={{0,8},{2,10},{4,12},{6,14},{8,0},{10,2},{12,4},{14,6},{16,24},{18,... | collective-permute-start | bytes 294920 | tf_op jit(solution)/shard_map/ppermute | solution.py:600
  80.9 2.1 %collective-permute-done.30.refs_3_ = bf16[1,48,1024]{2,1,0:T(8,128)(2,1)S(1)} collective-permute-done((bf16[1,48,1024]{2,1,0:T(8,128)(2,1)S(1)}, bf16[1,48,1024]{2,1,0:T(8,128)(2,1)S(1)}, u32[]{:S(2)}, u32[]{:S(2)}) %collective-permute-start.30) | collective-permute-done | bytes 98336 | tf_op jit(solution)/shard_map/ppermute | solution.py:442
  86.0 1.8 %collective-permute-start.35 = (bf16[2,48,1024]{2,1,0:T(8,128)(2,1)S(1)}, bf16[2,48,1024]{2,1,0:T(8,128)(2,1)S(1)}, u32[]{:S(2)}, u32[]{:S(2)}) collective-permute-start(bf16[2,48,1024]{2,1,0:T(8,128)(2,1)S(1)} %pad_maximum_fusion.1.refs_1_), channel_id=1, source_target_pairs={{0,6},{2,4},{4,2},{6,0},{8,14},{10,12},{12,10},{14,8},{16,22},{18,... | collective-permute-start | bytes 589832 | tf_op jit(solution)/shard_map/ppermute | solution.py:442
  87.9 1.5 %shard_map.117.refs_2_ = f32[768,2,512]{2,1,0:T(2,128)} custom-call(s32[4]{0:T(128)S(1)} %pad_add_fusion.scal, bf16[1,48,1024]{2,1,0:T(8,128)(2,1)S(1)} %shard_map.115.refs_0_, bf16[1,48,1024]{2,1,0:T(8,128)(2,1)S(1)} %collective-permute-done.28.refs_1_, bf16[1,48,1024]{2,1,0:T(8,128)(2,1)S(1)} %collective-permute-done.29.refs_2_, ...), custom_call_target="tpu_custom_call" | custom-call | tf_op jit(solution)/shard_map/pallas_call | solution.py:30
  89.4 1.2 %copy.15 = bf16[128,2,768]{2,1,0:T(2,128)(2,1)} copy(bf16[128,2,768]{2,0,1:T(8,128)(2,1)S(1)} %bitcast.19) | data formatting | bytes 786432
  91.8 1.6 %shard_map.118.refs_3_ = f32[768,2,512]{2,1,0:T(2,128)} custom-call(s32[4]{0:T(128)S(1)} %pad_add_fusion.scal, bf16[4,48,1024]{2,1,0:T(8,128)(2,1)S(1)} %collective-permute-done.36.refs_0_, bf16[2,48,1024]{2,1,0:T(8,128)(2,1)S(1)} %pad_maximum_fusion.1.refs_1_, f32[768,2,512]{2,1,0:T(2,128)} %shard_map.117.refs_2_), custom_call_target="tpu_custom_call", output_to_operand_aliasing={{}: (3, {})} | custom-call | tf_op jit(solution)/shard_map/pallas_call | solution.py:30
  93.6 1.6 %shard_map.119 = f32[768,2,512]{2,1,0:T(2,128)} custom-call(s32[4]{0:T(128)S(1)} %pad_add_fusion.scal, bf16[2,48,1024]{2,1,0:T(8,128)(2,1)S(1)} %collective-permute-done.33.refs_0_, bf16[2,48,1024]{2,1,0:T(8,128)(2,1)S(1)} %collective-permute-done.34.refs_1_, ...), custom_call_target="tpu_custom_call", output_to_operand_aliasing={{}: (4, {})} | custom-call | tf_op jit(solution)/shard_map/pallas_call | solution.py:30
  (73 shorter events, 23.1 us)
Async XLA Ops:
  2.7 5.8 %collective-permute-start = (bf16[16,384]{1,0:T(8,128)(2,1)S(1)}, bf16[16,384]{1,0:T(8,128)(2,1)S(1)}, u32[]{:S(2)}, u32[]{:S(2)}) collective-permute-start(bf16[16,384]{1,0:T(8,128)(2,1)S(1)} %shard_map.103.small), channel_id=1, source_target_pairs={{0,8},{2,10},{4,12},{6,14},{8,0},{10,2},{12,4},{14,6},{16,24},{18,... | collective-permute-start | bytes 36872 | tf_op jit(solution)/shard_map/ppermute | solution.py:449
  12.1 3.6 %collective-permute-start.5 = (f32[128,512]{1,0:T(8,128)S(1)}, f32[128,512]{1,0:T(8,128)S(1)}, u32[]{:S(2)}, u32[]{:S(2)}) collective-permute-start(f32[128,512]{1,0:T(8,128)S(1)} %get-tuple-element.74), channel_id=1, source_target_pairs={{0,1},{1,0},{2,3},{3,2},{4,5},{5,4},{6,7},{7,6},{8,9},{9,8},{10,11... | collective-permute-start | bytes 786440 | tf_op jit(solution)/shard_map/ppermute | solution.py:487
  12.2 7.6 %collective-permute-start.2 = (bf16[128,384]{1,0:T(8,128)(2,1)S(1)}, bf16[128,384]{1,0:T(8,128)(2,1)S(1)}, u32[]{:S(2)}, u32[]{:S(2)}) collective-permute-start(bf16[128,384]{1,0:T(8,128)(2,1)S(1)} %get-tuple-element.69), channel_id=1, source_target_pairs={{0,2},{2,0},{4,6},{6,4},{8,10},{10,8},{12,14},{14,12},{16,18},{18,... | collective-permute-start | bytes 294920 | tf_op jit(solution)/shard_map/ppermute | solution.py:442
  13.8 6.6 %collective-permute-start.3 = (bf16[128,384]{1,0:T(8,128)(2,1)S(1)}, bf16[128,384]{1,0:T(8,128)(2,1)S(1)}, u32[]{:S(2)}, u32[]{:S(2)}) collective-permute-start(bf16[128,384]{1,0:T(8,128)(2,1)S(1)} %get-tuple-element.70), channel_id=1, source_target_pairs={{0,4},{2,6},{4,0},{6,2},{8,12},{10,14},{12,8},{14,10},{16,20},{18,... | collective-permute-start | bytes 294920 | tf_op jit(solution)/shard_map/ppermute | solution.py:442
  15.3 6.4 %collective-permute-start.4 = (bf16[128,384]{1,0:T(8,128)(2,1)S(1)}, bf16[128,384]{1,0:T(8,128)(2,1)S(1)}, u32[]{:S(2)}, u32[]{:S(2)}) collective-permute-start(bf16[128,384]{1,0:T(8,128)(2,1)S(1)} %get-tuple-element.71), channel_id=1, source_target_pairs={{0,6},{2,4},{4,2},{6,0},{8,14},{10,12},{12,10},{14,8},{16,22},{18,... | collective-permute-start | bytes 294920 | tf_op jit(solution)/shard_map/ppermute | solution.py:442
  16.7 5.6 %collective-permute-start.6 = (bf16[272,128]{1,0:T(8,128)(2,1)S(1)}, bf16[272,128]{1,0:T(8,128)(2,1)S(1)}, u32[]{:S(2)}, u32[]{:S(2)}) collective-permute-start(bf16[272,128]{1,0:T(8,128)(2,1)S(1)} %get-tuple-element.79), channel_id=1, source_target_pairs={{0,2},{2,0},{4,6},{6,4},{8,10},{10,8},{12,14},{14,12},{16,18},{18,... | collective-permute-start | bytes 208904 | tf_op jit(solution)/shard_map/ppermute | solution.py:442
  18.3 5.1 %collective-permute-start.7 = (bf16[272,128]{1,0:T(8,128)(2,1)S(1)}, bf16[272,128]{1,0:T(8,128)(2,1)S(1)}, u32[]{:S(2)}, u32[]{:S(2)}) collective-permute-start(bf16[272,128]{1,0:T(8,128)(2,1)S(1)} %get-tuple-element.80), channel_id=1, source_target_pairs={{0,4},{2,6},{4,0},{6,2},{8,12},{10,14},{12,8},{14,10},{16,20},{18,... | collective-permute-start | bytes 208904 | tf_op jit(solution)/shard_map/ppermute | solution.py:442
  19.8 5.2 %collective-permute-start.8 = (bf16[272,128]{1,0:T(8,128)(2,1)S(1)}, bf16[272,128]{1,0:T(8,128)(2,1)S(1)}, u32[]{:S(2)}, u32[]{:S(2)}) collective-permute-start(bf16[272,128]{1,0:T(8,128)(2,1)S(1)} %get-tuple-element.81), channel_id=1, source_target_pairs={{0,6},{2,4},{4,2},{6,0},{8,14},{10,12},{12,10},{14,8},{16,22},{18,... | collective-permute-start | bytes 208904 | tf_op jit(solution)/shard_map/ppermute | solution.py:442
  25.6 13.4 %collective-permute-start.10 = (bf16[4,128,512]{2,1,0:T(8,128)(2,1)S(1)}, bf16[4,128,512]{2,1,0:T(8,128)(2,1)S(1)}, u32[]{:S(2)}, u32[]{:S(2)}) collective-permute-start(bf16[4,128,512]{2,1,0:T(8,128)(2,1)S(1)} %get-tuple-element.82.own), channel_id=1, source_target_pairs={{8,16},{10,18},{12,20},{14,22},{16,8},{18,10},{20,12},{22,14},{9,1... | collective-permute-start | bytes 1572872 | tf_op jit(solution)/shard_map/ppermute | solution.py:449
  26.4 17.0 %collective-permute-start.9 = (bf16[4,128,512]{2,1,0:T(8,128)(2,1)S(1)}, bf16[4,128,512]{2,1,0:T(8,128)(2,1)S(1)}, u32[]{:S(2)}, u32[]{:S(2)}) collective-permute-start(bf16[4,128,512]{2,1,0:T(8,128)(2,1)S(1)} %get-tuple-element.82.own), channel_id=1, source_target_pairs={{0,8},{2,10},{4,12},{6,14},{8,0},{10,2},{12,4},{14,6},{16,24},{18,... | collective-permute-start | bytes 1572872 | tf_op jit(solution)/shard_map/ppermute | solution.py:449
  38.4 6.1 %collective-permute-start.11 = (bf16[128,1280]{1,0:T(8,128)(2,1)S(1)}, bf16[128,1280]{1,0:T(8,128)(2,1)S(1)}, u32[]{:S(2)}, u32[]{:S(2)}) collective-permute-start(bf16[128,1280]{1,0:T(8,128)(2,1)S(1)} %get-tuple-element.86.refs_0_), channel_id=1, source_target_pairs={{0,1},{1,0},{2,3},{3,2},{4,5},{5,4},{6,7},{7,6},{8,9},{9,8},{10,11... | collective-permute-start | bytes 983048 | tf_op jit(solution)/shard_map/ppermute | solution.py:532
  38.5 6.1 %collective-permute-start.12 = (bf16[128,1280]{1,0:T(8,128)(2,1)S(1)}, bf16[128,1280]{1,0:T(8,128)(2,1)S(1)}, u32[]{:S(2)}, u32[]{:S(2)}) collective-permute-start(bf16[128,1280]{1,0:T(8,128)(2,1)S(1)} %get-tuple-element.87.refs_1_), channel_id=1, source_target_pairs={{0,1},{1,0},{2,3},{3,2},{4,5},{5,4},{6,7},{7,6},{8,9},{9,8},{10,11... | collective-permute-start | bytes 983048 | tf_op jit(solution)/shard_map/ppermute | solution.py:532
  39.0 5.6 %collective-permute-start.13 = (bf16[128,1280]{1,0:T(8,128)(2,1)S(1)}, bf16[128,1280]{1,0:T(8,128)(2,1)S(1)}, u32[]{:S(2)}, u32[]{:S(2)}) collective-permute-start(bf16[128,1280]{1,0:T(8,128)(2,1)S(1)} %get-tuple-element.88.refs_2_), channel_id=1, source_target_pairs={{0,1},{1,0},{2,3},{3,2},{4,5},{5,4},{6,7},{7,6},{8,9},{9,8},{10,11... | collective-permute-start | bytes 983048 | tf_op jit(solution)/shard_map/ppermute | solution.py:532
  39.1 5.5 %collective-permute-start.14 = (bf16[128,1280]{1,0:T(8,128)(2,1)S(1)}, bf16[128,1280]{1,0:T(8,128)(2,1)S(1)}, u32[]{:S(2)}, u32[]{:S(2)}) collective-permute-start(bf16[128,1280]{1,0:T(8,128)(2,1)S(1)} %get-tuple-element.89.refs_3_), channel_id=1, source_target_pairs={{0,1},{1,0},{2,3},{3,2},{4,5},{5,4},{6,7},{7,6},{8,9},{9,8},{10,11... | collective-permute-start | bytes 983048 | tf_op jit(solution)/shard_map/ppermute | solution.py:532
  47.0 7.6 %collective-permute-start.15 = (bf16[4,128,128]{2,1,0:T(8,128)(2,1)S(1)}, bf16[4,128,128]{2,1,0:T(8,128)(2,1)S(1)}, u32[]{:S(2)}, u32[]{:S(2)}) collective-permute-start(bf16[4,128,128]{2,1,0:T(8,128)(2,1)S(1)} %shard_map.111.refs_0_), channel_id=1, source_target_pairs={{0,2},{2,0},{4,6},{6,4},{8,10},{10,8},{12,14},{14,12},{16,18},{18,... | collective-permute-start | bytes 393224 | tf_op jit(solution)/shard_map/ppermute | solution.py:442
  48.1 6.5 %collective-permute-start.16 = (bf16[4,128,128]{2,1,0:T(8,128)(2,1)S(1)}, bf16[4,128,128]{2,1,0:T(8,128)(2,1)S(1)}, u32[]{:S(2)}, u32[]{:S(2)}) collective-permute-start(bf16[4,128,128]{2,1,0:T(8,128)(2,1)S(1)} %shard_map.111.refs_0_), channel_id=1, source_target_pairs={{0,4},{2,6},{4,0},{6,2},{8,12},{10,14},{12,8},{14,10},{16,20},{18,... | collective-permute-start | bytes 393224 | tf_op jit(solution)/shard_map/ppermute | solution.py:442
  48.8 5.9 %collective-permute-start.17 = (bf16[4,128,128]{2,1,0:T(8,128)(2,1)S(1)}, bf16[4,128,128]{2,1,0:T(8,128)(2,1)S(1)}, u32[]{:S(2)}, u32[]{:S(2)}) collective-permute-start(bf16[4,128,128]{2,1,0:T(8,128)(2,1)S(1)} %shard_map.111.refs_0_), channel_id=1, source_target_pairs={{0,6},{2,4},{4,2},{6,0},{8,14},{10,12},{12,10},{14,8},{16,22},{18,... | collective-permute-start | bytes 393224 | tf_op jit(solution)/shard_map/ppermute | solution.py:442
  58.8 5.9 %collective-permute-start.22 = (bf16[48,1024]{1,0:T(8,128)(2,1)S(1)}, bf16[48,1024]{1,0:T(8,128)(2,1)S(1)}, u32[]{:S(2)}, u32[]{:S(2)}) collective-permute-start(bf16[48,1024]{1,0:T(8,128)(2,1)S(1)} %get-tuple-element.101), channel_id=1, source_target_pairs={{0,8},{2,10},{4,12},{6,14},{8,0},{10,2},{12,4},{14,6},{16,24},{18,... | collective-permute-start | bytes 294920 | tf_op jit(solution)/shard_map/ppermute | solution.py:590
  61.3 10.8 %collective-permute-start.23 = (bf16[48,1024]{1,0:T(8,128)(2,1)S(1)}, bf16[48,1024]{1,0:T(8,128)(2,1)S(1)}, u32[]{:S(2)}, u32[]{:S(2)}) collective-permute-start(bf16[48,1024]{1,0:T(8,128)(2,1)S(1)} %get-tuple-element.107), channel_id=1, source_target_pairs={{0,16},{2,18},{4,20},{6,22},{8,24},{10,26},{12,28},{14,30},{16,0},... | collective-permute-start | bytes 294920 | tf_op jit(solution)/shard_map/ppermute | solution.py:590
  62.2 9.9 %collective-permute-start.24 = (bf16[48,1024]{1,0:T(8,128)(2,1)S(1)}, bf16[48,1024]{1,0:T(8,128)(2,1)S(1)}, u32[]{:S(2)}, u32[]{:S(2)}) collective-permute-start(bf16[48,1024]{1,0:T(8,128)(2,1)S(1)} %get-tuple-element.108), channel_id=1, source_target_pairs={{0,24},{2,26},{4,28},{6,30},{8,16},{10,18},{12,20},{14,22},{16,8},... | collective-permute-start | bytes 294920 | tf_op jit(solution)/shard_map/ppermute | solution.py:590
  64.6 7.5 %collective-permute-start.25 = (bf16[128,384]{1,0:T(8,128)(2,1)S(1)}, bf16[128,384]{1,0:T(8,128)(2,1)S(1)}, u32[]{:S(2)}, u32[]{:S(2)}) collective-permute-start(bf16[128,384]{1,0:T(8,128)(2,1)S(1)} %get-tuple-element.110), channel_id=1, source_target_pairs={{0,2},{2,0},{4,6},{6,4},{8,10},{10,8},{12,14},{14,12},{16,18},{18,... | collective-permute-start | bytes 294920 | tf_op jit(solution)/shard_map/ppermute | solution.py:442
  65.7 6.7 %collective-permute-start.26 = (bf16[128,384]{1,0:T(8,128)(2,1)S(1)}, bf16[128,384]{1,0:T(8,128)(2,1)S(1)}, u32[]{:S(2)}, u32[]{:S(2)}) collective-permute-start(bf16[128,384]{1,0:T(8,128)(2,1)S(1)} %get-tuple-element.111), channel_id=1, source_target_pairs={{0,4},{2,6},{4,0},{6,2},{8,12},{10,14},{12,8},{14,10},{16,20},{18,... | collective-permute-start | bytes 294920 | tf_op jit(solution)/shard_map/ppermute | solution.py:442
  66.8 5.7 %collective-permute-start.27 = (bf16[128,384]{1,0:T(8,128)(2,1)S(1)}, bf16[128,384]{1,0:T(8,128)(2,1)S(1)}, u32[]{:S(2)}, u32[]{:S(2)}) collective-permute-start(bf16[128,384]{1,0:T(8,128)(2,1)S(1)} %get-tuple-element.112), channel_id=1, source_target_pairs={{0,6},{2,4},{4,2},{6,0},{8,14},{10,12},{12,10},{14,8},{16,22},{18,... | collective-permute-start | bytes 294920 | tf_op jit(solution)/shard_map/ppermute | solution.py:442
  72.5 6.3 %collective-permute-start.31 = (bf16[48,1024]{1,0:T(8,128)(2,1)S(1)}, bf16[48,1024]{1,0:T(8,128)(2,1)S(1)}, u32[]{:S(2)}, u32[]{:S(2)}) collective-permute-start(bf16[48,1024]{1,0:T(8,128)(2,1)S(1)} %shard_map.114), channel_id=1, source_target_pairs={{0,16},{2,18},{4,20},{6,22},{8,24},{10,26},{12,28},{14,30},{16,0},... | collective-permute-start | bytes 294920 | tf_op jit(solution)/shard_map/ppermute | solution.py:599
  75.2 5.3 %collective-permute-start.28 = (bf16[1,48,1024]{2,1,0:T(8,128)(2,1)S(1)}, bf16[1,48,1024]{2,1,0:T(8,128)(2,1)S(1)}, u32[]{:S(2)}, u32[]{:S(2)}) collective-permute-start(bf16[1,48,1024]{2,1,0:T(8,128)(2,1)S(1)} %shard_map.115.refs_0_), channel_id=1, source_target_pairs={{0,2},{2,0},{4,6},{6,4},{8,10},{10,8},{12,14},{14,12},{16,18},{18,... | collective-permute-start | bytes 294920 | tf_op jit(solution)/shard_map/ppermute | solution.py:442
  76.1 4.8 %collective-permute-start.29 = (bf16[1,48,1024]{2,1,0:T(8,128)(2,1)S(1)}, bf16[1,48,1024]{2,1,0:T(8,128)(2,1)S(1)}, u32[]{:S(2)}, u32[]{:S(2)}) collective-permute-start(bf16[1,48,1024]{2,1,0:T(8,128)(2,1)S(1)} %shard_map.115.refs_0_), channel_id=1, source_target_pairs={{0,4},{2,6},{4,0},{6,2},{8,12},{10,14},{12,8},{14,10},{16,20},{18,... | collective-permute-start | bytes 294920 | tf_op jit(solution)/shard_map/ppermute | solution.py:442
  77.5 5.5 %collective-permute-start.30 = (bf16[1,48,1024]{2,1,0:T(8,128)(2,1)S(1)}, bf16[1,48,1024]{2,1,0:T(8,128)(2,1)S(1)}, u32[]{:S(2)}, u32[]{:S(2)}) collective-permute-start(bf16[1,48,1024]{2,1,0:T(8,128)(2,1)S(1)} %shard_map.115.refs_0_), channel_id=1, source_target_pairs={{0,6},{2,4},{4,2},{6,0},{8,14},{10,12},{12,10},{14,8},{16,22},{18,... | collective-permute-start | bytes 294920 | tf_op jit(solution)/shard_map/ppermute | solution.py:442
  78.8 5.5 %collective-permute-start.32 = (bf16[48,1024]{1,0:T(8,128)(2,1)S(1)}, bf16[48,1024]{1,0:T(8,128)(2,1)S(1)}, u32[]{:S(2)}, u32[]{:S(2)}) collective-permute-start(bf16[48,1024]{1,0:T(8,128)(2,1)S(1)} %collective-permute-done.31), channel_id=1, source_target_pairs={{0,8},{2,10},{4,12},{6,14},{8,0},{10,2},{12,4},{14,6},{16,24},{18,... | collective-permute-start | bytes 294920 | tf_op jit(solution)/shard_map/ppermute | solution.py:600
  83.1 8.8 %collective-permute-start.36 = (bf16[4,48,1024]{2,1,0:T(8,128)(2,1)S(1)}, bf16[4,48,1024]{2,1,0:T(8,128)(2,1)S(1)}, u32[]{:S(2)}, u32[]{:S(2)}) collective-permute-start(bf16[4,48,1024]{2,1,0:T(8,128)(2,1)S(1)} %pad_maximum_fusion), channel_id=1, source_target_pairs={{0,8},{2,10},{4,12},{6,14},{8,0},{10,2},{12,4},{14,6},{16,24},{18,... | collective-permute-start | bytes 1179656 | tf_op jit(solution)/shard_map/ppermute | solution.py:636
  84.3 9.2 %collective-permute-start.33 = (bf16[2,48,1024]{2,1,0:T(8,128)(2,1)S(1)}, bf16[2,48,1024]{2,1,0:T(8,128)(2,1)S(1)}, u32[]{:S(2)}, u32[]{:S(2)}) collective-permute-start(bf16[2,48,1024]{2,1,0:T(8,128)(2,1)S(1)} %pad_maximum_fusion.1.refs_1_), channel_id=1, source_target_pairs={{0,2},{2,0},{4,6},{6,4},{8,10},{10,8},{12,14},{14,12},{16,18},{18,... | collective-permute-start | bytes 589832 | tf_op jit(solution)/shard_map/ppermute | solution.py:442
  85.4 8.2 %collective-permute-start.34 = (bf16[2,48,1024]{2,1,0:T(8,128)(2,1)S(1)}, bf16[2,48,1024]{2,1,0:T(8,128)(2,1)S(1)}, u32[]{:S(2)}, u32[]{:S(2)}) collective-permute-start(bf16[2,48,1024]{2,1,0:T(8,128)(2,1)S(1)} %pad_maximum_fusion.1.refs_1_), channel_id=1, source_target_pairs={{0,4},{2,6},{4,0},{6,2},{8,12},{10,14},{12,8},{14,10},{16,20},{18,... | collective-permute-start | bytes 589832 | tf_op jit(solution)/shard_map/ppermute | solution.py:442
  86.0 7.6 %collective-permute-start.35 = (bf16[2,48,1024]{2,1,0:T(8,128)(2,1)S(1)}, bf16[2,48,1024]{2,1,0:T(8,128)(2,1)S(1)}, u32[]{:S(2)}, u32[]{:S(2)}) collective-permute-start(bf16[2,48,1024]{2,1,0:T(8,128)(2,1)S(1)} %pad_maximum_fusion.1.refs_1_), channel_id=1, source_target_pairs={{0,6},{2,4},{4,2},{6,0},{8,14},{10,12},{12,10},{14,8},{16,22},{18,... | collective-permute-start | bytes 589832 | tf_op jit(solution)/shard_map/ppermute | solution.py:442
  (7 other events, 24.6 us)

commit v8 on v7

--- a/solution.py
+++ b/solution.py
@@ -627,15 +627,17 @@
     if direct:
         mine = call(copy_body, struct(1, rows, 2 * panel), [VMEM], (mine,), flops=WEIGHT, moved=WEIGHT // 256)
     near_pieces = swap([mine] * GROUP)
-    intersection = write(near_pieces, [(k, 0, k, 0) for k in everywhere])
-    if direct:
+    plan = [(k, 0, k, 0) for k in everywhere]
+    if not direct:
+        intersection = write(near_pieces, plan)
+    else:
         far = jnp.stack(stack[2:])
         twin_pieces = jnp.concatenate(near_pieces)
         _, far, filtered, rotated = lax.optimization_barrier((twin_pieces, far, filtered, rotated))
         far_pieces = swap([far] * GROUP)
         twin_pieces = lax.ppermute(twin_pieces, "elem", twins)
-        plan = [(0, k, k, 1) for k in everywhere] + [(1, j - 2, 0, j) for j in range(2, split)]
-        intersection = write([twin_pieces, far], plan, intersection)
+        plan += [(GROUP, k, k, 1) for k in everywhere] + [(GROUP + 1, j - 2, 0, j) for j in range(2, split)]
+        intersection = write([*near_pieces, twin_pieces, far], plan)
         plan = [(k - 1, j - 2, k, j) for k in range(1, GROUP) for j in range(2, split)]
         intersection = write(far_pieces[1:], plan, intersection)
     return (filtered, rotated, intersection)

time: 95.7 us -> 96 us (level)
  waiting for transfers between devices: 17.8 us -> 21 us
  starting transfers between devices: 44.5 us -> 42.4 us
    ppermute x1, waiting for transfers between devices: 0.2 us -> 2.63 us  [on_device(): stack.append(lax.ppermute(stack[2], 'elem', twins))]
    ppermute x1, waiting for transfers between devices: 0.01 us -> 1.95 us  [on_device(): lax.ppermute(own, 'elem', [(i, i ^ 2 * GROUP) for i in range(blocks)])]
    ppermute x1, starting transfers between devices: 1.49 us -> 0.23 us  [on_device(): stack.append(lax.ppermute(stack[2], 'elem', twins))]
    ppermute x2, starting transfers between devices: 10.3 us -> 9.23 us  [neighbours(): lax.ppermute(value, 'elem', twins)]
    pallas_call x17 -> x16, Pallas kernels: 24.3 us -> 23.6 us  [call(): pl.pallas_call(body, out_shape=out_shape, in_specs=specs, out_specs=out_s...]
  transfers between devices with their start and end apart: 37 -> 37, of which waited for: 17 -> 16; matrix products, arithmetic and copies ran while one was open for 3% -> 3% of each run, Pallas kernels for 17% -> 16%
where the time goes in v8:
time: 96 us; the launch traced here: 95.6 us
  starting transfers between devices  42.4 us (44%)
  Pallas kernels  23.6 us (25%)
  waiting for transfers between devices  21 us (22%)
  local copies, waits for them, and re-layouts  6.1 us (6%)
  between operations  1.76 us (2%)
    pallas_call x16, Pallas kernels, call(): pl.pallas_call(body, out_shape=out_shape, in_specs=specs, out_specs=out_s...  23.6 us
    ppermute x18, starting transfers between devices, swap(): lax.ppermute(values[k], 'elem', in_group(k))  21.3 us
    ppermute x2, starting transfers between devices, neighbours(): lax.ppermute(value, 'elem', twins)  9.23 us
    ppermute x18, waiting for transfers between devices, swap(): lax.ppermute(values[k], 'elem', in_group(k))  7.37 us
    ppermute x3, starting transfers between devices, across(): lax.ppermute(values[j], 'elem', [(i, i ^ GROUP * j) for i in range(blocks)])  5.97 us
    ppermute x3, waiting for transfers between devices, across(): lax.ppermute(values[j], 'elem', [(i, i ^ GROUP * j) for i in range(blocks)])  4.48 us
    ppermute x2, waiting for transfers between devices, neighbours(): lax.ppermute(value, 'elem', twins)  3.48 us
    ppermute x1, waiting for transfers between devices, on_device(): stack.append(lax.ppermute(stack[2], 'elem', twins))  2.63 us
  transfers between devices with their start and end apart: 37, of which 16 were waited for; matrix products, arithmetic and copies ran while one was open for 3% of the time, Pallas kernels for 16%

profile of v8, /device:TPU:0, one launch (start us, length us, event | category | flops | bytes accessed | tf_op | source)
XLA Modules:
  0.0 95.6 jit_solution(1284744939661927627)
XLA Ops:
  3.4 5.9 %collective-permute-start = (bf16[16,384]{1,0:T(8,128)(2,1)S(1)}, bf16[16,384]{1,0:T(8,128)(2,1)S(1)}, u32[]{:S(2)}, u32[]{:S(2)}) collective-permute-start(bf16[16,384]{1,0:T(8,128)(2,1)S(1)} %shard_map.103.small), channel_id=1, source_target_pairs={{0,8},{2,10},{4,12},{6,14},{8,0},{10,2},{12,4},{14,6},{16,24},{18,... | collective-permute-start | bytes 36872 | tf_op jit(solution)/shard_map/ppermute | solution.py:449
  11.4 2.4 %copy.18 = bf16[1536,2,512]{2,0,1:T(8,128)(2,1)S(1)} copy(bf16[1536,2,512]{2,1,0:T(2,128)(2,1)} %param.15) | data formatting | bytes 6291456 | tf_op jit(solution)/shard_map/optimization_barrier | solution.py:471
  13.8 1.2 %shard_map.106 = (f32[128,512]{1,0:T(8,128)S(1)}, f32[128,512]{1,0:T(8,128)S(1)}) custom-call(s32[4]{0:T(128)S(1)} %pad_add_fusion.scal, bf16[2,128,768]{2,1,0:T(8,128)(2,1)S(1)} %bitcast.18, bf16[2,1536,512]{2,1,0:T(8,128)(2,1)S(1)} %bitcast.16), custom_call_target="tpu_custom_call" | custom-call | flops 4000000000 | bytes 15625000 | tf_op jit(solution)/shard_map/pallas_call | solution.py:30
  15.0 1.6 %collective-permute-start.2 = (bf16[128,384]{1,0:T(8,128)(2,1)S(1)}, bf16[128,384]{1,0:T(8,128)(2,1)S(1)}, u32[]{:S(2)}, u32[]{:S(2)}) collective-permute-start(bf16[128,384]{1,0:T(8,128)(2,1)S(1)} %get-tuple-element.69), channel_id=1, source_target_pairs={{0,2},{2,0},{4,6},{6,4},{8,10},{10,8},{12,14},{14,12},{16,18},{18,... | collective-permute-start | bytes 294920 | tf_op jit(solution)/shard_map/ppermute | solution.py:442
  16.6 1.5 %collective-permute-start.3 = (bf16[128,384]{1,0:T(8,128)(2,1)S(1)}, bf16[128,384]{1,0:T(8,128)(2,1)S(1)}, u32[]{:S(2)}, u32[]{:S(2)}) collective-permute-start(bf16[128,384]{1,0:T(8,128)(2,1)S(1)} %get-tuple-element.70), channel_id=1, source_target_pairs={{0,4},{2,6},{4,0},{6,2},{8,12},{10,14},{12,8},{14,10},{16,20},{18,... | collective-permute-start | bytes 294920 | tf_op jit(solution)/shard_map/ppermute | solution.py:442
  19.5 1.6 %collective-permute-start.6 = (bf16[272,128]{1,0:T(8,128)(2,1)S(1)}, bf16[272,128]{1,0:T(8,128)(2,1)S(1)}, u32[]{:S(2)}, u32[]{:S(2)}) collective-permute-start(bf16[272,128]{1,0:T(8,128)(2,1)S(1)} %get-tuple-element.79), channel_id=1, source_target_pairs={{0,2},{2,0},{4,6},{6,4},{8,10},{10,8},{12,14},{14,12},{16,18},{18,... | collective-permute-start | bytes 208904 | tf_op jit(solution)/shard_map/ppermute | solution.py:442
  21.1 1.5 %collective-permute-start.7 = (bf16[272,128]{1,0:T(8,128)(2,1)S(1)}, bf16[272,128]{1,0:T(8,128)(2,1)S(1)}, u32[]{:S(2)}, u32[]{:S(2)}) collective-permute-start(bf16[272,128]{1,0:T(8,128)(2,1)S(1)} %get-tuple-element.80), channel_id=1, source_target_pairs={{0,4},{2,6},{4,0},{6,2},{8,12},{10,14},{12,8},{14,10},{16,20},{18,... | collective-permute-start | bytes 208904 | tf_op jit(solution)/shard_map/ppermute | solution.py:442
  23.1 1.3 %collective-permute-done.4.a3 = bf16[128,384]{1,0:T(8,128)(2,1)S(1)} collective-permute-done((bf16[128,384]{1,0:T(8,128)(2,1)S(1)}, bf16[128,384]{1,0:T(8,128)(2,1)S(1)}, u32[]{:S(2)}, u32[]{:S(2)}) %collective-permute-start.4) | collective-permute-done | bytes 98336 | tf_op jit(solution)/shard_map/ppermute | solution.py:442
  25.1 1.0 %collective-permute-done.7.a2 = bf16[272,128]{1,0:T(8,128)(2,1)S(1)} collective-permute-done((bf16[272,128]{1,0:T(8,128)(2,1)S(1)}, bf16[272,128]{1,0:T(8,128)(2,1)S(1)}, u32[]{:S(2)}, u32[]{:S(2)}) %collective-permute-start.7) | collective-permute-done | bytes 69664 | tf_op jit(solution)/shard_map/ppermute | solution.py:442
  26.1 1.7 %collective-permute-done.8.a3 = bf16[272,128]{1,0:T(8,128)(2,1)S(1)} collective-permute-done((bf16[272,128]{1,0:T(8,128)(2,1)S(1)}, bf16[272,128]{1,0:T(8,128)(2,1)S(1)}, u32[]{:S(2)}, u32[]{:S(2)}) %collective-permute-start.8) | collective-permute-done | bytes 69664 | tf_op jit(solution)/shard_map/ppermute | solution.py:442
  29.2 3.3 %collective-permute-start.9 = (bf16[4,128,512]{2,1,0:T(8,128)(2,1)S(1)}, bf16[4,128,512]{2,1,0:T(8,128)(2,1)S(1)}, u32[]{:S(2)}, u32[]{:S(2)}) collective-permute-start(bf16[4,128,512]{2,1,0:T(8,128)(2,1)S(1)} %get-tuple-element.82.own), channel_id=1, source_target_pairs={{0,8},{2,10},{4,12},{6,14},{8,0},{10,2},{12,4},{14,6},{16,24},{18,... | collective-permute-start | bytes 1572872 | tf_op jit(solution)/shard_map/ppermute | solution.py:449
  32.5 5.2 %shard_map.110 = (bf16[128,1280]{1,0:T(8,128)(2,1)S(1)}, bf16[128,1280]{1,0:T(8,128)(2,1)S(1)}, bf16[128,1280]{1,0:T(8,128)(2,1)S(1)}, bf16[128,1280]{1,0:T(8,128)(2,1)S(1)}) custom-call(s32[4]{0:T(128)S(1)} %pad_add_fusion.scal, s32[1]{0:T(128)} %bitcast.2.side_s, bf16[4,144,128]{2,1,0:T(8,128)(2,1)S(1)} %get-tuple-element.83.small, ...), custom_call_target="tpu_custom_call" | custom-call | flops 2717908992 | bytes 2621440 | tf_op jit(solution)/shard_map/pallas_call | solution.py:30
  38.8 3.5 %collective-permute-done.9.twin = bf16[4,128,512]{2,1,0:T(8,128)(2,1)S(1)} collective-permute-done((bf16[4,128,512]{2,1,0:T(8,128)(2,1)S(1)}, bf16[4,128,512]{2,1,0:T(8,128)(2,1)S(1)}, u32[]{:S(2)}, u32[]{:S(2)}) %collective-permute-start.9) | collective-permute-done | bytes 524320 | tf_op jit(solution)/shard_map/ppermute | solution.py:449
  42.3 1.1 %shard_map.109 = (bf16[1536,512]{1,0:T(8,128)(2,1)S(1)}, f32[8,128,128]{2,1,0:T(8,128)S(1)}) custom-call(s32[4]{0:T(128)S(1)} %pad_add_fusion.scal, bf16[4,128,512]{2,1,0:T(8,128)(2,1)S(1)} %get-tuple-element.82.own, bf16[4,128,512]{2,1,0:T(8,128)(2,1)S(1)} %collective-permute-done.9.twin, bf16[4,128,512]{2,1,0:T(8,128)(2,1)S(1)} %collective-permute-done.10.next_, ...), custom_call_target="tpu_custom_call" | custom-call | tf_op jit(solution)/shard_map/pallas_call | solution.py:30
  43.5 2.4 %shard_map.111.refs_0_ = bf16[4,128,128]{2,1,0:T(8,128)(2,1)S(1)} custom-call(s32[4]{0:T(128)S(1)} %pad_add_fusion.scal, s32[1]{0:T(128)} %bitcast.2.side_s, bf16[1536,512]{1,0:T(8,128)(2,1)S(1)} %get-tuple-element.84.vec, f32[8,128,128]{2,1,0:T(8,128)S(1)} %get-tuple-element.85.cols, bf16[128,1280]{1,0:T(8,128)(2,1)S(1)} %get-tuple-element.86.refs_0_, ...), custom_call_target="tpu_custom_call" | custom-call | flops 503316480 | bytes 2621440 | tf_op jit(solution)/shard_map/pallas_call | solution.py:30
  45.9 1.2 %collective-permute-start.17 = (bf16[4,128,128]{2,1,0:T(8,128)(2,1)S(1)}, bf16[4,128,128]{2,1,0:T(8,128)(2,1)S(1)}, u32[]{:S(2)}, u32[]{:S(2)}) collective-permute-start(bf16[4,128,128]{2,1,0:T(8,128)(2,1)S(1)} %shard_map.111.refs_0_), channel_id=1, source_target_pairs={{0,6},{2,4},{4,2},{6,0},{8,14},{10,12},{12,10},{14,8},{16,22},{18,... | collective-permute-start | bytes 393224 | tf_op jit(solution)/shard_map/ppermute | solution.py:442
  47.1 1.4 %collective-permute-start.16 = (bf16[4,128,128]{2,1,0:T(8,128)(2,1)S(1)}, bf16[4,128,128]{2,1,0:T(8,128)(2,1)S(1)}, u32[]{:S(2)}, u32[]{:S(2)}) collective-permute-start(bf16[4,128,128]{2,1,0:T(8,128)(2,1)S(1)} %shard_map.111.refs_0_), channel_id=1, source_target_pairs={{0,4},{2,6},{4,0},{6,2},{8,12},{10,14},{12,8},{14,10},{16,20},{18,... | collective-permute-start | bytes 393224 | tf_op jit(solution)/shard_map/ppermute | solution.py:442
  49.4 4.1 %shard_map.112 = (bf16[128,384]{1,0:T(8,128)(2,1)S(1)}, bf16[128,384]{1,0:T(8,128)(2,1)S(1)}, bf16[128,384]{1,0:T(8,128)(2,1)S(1)}, bf16[128,384]{1,0:T(8,128)(2,1)S(1)}, bf16[384,512]{1,0:T(8,128)(2,1)S(1)}) custom-call(s32[4]{0:T(128)S(1)} %pad_add_fusion.scal, s32[1]{0:T(128)} %bitcast.2.side_s, bf16[1536,512]{1,0:T(8,128)(2,1)S(1)} %get-tuple-element.84.vec, ...), custom_call_target="tpu_custom_call" | custom-call | flops 1509949440 | bytes 2621440 | tf_op jit(solution)/shard_map/pallas_call | solution.py:30
  55.6 2.0 %shard_map.113 = (bf16[48,1024]{1,0:T(8,128)(2,1)S(1)}, bf16[48,1024]{1,0:T(8,128)(2,1)S(1)}, bf16[48,1024]{1,0:T(8,128)(2,1)S(1)}, bf16[48,1024]{1,0:T(8,128)(2,1)S(1)}, bf16[2,128,256]{2,1,0:T(8,128)(2,1)S(1)}) custom-call(s32[4]{0:T(128)S(1)} %pad_add_fusion.scal, bf16[384,512]{1,0:T(8,128)(2,1)S(1)} %get-tuple-element.95.left, ...), custom_call_target="tpu_custom_call" | custom-call | flops 402653184 | bytes 1048576 | tf_op jit(solution)/shard_map/pallas_call | solution.py:30
  57.7 3.5 %collective-permute-start.22 = (bf16[48,1024]{1,0:T(8,128)(2,1)S(1)}, bf16[48,1024]{1,0:T(8,128)(2,1)S(1)}, u32[]{:S(2)}, u32[]{:S(2)}) collective-permute-start(bf16[48,1024]{1,0:T(8,128)(2,1)S(1)} %get-tuple-element.101), channel_id=1, source_target_pairs={{0,8},{2,10},{4,12},{6,14},{8,0},{10,2},{12,4},{14,6},{16,24},{18,... | collective-permute-start | bytes 294920 | tf_op jit(solution)/shard_map/ppermute | solution.py:590
  61.2 2.4 %collective-permute-start.24 = (bf16[48,1024]{1,0:T(8,128)(2,1)S(1)}, bf16[48,1024]{1,0:T(8,128)(2,1)S(1)}, u32[]{:S(2)}, u32[]{:S(2)}) collective-permute-start(bf16[48,1024]{1,0:T(8,128)(2,1)S(1)} %get-tuple-element.108), channel_id=1, source_target_pairs={{0,24},{2,26},{4,28},{6,30},{8,16},{10,18},{12,20},{14,22},{16,8},... | collective-permute-start | bytes 294920 | tf_op jit(solution)/shard_map/ppermute | solution.py:590
  64.5 1.2 %collective-permute-start.25 = (bf16[128,384]{1,0:T(8,128)(2,1)S(1)}, bf16[128,384]{1,0:T(8,128)(2,1)S(1)}, u32[]{:S(2)}, u32[]{:S(2)}) collective-permute-start(bf16[128,384]{1,0:T(8,128)(2,1)S(1)} %get-tuple-element.110), channel_id=1, source_target_pairs={{0,2},{2,0},{4,6},{6,4},{8,10},{10,8},{12,14},{14,12},{16,18},{18,... | collective-permute-start | bytes 294920 | tf_op jit(solution)/shard_map/ppermute | solution.py:442
  66.2 1.7 %collective-permute-start.27 = (bf16[128,384]{1,0:T(8,128)(2,1)S(1)}, bf16[128,384]{1,0:T(8,128)(2,1)S(1)}, u32[]{:S(2)}, u32[]{:S(2)}) collective-permute-start(bf16[128,384]{1,0:T(8,128)(2,1)S(1)} %get-tuple-element.112), channel_id=1, source_target_pairs={{0,6},{2,4},{4,2},{6,0},{8,14},{10,12},{12,10},{14,8},{16,22},{18,... | collective-permute-start | bytes 294920 | tf_op jit(solution)/shard_map/ppermute | solution.py:442
  68.0 3.6 %collective-permute-done.23.s2 = bf16[48,1024]{1,0:T(8,128)(2,1)S(1)} collective-permute-done((bf16[48,1024]{1,0:T(8,128)(2,1)S(1)}, bf16[48,1024]{1,0:T(8,128)(2,1)S(1)}, u32[]{:S(2)}, u32[]{:S(2)}) %collective-permute-start.23) | collective-permute-done | bytes 98336 | tf_op jit(solution)/shard_map/ppermute | solution.py:590
  72.3 1.8 %collective-permute-start.31 = (bf16[48,1024]{1,0:T(8,128)(2,1)S(1)}, bf16[48,1024]{1,0:T(8,128)(2,1)S(1)}, u32[]{:S(2)}, u32[]{:S(2)}) collective-permute-start(bf16[48,1024]{1,0:T(8,128)(2,1)S(1)} %shard_map.114), channel_id=1, source_target_pairs={{0,16},{2,18},{4,20},{6,22},{8,24},{10,26},{12,28},{14,30},{16,0},... | collective-permute-start | bytes 294920 | tf_op jit(solution)/shard_map/ppermute | solution.py:599
  74.1 1.8 %collective-permute-start.30 = (bf16[1,48,1024]{2,1,0:T(8,128)(2,1)S(1)}, bf16[1,48,1024]{2,1,0:T(8,128)(2,1)S(1)}, u32[]{:S(2)}, u32[]{:S(2)}) collective-permute-start(bf16[1,48,1024]{2,1,0:T(8,128)(2,1)S(1)} %shard_map.115.refs_0_), channel_id=1, source_target_pairs={{0,6},{2,4},{4,2},{6,0},{8,14},{10,12},{12,10},{14,8},{16,22},{18,... | collective-permute-start | bytes 294920 | tf_op jit(solution)/shard_map/ppermute | solution.py:442
  77.6 2.0 %collective-permute-done.31 = bf16[48,1024]{1,0:T(8,128)(2,1)S(1)} collective-permute-done((bf16[48,1024]{1,0:T(8,128)(2,1)S(1)}, bf16[48,1024]{1,0:T(8,128)(2,1)S(1)}, u32[]{:S(2)}, u32[]{:S(2)}) %collective-permute-start.31) | collective-permute-done | bytes 98336 | tf_op jit(solution)/shard_map/ppermute | solution.py:599
  82.7 2.6 %collective-permute-done.32 = bf16[48,1024]{1,0:T(8,128)(2,1)S(1)} collective-permute-done((bf16[48,1024]{1,0:T(8,128)(2,1)S(1)}, bf16[48,1024]{1,0:T(8,128)(2,1)S(1)}, u32[]{:S(2)}, u32[]{:S(2)}) %collective-permute-start.32) | collective-permute-done | bytes 98336 | tf_op jit(solution)/shard_map/ppermute | solution.py:600
  85.4 2.6 %collective-permute-start.34 = (bf16[2,48,1024]{2,1,0:T(8,128)(2,1)S(1)}, bf16[2,48,1024]{2,1,0:T(8,128)(2,1)S(1)}, u32[]{:S(2)}, u32[]{:S(2)}) collective-permute-start(bf16[2,48,1024]{2,1,0:T(8,128)(2,1)S(1)} %pad_maximum_fusion.1.refs_5_), channel_id=1, source_target_pairs={{0,4},{2,6},{4,0},{6,2},{8,12},{10,14},{12,8},{14,10},{16,20},{18,... | collective-permute-start | bytes 589832 | tf_op jit(solution)/shard_map/ppermute | solution.py:442
  88.9 1.1 %copy.14 = bf16[128,2,768]{2,1,0:T(2,128)(2,1)} copy(bf16[128,2,768]{2,0,1:T(8,128)(2,1)S(1)} %bitcast.19) | data formatting | bytes 786432
  90.9 1.9 %shard_map.117.refs_3_ = f32[768,2,512]{2,1,0:T(2,128)} custom-call(s32[4]{0:T(128)S(1)} %pad_add_fusion.scal, bf16[1,48,1024]{2,1,0:T(8,128)(2,1)S(1)} %shard_map.115.refs_0_, bf16[1,48,1024]{2,1,0:T(8,128)(2,1)S(1)} %collective-permute-done.28.refs_1_, bf16[1,48,1024]{2,1,0:T(8,128)(2,1)S(1)} %collective-permute-done.29.refs_2_, ...), custom_call_target="tpu_custom_call" | custom-call | tf_op jit(solution)/shard_map/pallas_call | solution.py:30
  93.8 1.6 %shard_map.118 = f32[768,2,512]{2,1,0:T(2,128)} custom-call(s32[4]{0:T(128)S(1)} %pad_add_fusion.scal, bf16[2,48,1024]{2,1,0:T(8,128)(2,1)S(1)} %collective-permute-done.33.refs_0_, bf16[2,48,1024]{2,1,0:T(8,128)(2,1)S(1)} %collective-permute-done.34.refs_1_, ...), custom_call_target="tpu_custom_call", output_to_operand_aliasing={{}: (4, {})} | custom-call | tf_op jit(solution)/shard_map/pallas_call | solution.py:30
  (72 shorter events, 21.9 us)
Async XLA Ops:
  2.7 8.6 %collective-permute-start.1 = (bf16[16,384]{1,0:T(8,128)(2,1)S(1)}, bf16[16,384]{1,0:T(8,128)(2,1)S(1)}, u32[]{:S(2)}, u32[]{:S(2)}) collective-permute-start(bf16[16,384]{1,0:T(8,128)(2,1)S(1)} %shard_map.103.small), channel_id=1, source_target_pairs={{8,16},{10,18},{12,20},{14,22},{16,8},{18,10},{20,12},{22,14},{9,1... | collective-permute-start | bytes 36872 | tf_op jit(solution)/shard_map/ppermute | solution.py:449
  3.4 8.0 %collective-permute-start = (bf16[16,384]{1,0:T(8,128)(2,1)S(1)}, bf16[16,384]{1,0:T(8,128)(2,1)S(1)}, u32[]{:S(2)}, u32[]{:S(2)}) collective-permute-start(bf16[16,384]{1,0:T(8,128)(2,1)S(1)} %shard_map.103.small), channel_id=1, source_target_pairs={{0,8},{2,10},{4,12},{6,14},{8,0},{10,2},{12,4},{14,6},{16,24},{18,... | collective-permute-start | bytes 36872 | tf_op jit(solution)/shard_map/ppermute | solution.py:449
  15.0 7.6 %collective-permute-start.2 = (bf16[128,384]{1,0:T(8,128)(2,1)S(1)}, bf16[128,384]{1,0:T(8,128)(2,1)S(1)}, u32[]{:S(2)}, u32[]{:S(2)}) collective-permute-start(bf16[128,384]{1,0:T(8,128)(2,1)S(1)} %get-tuple-element.69), channel_id=1, source_target_pairs={{0,2},{2,0},{4,6},{6,4},{8,10},{10,8},{12,14},{14,12},{16,18},{18,... | collective-permute-start | bytes 294920 | tf_op jit(solution)/shard_map/ppermute | solution.py:442
  16.6 6.6 %collective-permute-start.3 = (bf16[128,384]{1,0:T(8,128)(2,1)S(1)}, bf16[128,384]{1,0:T(8,128)(2,1)S(1)}, u32[]{:S(2)}, u32[]{:S(2)}) collective-permute-start(bf16[128,384]{1,0:T(8,128)(2,1)S(1)} %get-tuple-element.70), channel_id=1, source_target_pairs={{0,4},{2,6},{4,0},{6,2},{8,12},{10,14},{12,8},{14,10},{16,20},{18,... | collective-permute-start | bytes 294920 | tf_op jit(solution)/shard_map/ppermute | solution.py:442
  18.1 6.4 %collective-permute-start.4 = (bf16[128,384]{1,0:T(8,128)(2,1)S(1)}, bf16[128,384]{1,0:T(8,128)(2,1)S(1)}, u32[]{:S(2)}, u32[]{:S(2)}) collective-permute-start(bf16[128,384]{1,0:T(8,128)(2,1)S(1)} %get-tuple-element.71), channel_id=1, source_target_pairs={{0,6},{2,4},{4,2},{6,0},{8,14},{10,12},{12,10},{14,8},{16,22},{18,... | collective-permute-start | bytes 294920 | tf_op jit(solution)/shard_map/ppermute | solution.py:442
  19.5 5.6 %collective-permute-start.6 = (bf16[272,128]{1,0:T(8,128)(2,1)S(1)}, bf16[272,128]{1,0:T(8,128)(2,1)S(1)}, u32[]{:S(2)}, u32[]{:S(2)}) collective-permute-start(bf16[272,128]{1,0:T(8,128)(2,1)S(1)} %get-tuple-element.79), channel_id=1, source_target_pairs={{0,2},{2,0},{4,6},{6,4},{8,10},{10,8},{12,14},{14,12},{16,18},{18,... | collective-permute-start | bytes 208904 | tf_op jit(solution)/shard_map/ppermute | solution.py:442
  21.1 5.1 %collective-permute-start.7 = (bf16[272,128]{1,0:T(8,128)(2,1)S(1)}, bf16[272,128]{1,0:T(8,128)(2,1)S(1)}, u32[]{:S(2)}, u32[]{:S(2)}) collective-permute-start(bf16[272,128]{1,0:T(8,128)(2,1)S(1)} %get-tuple-element.80), channel_id=1, source_target_pairs={{0,4},{2,6},{4,0},{6,2},{8,12},{10,14},{12,8},{14,10},{16,20},{18,... | collective-permute-start | bytes 208904 | tf_op jit(solution)/shard_map/ppermute | solution.py:442
  22.6 5.2 %collective-permute-start.8 = (bf16[272,128]{1,0:T(8,128)(2,1)S(1)}, bf16[272,128]{1,0:T(8,128)(2,1)S(1)}, u32[]{:S(2)}, u32[]{:S(2)}) collective-permute-start(bf16[272,128]{1,0:T(8,128)(2,1)S(1)} %get-tuple-element.81), channel_id=1, source_target_pairs={{0,6},{2,4},{4,2},{6,0},{8,14},{10,12},{12,10},{14,8},{16,22},{18,... | collective-permute-start | bytes 208904 | tf_op jit(solution)/shard_map/ppermute | solution.py:442
  28.4 10.1 %collective-permute-start.10 = (bf16[4,128,512]{2,1,0:T(8,128)(2,1)S(1)}, bf16[4,128,512]{2,1,0:T(8,128)(2,1)S(1)}, u32[]{:S(2)}, u32[]{:S(2)}) collective-permute-start(bf16[4,128,512]{2,1,0:T(8,128)(2,1)S(1)} %get-tuple-element.82.own), channel_id=1, source_target_pairs={{8,16},{10,18},{12,20},{14,22},{16,8},{18,10},{20,12},{22,14},{9,1... | collective-permute-start | bytes 1572872 | tf_op jit(solution)/shard_map/ppermute | solution.py:449
  29.2 13.1 %collective-permute-start.9 = (bf16[4,128,512]{2,1,0:T(8,128)(2,1)S(1)}, bf16[4,128,512]{2,1,0:T(8,128)(2,1)S(1)}, u32[]{:S(2)}, u32[]{:S(2)}) collective-permute-start(bf16[4,128,512]{2,1,0:T(8,128)(2,1)S(1)} %get-tuple-element.82.own), channel_id=1, source_target_pairs={{0,8},{2,10},{4,12},{6,14},{8,0},{10,2},{12,4},{14,6},{16,24},{18,... | collective-permute-start | bytes 1572872 | tf_op jit(solution)/shard_map/ppermute | solution.py:449
  37.7 5.7 %collective-permute-start.11 = (bf16[128,1280]{1,0:T(8,128)(2,1)S(1)}, bf16[128,1280]{1,0:T(8,128)(2,1)S(1)}, u32[]{:S(2)}, u32[]{:S(2)}) collective-permute-start(bf16[128,1280]{1,0:T(8,128)(2,1)S(1)} %get-tuple-element.86.refs_0_), channel_id=1, source_target_pairs={{0,1},{1,0},{2,3},{3,2},{4,5},{5,4},{6,7},{7,6},{8,9},{9,8},{10,11... | collective-permute-start | bytes 983048 | tf_op jit(solution)/shard_map/ppermute | solution.py:532
  38.0 5.4 %collective-permute-start.12 = (bf16[128,1280]{1,0:T(8,128)(2,1)S(1)}, bf16[128,1280]{1,0:T(8,128)(2,1)S(1)}, u32[]{:S(2)}, u32[]{:S(2)}) collective-permute-start(bf16[128,1280]{1,0:T(8,128)(2,1)S(1)} %get-tuple-element.87.refs_1_), channel_id=1, source_target_pairs={{0,1},{1,0},{2,3},{3,2},{4,5},{5,4},{6,7},{7,6},{8,9},{9,8},{10,11... | collective-permute-start | bytes 983048 | tf_op jit(solution)/shard_map/ppermute | solution.py:532
  38.3 5.1 %collective-permute-start.13 = (bf16[128,1280]{1,0:T(8,128)(2,1)S(1)}, bf16[128,1280]{1,0:T(8,128)(2,1)S(1)}, u32[]{:S(2)}, u32[]{:S(2)}) collective-permute-start(bf16[128,1280]{1,0:T(8,128)(2,1)S(1)} %get-tuple-element.88.refs_2_), channel_id=1, source_target_pairs={{0,1},{1,0},{2,3},{3,2},{4,5},{5,4},{6,7},{7,6},{8,9},{9,8},{10,11... | collective-permute-start | bytes 983048 | tf_op jit(solution)/shard_map/ppermute | solution.py:532
  38.5 4.9 %collective-permute-start.14 = (bf16[128,1280]{1,0:T(8,128)(2,1)S(1)}, bf16[128,1280]{1,0:T(8,128)(2,1)S(1)}, u32[]{:S(2)}, u32[]{:S(2)}) collective-permute-start(bf16[128,1280]{1,0:T(8,128)(2,1)S(1)} %get-tuple-element.89.refs_3_), channel_id=1, source_target_pairs={{0,1},{1,0},{2,3},{3,2},{4,5},{5,4},{6,7},{7,6},{8,9},{9,8},{10,11... | collective-permute-start | bytes 983048 | tf_op jit(solution)/shard_map/ppermute | solution.py:532
  45.9 7.6 %collective-permute-start.17 = (bf16[4,128,128]{2,1,0:T(8,128)(2,1)S(1)}, bf16[4,128,128]{2,1,0:T(8,128)(2,1)S(1)}, u32[]{:S(2)}, u32[]{:S(2)}) collective-permute-start(bf16[4,128,128]{2,1,0:T(8,128)(2,1)S(1)} %shard_map.111.refs_0_), channel_id=1, source_target_pairs={{0,6},{2,4},{4,2},{6,0},{8,14},{10,12},{12,10},{14,8},{16,22},{18,... | collective-permute-start | bytes 393224 | tf_op jit(solution)/shard_map/ppermute | solution.py:442
  47.1 6.4 %collective-permute-start.16 = (bf16[4,128,128]{2,1,0:T(8,128)(2,1)S(1)}, bf16[4,128,128]{2,1,0:T(8,128)(2,1)S(1)}, u32[]{:S(2)}, u32[]{:S(2)}) collective-permute-start(bf16[4,128,128]{2,1,0:T(8,128)(2,1)S(1)} %shard_map.111.refs_0_), channel_id=1, source_target_pairs={{0,4},{2,6},{4,0},{6,2},{8,12},{10,14},{12,8},{14,10},{16,20},{18,... | collective-permute-start | bytes 393224 | tf_op jit(solution)/shard_map/ppermute | solution.py:442
  48.5 5.0 %collective-permute-start.15 = (bf16[4,128,128]{2,1,0:T(8,128)(2,1)S(1)}, bf16[4,128,128]{2,1,0:T(8,128)(2,1)S(1)}, u32[]{:S(2)}, u32[]{:S(2)}) collective-permute-start(bf16[4,128,128]{2,1,0:T(8,128)(2,1)S(1)} %shard_map.111.refs_0_), channel_id=1, source_target_pairs={{0,2},{2,0},{4,6},{6,4},{8,10},{10,8},{12,14},{14,12},{16,18},{18,... | collective-permute-start | bytes 393224 | tf_op jit(solution)/shard_map/ppermute | solution.py:442
  57.7 6.8 %collective-permute-start.22 = (bf16[48,1024]{1,0:T(8,128)(2,1)S(1)}, bf16[48,1024]{1,0:T(8,128)(2,1)S(1)}, u32[]{:S(2)}, u32[]{:S(2)}) collective-permute-start(bf16[48,1024]{1,0:T(8,128)(2,1)S(1)} %get-tuple-element.101), channel_id=1, source_target_pairs={{0,8},{2,10},{4,12},{6,14},{8,0},{10,2},{12,4},{14,6},{16,24},{18,... | collective-permute-start | bytes 294920 | tf_op jit(solution)/shard_map/ppermute | solution.py:590
  61.2 10.4 %collective-permute-start.23 = (bf16[48,1024]{1,0:T(8,128)(2,1)S(1)}, bf16[48,1024]{1,0:T(8,128)(2,1)S(1)}, u32[]{:S(2)}, u32[]{:S(2)}) collective-permute-start(bf16[48,1024]{1,0:T(8,128)(2,1)S(1)} %get-tuple-element.107), channel_id=1, source_target_pairs={{0,16},{2,18},{4,20},{6,22},{8,24},{10,26},{12,28},{14,30},{16,0},... | collective-permute-start | bytes 294920 | tf_op jit(solution)/shard_map/ppermute | solution.py:590
  61.2 10.4 %collective-permute-start.24 = (bf16[48,1024]{1,0:T(8,128)(2,1)S(1)}, bf16[48,1024]{1,0:T(8,128)(2,1)S(1)}, u32[]{:S(2)}, u32[]{:S(2)}) collective-permute-start(bf16[48,1024]{1,0:T(8,128)(2,1)S(1)} %get-tuple-element.108), channel_id=1, source_target_pairs={{0,24},{2,26},{4,28},{6,30},{8,16},{10,18},{12,20},{14,22},{16,8},... | collective-permute-start | bytes 294920 | tf_op jit(solution)/shard_map/ppermute | solution.py:590
  64.5 7.1 %collective-permute-start.25 = (bf16[128,384]{1,0:T(8,128)(2,1)S(1)}, bf16[128,384]{1,0:T(8,128)(2,1)S(1)}, u32[]{:S(2)}, u32[]{:S(2)}) collective-permute-start(bf16[128,384]{1,0:T(8,128)(2,1)S(1)} %get-tuple-element.110), channel_id=1, source_target_pairs={{0,2},{2,0},{4,6},{6,4},{8,10},{10,8},{12,14},{14,12},{16,18},{18,... | collective-permute-start | bytes 294920 | tf_op jit(solution)/shard_map/ppermute | solution.py:442
  65.6 6.6 %collective-permute-start.26 = (bf16[128,384]{1,0:T(8,128)(2,1)S(1)}, bf16[128,384]{1,0:T(8,128)(2,1)S(1)}, u32[]{:S(2)}, u32[]{:S(2)}) collective-permute-start(bf16[128,384]{1,0:T(8,128)(2,1)S(1)} %get-tuple-element.111), channel_id=1, source_target_pairs={{0,4},{2,6},{4,0},{6,2},{8,12},{10,14},{12,8},{14,10},{16,20},{18,... | collective-permute-start | bytes 294920 | tf_op jit(solution)/shard_map/ppermute | solution.py:442
  66.2 6.0 %collective-permute-start.27 = (bf16[128,384]{1,0:T(8,128)(2,1)S(1)}, bf16[128,384]{1,0:T(8,128)(2,1)S(1)}, u32[]{:S(2)}, u32[]{:S(2)}) collective-permute-start(bf16[128,384]{1,0:T(8,128)(2,1)S(1)} %get-tuple-element.112), channel_id=1, source_target_pairs={{0,6},{2,4},{4,2},{6,0},{8,14},{10,12},{12,10},{14,8},{16,22},{18,... | collective-permute-start | bytes 294920 | tf_op jit(solution)/shard_map/ppermute | solution.py:442
  72.3 7.3 %collective-permute-start.31 = (bf16[48,1024]{1,0:T(8,128)(2,1)S(1)}, bf16[48,1024]{1,0:T(8,128)(2,1)S(1)}, u32[]{:S(2)}, u32[]{:S(2)}) collective-permute-start(bf16[48,1024]{1,0:T(8,128)(2,1)S(1)} %shard_map.114), channel_id=1, source_target_pairs={{0,16},{2,18},{4,20},{6,22},{8,24},{10,26},{12,28},{14,30},{16,0},... | collective-permute-start | bytes 294920 | tf_op jit(solution)/shard_map/ppermute | solution.py:599
  74.1 5.7 %collective-permute-start.30 = (bf16[1,48,1024]{2,1,0:T(8,128)(2,1)S(1)}, bf16[1,48,1024]{2,1,0:T(8,128)(2,1)S(1)}, u32[]{:S(2)}, u32[]{:S(2)}) collective-permute-start(bf16[1,48,1024]{2,1,0:T(8,128)(2,1)S(1)} %shard_map.115.refs_0_), channel_id=1, source_target_pairs={{0,6},{2,4},{4,2},{6,0},{8,14},{10,12},{12,10},{14,8},{16,22},{18,... | collective-permute-start | bytes 294920 | tf_op jit(solution)/shard_map/ppermute | solution.py:442
  75.9 4.8 %collective-permute-start.29 = (bf16[1,48,1024]{2,1,0:T(8,128)(2,1)S(1)}, bf16[1,48,1024]{2,1,0:T(8,128)(2,1)S(1)}, u32[]{:S(2)}, u32[]{:S(2)}) collective-permute-start(bf16[1,48,1024]{2,1,0:T(8,128)(2,1)S(1)} %shard_map.115.refs_0_), channel_id=1, source_target_pairs={{0,4},{2,6},{4,0},{6,2},{8,12},{10,14},{12,8},{14,10},{16,20},{18,... | collective-permute-start | bytes 294920 | tf_op jit(solution)/shard_map/ppermute | solution.py:442
  76.8 4.6 %collective-permute-start.28 = (bf16[1,48,1024]{2,1,0:T(8,128)(2,1)S(1)}, bf16[1,48,1024]{2,1,0:T(8,128)(2,1)S(1)}, u32[]{:S(2)}, u32[]{:S(2)}) collective-permute-start(bf16[1,48,1024]{2,1,0:T(8,128)(2,1)S(1)} %shard_map.115.refs_0_), channel_id=1, source_target_pairs={{0,2},{2,0},{4,6},{6,4},{8,10},{10,8},{12,14},{14,12},{16,18},{18,... | collective-permute-start | bytes 294920 | tf_op jit(solution)/shard_map/ppermute | solution.py:442
  79.6 5.7 %collective-permute-start.32 = (bf16[48,1024]{1,0:T(8,128)(2,1)S(1)}, bf16[48,1024]{1,0:T(8,128)(2,1)S(1)}, u32[]{:S(2)}, u32[]{:S(2)}) collective-permute-start(bf16[48,1024]{1,0:T(8,128)(2,1)S(1)} %collective-permute-done.31), channel_id=1, source_target_pairs={{0,8},{2,10},{4,12},{6,14},{8,0},{10,2},{12,4},{14,6},{16,24},{18,... | collective-permute-start | bytes 294920 | tf_op jit(solution)/shard_map/ppermute | solution.py:600
  81.5 9.3 %collective-permute-start.36 = (bf16[4,48,1024]{2,1,0:T(8,128)(2,1)S(1)}, bf16[4,48,1024]{2,1,0:T(8,128)(2,1)S(1)}, u32[]{:S(2)}, u32[]{:S(2)}) collective-permute-start(bf16[4,48,1024]{2,1,0:T(8,128)(2,1)S(1)} %pad_maximum_fusion), channel_id=1, source_target_pairs={{0,8},{2,10},{4,12},{6,14},{8,0},{10,2},{12,4},{14,6},{16,24},{18,... | collective-permute-start | bytes 1179656 | tf_op jit(solution)/shard_map/ppermute | solution.py:638
  85.4 7.4 %collective-permute-start.35 = (bf16[2,48,1024]{2,1,0:T(8,128)(2,1)S(1)}, bf16[2,48,1024]{2,1,0:T(8,128)(2,1)S(1)}, u32[]{:S(2)}, u32[]{:S(2)}) collective-permute-start(bf16[2,48,1024]{2,1,0:T(8,128)(2,1)S(1)} %pad_maximum_fusion.1.refs_5_), channel_id=1, source_target_pairs={{0,6},{2,4},{4,2},{6,0},{8,14},{10,12},{12,10},{14,8},{16,22},{18,... | collective-permute-start | bytes 589832 | tf_op jit(solution)/shard_map/ppermute | solution.py:442
  85.4 8.4 %collective-permute-start.34 = (bf16[2,48,1024]{2,1,0:T(8,128)(2,1)S(1)}, bf16[2,48,1024]{2,1,0:T(8,128)(2,1)S(1)}, u32[]{:S(2)}, u32[]{:S(2)}) collective-permute-start(bf16[2,48,1024]{2,1,0:T(8,128)(2,1)S(1)} %pad_maximum_fusion.1.refs_5_), channel_id=1, source_target_pairs={{0,4},{2,6},{4,0},{6,2},{8,12},{10,14},{12,8},{14,10},{16,20},{18,... | collective-permute-start | bytes 589832 | tf_op jit(solution)/shard_map/ppermute | solution.py:442
  88.1 5.8 %collective-permute-start.33 = (bf16[2,48,1024]{2,1,0:T(8,128)(2,1)S(1)}, bf16[2,48,1024]{2,1,0:T(8,128)(2,1)S(1)}, u32[]{:S(2)}, u32[]{:S(2)}) collective-permute-start(bf16[2,48,1024]{2,1,0:T(8,128)(2,1)S(1)} %pad_maximum_fusion.1.refs_5_), channel_id=1, source_target_pairs={{0,2},{2,0},{4,6},{6,4},{8,10},{10,8},{12,14},{14,12},{16,18},{18,... | collective-permute-start | bytes 589832 | tf_op jit(solution)/shard_map/ppermute | solution.py:442
  (7 other events, 25.4 us)

commit v9 on v8

--- a/solution.py
+++ b/solution.py
@@ -198,7 +198,7 @@
     live = jnp.int32(0)
     for e in range(e_cap):
         live = live + (coefs_s[t, e] != 0.0).astype(jnp.int32)
-    steps = [n for n in (1, 2, 3) if n < e_cap] + [e_cap]
+    steps = [n for n in ((1, 2, 3) if thirds > 1 else (2,)) if n < e_cap] + [e_cap]
     for at, count in enumerate(steps):
         least = steps[at - 1] if at else 0
 

time: 96 us -> 96.1 us (level)
  no operation moved by 1% of the time
where the time goes in v9:
time: 96.1 us; the launch traced here: 95.8 us
  starting transfers between devices  43 us (45%)
  Pallas kernels  23.6 us (25%)
  waiting for transfers between devices  20.5 us (21%)
  local copies, waits for them, and re-layouts  6.1 us (6%)
  between operations  1.76 us (2%)
    pallas_call x16, Pallas kernels, call(): pl.pallas_call(body, out_shape=out_shape, in_specs=specs, out_specs=out_s...  23.6 us
    ppermute x18, starting transfers between devices, swap(): lax.ppermute(values[k], 'elem', in_group(k))  21.3 us
    ppermute x2, starting transfers between devices, neighbours(): lax.ppermute(value, 'elem', twins)  9.23 us
    ppermute x18, waiting for transfers between devices, swap(): lax.ppermute(values[k], 'elem', in_group(k))  7.34 us
    ppermute x3, starting transfers between devices, across(): lax.ppermute(values[j], 'elem', [(i, i ^ GROUP * j) for i in range(blocks)])  5.89 us
    ppermute x3, waiting for transfers between devices, across(): lax.ppermute(values[j], 'elem', [(i, i ^ GROUP * j) for i in range(blocks)])  4.48 us
    ppermute x2, waiting for transfers between devices, neighbours(): lax.ppermute(value, 'elem', twins)  3.02 us
    ppermute x1, waiting for transfers between devices, on_device(): stack.append(lax.ppermute(stack[2], 'elem', twins))  2.64 us
  transfers between devices with their start and end apart: 37, of which 16 were waited for; matrix products, arithmetic and copies ran while one was open for 3% of the time, Pallas kernels for 16%

profile of v9, /device:TPU:0, one launch (start us, length us, event | category | flops | bytes accessed | tf_op | source)
XLA Modules:
  0.0 95.8 jit_solution(14376783521755774175)
XLA Ops:
  3.4 5.9 %collective-permute-start = (bf16[16,384]{1,0:T(8,128)(2,1)S(1)}, bf16[16,384]{1,0:T(8,128)(2,1)S(1)}, u32[]{:S(2)}, u32[]{:S(2)}) collective-permute-start(bf16[16,384]{1,0:T(8,128)(2,1)S(1)} %shard_map.103.small), channel_id=1, source_target_pairs={{0,8},{2,10},{4,12},{6,14},{8,0},{10,2},{12,4},{14,6},{16,24},{18,... | collective-permute-start | bytes 36872 | tf_op jit(solution)/shard_map/ppermute | solution.py:449
  11.4 2.4 %copy.18 = bf16[1536,2,512]{2,0,1:T(8,128)(2,1)S(1)} copy(bf16[1536,2,512]{2,1,0:T(2,128)(2,1)} %param.15) | data formatting | bytes 6291456 | tf_op jit(solution)/shard_map/optimization_barrier | solution.py:471
  13.8 1.2 %shard_map.106 = (f32[128,512]{1,0:T(8,128)S(1)}, f32[128,512]{1,0:T(8,128)S(1)}) custom-call(s32[4]{0:T(128)S(1)} %pad_add_fusion.scal, bf16[2,128,768]{2,1,0:T(8,128)(2,1)S(1)} %bitcast.18, bf16[2,1536,512]{2,1,0:T(8,128)(2,1)S(1)} %bitcast.16), custom_call_target="tpu_custom_call" | custom-call | flops 4000000000 | bytes 15625000 | tf_op jit(solution)/shard_map/pallas_call | solution.py:30
  15.0 1.6 %collective-permute-start.2 = (bf16[128,384]{1,0:T(8,128)(2,1)S(1)}, bf16[128,384]{1,0:T(8,128)(2,1)S(1)}, u32[]{:S(2)}, u32[]{:S(2)}) collective-permute-start(bf16[128,384]{1,0:T(8,128)(2,1)S(1)} %get-tuple-element.69), channel_id=1, source_target_pairs={{0,2},{2,0},{4,6},{6,4},{8,10},{10,8},{12,14},{14,12},{16,18},{18,... | collective-permute-start | bytes 294920 | tf_op jit(solution)/shard_map/ppermute | solution.py:442
  16.6 1.5 %collective-permute-start.3 = (bf16[128,384]{1,0:T(8,128)(2,1)S(1)}, bf16[128,384]{1,0:T(8,128)(2,1)S(1)}, u32[]{:S(2)}, u32[]{:S(2)}) collective-permute-start(bf16[128,384]{1,0:T(8,128)(2,1)S(1)} %get-tuple-element.70), channel_id=1, source_target_pairs={{0,4},{2,6},{4,0},{6,2},{8,12},{10,14},{12,8},{14,10},{16,20},{18,... | collective-permute-start | bytes 294920 | tf_op jit(solution)/shard_map/ppermute | solution.py:442
  19.5 1.6 %collective-permute-start.6 = (bf16[272,128]{1,0:T(8,128)(2,1)S(1)}, bf16[272,128]{1,0:T(8,128)(2,1)S(1)}, u32[]{:S(2)}, u32[]{:S(2)}) collective-permute-start(bf16[272,128]{1,0:T(8,128)(2,1)S(1)} %get-tuple-element.79), channel_id=1, source_target_pairs={{0,2},{2,0},{4,6},{6,4},{8,10},{10,8},{12,14},{14,12},{16,18},{18,... | collective-permute-start | bytes 208904 | tf_op jit(solution)/shard_map/ppermute | solution.py:442
  21.1 1.5 %collective-permute-start.7 = (bf16[272,128]{1,0:T(8,128)(2,1)S(1)}, bf16[272,128]{1,0:T(8,128)(2,1)S(1)}, u32[]{:S(2)}, u32[]{:S(2)}) collective-permute-start(bf16[272,128]{1,0:T(8,128)(2,1)S(1)} %get-tuple-element.80), channel_id=1, source_target_pairs={{0,4},{2,6},{4,0},{6,2},{8,12},{10,14},{12,8},{14,10},{16,20},{18,... | collective-permute-start | bytes 208904 | tf_op jit(solution)/shard_map/ppermute | solution.py:442
  23.1 1.3 %collective-permute-done.4.a3 = bf16[128,384]{1,0:T(8,128)(2,1)S(1)} collective-permute-done((bf16[128,384]{1,0:T(8,128)(2,1)S(1)}, bf16[128,384]{1,0:T(8,128)(2,1)S(1)}, u32[]{:S(2)}, u32[]{:S(2)}) %collective-permute-start.4) | collective-permute-done | bytes 98336 | tf_op jit(solution)/shard_map/ppermute | solution.py:442
  26.1 1.7 %collective-permute-done.8.a3 = bf16[272,128]{1,0:T(8,128)(2,1)S(1)} collective-permute-done((bf16[272,128]{1,0:T(8,128)(2,1)S(1)}, bf16[272,128]{1,0:T(8,128)(2,1)S(1)}, u32[]{:S(2)}, u32[]{:S(2)}) %collective-permute-start.8) | collective-permute-done | bytes 69664 | tf_op jit(solution)/shard_map/ppermute | solution.py:442
  29.2 3.3 %collective-permute-start.9 = (bf16[4,128,512]{2,1,0:T(8,128)(2,1)S(1)}, bf16[4,128,512]{2,1,0:T(8,128)(2,1)S(1)}, u32[]{:S(2)}, u32[]{:S(2)}) collective-permute-start(bf16[4,128,512]{2,1,0:T(8,128)(2,1)S(1)} %get-tuple-element.82.own), channel_id=1, source_target_pairs={{0,8},{2,10},{4,12},{6,14},{8,0},{10,2},{12,4},{14,6},{16,24},{18,... | collective-permute-start | bytes 1572872 | tf_op jit(solution)/shard_map/ppermute | solution.py:449
  32.5 5.0 %shard_map.110 = (bf16[128,1280]{1,0:T(8,128)(2,1)S(1)}, bf16[128,1280]{1,0:T(8,128)(2,1)S(1)}, bf16[128,1280]{1,0:T(8,128)(2,1)S(1)}, bf16[128,1280]{1,0:T(8,128)(2,1)S(1)}) custom-call(s32[4]{0:T(128)S(1)} %pad_add_fusion.scal, s32[1]{0:T(128)} %bitcast.2.side_s, bf16[4,144,128]{2,1,0:T(8,128)(2,1)S(1)} %get-tuple-element.83.small, ...), custom_call_target="tpu_custom_call" | custom-call | flops 2717908992 | bytes 2621440 | tf_op jit(solution)/shard_map/pallas_call | solution.py:30
  37.5 1.2 %collective-permute-start.11 = (bf16[128,1280]{1,0:T(8,128)(2,1)S(1)}, bf16[128,1280]{1,0:T(8,128)(2,1)S(1)}, u32[]{:S(2)}, u32[]{:S(2)}) collective-permute-start(bf16[128,1280]{1,0:T(8,128)(2,1)S(1)} %get-tuple-element.86.refs_0_), channel_id=1, source_target_pairs={{0,1},{1,0},{2,3},{3,2},{4,5},{5,4},{6,7},{7,6},{8,9},{9,8},{10,11... | collective-permute-start | bytes 983048 | tf_op jit(solution)/shard_map/ppermute | solution.py:532
  39.3 3.0 %collective-permute-done.9.twin = bf16[4,128,512]{2,1,0:T(8,128)(2,1)S(1)} collective-permute-done((bf16[4,128,512]{2,1,0:T(8,128)(2,1)S(1)}, bf16[4,128,512]{2,1,0:T(8,128)(2,1)S(1)}, u32[]{:S(2)}, u32[]{:S(2)}) %collective-permute-start.9) | collective-permute-done | bytes 524320 | tf_op jit(solution)/shard_map/ppermute | solution.py:449
  42.3 1.3 %shard_map.109 = (bf16[1536,512]{1,0:T(8,128)(2,1)S(1)}, f32[8,128,128]{2,1,0:T(8,128)S(1)}) custom-call(s32[4]{0:T(128)S(1)} %pad_add_fusion.scal, bf16[4,128,512]{2,1,0:T(8,128)(2,1)S(1)} %get-tuple-element.82.own, bf16[4,128,512]{2,1,0:T(8,128)(2,1)S(1)} %collective-permute-done.9.twin, bf16[4,128,512]{2,1,0:T(8,128)(2,1)S(1)} %collective-permute-done.10.next_, ...), custom_call_target="tpu_custom_call" | custom-call | tf_op jit(solution)/shard_map/pallas_call | solution.py:30
  43.7 2.4 %shard_map.111.refs_0_ = bf16[4,128,128]{2,1,0:T(8,128)(2,1)S(1)} custom-call(s32[4]{0:T(128)S(1)} %pad_add_fusion.scal, s32[1]{0:T(128)} %bitcast.2.side_s, bf16[1536,512]{1,0:T(8,128)(2,1)S(1)} %get-tuple-element.84.vec, f32[8,128,128]{2,1,0:T(8,128)S(1)} %get-tuple-element.85.cols, bf16[128,1280]{1,0:T(8,128)(2,1)S(1)} %get-tuple-element.86.refs_0_, ...), custom_call_target="tpu_custom_call" | custom-call | flops 503316480 | bytes 2621440 | tf_op jit(solution)/shard_map/pallas_call | solution.py:30
  46.1 1.2 %collective-permute-start.17 = (bf16[4,128,128]{2,1,0:T(8,128)(2,1)S(1)}, bf16[4,128,128]{2,1,0:T(8,128)(2,1)S(1)}, u32[]{:S(2)}, u32[]{:S(2)}) collective-permute-start(bf16[4,128,128]{2,1,0:T(8,128)(2,1)S(1)} %shard_map.111.refs_0_), channel_id=1, source_target_pairs={{0,6},{2,4},{4,2},{6,0},{8,14},{10,12},{12,10},{14,8},{16,22},{18,... | collective-permute-start | bytes 393224 | tf_op jit(solution)/shard_map/ppermute | solution.py:442
  47.3 1.4 %collective-permute-start.16 = (bf16[4,128,128]{2,1,0:T(8,128)(2,1)S(1)}, bf16[4,128,128]{2,1,0:T(8,128)(2,1)S(1)}, u32[]{:S(2)}, u32[]{:S(2)}) collective-permute-start(bf16[4,128,128]{2,1,0:T(8,128)(2,1)S(1)} %shard_map.111.refs_0_), channel_id=1, source_target_pairs={{0,4},{2,6},{4,0},{6,2},{8,12},{10,14},{12,8},{14,10},{16,20},{18,... | collective-permute-start | bytes 393224 | tf_op jit(solution)/shard_map/ppermute | solution.py:442
  49.7 4.1 %shard_map.112 = (bf16[128,384]{1,0:T(8,128)(2,1)S(1)}, bf16[128,384]{1,0:T(8,128)(2,1)S(1)}, bf16[128,384]{1,0:T(8,128)(2,1)S(1)}, bf16[128,384]{1,0:T(8,128)(2,1)S(1)}, bf16[384,512]{1,0:T(8,128)(2,1)S(1)}) custom-call(s32[4]{0:T(128)S(1)} %pad_add_fusion.scal, s32[1]{0:T(128)} %bitcast.2.side_s, bf16[1536,512]{1,0:T(8,128)(2,1)S(1)} %get-tuple-element.84.vec, ...), custom_call_target="tpu_custom_call" | custom-call | flops 1509949440 | bytes 2621440 | tf_op jit(solution)/shard_map/pallas_call | solution.py:30
  55.9 2.0 %shard_map.113 = (bf16[48,1024]{1,0:T(8,128)(2,1)S(1)}, bf16[48,1024]{1,0:T(8,128)(2,1)S(1)}, bf16[48,1024]{1,0:T(8,128)(2,1)S(1)}, bf16[48,1024]{1,0:T(8,128)(2,1)S(1)}, bf16[2,128,256]{2,1,0:T(8,128)(2,1)S(1)}) custom-call(s32[4]{0:T(128)S(1)} %pad_add_fusion.scal, bf16[384,512]{1,0:T(8,128)(2,1)S(1)} %get-tuple-element.95.left, ...), custom_call_target="tpu_custom_call" | custom-call | flops 402653184 | bytes 1048576 | tf_op jit(solution)/shard_map/pallas_call | solution.py:30
  57.9 3.4 %collective-permute-start.22 = (bf16[48,1024]{1,0:T(8,128)(2,1)S(1)}, bf16[48,1024]{1,0:T(8,128)(2,1)S(1)}, u32[]{:S(2)}, u32[]{:S(2)}) collective-permute-start(bf16[48,1024]{1,0:T(8,128)(2,1)S(1)} %get-tuple-element.101), channel_id=1, source_target_pairs={{0,8},{2,10},{4,12},{6,14},{8,0},{10,2},{12,4},{14,6},{16,24},{18,... | collective-permute-start | bytes 294920 | tf_op jit(solution)/shard_map/ppermute | solution.py:590
  61.3 2.4 %collective-permute-start.24 = (bf16[48,1024]{1,0:T(8,128)(2,1)S(1)}, bf16[48,1024]{1,0:T(8,128)(2,1)S(1)}, u32[]{:S(2)}, u32[]{:S(2)}) collective-permute-start(bf16[48,1024]{1,0:T(8,128)(2,1)S(1)} %get-tuple-element.108), channel_id=1, source_target_pairs={{0,24},{2,26},{4,28},{6,30},{8,16},{10,18},{12,20},{14,22},{16,8},... | collective-permute-start | bytes 294920 | tf_op jit(solution)/shard_map/ppermute | solution.py:590
  64.6 1.2 %collective-permute-start.25 = (bf16[128,384]{1,0:T(8,128)(2,1)S(1)}, bf16[128,384]{1,0:T(8,128)(2,1)S(1)}, u32[]{:S(2)}, u32[]{:S(2)}) collective-permute-start(bf16[128,384]{1,0:T(8,128)(2,1)S(1)} %get-tuple-element.110), channel_id=1, source_target_pairs={{0,2},{2,0},{4,6},{6,4},{8,10},{10,8},{12,14},{14,12},{16,18},{18,... | collective-permute-start | bytes 294920 | tf_op jit(solution)/shard_map/ppermute | solution.py:442
  66.4 1.7 %collective-permute-start.27 = (bf16[128,384]{1,0:T(8,128)(2,1)S(1)}, bf16[128,384]{1,0:T(8,128)(2,1)S(1)}, u32[]{:S(2)}, u32[]{:S(2)}) collective-permute-start(bf16[128,384]{1,0:T(8,128)(2,1)S(1)} %get-tuple-element.112), channel_id=1, source_target_pairs={{0,6},{2,4},{4,2},{6,0},{8,14},{10,12},{12,10},{14,8},{16,22},{18,... | collective-permute-start | bytes 294920 | tf_op jit(solution)/shard_map/ppermute | solution.py:442
  68.1 3.6 %collective-permute-done.23.s2 = bf16[48,1024]{1,0:T(8,128)(2,1)S(1)} collective-permute-done((bf16[48,1024]{1,0:T(8,128)(2,1)S(1)}, bf16[48,1024]{1,0:T(8,128)(2,1)S(1)}, u32[]{:S(2)}, u32[]{:S(2)}) %collective-permute-start.23) | collective-permute-done | bytes 98336 | tf_op jit(solution)/shard_map/ppermute | solution.py:590
  72.4 1.8 %collective-permute-start.31 = (bf16[48,1024]{1,0:T(8,128)(2,1)S(1)}, bf16[48,1024]{1,0:T(8,128)(2,1)S(1)}, u32[]{:S(2)}, u32[]{:S(2)}) collective-permute-start(bf16[48,1024]{1,0:T(8,128)(2,1)S(1)} %shard_map.114), channel_id=1, source_target_pairs={{0,16},{2,18},{4,20},{6,22},{8,24},{10,26},{12,28},{14,30},{16,0},... | collective-permute-start | bytes 294920 | tf_op jit(solution)/shard_map/ppermute | solution.py:599
  74.2 1.8 %collective-permute-start.30 = (bf16[1,48,1024]{2,1,0:T(8,128)(2,1)S(1)}, bf16[1,48,1024]{2,1,0:T(8,128)(2,1)S(1)}, u32[]{:S(2)}, u32[]{:S(2)}) collective-permute-start(bf16[1,48,1024]{2,1,0:T(8,128)(2,1)S(1)} %shard_map.115.refs_0_), channel_id=1, source_target_pairs={{0,6},{2,4},{4,2},{6,0},{8,14},{10,12},{12,10},{14,8},{16,22},{18,... | collective-permute-start | bytes 294920 | tf_op jit(solution)/shard_map/ppermute | solution.py:442
  77.8 2.0 %collective-permute-done.31 = bf16[48,1024]{1,0:T(8,128)(2,1)S(1)} collective-permute-done((bf16[48,1024]{1,0:T(8,128)(2,1)S(1)}, bf16[48,1024]{1,0:T(8,128)(2,1)S(1)}, u32[]{:S(2)}, u32[]{:S(2)}) %collective-permute-start.31) | collective-permute-done | bytes 98336 | tf_op jit(solution)/shard_map/ppermute | solution.py:599
  82.9 2.6 %collective-permute-done.32 = bf16[48,1024]{1,0:T(8,128)(2,1)S(1)} collective-permute-done((bf16[48,1024]{1,0:T(8,128)(2,1)S(1)}, bf16[48,1024]{1,0:T(8,128)(2,1)S(1)}, u32[]{:S(2)}, u32[]{:S(2)}) %collective-permute-start.32) | collective-permute-done | bytes 98336 | tf_op jit(solution)/shard_map/ppermute | solution.py:600
  85.6 2.6 %collective-permute-start.34 = (bf16[2,48,1024]{2,1,0:T(8,128)(2,1)S(1)}, bf16[2,48,1024]{2,1,0:T(8,128)(2,1)S(1)}, u32[]{:S(2)}, u32[]{:S(2)}) collective-permute-start(bf16[2,48,1024]{2,1,0:T(8,128)(2,1)S(1)} %pad_maximum_fusion.1.refs_5_), channel_id=1, source_target_pairs={{0,4},{2,6},{4,0},{6,2},{8,12},{10,14},{12,8},{14,10},{16,20},{18,... | collective-permute-start | bytes 589832 | tf_op jit(solution)/shard_map/ppermute | solution.py:442
  89.1 1.1 %copy.14 = bf16[128,2,768]{2,1,0:T(2,128)(2,1)} copy(bf16[128,2,768]{2,0,1:T(8,128)(2,1)S(1)} %bitcast.19) | data formatting | bytes 786432
  91.0 1.9 %shard_map.117.refs_3_ = f32[768,2,512]{2,1,0:T(2,128)} custom-call(s32[4]{0:T(128)S(1)} %pad_add_fusion.scal, bf16[1,48,1024]{2,1,0:T(8,128)(2,1)S(1)} %shard_map.115.refs_0_, bf16[1,48,1024]{2,1,0:T(8,128)(2,1)S(1)} %collective-permute-done.28.refs_1_, bf16[1,48,1024]{2,1,0:T(8,128)(2,1)S(1)} %collective-permute-done.29.refs_2_, ...), custom_call_target="tpu_custom_call" | custom-call | tf_op jit(solution)/shard_map/pallas_call | solution.py:30
  94.0 1.6 %shard_map.118 = f32[768,2,512]{2,1,0:T(2,128)} custom-call(s32[4]{0:T(128)S(1)} %pad_add_fusion.scal, bf16[2,48,1024]{2,1,0:T(8,128)(2,1)S(1)} %collective-permute-done.33.refs_0_, bf16[2,48,1024]{2,1,0:T(8,128)(2,1)S(1)} %collective-permute-done.34.refs_1_, ...), custom_call_target="tpu_custom_call", output_to_operand_aliasing={{}: (4, {})} | custom-call | tf_op jit(solution)/shard_map/pallas_call | solution.py:30
  (72 shorter events, 22.5 us)
Async XLA Ops:
  2.7 8.6 %collective-permute-start.1 = (bf16[16,384]{1,0:T(8,128)(2,1)S(1)}, bf16[16,384]{1,0:T(8,128)(2,1)S(1)}, u32[]{:S(2)}, u32[]{:S(2)}) collective-permute-start(bf16[16,384]{1,0:T(8,128)(2,1)S(1)} %shard_map.103.small), channel_id=1, source_target_pairs={{8,16},{10,18},{12,20},{14,22},{16,8},{18,10},{20,12},{22,14},{9,1... | collective-permute-start | bytes 36872 | tf_op jit(solution)/shard_map/ppermute | solution.py:449
  3.4 8.0 %collective-permute-start = (bf16[16,384]{1,0:T(8,128)(2,1)S(1)}, bf16[16,384]{1,0:T(8,128)(2,1)S(1)}, u32[]{:S(2)}, u32[]{:S(2)}) collective-permute-start(bf16[16,384]{1,0:T(8,128)(2,1)S(1)} %shard_map.103.small), channel_id=1, source_target_pairs={{0,8},{2,10},{4,12},{6,14},{8,0},{10,2},{12,4},{14,6},{16,24},{18,... | collective-permute-start | bytes 36872 | tf_op jit(solution)/shard_map/ppermute | solution.py:449
  15.0 7.6 %collective-permute-start.2 = (bf16[128,384]{1,0:T(8,128)(2,1)S(1)}, bf16[128,384]{1,0:T(8,128)(2,1)S(1)}, u32[]{:S(2)}, u32[]{:S(2)}) collective-permute-start(bf16[128,384]{1,0:T(8,128)(2,1)S(1)} %get-tuple-element.69), channel_id=1, source_target_pairs={{0,2},{2,0},{4,6},{6,4},{8,10},{10,8},{12,14},{14,12},{16,18},{18,... | collective-permute-start | bytes 294920 | tf_op jit(solution)/shard_map/ppermute | solution.py:442
  16.6 6.6 %collective-permute-start.3 = (bf16[128,384]{1,0:T(8,128)(2,1)S(1)}, bf16[128,384]{1,0:T(8,128)(2,1)S(1)}, u32[]{:S(2)}, u32[]{:S(2)}) collective-permute-start(bf16[128,384]{1,0:T(8,128)(2,1)S(1)} %get-tuple-element.70), channel_id=1, source_target_pairs={{0,4},{2,6},{4,0},{6,2},{8,12},{10,14},{12,8},{14,10},{16,20},{18,... | collective-permute-start | bytes 294920 | tf_op jit(solution)/shard_map/ppermute | solution.py:442
  18.1 6.4 %collective-permute-start.4 = (bf16[128,384]{1,0:T(8,128)(2,1)S(1)}, bf16[128,384]{1,0:T(8,128)(2,1)S(1)}, u32[]{:S(2)}, u32[]{:S(2)}) collective-permute-start(bf16[128,384]{1,0:T(8,128)(2,1)S(1)} %get-tuple-element.71), channel_id=1, source_target_pairs={{0,6},{2,4},{4,2},{6,0},{8,14},{10,12},{12,10},{14,8},{16,22},{18,... | collective-permute-start | bytes 294920 | tf_op jit(solution)/shard_map/ppermute | solution.py:442
  19.5 5.6 %collective-permute-start.6 = (bf16[272,128]{1,0:T(8,128)(2,1)S(1)}, bf16[272,128]{1,0:T(8,128)(2,1)S(1)}, u32[]{:S(2)}, u32[]{:S(2)}) collective-permute-start(bf16[272,128]{1,0:T(8,128)(2,1)S(1)} %get-tuple-element.79), channel_id=1, source_target_pairs={{0,2},{2,0},{4,6},{6,4},{8,10},{10,8},{12,14},{14,12},{16,18},{18,... | collective-permute-start | bytes 208904 | tf_op jit(solution)/shard_map/ppermute | solution.py:442
  21.1 5.1 %collective-permute-start.7 = (bf16[272,128]{1,0:T(8,128)(2,1)S(1)}, bf16[272,128]{1,0:T(8,128)(2,1)S(1)}, u32[]{:S(2)}, u32[]{:S(2)}) collective-permute-start(bf16[272,128]{1,0:T(8,128)(2,1)S(1)} %get-tuple-element.80), channel_id=1, source_target_pairs={{0,4},{2,6},{4,0},{6,2},{8,12},{10,14},{12,8},{14,10},{16,20},{18,... | collective-permute-start | bytes 208904 | tf_op jit(solution)/shard_map/ppermute | solution.py:442
  22.6 5.2 %collective-permute-start.8 = (bf16[272,128]{1,0:T(8,128)(2,1)S(1)}, bf16[272,128]{1,0:T(8,128)(2,1)S(1)}, u32[]{:S(2)}, u32[]{:S(2)}) collective-permute-start(bf16[272,128]{1,0:T(8,128)(2,1)S(1)} %get-tuple-element.81), channel_id=1, source_target_pairs={{0,6},{2,4},{4,2},{6,0},{8,14},{10,12},{12,10},{14,8},{16,22},{18,... | collective-permute-start | bytes 208904 | tf_op jit(solution)/shard_map/ppermute | solution.py:442
  28.4 10.8 %collective-permute-start.10 = (bf16[4,128,512]{2,1,0:T(8,128)(2,1)S(1)}, bf16[4,128,512]{2,1,0:T(8,128)(2,1)S(1)}, u32[]{:S(2)}, u32[]{:S(2)}) collective-permute-start(bf16[4,128,512]{2,1,0:T(8,128)(2,1)S(1)} %get-tuple-element.82.own), channel_id=1, source_target_pairs={{8,16},{10,18},{12,20},{14,22},{16,8},{18,10},{20,12},{22,14},{9,1... | collective-permute-start | bytes 1572872 | tf_op jit(solution)/shard_map/ppermute | solution.py:449
  29.2 13.1 %collective-permute-start.9 = (bf16[4,128,512]{2,1,0:T(8,128)(2,1)S(1)}, bf16[4,128,512]{2,1,0:T(8,128)(2,1)S(1)}, u32[]{:S(2)}, u32[]{:S(2)}) collective-permute-start(bf16[4,128,512]{2,1,0:T(8,128)(2,1)S(1)} %get-tuple-element.82.own), channel_id=1, source_target_pairs={{0,8},{2,10},{4,12},{6,14},{8,0},{10,2},{12,4},{14,6},{16,24},{18,... | collective-permute-start | bytes 1572872 | tf_op jit(solution)/shard_map/ppermute | solution.py:449
  37.5 6.1 %collective-permute-start.11 = (bf16[128,1280]{1,0:T(8,128)(2,1)S(1)}, bf16[128,1280]{1,0:T(8,128)(2,1)S(1)}, u32[]{:S(2)}, u32[]{:S(2)}) collective-permute-start(bf16[128,1280]{1,0:T(8,128)(2,1)S(1)} %get-tuple-element.86.refs_0_), channel_id=1, source_target_pairs={{0,1},{1,0},{2,3},{3,2},{4,5},{5,4},{6,7},{7,6},{8,9},{9,8},{10,11... | collective-permute-start | bytes 983048 | tf_op jit(solution)/shard_map/ppermute | solution.py:532
  38.7 5.0 %collective-permute-start.12 = (bf16[128,1280]{1,0:T(8,128)(2,1)S(1)}, bf16[128,1280]{1,0:T(8,128)(2,1)S(1)}, u32[]{:S(2)}, u32[]{:S(2)}) collective-permute-start(bf16[128,1280]{1,0:T(8,128)(2,1)S(1)} %get-tuple-element.87.refs_1_), channel_id=1, source_target_pairs={{0,1},{1,0},{2,3},{3,2},{4,5},{5,4},{6,7},{7,6},{8,9},{9,8},{10,11... | collective-permute-start | bytes 983048 | tf_op jit(solution)/shard_map/ppermute | solution.py:532
  38.8 4.9 %collective-permute-start.13 = (bf16[128,1280]{1,0:T(8,128)(2,1)S(1)}, bf16[128,1280]{1,0:T(8,128)(2,1)S(1)}, u32[]{:S(2)}, u32[]{:S(2)}) collective-permute-start(bf16[128,1280]{1,0:T(8,128)(2,1)S(1)} %get-tuple-element.88.refs_2_), channel_id=1, source_target_pairs={{0,1},{1,0},{2,3},{3,2},{4,5},{5,4},{6,7},{7,6},{8,9},{9,8},{10,11... | collective-permute-start | bytes 983048 | tf_op jit(solution)/shard_map/ppermute | solution.py:532
  39.2 4.5 %collective-permute-start.14 = (bf16[128,1280]{1,0:T(8,128)(2,1)S(1)}, bf16[128,1280]{1,0:T(8,128)(2,1)S(1)}, u32[]{:S(2)}, u32[]{:S(2)}) collective-permute-start(bf16[128,1280]{1,0:T(8,128)(2,1)S(1)} %get-tuple-element.89.refs_3_), channel_id=1, source_target_pairs={{0,1},{1,0},{2,3},{3,2},{4,5},{5,4},{6,7},{7,6},{8,9},{9,8},{10,11... | collective-permute-start | bytes 983048 | tf_op jit(solution)/shard_map/ppermute | solution.py:532
  46.1 7.6 %collective-permute-start.17 = (bf16[4,128,128]{2,1,0:T(8,128)(2,1)S(1)}, bf16[4,128,128]{2,1,0:T(8,128)(2,1)S(1)}, u32[]{:S(2)}, u32[]{:S(2)}) collective-permute-start(bf16[4,128,128]{2,1,0:T(8,128)(2,1)S(1)} %shard_map.111.refs_0_), channel_id=1, source_target_pairs={{0,6},{2,4},{4,2},{6,0},{8,14},{10,12},{12,10},{14,8},{16,22},{18,... | collective-permute-start | bytes 393224 | tf_op jit(solution)/shard_map/ppermute | solution.py:442
  47.3 6.4 %collective-permute-start.16 = (bf16[4,128,128]{2,1,0:T(8,128)(2,1)S(1)}, bf16[4,128,128]{2,1,0:T(8,128)(2,1)S(1)}, u32[]{:S(2)}, u32[]{:S(2)}) collective-permute-start(bf16[4,128,128]{2,1,0:T(8,128)(2,1)S(1)} %shard_map.111.refs_0_), channel_id=1, source_target_pairs={{0,4},{2,6},{4,0},{6,2},{8,12},{10,14},{12,8},{14,10},{16,20},{18,... | collective-permute-start | bytes 393224 | tf_op jit(solution)/shard_map/ppermute | solution.py:442
  48.7 5.0 %collective-permute-start.15 = (bf16[4,128,128]{2,1,0:T(8,128)(2,1)S(1)}, bf16[4,128,128]{2,1,0:T(8,128)(2,1)S(1)}, u32[]{:S(2)}, u32[]{:S(2)}) collective-permute-start(bf16[4,128,128]{2,1,0:T(8,128)(2,1)S(1)} %shard_map.111.refs_0_), channel_id=1, source_target_pairs={{0,2},{2,0},{4,6},{6,4},{8,10},{10,8},{12,14},{14,12},{16,18},{18,... | collective-permute-start | bytes 393224 | tf_op jit(solution)/shard_map/ppermute | solution.py:442
  57.9 6.7 %collective-permute-start.22 = (bf16[48,1024]{1,0:T(8,128)(2,1)S(1)}, bf16[48,1024]{1,0:T(8,128)(2,1)S(1)}, u32[]{:S(2)}, u32[]{:S(2)}) collective-permute-start(bf16[48,1024]{1,0:T(8,128)(2,1)S(1)} %get-tuple-element.101), channel_id=1, source_target_pairs={{0,8},{2,10},{4,12},{6,14},{8,0},{10,2},{12,4},{14,6},{16,24},{18,... | collective-permute-start | bytes 294920 | tf_op jit(solution)/shard_map/ppermute | solution.py:590
  61.3 10.4 %collective-permute-start.23 = (bf16[48,1024]{1,0:T(8,128)(2,1)S(1)}, bf16[48,1024]{1,0:T(8,128)(2,1)S(1)}, u32[]{:S(2)}, u32[]{:S(2)}) collective-permute-start(bf16[48,1024]{1,0:T(8,128)(2,1)S(1)} %get-tuple-element.107), channel_id=1, source_target_pairs={{0,16},{2,18},{4,20},{6,22},{8,24},{10,26},{12,28},{14,30},{16,0},... | collective-permute-start | bytes 294920 | tf_op jit(solution)/shard_map/ppermute | solution.py:590
  61.3 10.4 %collective-permute-start.24 = (bf16[48,1024]{1,0:T(8,128)(2,1)S(1)}, bf16[48,1024]{1,0:T(8,128)(2,1)S(1)}, u32[]{:S(2)}, u32[]{:S(2)}) collective-permute-start(bf16[48,1024]{1,0:T(8,128)(2,1)S(1)} %get-tuple-element.108), channel_id=1, source_target_pairs={{0,24},{2,26},{4,28},{6,30},{8,16},{10,18},{12,20},{14,22},{16,8},... | collective-permute-start | bytes 294920 | tf_op jit(solution)/shard_map/ppermute | solution.py:590
  64.6 7.1 %collective-permute-start.25 = (bf16[128,384]{1,0:T(8,128)(2,1)S(1)}, bf16[128,384]{1,0:T(8,128)(2,1)S(1)}, u32[]{:S(2)}, u32[]{:S(2)}) collective-permute-start(bf16[128,384]{1,0:T(8,128)(2,1)S(1)} %get-tuple-element.110), channel_id=1, source_target_pairs={{0,2},{2,0},{4,6},{6,4},{8,10},{10,8},{12,14},{14,12},{16,18},{18,... | collective-permute-start | bytes 294920 | tf_op jit(solution)/shard_map/ppermute | solution.py:442
  65.8 6.6 %collective-permute-start.26 = (bf16[128,384]{1,0:T(8,128)(2,1)S(1)}, bf16[128,384]{1,0:T(8,128)(2,1)S(1)}, u32[]{:S(2)}, u32[]{:S(2)}) collective-permute-start(bf16[128,384]{1,0:T(8,128)(2,1)S(1)} %get-tuple-element.111), channel_id=1, source_target_pairs={{0,4},{2,6},{4,0},{6,2},{8,12},{10,14},{12,8},{14,10},{16,20},{18,... | collective-permute-start | bytes 294920 | tf_op jit(solution)/shard_map/ppermute | solution.py:442
  66.4 6.0 %collective-permute-start.27 = (bf16[128,384]{1,0:T(8,128)(2,1)S(1)}, bf16[128,384]{1,0:T(8,128)(2,1)S(1)}, u32[]{:S(2)}, u32[]{:S(2)}) collective-permute-start(bf16[128,384]{1,0:T(8,128)(2,1)S(1)} %get-tuple-element.112), channel_id=1, source_target_pairs={{0,6},{2,4},{4,2},{6,0},{8,14},{10,12},{12,10},{14,8},{16,22},{18,... | collective-permute-start | bytes 294920 | tf_op jit(solution)/shard_map/ppermute | solution.py:442
  72.4 7.3 %collective-permute-start.31 = (bf16[48,1024]{1,0:T(8,128)(2,1)S(1)}, bf16[48,1024]{1,0:T(8,128)(2,1)S(1)}, u32[]{:S(2)}, u32[]{:S(2)}) collective-permute-start(bf16[48,1024]{1,0:T(8,128)(2,1)S(1)} %shard_map.114), channel_id=1, source_target_pairs={{0,16},{2,18},{4,20},{6,22},{8,24},{10,26},{12,28},{14,30},{16,0},... | collective-permute-start | bytes 294920 | tf_op jit(solution)/shard_map/ppermute | solution.py:599
  74.2 5.7 %collective-permute-start.30 = (bf16[1,48,1024]{2,1,0:T(8,128)(2,1)S(1)}, bf16[1,48,1024]{2,1,0:T(8,128)(2,1)S(1)}, u32[]{:S(2)}, u32[]{:S(2)}) collective-permute-start(bf16[1,48,1024]{2,1,0:T(8,128)(2,1)S(1)} %shard_map.115.refs_0_), channel_id=1, source_target_pairs={{0,6},{2,4},{4,2},{6,0},{8,14},{10,12},{12,10},{14,8},{16,22},{18,... | collective-permute-start | bytes 294920 | tf_op jit(solution)/shard_map/ppermute | solution.py:442
  76.0 4.8 %collective-permute-start.29 = (bf16[1,48,1024]{2,1,0:T(8,128)(2,1)S(1)}, bf16[1,48,1024]{2,1,0:T(8,128)(2,1)S(1)}, u32[]{:S(2)}, u32[]{:S(2)}) collective-permute-start(bf16[1,48,1024]{2,1,0:T(8,128)(2,1)S(1)} %shard_map.115.refs_0_), channel_id=1, source_target_pairs={{0,4},{2,6},{4,0},{6,2},{8,12},{10,14},{12,8},{14,10},{16,20},{18,... | collective-permute-start | bytes 294920 | tf_op jit(solution)/shard_map/ppermute | solution.py:442
  77.0 4.6 %collective-permute-start.28 = (bf16[1,48,1024]{2,1,0:T(8,128)(2,1)S(1)}, bf16[1,48,1024]{2,1,0:T(8,128)(2,1)S(1)}, u32[]{:S(2)}, u32[]{:S(2)}) collective-permute-start(bf16[1,48,1024]{2,1,0:T(8,128)(2,1)S(1)} %shard_map.115.refs_0_), channel_id=1, source_target_pairs={{0,2},{2,0},{4,6},{6,4},{8,10},{10,8},{12,14},{14,12},{16,18},{18,... | collective-permute-start | bytes 294920 | tf_op jit(solution)/shard_map/ppermute | solution.py:442
  79.8 5.7 %collective-permute-start.32 = (bf16[48,1024]{1,0:T(8,128)(2,1)S(1)}, bf16[48,1024]{1,0:T(8,128)(2,1)S(1)}, u32[]{:S(2)}, u32[]{:S(2)}) collective-permute-start(bf16[48,1024]{1,0:T(8,128)(2,1)S(1)} %collective-permute-done.31), channel_id=1, source_target_pairs={{0,8},{2,10},{4,12},{6,14},{8,0},{10,2},{12,4},{14,6},{16,24},{18,... | collective-permute-start | bytes 294920 | tf_op jit(solution)/shard_map/ppermute | solution.py:600
  81.6 9.4 %collective-permute-start.36 = (bf16[4,48,1024]{2,1,0:T(8,128)(2,1)S(1)}, bf16[4,48,1024]{2,1,0:T(8,128)(2,1)S(1)}, u32[]{:S(2)}, u32[]{:S(2)}) collective-permute-start(bf16[4,48,1024]{2,1,0:T(8,128)(2,1)S(1)} %pad_maximum_fusion), channel_id=1, source_target_pairs={{0,8},{2,10},{4,12},{6,14},{8,0},{10,2},{12,4},{14,6},{16,24},{18,... | collective-permute-start | bytes 1179656 | tf_op jit(solution)/shard_map/ppermute | solution.py:638
  85.5 7.4 %collective-permute-start.35 = (bf16[2,48,1024]{2,1,0:T(8,128)(2,1)S(1)}, bf16[2,48,1024]{2,1,0:T(8,128)(2,1)S(1)}, u32[]{:S(2)}, u32[]{:S(2)}) collective-permute-start(bf16[2,48,1024]{2,1,0:T(8,128)(2,1)S(1)} %pad_maximum_fusion.1.refs_5_), channel_id=1, source_target_pairs={{0,6},{2,4},{4,2},{6,0},{8,14},{10,12},{12,10},{14,8},{16,22},{18,... | collective-permute-start | bytes 589832 | tf_op jit(solution)/shard_map/ppermute | solution.py:442
  85.6 8.4 %collective-permute-start.34 = (bf16[2,48,1024]{2,1,0:T(8,128)(2,1)S(1)}, bf16[2,48,1024]{2,1,0:T(8,128)(2,1)S(1)}, u32[]{:S(2)}, u32[]{:S(2)}) collective-permute-start(bf16[2,48,1024]{2,1,0:T(8,128)(2,1)S(1)} %pad_maximum_fusion.1.refs_5_), channel_id=1, source_target_pairs={{0,4},{2,6},{4,0},{6,2},{8,12},{10,14},{12,8},{14,10},{16,20},{18,... | collective-permute-start | bytes 589832 | tf_op jit(solution)/shard_map/ppermute | solution.py:442
  88.2 5.8 %collective-permute-start.33 = (bf16[2,48,1024]{2,1,0:T(8,128)(2,1)S(1)}, bf16[2,48,1024]{2,1,0:T(8,128)(2,1)S(1)}, u32[]{:S(2)}, u32[]{:S(2)}) collective-permute-start(bf16[2,48,1024]{2,1,0:T(8,128)(2,1)S(1)} %pad_maximum_fusion.1.refs_5_), channel_id=1, source_target_pairs={{0,2},{2,0},{4,6},{6,4},{8,10},{10,8},{12,14},{14,12},{16,18},{18,... | collective-permute-start | bytes 589832 | tf_op jit(solution)/shard_map/ppermute | solution.py:442
  (7 other events, 25.4 us)
